TPU v7x, 128 devices: a whole 4x4x4 slice. The times are simulated.
128 devices in a mesh: dom: 32 (over z, x, core), rep: 4 (over y).
Axes of the slice: x: 4, y: 4, z: 4, core: 2. Of those that a mesh axis runs over, the one named last changes fastest.
Arguments:
- features: bfloat16 [98304, 512], P('dom', 'rep'), may hold values from -6 to 6
- stale_features: bfloat16 [98304, 512], P('dom', 'rep'), may hold values from -6 to 6
- grad_output: bfloat16 [98304, 512], P('dom', 'rep'), may hold values from -6 to 6
- w_neigh: bfloat16 [512, 512], replicated, may hold values from -0.25 to 0.25
- w_self: bfloat16 [512, 512], replicated, may hold values from -0.25 to 0.25
- adj_tiles: bfloat16 [32, 24, 20, 128, 128], P('dom'), may hold values from -0.125 to 0.125
- tile_cols: int32 [32, 24, 20], P('dom'), may hold values from 0 to 119
- send_idx: int32 [32, 32, 384], P('dom'), may hold values from 0 to 3071
- counts: int32 [32, 32], P('dom'), may hold values from 192 to 384, as said below
Outputs:
- out: bfloat16 [98304, 512], P('dom', 'rep')
- grad_input: bfloat16 [98304, 512], P('dom', 'rep')
- grad_stale: float32 [98304, 512], P('dom', 'rep')
- grad_neigh: float32 [512, 512], P('rep')
- grad_self: float32 [512, 512], P('rep')
Inputs may be any that keep to these rules, and one draw needn't show every extreme that they name: `counts`: every partition sends exactly 384 live rows to at least one peer; slots at or past the count hold arbitrary rows and are ignored.
All inputs are finite; a program needn't handle non-finite values.
Results may differ from a plain program's by a relative error of at most 0.02.
Values may be sent and summed in bfloat16 or wider, within the bound.
No kernel may reach another device: no remote copies, remote signals or barrier semaphores. Data moves between devices by JAX's collectives and lax.ppermute only.
A program may use at most 192 MiB of HBM per device.

v0:
```python
import math

import jax
import jax.numpy as jnp
from jax import lax
from jax.sharding import PartitionSpec as P

TILE = 128
B = 384


def gelu_tanh(value):
    return jax.nn.gelu(value, approximate=True)


def per_device(
    features, stale_features, grad_output, w_neigh, w_self, adj_tiles, tile_cols, send_idx, counts
):
    dom_count = lax.axis_size("dom")
    row_count, col_width = features.shape
    col_tiles = (row_count + dom_count * B) // TILE
    row_tiles = row_count // TILE
    send_list = send_idx[0]
    live_slots = jnp.arange(B, dtype=jnp.int32)[None, :] < counts[0][:, None]
    chosen = stale_features[send_list]
    packed = jnp.where(live_slots[:, :, None], chosen, jnp.zeros_like(chosen))
    halo_rows = lax.all_to_all(packed, "dom", split_axis=0, concat_axis=0, tiled=True)
    extended = jnp.concatenate([features, halo_rows.reshape(dom_count * B, col_width)], axis=0)
    block_ids = tile_cols[0]
    blocks = adj_tiles[0]
    tile_count = block_ids.shape[1]
    flat_ids = block_ids.reshape(-1)
    selector = (flat_ids[:, None] == jnp.arange(col_tiles, dtype=jnp.int32)[None, :]).astype(
        jnp.bfloat16
    )
    picked = jnp.dot(
        selector, extended.reshape(col_tiles, TILE * col_width), preferred_element_type=jnp.float32
    )
    picked = picked.astype(jnp.bfloat16).reshape(row_tiles, tile_count, TILE, col_width)
    aggregate = jnp.einsum("rtij,rtjf->rif", blocks, picked, preferred_element_type=jnp.float32)
    aggregate = aggregate.reshape(row_count, col_width).astype(jnp.bfloat16)
    share = lax.axis_index("rep")
    neigh_rows = lax.dynamic_slice_in_dim(w_neigh, share * col_width, col_width, 0)
    self_rows = lax.dynamic_slice_in_dim(w_self, share * col_width, col_width, 0)
    agg_full, feat_full = (
        lax.all_gather(aggregate, "rep", axis=1, tiled=True),
        lax.all_gather(features, "rep", axis=1, tiled=True),
    )
    neigh_cols = lax.dynamic_slice_in_dim(w_neigh, share * col_width, col_width, 1)
    self_cols = lax.dynamic_slice_in_dim(w_self, share * col_width, col_width, 1)
    pre_act = jnp.dot(agg_full, neigh_cols, preferred_element_type=jnp.float32) + jnp.dot(
        feat_full, self_cols, preferred_element_type=jnp.float32
    )
    activated, pullback = jax.vjp(gelu_tanh, pre_act)
    grad_pre = pullback(grad_output.astype(jnp.float32))[0].astype(jnp.bfloat16)
    grad_full = lax.all_gather(grad_pre, "rep", axis=1, tiled=True)
    contract_rows = (((0,), (0,)), ((), ()))
    contract_cols = (((1,), (1,)), ((), ()))
    part_neigh = lax.dot_general(
        aggregate, grad_full, contract_rows, preferred_element_type=jnp.float32
    )
    part_self = lax.dot_general(
        features, grad_full, contract_rows, preferred_element_type=jnp.float32
    )
    grad_neigh, grad_self = (
        lax.psum(part_neigh.astype(jnp.bfloat16), "dom").astype(jnp.float32),
        lax.psum(part_self.astype(jnp.bfloat16), "dom").astype(jnp.float32),
    )
    grad_agg = lax.dot_general(
        grad_full, neigh_rows, contract_cols, preferred_element_type=jnp.float32
    ).astype(jnp.bfloat16)
    grad_direct = lax.dot_general(
        grad_full, self_rows, contract_cols, preferred_element_type=jnp.float32
    )
    contrib = jnp.einsum(
        "rtij,rif->rtjf",
        blocks,
        grad_agg.reshape(row_tiles, TILE, col_width),
        preferred_element_type=jnp.float32,
    )
    flat_terms = contrib.reshape(-1, TILE * col_width)
    upper_part = flat_terms.astype(jnp.bfloat16)
    lower_part = (flat_terms - upper_part.astype(jnp.float32)).astype(jnp.bfloat16)
    grad_ext = lax.dot_general(
        selector, upper_part, contract_rows, preferred_element_type=jnp.float32
    )
    grad_ext = grad_ext + lax.dot_general(
        selector, lower_part, contract_rows, preferred_element_type=jnp.float32
    )
    grad_ext = grad_ext.reshape(-1, col_width)
    grad_input = (grad_direct + grad_ext[:row_count]).astype(jnp.bfloat16)
    grad_halo = grad_ext[row_count:].reshape(dom_count, B, col_width).astype(jnp.bfloat16)
    returned = lax.all_to_all(grad_halo, "dom", split_axis=0, concat_axis=0, tiled=True)
    returned = jnp.where(live_slots[:, :, None], returned, jnp.zeros_like(returned))
    group_size = math.gcd(dom_count, 8)
    group_count = dom_count // group_size
    grouped_rows = returned.reshape(group_count, group_size * B, col_width)
    grouped_ids = send_list.reshape(group_count, group_size * B)
    row_range = jnp.arange(row_count, dtype=jnp.int32)

    def add_group(total, pieces):
        index_group, value_group = pieces
        onehot = (index_group[:, None] == row_range[None, :]).astype(jnp.bfloat16)
        return (
            total
            + lax.dot_general(
                onehot, value_group, contract_rows, preferred_element_type=jnp.float32
            ),
            None,
        )

    grad_stale, _ = lax.scan(
        add_group, jnp.zeros((row_count, col_width), jnp.float32), (grouped_ids, grouped_rows)
    )
    return (activated.astype(jnp.bfloat16), grad_input, grad_stale, grad_neigh, grad_self)


def solution(mesh):
    in_specs = (
        P("dom", "rep"),
        P("dom", "rep"),
        P("dom", "rep"),
        P(),
        P(),
        P("dom", None, None, None, None),
        P("dom", None, None),
        P("dom", None, None),
        P("dom", None),
    )
    out_specs = (P("dom", "rep"), P("dom", "rep"), P("dom", "rep"), P("rep", None), P("rep", None))
    return jax.shard_map(
        per_device, mesh=mesh, in_specs=in_specs, out_specs=out_specs, check_vma=False
    )
```

profile of v0, /device:TPU:1, one launch (start us, length us, event | category | flops | bytes accessed | tf_op | source)
XLA Modules:
  0.0 617.9 jit_solution(11612865641649918477)
XLA Ops:
  8.8 43.7 %gather_fusion = bf16[12288,128]{1,0:T(8,128)(2,1)} fusion(bf16[3072,128]{1,0:T(8,128)(2,1)S(1)} %copy-done, s32[12288]{0:T(1024)S(1)} %broadcast_clamp_fusion), kind=kCustom, calls=%fused_computation | custom fusion | bytes 6340608 | tf_op jit(solution)/shard_map/gather | solution.py:25
  52.5 7.2 %broadcast_select_fusion.1 = bf16[32,384,128]{2,1,0:T(8,128)(2,1)} fusion(bf16[32,384,128]{2,1,0:T(8,128)(2,1)} %bitcast.73, pred[32,384]{1,0:T(8,128)(4,1)S(1)} %iota_compare_fusion.8), kind=kLoop, calls=%fused_computation.30 | loop fusion | flops 1572864 | bytes 6303744 | tf_op jit(solution)/shard_map/jit(_where)/select_n | solution.py:26
  59.6 9.6 %all-to-all-start = ((bf16[32,384,128]{2,1,0:T(8,128)(2,1)}), bf16[32,384,128]{2,1,0:T(8,128)(2,1)}, u32[]{:S(2)}, u32[]{:S(2)}) async-start(bf16[32,384,128]{2,1,0:T(8,128)(2,1)} %broadcast_select_fusion.1), calls=%async_computation | async-start | bytes 6291456 | tf_op jit(solution)/shard_map/all_to_all | solution.py:27
  69.5 39.0 %all-to-all-done = bf16[32,384,128]{2,1,0:T(8,128)(2,1)} async-done(((bf16[32,384,128]{2,1,0:T(8,128)(2,1)}), bf16[32,384,128]{2,1,0:T(8,128)(2,1)}, u32[]{:S(2)}, u32[]{:S(2)}) %all-to-all-start) | async-done | bytes 3145760 | tf_op jit(solution)/shard_map/all_to_all | solution.py:27
  114.1 7.1 %reshape.93 = bf16[120,16384]{1,0:T(8,128)(2,1)} reshape(bf16[15360,128]{1,0:T(8,128)(2,1)} %pad_maximum_fusion) | data formatting | bytes 7864320 | tf_op jit(solution)/shard_map/reshape | solution.py:37
  121.2 6.7 %fusion.18 = bf16[60,8,128,128]{3,1,2,0:T(8,128)(2,1)S(1)} fusion(bf16[120,16384]{1,0:T(8,128)(2,1)} %reshape.93, s32[480]{0:T(512)S(1)} %eq.30), kind=kOutput, calls=%fused_computation.21 | convolution fusion | flops 1895358720 | bytes 19662720 | tf_op jit(solution)/shard_map/dot_general | solution.py:36
  127.9 8.5 %copy.27 = bf16[60,8,128,128]{3,2,1,0:T(8,128)(2,1)} copy(bf16[60,8,128,128]{3,1,2,0:T(8,128)(2,1)S(1)} %fusion.18) | data formatting | bytes 31457280
  136.4 15.1 %bitcast_convert_fusion.2 = bf16[24,128,128]{1,2,0:T(8,128)(2,1)} fusion(bf16[24,20,128,128]{3,2,1,0:T(8,128)(2,1)} %bitcast.72, bf16[1,24,20,128,128]{4,3,2,1,0:T(8,128)(2,1)} %param.16), kind=kOutput, calls=%fused_computation.45 | convolution fusion | flops 2013659136 | bytes 32243712 | tf_op jit(solution)/shard_map/rtij,rtjf->rif/dot_general | solution.py:40
  152.6 40.6 %all-gather.4.cloned.1.call-done = bf16[3072,512]{1,0:T(8,128)(2,1)} async-done(((bf16[3072,128]{1,0:T(8,128)(2,1)}), bf16[3072,512]{1,0:T(8,128)(2,1)}) %all-gather.4.cloned.1.call-update) | async-done | bytes 3145744 | tf_op jit(solution)/shard_map/all_gather | solution.py:46
  196.1 43.0 %all-gather.6.cloned.1.call-done = bf16[3072,512]{1,0:T(8,128)(2,1)} async-done(((bf16[3072,128]{1,0:T(8,128)(2,1)}), bf16[3072,512]{1,0:T(8,128)(2,1)}) %all-gather.6.cloned.1.call-update) | async-done | bytes 3145744 | tf_op jit(solution)/shard_map/all_gather | solution.py:47
  243.7 44.3 %all-gather.8.cloned.1.call-done = bf16[3072,512]{1,0:T(8,128)(2,1)} async-done(((bf16[3072,128]{1,0:T(8,128)(2,1)}), bf16[3072,512]{1,0:T(8,128)(2,1)}) %all-gather.8.cloned.1.call-update) | async-done | bytes 3145744 | tf_op jit(solution)/shard_map/all_gather | solution.py:56
  290.9 20.1 %fusion.15 = f32[24,20,128,128]{2,3,1,0:T(8,128)} fusion(bf16[24,128,128,1]{2,1,3,0:T(8,128)(2,1)S(1)} %bitcast.74, bf16[1,24,20,128,128]{4,3,2,1,0:T(8,128)(2,1)} %param.16), kind=kOutput, calls=%fused_computation.20 | convolution fusion | flops 2013265920 | bytes 47972352 | tf_op jit(solution)/shard_map/rtij,rif->rtjf/dot_general | solution.py:75
  311.0 31.3 %copy.20 = f32[24,20,128,128]{3,2,1,0:T(8,128)} copy(f32[24,20,128,128]{2,3,1,0:T(8,128)} %fusion.15) | data formatting | bytes 62914560 | tf_op jit(solution)/shard_map/rtij,rif->rtjf/dot_general | solution.py:75
  342.3 31.3 %fusion.9 = f32[120,16384]{1,0:T(8,128)} fusion(f32[60,8,128,128]{3,2,1,0:T(8,128)} %bitcast.70, s32[480]{0:T(512)S(1)} %eq.30), kind=kOutput, calls=%fused_computation.14 | convolution fusion | flops 1887494400 | bytes 39323520 | tf_op jit(solution)/shard_map/dot_general | solution.py:84
  373.6 34.6 %convolution_add_fusion = f32[120,16384]{1,0:T(8,128)} fusion(f32[120,16384]{1,0:T(8,128)} %fusion.9, f32[60,8,128,128]{3,2,1,0:T(8,128)} %bitcast.71, s32[480]{0:T(512)S(1)} %eq.30), kind=kOutput, calls=%fused_computation.15 | convolution fusion | flops 1920917760 | bytes 47187840 | tf_op jit(solution)/shard_map/dot_general | solution.py:87
  412.9 5.8 convert_element_type.69
  418.8 8.7 %all-to-all-start.1 = ((bf16[32,384,128]{2,1,0:T(8,128)(2,1)}), bf16[32,384,128]{2,1,0:T(8,128)(2,1)}, u32[]{:S(2)}, u32[]{:S(2)}) async-start(bf16[32,384,128]{2,1,0:T(8,128)(2,1)} %convert_element_type.69), calls=%async_computation.1 | async-start | bytes 6291456 | tf_op jit(solution)/shard_map/all_to_all | solution.py:93
  439.2 110.7 %all-reduce.3.cloned.1.call-done = (bf16[128,512]{0,1:T(8,128)(2,1)}, bf16[128,512]{1,0:T(8,128)(2,1)}) async-done(((bf16[128,512]{0,1:T(8,128)(2,1)}, bf16[128,512]{1,0:T(8,128)(2,1)}), (bf16[128,512]{0,1:T(8,128)(2,1)}, bf16[128,512]{1,0:T(8,128)(2,1)})) %all-reduce.3.cloned.1.call-update) | async-done | bytes 262160 | tf_op jit(solution)/shard_map/psum | solution.py:67
  553.3 7.3 %broadcast_select_fusion = bf16[32,384,128]{2,1,0:T(8,128)(2,1)} fusion(bf16[32,384,128]{2,1,0:T(8,128)(2,1)} %all-to-all-done.1, pred[32,384]{1,0:T(8,128)(4,1)S(1)} %iota_compare_fusion.8), kind=kLoop, calls=%fused_computation.29 | loop fusion | flops 1572864 | bytes 6303744 | tf_op jit(solution)/shard_map/jit(_where)/select_n | solution.py:94
  560.5 48.7 %while.11 = (s32[]{:T(128)}, f32[3072,128]{1,0:T(8,128)S(1)}, s32[4,3072]{1,0:T(4,128)S(1)}, bf16[4,3072,128]{2,1,0:T(8,128)(2,1)}, s32[]{:T(128)}, /*index=5*/s32[]{:T(128)}) while((s32[]{:T(128)}, f32[3072,128]{1,0:T(8,128)S(1)}, s32[4,3072]{1,0:T(4,128)S(1)}, bf16[4,3072,128]{2,1,0:T(8,128)(2,1)}, s32[]{:T(128)}, ...), condition=%wide.region_1.2_spmd.clone, body=%wide.region_0.1_spmd.clone.sunk | while | flops 2426142720 | bytes 3969119 | solution.py:112
  560.6 12.1 %fusion.60 = f32[3072,128]{1,0:T(8,128)S(1)} fusion(s32[3072]{0:T(1024)S(1)} %bitcast.78, f32[3072,128]{1,0:T(8,128)S(1)} %get-tuple-element.104, bf16[4,3072,128]{2,1,0:T(8,128)(2,1)} %get-tuple-element.112, s32[]{:T(128)S(6)} %copy.37, pred[]{:T(512)S(6)} %compare.3), kind=kOutput, calls=%fused_computation.5.clone.1 | convolution fusion | flops 2426142720 | bytes 3944453 | tf_op jit(solution)/shard_map/while/body/eval_jaxpr/dot_general | solution.py:106
  572.8 12.1 %fusion.60 = f32[3072,128]{1,0:T(8,128)S(1)} fusion(s32[3072]{0:T(1024)S(1)} %bitcast.78, f32[3072,128]{1,0:T(8,128)S(1)} %get-tuple-element.104, bf16[4,3072,128]{2,1,0:T(8,128)(2,1)} %get-tuple-element.112, s32[]{:T(128)S(6)} %copy.37, pred[]{:T(512)S(6)} %compare.3), kind=kOutput, calls=%fused_computation.5.clone.1 | convolution fusion | flops 2426142720 | bytes 3944453 | tf_op jit(solution)/shard_map/while/body/eval_jaxpr/dot_general | solution.py:106
  584.9 12.1 %fusion.60 = f32[3072,128]{1,0:T(8,128)S(1)} fusion(s32[3072]{0:T(1024)S(1)} %bitcast.78, f32[3072,128]{1,0:T(8,128)S(1)} %get-tuple-element.104, bf16[4,3072,128]{2,1,0:T(8,128)(2,1)} %get-tuple-element.112, s32[]{:T(128)S(6)} %copy.37, pred[]{:T(512)S(6)} %compare.3), kind=kOutput, calls=%fused_computation.5.clone.1 | convolution fusion | flops 2426142720 | bytes 3944453 | tf_op jit(solution)/shard_map/while/body/eval_jaxpr/dot_general | solution.py:106
  597.1 12.1 %fusion.60 = f32[3072,128]{1,0:T(8,128)S(1)} fusion(s32[3072]{0:T(1024)S(1)} %bitcast.78, f32[3072,128]{1,0:T(8,128)S(1)} %get-tuple-element.104, bf16[4,3072,128]{2,1,0:T(8,128)(2,1)} %get-tuple-element.112, s32[]{:T(128)S(6)} %copy.37, pred[]{:T(512)S(6)} %compare.3), kind=kOutput, calls=%fused_computation.5.clone.1 | convolution fusion | flops 2426142720 | bytes 3944453 | tf_op jit(solution)/shard_map/while/body/eval_jaxpr/dot_general | solution.py:106
  (60 shorter events, 40.4 us)
Async XLA Ops:
  7.2 1.7 copy-start
  59.6 9.7 %copy-start.9 = (s32[1,24,20]{1,0,2:T(1,128)S(1)}, s32[1,24,20]{1,0,2:T(1,128)}, u32[]{:S(2)}) copy-start(s32[1,24,20]{1,0,2:T(1,128)} %param.17) | copy-start | bytes 5764
  59.6 48.8 %copy-start.5 = (bf16[3072,128]{1,0:T(8,128)(2,1)S(1)}, bf16[3072,128]{1,0:T(8,128)(2,1)}, u32[]{:S(2)}) copy-start(bf16[3072,128]{1,0:T(8,128)(2,1)} %param.11) | copy-start | bytes 2359300
  59.6 48.8 %all-to-all-start = ((bf16[32,384,128]{2,1,0:T(8,128)(2,1)}), bf16[32,384,128]{2,1,0:T(8,128)(2,1)}, u32[]{:S(2)}, u32[]{:S(2)}) async-start(bf16[32,384,128]{2,1,0:T(8,128)(2,1)} %broadcast_select_fusion.1), calls=%async_computation | async-start | bytes 6291456 | tf_op jit(solution)/shard_map/all_to_all | solution.py:27
  69.3 123.9 %all-gather.4.cloned.1.call-start = ((), (), s32[]{:S(2)}) async-start(), calls=%async_computation.2 | async-start | bytes 3932160 | tf_op jit(solution)/shard_map/all_gather | solution.py:46
  136.4 56.8 %copy-start.8 = (bf16[512,512]{1,0:T(8,128)(2,1)S(1)}, bf16[512,512]{1,0:T(8,128)(2,1)}, u32[]{:S(2)}) copy-start(bf16[512,512]{1,0:T(8,128)(2,1)} %param.14) | copy-start | bytes 1572868
  151.6 87.5 %all-gather.6.cloned.1.call-start = ((), (), s32[]{:S(2)}) async-start(), calls=%async_computation.3 | async-start | bytes 3932160 | tf_op jit(solution)/shard_map/all_gather | solution.py:47
  152.3 135.7 %all-gather.8.cloned.1.call-start = ((), (), s32[]{:S(2)}) async-start(), calls=%async_computation.4 | async-start | bytes 3932160 | tf_op jit(solution)/shard_map/all_gather | solution.py:56
  152.6 86.5 %copy-start.10 = (bf16[3072,128]{1,0:T(8,128)(2,1)S(1)}, bf16[3072,128]{1,0:T(8,128)(2,1)}, u32[]{:S(2)}) copy-start(bf16[3072,128]{1,0:T(8,128)(2,1)} %param.13) | copy-start | bytes 2359300
  418.8 8.8 %copy-start.7 = (s32[1,32,384]{2,1,0:T(8,128)S(1)}, s32[1,32,384]{2,1,0:T(8,128)}, u32[]{:S(2)}) copy-start(s32[1,32,384]{2,1,0:T(8,128)} %param.18) | copy-start | bytes 147460
  418.8 134.5 %all-to-all-start.1 = ((bf16[32,384,128]{2,1,0:T(8,128)(2,1)}), bf16[32,384,128]{2,1,0:T(8,128)(2,1)}, u32[]{:S(2)}, u32[]{:S(2)}) async-start(bf16[32,384,128]{2,1,0:T(8,128)(2,1)} %convert_element_type.69), calls=%async_computation.1 | async-start | bytes 6291456 | tf_op jit(solution)/shard_map/all_to_all | solution.py:93
  427.5 1.4 slice-start
  427.5 122.4 %all-reduce.3.cloned.1.call-start = ((), (), s32[]{:S(2)}) async-start(), calls=%async_computation.5 | async-start | bytes 524288 | tf_op jit(solution)/shard_map/psum | solution.py:67
  427.6 2.7 copy-start.6
  428.9 5.1 copy-start.4
  430.3 3.7 copy-start.2
  434.0 1.4 copy-start.3
  553.3 7.3 %copy-start.11 = (f32[3072,128]{1,0:T(8,128)S(1)}, f32[3072,128]{1,0:T(8,128)}, u32[]{:S(2)}) copy-start(f32[3072,128]{1,0:T(8,128)} %custom-call) | copy-start | bytes 4718596
  609.3 1.1 copy-start.12
  609.3 1.7 copy-start.1
Sparse Core Ops, SparseCore 0:
  151.7 41.4 all-gather.3
  194.8 44.1 all-gather.5
  243.8 44.1 all-gather.7
  435.5 114.4 all-reduce.2
where the time goes:
time: 627 us; the launch traced here: 618 us
  waiting for transfers between devices  278 us (44%)
  matrix products  175 us (28%)
  local copies, waits for them, and re-layouts  108 us (17%)
  other arithmetic  23.3 us (4%)
  starting transfers between devices  18.7 us (3%)
  between operations  14.3 us (2%)
    psum x1, waiting for transfers between devices, per_device(): lax.psum(part_self.astype(jnp.bfloat16), 'dom').astype(jnp.float32)  111 us
    dot_general x4, matrix products, add_group(): lax.dot_general(onehot, value_group, contract_rows, preferred_element_typ...  48.6 us
    all_gather x1, waiting for transfers between devices, per_device(): grad_full = lax.all_gather(grad_pre, 'rep', axis=1, tiled=True)  44.3 us
    gather x1, local copies, waits for them, and re-layouts, per_device(): chosen = stale_features[send_list]  43.7 us
    all_gather x1, waiting for transfers between devices, per_device(): lax.all_gather(features, 'rep', axis=1, tiled=True)  43 us
    all_gather x1, waiting for transfers between devices, per_device(): lax.all_gather(aggregate, 'rep', axis=1, tiled=True)  40.6 us
    all_to_all x1, waiting for transfers between devices, per_device(): lax.all_to_all(packed, 'dom', split_axis=0, concat_axis=0, tiled=True)  39 us
    dot_general x1, matrix products, per_device(): lax.dot_general(selector, lower_part, contract_rows, preferred_element_ty...  34.6 us
  transfers between devices with their start and end apart: 6, of which 5 were waited for; matrix products, arithmetic and copies ran while one was open for 3% of the time, Pallas kernels for 0%

commit v1 on v0

v1 whole, which is shorter than its diff:
```python
import functools

import jax
import jax.numpy as jnp
from jax import lax
from jax.experimental import pallas as pl
from jax.experimental.pallas import tpu as pltpu
from jax.sharding import PartitionSpec as P

TILE = 128
B = 384
CHUNKS = B // TILE
LOW = 512
F32 = jnp.float32
BF16 = jnp.bfloat16
NT = (((1,), (1,)), ((), ()))
TN = (((0,), (0,)), ((), ()))


def params(mib):
    return pltpu.CompilerParams(vmem_limit_bytes=mib * 1024 * 1024)


def cost(flops, nbytes, trans=0):
    return pl.CostEstimate(flops=int(flops), bytes_accessed=int(nbytes), transcendentals=int(trans))


def shape(dims, dtype):
    return jax.ShapeDtypeStruct(dims, dtype)


def turned(block):
    return jnp.transpose(block.astype(F32))


def gather_kernel(ids_ref, table_ref, out_ref, flipped):
    rows = table_ref.shape[0]
    groups = rows // LOW

    @pl.when(pl.program_id(0) == 0)
    def _():
        for g in range(groups):
            for k in range(LOW // TILE):
                block = table_ref[g * LOW + k * TILE : g * LOW + (k + 1) * TILE, :]
                flipped[g * TILE : (g + 1) * TILE, k * TILE : (k + 1) * TILE] = turned(block).astype(
                    BF16
                )

    spot = lax.broadcasted_iota(jnp.int32, (LOW, LOW), 0)
    for n in range(ids_ref.shape[1]):
        ids = ids_ref[0, n : n + 1, :]
        onehot = jnp.where(spot == (ids & (LOW - 1)), 1.0, 0.0).astype(BF16)
        found = jnp.dot(flipped[...], onehot, preferred_element_type=F32)
        total = jnp.zeros((TILE, LOW), F32)
        for g in range(groups):
            here = (ids >= g * LOW) & (ids < (g + 1) * LOW)
            total = jnp.where(here, found[g * TILE : (g + 1) * TILE, :], total)
        total = total.astype(BF16)
        for p in range(LOW // TILE):
            out_ref[n * (LOW // TILE) + p] = total[:, p * TILE : (p + 1) * TILE]


def gather_rows(ids, table):
    steps, parts, width = ids.shape
    blocks = parts * width // TILE
    rows, cols = table.shape
    return pl.pallas_call(
        gather_kernel,
        grid=(steps,),
        in_specs=[
            pl.BlockSpec((1, parts, width), lambda i: (i, 0, 0)),
            pl.BlockSpec((rows, cols), lambda i: (0, 0)),
        ],
        out_specs=pl.BlockSpec((blocks, TILE, TILE), lambda i: (i, 0, 0)),
        out_shape=shape((steps * blocks, TILE, TILE), BF16),
        scratch_shapes=[pltpu.VMEM((rows // LOW * TILE, LOW), BF16)],
        compiler_params=params(32),
        cost_estimate=cost(2 * ids.size * rows * cols, 4e6),
        name="gather_rows",
    )(ids, table)


def exchange(pieces):
    n = len(pieces)
    return [pieces[0]] + [
        lax.ppermute(pieces[s], "rep", [(i, (i + s) % n) for i in range(n)]) for s in range(1, n)
    ]


def relative(received):
    n = len(received)
    return [received[(n - j) % n] for j in range(n)]


def prep_kernel(me_ref, feat_ref, up_ref, wn_ref, ws_ref, after_ref, own_ref, wn_out, ws_out, *pieces):
    del after_ref
    step = pl.program_id(0)
    n = len(pieces)
    for k in range(own_ref.shape[0]):
        own_ref[k] = turned(feat_ref[k * TILE : (k + 1) * TILE, :]).astype(BF16)
    for j, piece in enumerate(pieces):
        column = pl.multiple_of(lax.rem(me_ref[0] + j, n) * TILE, TILE)
        wn_out[:, j * TILE : (j + 1) * TILE] = wn_ref[:, pl.ds(column, TILE)]
        ws_out[:, j * TILE : (j + 1) * TILE] = ws_ref[:, pl.ds(column, TILE)]

        @pl.when(step == j)
        def _():
            piece[0] = feat_ref[...]
            piece[1] = up_ref[...]


def prep(me, features, upstream, wn, ws, after, n):
    rows, width = features.shape
    share = rows // n
    full = wn.shape[0]
    chunk = pl.BlockSpec((share, width), lambda i, me: (lax.rem(me[0] + i, n), 0))
    weight = pl.BlockSpec((width, full), lambda i, me: (lax.rem(me[0] + i, n), 0))
    placed = pl.BlockSpec((width, full), lambda i, me: (i, 0))
    own, wn, ws, *pieces = pl.pallas_call(
        prep_kernel,
        grid_spec=pltpu.PrefetchScalarGridSpec(
            num_scalar_prefetch=1,
            grid=(n,),
            in_specs=[chunk, chunk, weight, weight, pl.BlockSpec(memory_space=pl.ANY)],
            out_specs=[
                pl.BlockSpec(
                    (share // TILE, TILE, TILE), lambda i, me: (lax.rem(me[0] + i, n), 0, 0)
                ),
                placed,
                placed,
            ]
            + [pl.BlockSpec((2, share, width), lambda i, me: (0, 0, 0))] * n,
        ),
        out_shape=[
            shape((rows // TILE, TILE, TILE), BF16),
            shape((full, full), BF16),
            shape((full, full), BF16),
        ]
        + [shape((2, share, width), BF16)] * n,
        compiler_params=params(32),
        cost_estimate=cost(1e10, 6e6),
        name="prep",
    )(me, features, upstream, wn, ws, after)
    return own, wn, ws, pieces


def spmm_kernel(me_ref, pos_ref, adj_ref, *refs, n):
    parts, outs, (ext, sems) = refs[: -n - 2], refs[-n - 2 : -2], refs[-2:]
    chunk, part = pl.program_id(0), pl.program_id(1)
    blocks, per_row = adj_ref.shape[:2]

    @pl.when((chunk == 0) & (part == 0))
    def _():
        copies, start = [], 0
        for k, source in enumerate(parts):
            size = source.shape[0]
            copies.append(pltpu.make_async_copy(source, ext.at[pl.ds(start, size)], sems.at[k]))
            start += size
        for copy in copies:
            copy.start()
        for copy in copies:
            copy.wait()

    first = (lax.rem(me_ref[0] + chunk, n) * pl.num_programs(1) + part) * blocks
    done = []
    for r in range(blocks):
        base = (first + r) * per_row
        total = None
        for t in range(0, per_row, 2):
            left = jnp.concatenate([adj_ref[r, t], adj_ref[r, t + 1]], axis=1)
            right = jnp.concatenate([ext[pos_ref[base + t]], ext[pos_ref[base + t + 1]]], axis=1)
            term = lax.dot_general(left, right, NT, preferred_element_type=F32)
            total = term if total is None else total + term
        done.append(total.astype(BF16))
    done = jnp.concatenate(done, axis=0)
    place = pl.ds(pl.multiple_of(part * blocks * TILE, blocks * TILE), blocks * TILE)
    for j, out in enumerate(outs):

        @pl.when(chunk == j)
        def _():
            out[place, :] = done


def spmm(me, pos, adj, parts, n):
    row_tiles, per_row = adj.shape[:2]
    blocks = 3
    inner = row_tiles // n // blocks
    share = row_tiles // n * TILE
    col_tiles = sum(p.shape[0] for p in parts)
    return pl.pallas_call(
        functools.partial(spmm_kernel, n=n),
        grid_spec=pltpu.PrefetchScalarGridSpec(
            num_scalar_prefetch=2,
            grid=(n, inner),
            in_specs=[
                pl.BlockSpec(
                    (blocks, per_row, TILE, TILE),
                    lambda i, k, me, pos: (lax.rem(me[0] + i, n) * inner + k, 0, 0, 0),
                )
            ]
            + [pl.BlockSpec(memory_space=pl.ANY)] * len(parts),
            out_specs=[pl.BlockSpec((share, TILE), lambda i, k, me, pos: (0, 0))] * n,
            scratch_shapes=[
                pltpu.VMEM((col_tiles, TILE, TILE), BF16),
                pltpu.SemaphoreType.DMA((len(parts),)),
            ],
        ),
        out_shape=[shape((share, TILE), BF16)] * n,
        compiler_params=params(52),
        cost_estimate=cost(2 * row_tiles * per_row * TILE**3 * 2, 2e7),
        name="spmm",
    )(me, pos, adj, *parts)


def joined(refs):
    return jnp.concatenate([ref[...] for ref in refs], axis=1)


def dense_kernel(*refs, n):
    agg, both, (wn_ref, ws_ref), rest = refs[:n], refs[n : 2 * n], refs[2 * n : 2 * n + 2], refs[2 * n + 2 :]
    ga, (act_ref, gp_ref) = rest[:n], rest[n:]
    wn = wn_ref[...]
    v = jnp.dot(joined(agg), wn, preferred_element_type=F32) + jnp.dot(
        joined([ref.at[0] for ref in both]), ws_ref[...], preferred_element_type=F32
    )
    root = 0.7978845608028654
    square = v * v
    t = jnp.tanh(root * v * (1.0 + 0.044715 * square))
    half = 0.5 * (1.0 + t)
    slope = half + 0.5 * v * (1.0 - t * t) * (root * (1.0 + 0.134145 * square))
    gp = (joined([ref.at[1] for ref in both]).astype(F32) * slope).astype(BF16)
    act_ref[...] = (v * half).astype(BF16)
    gp_ref[...] = gp
    back = lax.dot_general(wn, gp, NT, preferred_element_type=F32).astype(BF16)
    width = back.shape[0] // n
    for q in range(n):
        ga[q][...] = back[q * width : (q + 1) * width, :]


def dense(agg, both, wn, ws):
    n = len(agg)
    rows, width = agg[0].shape
    full = n * width
    size = 256
    weight = pl.BlockSpec((full, full), lambda i: (0, 0))
    whole = pl.BlockSpec((size, full), lambda i: (i, 0))
    results = pl.pallas_call(
        functools.partial(dense_kernel, n=n),
        grid=(rows // size,),
        in_specs=[pl.BlockSpec((size, width), lambda i: (i, 0))] * n
        + [pl.BlockSpec((2, size, width), lambda i: (0, i, 0))] * n
        + [weight, weight],
        out_specs=[pl.BlockSpec((width, size), lambda i: (0, i))] * n + [whole, whole],
        out_shape=[shape((width, rows), BF16)] * n + [shape((rows, full), BF16)] * 2,
        compiler_params=params(24),
        cost_estimate=cost(6 * rows * full * full, 7e6, rows * full),
        name="dense",
    )(*agg, *both, wn, ws)
    return results[:n], results[n], results[n + 1]


def wgrad_kernel(me_ref, *refs, n):
    agg, both, gp_ref, out_ref = refs[:n], refs[n : 2 * n], refs[2 * n], refs[2 * n + 1]
    gp = gp_ref[...]
    rows = out_ref.shape[2]
    width = agg[0].shape[1]
    for j in range(n):
        for kind, left in enumerate((agg[j][...], both[j][0])):
            term = lax.dot_general(left, gp, TN, preferred_element_type=F32).astype(BF16)
            for i in range(n):
                q = lax.rem(me_ref[0] + i, n)
                for k in range(width // rows):
                    at = (kind * (width // rows) + k) * n + q
                    out_ref[at, j] = term[k * rows : (k + 1) * rows, i * TILE : (i + 1) * TILE]


def wgrad(me, agg, both, gp, dom_count):
    n = len(agg)
    rows, width = agg[0].shape
    size = 2 * width * n // dom_count
    vmem = pl.BlockSpec(memory_space=pltpu.VMEM)
    return pl.pallas_call(
        functools.partial(wgrad_kernel, n=n),
        in_specs=[pl.BlockSpec(memory_space=pltpu.SMEM)] + [vmem] * (2 * n + 1),
        out_specs=vmem,
        out_shape=shape((dom_count, n, size, TILE), BF16),
        compiler_params=params(24),
        cost_estimate=cost(4 * rows * (n * width) ** 2, 4e6),
        name="wgrad",
    )(me, *agg, *both, gp)


def spmm_back_kernel(me_ref, pos_ref, adj_ref, *refs, n):
    ga, outs, (total, left_ref) = refs[:n], refs[n:-2], refs[-2:]
    chunk, part = pl.program_id(0), pl.program_id(1)
    blocks, per_row = adj_ref.shape[:2]

    @pl.when((chunk == 0) & (part == 0))
    def _():
        total[...] = jnp.zeros_like(total)

    for s in range(n):

        @pl.when((chunk == s) & (part == 0))
        def _():
            for k in range(left_ref.shape[0]):
                left_ref[k] = ga[s][:, k * blocks * TILE : (k + 1) * blocks * TILE]

    first = (lax.rem(me_ref[0] + n - chunk, n) * pl.num_programs(1) + part) * blocks
    for r in range(blocks):
        base = (first + r) * per_row
        left = left_ref[part, :, r * TILE : (r + 1) * TILE]
        for t in range(0, per_row, 2):
            right = jnp.concatenate([adj_ref[r, t], adj_ref[r, t + 1]], axis=1)
            both = jnp.dot(left, right, preferred_element_type=F32)
            total[pos_ref[base + t]] += both[:, :TILE]
            total[pos_ref[base + t + 1]] += both[:, TILE:]

    @pl.when((chunk == n - 1) & (part == pl.num_programs(1) - 1))
    def _():
        start = 0
        for out in outs:
            size = out.shape[0]
            out[...] = total[start : start + size].astype(out.dtype)
            start += size


def spmm_back(me, pos, adj, ga, sizes):
    n = len(ga)
    row_tiles, per_row = adj.shape[:2]
    rows = ga[0].shape[1]
    blocks = 3
    inner = row_tiles // n // blocks
    outs = [shape((size, TILE, TILE), F32 if i == 0 else BF16) for i, size in enumerate(sizes)]
    return pl.pallas_call(
        functools.partial(spmm_back_kernel, n=n),
        grid_spec=pltpu.PrefetchScalarGridSpec(
            num_scalar_prefetch=2,
            grid=(n, inner),
            in_specs=[
                pl.BlockSpec(
                    (blocks, per_row, TILE, TILE),
                    lambda i, k, me, pos: (lax.rem(me[0] + n - i, n) * inner + k, 0, 0, 0),
                )
            ]
            + [pl.BlockSpec((TILE, rows), lambda i, k, me, pos: (0, 0))] * n,
            out_specs=[
                pl.BlockSpec((size, TILE, TILE), lambda i, k, me, pos: (0, 0, 0)) for size in sizes
            ],
            scratch_shapes=[
                pltpu.VMEM((sum(sizes), TILE, TILE), F32),
                pltpu.VMEM((inner, TILE, blocks * TILE), BF16),
            ],
        ),
        out_shape=outs,
        compiler_params=params(48),
        cost_estimate=cost(2 * row_tiles * per_row * TILE**3 * 2, 2.2e7),
        name="spmm_back",
    )(me, pos, adj, *ga)


def late_kernel(act_ref, gp_ref, ws_ref, after_ref, *pieces):
    del after_ref
    direct = lax.dot_general(gp_ref[...], ws_ref[...], NT, preferred_element_type=F32).astype(BF16)
    for j, piece in enumerate(pieces):
        piece[0] = act_ref[:, j * TILE : (j + 1) * TILE]
        piece[1] = direct[:, j * TILE : (j + 1) * TILE]


def late(act, gp, ws, after, n):
    rows, full = act.shape
    size = 256
    share = pl.BlockSpec((size, full), lambda i: (i, 0))
    return pl.pallas_call(
        late_kernel,
        grid=(rows // size,),
        in_specs=[
            share,
            share,
            pl.BlockSpec((full, full), lambda i: (0, 0)),
            pl.BlockSpec(memory_space=pl.ANY),
        ],
        out_specs=[pl.BlockSpec((2, size, TILE), lambda i: (0, i, 0))] * n,
        out_shape=[shape((2, rows, TILE), BF16)] * n,
        compiler_params=params(24),
        cost_estimate=cost(1e10, 6e6),
        name="late",
    )(act, gp, ws, after)


def finish_kernel(me_ref, ext_ref, *refs):
    pieces, (out_ref, grad_ref) = refs[:-2], refs[-2:]
    for s, piece in enumerate(pieces):

        @pl.when(pl.program_id(0) == s)
        def _():
            out_ref[...] = piece[0]
            for k in range(ext_ref.shape[0]):
                rows = slice(k * TILE, (k + 1) * TILE)
                total = piece[1, rows, :].astype(F32) + jnp.transpose(ext_ref[k])
                grad_ref[rows, :] = total.astype(BF16)


def finish(me, ext, pieces):
    n = len(pieces)
    share = pieces[0].shape[1]
    placed = pl.BlockSpec((share, TILE), lambda i, me: (lax.rem(me[0] + n - i, n), 0))
    return pl.pallas_call(
        finish_kernel,
        grid_spec=pltpu.PrefetchScalarGridSpec(
            num_scalar_prefetch=1,
            grid=(n,),
            in_specs=[
                pl.BlockSpec(
                    (share // TILE, TILE, TILE), lambda i, me: (lax.rem(me[0] + n - i, n), 0, 0)
                )
            ]
            + [pl.BlockSpec((2, share, TILE), lambda i, me: (0, 0, 0))] * n,
            out_specs=[placed, placed],
        ),
        out_shape=[shape((n * share, TILE), BF16)] * 2,
        compiler_params=params(24),
        cost_estimate=cost(1e6, 7e6),
        name="finish",
    )(me, ext, *pieces)


def scatter_kernel(ids_ref, val_ref, out_ref):
    groups = out_ref.shape[0] // LOW

    @pl.when(pl.program_id(0) == 0)
    def _():
        out_ref[...] = jnp.zeros_like(out_ref)

    ids = ids_ref[0]
    width = ids.shape[1]
    spot = lax.broadcasted_iota(jnp.int32, (LOW, width), 0)
    onehot = jnp.where(spot == (ids & (LOW - 1)), 1.0, 0.0).astype(BF16)
    values = jnp.concatenate([val_ref[p] for p in range(val_ref.shape[0])], axis=1)
    zero = jnp.zeros_like(values)
    for g in range(0, groups, 2):
        pair = [
            jnp.where((ids >= k * LOW) & (ids < (k + 1) * LOW), values, zero) for k in (g, g + 1)
        ]
        both = lax.dot_general(
            onehot, jnp.concatenate(pair, axis=0), NT, preferred_element_type=F32
        )
        out_ref[g * LOW : (g + 1) * LOW, :] += both[:, :TILE]
        out_ref[(g + 1) * LOW : (g + 2) * LOW, :] += both[:, TILE:]


def scatter_rows(ids, values, rows):
    steps, _, width = ids.shape
    blocks = width // TILE
    return pl.pallas_call(
        scatter_kernel,
        grid=(steps,),
        in_specs=[
            pl.BlockSpec((1, 1, width), lambda i: (i, 0, 0)),
            pl.BlockSpec((blocks, TILE, TILE), lambda i: (i, 0, 0)),
        ],
        out_specs=pl.BlockSpec((rows, TILE), lambda i: (0, 0)),
        out_shape=shape((rows, TILE), F32),
        compiler_params=params(32),
        cost_estimate=cost(2 * ids.size * rows * TILE, 4e6),
        name="scatter_rows",
    )(ids, values)


def per_device(
    features, stale_features, grad_output, w_neigh, w_self, adj_tiles, tile_cols, send_idx, counts
):
    dom_count = lax.axis_size("dom")
    n = lax.axis_size("rep")
    row_count, width = features.shape
    row_tiles = row_count // TILE
    swap = functools.partial(
        lax.all_to_all, axis_name="dom", split_axis=0, concat_axis=0, tiled=True
    )
    me = lax.axis_index("rep").astype(jnp.int32).reshape(1)

    live = jnp.arange(B, dtype=jnp.int32)[None, :] < counts[0][:, None]
    ids = jnp.where(live, send_idx[0], -1)
    pos = tile_cols[0].reshape(-1)
    adj = adj_tiles[0]

    packed = gather_rows(ids.reshape(-1, 2, LOW), stale_features)
    halo = swap(packed)
    own, wn, ws, pieces = prep(me, features, grad_output, w_neigh, w_self, packed, n)
    both = relative(exchange(pieces))

    agg = relative(exchange(spmm(me, pos, adj, [own, halo], n)))
    grad_agg, act, grad_pre = dense(agg, both, wn, ws)
    grad_agg = exchange(grad_agg)
    terms = swap(wgrad(me, agg, both, grad_pre, dom_count))

    local, away = spmm_back(me, pos, adj, grad_agg, [row_tiles, dom_count * CHUNKS])
    returned = swap(away)
    pieces = exchange(late(act, grad_pre, ws, away, n))
    out, grad_input = finish(me, local, pieces)

    terms = jnp.sum(terms.astype(F32), axis=0).astype(BF16)
    terms = exchange([terms[j] for j in range(n)])
    terms = sum(t.astype(F32) for t in terms).astype(BF16)
    terms = swap(jnp.broadcast_to(terms[None], (dom_count, *terms.shape)))
    terms = terms.reshape(dom_count // n, n, -1, TILE).astype(F32)
    terms = jnp.transpose(terms, (0, 2, 1, 3)).reshape(2 * width, n * TILE)

    grad_stale = scatter_rows(ids.reshape(-1, 1, 2 * LOW), returned, row_count)
    return (out, grad_input, grad_stale, terms[:width], terms[width:])


def solution(mesh):
    in_specs = (
        P("dom", "rep"),
        P("dom", "rep"),
        P("dom", "rep"),
        P(),
        P(),
        P("dom", None, None, None, None),
        P("dom", None, None),
        P("dom", None, None),
        P("dom", None),
    )
    out_specs = (P("dom", "rep"), P("dom", "rep"), P("dom", "rep"), P("rep", None), P("rep", None))
    return jax.shard_map(
        per_device, mesh=mesh, in_specs=in_specs, out_specs=out_specs, check_vma=False
    )
```

time: 627 us -> 213 us (0.34); the launches traced: 618 us -> 211 us
  waiting for transfers between devices: 278 us -> 62.1 us
  matrix products: 175 us -> 0 us
  local copies, waits for them, and re-layouts: 108 us -> 16.3 us
  Pallas kernels: 0 us -> 65 us
  blocking collectives: 0 us -> 24.1 us
  starting transfers between devices: 18.7 us -> 39.9 us
  other arithmetic: 23.3 us -> 2.51 us
  between operations: 14.3 us -> 0.87 us
    dot_general x15 -> x0, matrix products: 175 us -> none  [the longest x4 48.6 us: add_group(): lax.dot_general(onehot, value_group, contract_rows, preferred_element_typ...]
    all_gather x3 -> x0, waiting for transfers between devices: 128 us -> none  [the longest x1 44.3 us: per_device(): grad_full = lax.all_gather(grad_pre, 'rep', axis=1, tiled=True)]
    psum x1 -> x0, waiting for transfers between devices: 111 us -> none  [per_device(): lax.psum(part_self.astype(jnp.bfloat16), 'dom').astype(jnp.float32)]
    pallas_call x0 -> x9, Pallas kernels: none -> 65 us  [the longest x1 13.7 us: scatter_rows(): pl.pallas_call(scatter_kernel, grid=(steps,), in_specs=[pl.BlockSpec((1,...]
    gather x1 -> x0, local copies, waits for them, and re-layouts: 43.7 us -> none  [per_device(): chosen = stale_features[send_list]]
    dot_general x1 -> x0, local copies, waits for them, and re-layouts: 31.3 us -> none  [per_device(): jnp.einsum('rtij,rif->rtjf', blocks, grad_agg.reshape(row_tiles, TILE, co...]
    ppermute x0 -> x15, waiting for transfers between devices: none -> 25.1 us  [exchange(): lax.ppermute(pieces[s], 'rep', [(i, (i + s) % n) for i in range(n)])]
    all_to_all x0 -> x1, blocking collectives: none -> 24.1 us  [per_device(): terms = swap(wgrad(me, agg, both, grad_pre, dom_count))]
  transfers between devices with their start and end apart: 6 -> 18, of which waited for: 5 -> 9; matrix products, arithmetic and copies ran while one was open for 3% -> 3% of each run, Pallas kernels for 0% -> 16%
where the time goes in v1:
time: 213 us; the launch traced here: 211 us
  Pallas kernels  65 us (31%)
  waiting for transfers between devices  62.1 us (29%)
  starting transfers between devices  39.9 us (19%)
  blocking collectives  24.1 us (11%)
  local copies, waits for them, and re-layouts  16.3 us (8%)
  other arithmetic  2.51 us (1%)
    all_to_all x1, waiting for transfers between devices, per_device(): halo = swap(packed)  30.7 us
    ppermute x15, waiting for transfers between devices, exchange(): lax.ppermute(pieces[s], 'rep', [(i, (i + s) % n) for i in range(n)])  25.1 us
    all_to_all x1, blocking collectives, per_device(): terms = swap(wgrad(me, agg, both, grad_pre, dom_count))  24.1 us
    ppermute x15, starting transfers between devices, exchange(): lax.ppermute(pieces[s], 'rep', [(i, (i + s) % n) for i in range(n)])  17.6 us
    pallas_call x1, Pallas kernels, scatter_rows(): pl.pallas_call(scatter_kernel, grid=(steps,), in_specs=[pl.BlockSpec((1,...  13.7 us
    pallas_call x1, Pallas kernels, spmm_back(): pl.pallas_call(functools.partial(spmm_back_kernel, n=n), grid_spec=pltpu....  13.5 us
    pallas_call x1, Pallas kernels, gather_rows(): pl.pallas_call(gather_kernel, grid=(steps,), in_specs=[pl.BlockSpec((1, p...  13.1 us
    pallas_call x1, Pallas kernels, spmm(): pl.pallas_call(functools.partial(spmm_kernel, n=n), grid_spec=pltpu.Prefe...  12.9 us
  transfers between devices with their start and end apart: 18, of which 9 were waited for; matrix products, arithmetic and copies ran while one was open for 3% of the time, Pallas kernels for 16%

profile of v1, /device:TPU:1, one launch (start us, length us, event | category | flops | bytes accessed | tf_op | source)
XLA Modules:
  0.0 210.8 jit_solution(6054609675545259112)
XLA Ops:
  3.4 13.1 %gather_rows.1.after_ref = bf16[96,128,128]{2,1,0:T(8,128)(2,1)} custom-call(s32[12,2,512]{2,1,0:T(2,128)S(1)} %broadcast_select_fusion.1.ids_ref, bf16[3072,128]{1,0:T(8,128)(2,1)S(1)} %copy-done.5), custom_call_target="tpu_custom_call" | custom-call | flops 9663676416 | bytes 4000000 | tf_op jit(solution)/shard_map/gather_rows/pallas_call | solution.py:67
  16.5 9.6 %all-to-all-start = ((bf16[96,128,128]{2,1,0:T(8,128)(2,1)}), bf16[96,128,128]{2,1,0:T(8,128)(2,1)}, u32[]{:S(2)}, u32[]{:S(2)}) async-start(bf16[96,128,128]{2,1,0:T(8,128)(2,1)} %gather_rows.1.after_ref), calls=%async_computation | async-start | bytes 6291456 | tf_op jit(solution)/shard_map/all_to_all | solution.py:488
  27.2 1.9 prep.1
  30.7 2.7 %collective-permute-start.3 = (bf16[2,768,128]{2,1,0:T(8,128)(2,1)}, bf16[2,768,128]{2,1,0:T(8,128)(2,1)S(1)}, u32[]{:S(2)}, u32[]{:S(2)}) collective-permute-start(bf16[2,768,128]{2,1,0:T(8,128)(2,1)} %get-tuple-element.36), channel_id=1, source_target_pairs={{0,3},{1,0},{2,1},{3,2},{4,7},{5,4},{6,5},{7,6},{8,11},{9,8},{10,9... | collective-permute-start | bytes 1179656 | tf_op jit(solution)/shard_map/ppermute | solution.py:86
  34.7 30.7 %all-to-all-done.refs_1_ = bf16[96,128,128]{2,1,0:T(8,128)(2,1)} async-done(((bf16[96,128,128]{2,1,0:T(8,128)(2,1)}), bf16[96,128,128]{2,1,0:T(8,128)(2,1)}, u32[]{:S(2)}, u32[]{:S(2)}) %all-to-all-start) | async-done | bytes 3145760 | tf_op jit(solution)/shard_map/all_to_all | solution.py:488
  65.4 12.9 %spmm.1 = (bf16[768,128]{1,0:T(8,128)(2,1)S(1)}, bf16[768,128]{1,0:T(8,128)(2,1)S(1)}, bf16[768,128]{1,0:T(8,128)(2,1)S(1)}, bf16[768,128]{1,0:T(8,128)(2,1)S(1)}) custom-call(s32[1]{0:T(128)} %bitcast.me_ref, s32[480]{0:T(512)S(1)} %reshape_squeeze.3.pos_ref, bf16[24,20,128,128]{3,2,1,0:T(8,128)(2,1)} %bitcast.26, ...), custom_call_target="tpu_custom_call" | custom-call | flops 4026531840 | bytes 20000000 | tf_op jit(solution)/shard_map/spmm/pallas_call | solution.py:190
  78.2 2.8 %collective-permute-start = (bf16[768,128]{1,0:T(8,128)(2,1)S(1)}, bf16[768,128]{1,0:T(8,128)(2,1)S(1)}, u32[]{:S(2)}, u32[]{:S(2)}) collective-permute-start(bf16[768,128]{1,0:T(8,128)(2,1)S(1)} %get-tuple-element.32), channel_id=1, source_target_pairs={{0,3},{1,0},{2,1},{3,2},{4,7},{5,4},{6,5},{7,6},{8,11},{9,8},{10,9... | collective-permute-start | bytes 589832 | tf_op jit(solution)/shard_map/ppermute | solution.py:86
  82.1 4.0 %collective-permute-done.refs_1_ = bf16[768,128]{1,0:T(8,128)(2,1)S(1)} collective-permute-done((bf16[768,128]{1,0:T(8,128)(2,1)S(1)}, bf16[768,128]{1,0:T(8,128)(2,1)S(1)}, u32[]{:S(2)}, u32[]{:S(2)}) %collective-permute-start) | collective-permute-done | bytes 196640 | tf_op jit(solution)/shard_map/ppermute | solution.py:86
  87.2 4.8 %collective-permute-done.2.refs_3_ = bf16[768,128]{1,0:T(8,128)(2,1)S(1)} collective-permute-done((bf16[768,128]{1,0:T(8,128)(2,1)S(1)}, bf16[768,128]{1,0:T(8,128)(2,1)S(1)}, u32[]{:S(2)}, u32[]{:S(2)}) %collective-permute-start.2) | collective-permute-done | bytes 196640 | tf_op jit(solution)/shard_map/ppermute | solution.py:86
  91.9 3.3 %dense.1 = (bf16[128,768]{1,0:T(8,128)(2,1)S(1)}, bf16[128,768]{1,0:T(8,128)(2,1)S(1)}, bf16[128,768]{1,0:T(8,128)(2,1)S(1)}, bf16[128,768]{1,0:T(8,128)(2,1)S(1...) custom-call(bf16[768,128]{1,0:T(8,128)(2,1)S(1)} %get-tuple-element.31.refs_0_, ...), custom_call_target="tpu_custom_call" | custom-call | flops 1207959552 | bytes 7000000 | tf_op jit(solution)/shard_map/dense/pallas_call | solution.py:247
  97.3 24.1 %all_to_all.20 = bf16[32,4,32,128]{3,2,1,0:T(8,128)(2,1)S(1)} all-to-all(bf16[32,4,32,128]{3,2,1,0:T(8,128)(2,1)S(1)} %wgrad.1), channel_id=1, replica_groups=mesh['dom'=32,'rep'=4] {'dom'}, dimensions={0} | all-to-all | bytes 2097152 | tf_op jit(solution)/shard_map/all_to_all | solution.py:495
  124.8 1.8 collective-permute-start.7
  126.6 2.1 collective-permute-start.8
  129.4 5.6 %all-to-all-start.3 = ((bf16[32,32,128]{2,1,0:T(8,128)(2,1)}), bf16[32,32,128]{2,1,0:T(8,128)(2,1)S(1)}, u32[]{:S(2)}, u32[]{:S(2)}) async-start(bf16[32,32,128]{2,1,0:T(8,128)(2,1)} %broadcast_in_dim.15), calls=%async_computation.3 | async-start | bytes 524288 | tf_op jit(solution)/shard_map/all_to_all | solution.py:505
  135.4 13.5 %spmm_back.1 = (f32[24,128,128]{2,1,0:T(8,128)S(1)}, bf16[96,128,128]{2,1,0:T(8,128)(2,1)}) custom-call(s32[1]{0:T(128)} %bitcast.me_ref, s32[480]{0:T(512)S(1)} %reshape_squeeze.3.pos_ref, bf16[24,20,128,128]{3,2,1,0:T(8,128)(2,1)} %bitcast.27, bf16[128,768]{1,0:T(8,128)(2,1)S(1)} %get-tuple-element.41.refs_0_, ...), custom_call_target="tpu_custom_call" | custom-call | flops 4026531840 | bytes 22000000 | tf_op jit(solution)/shard_map/spmm_back/pallas_call | solution.py:335
  150.8 7.2 %all-to-all-start.1 = ((bf16[96,128,128]{2,1,0:T(8,128)(2,1)}), bf16[96,128,128]{2,1,0:T(8,128)(2,1)S(1)}, u32[]{:S(2)}, u32[]{:S(2)}) async-start(bf16[96,128,128]{2,1,0:T(8,128)(2,1)} %get-tuple-element.48.after_ref), calls=%async_computation.1 | async-start | bytes 6291456 | tf_op jit(solution)/shard_map/all_to_all | solution.py:498
  161.2 2.1 %late.1 = (bf16[2,768,128]{2,1,0:T(8,128)(2,1)S(1)}, bf16[2,768,128]{2,1,0:T(8,128)(2,1)}, bf16[2,768,128]{2,1,0:T(8,128)(2,1)}, bf16[2,768,128]{2,1,0:T(8,128)(2,1)}) custom-call(bf16[768,512]{1,0:T(8,128)(2,1)S(1)} %copy-done.11, bf16[768,512]{1,0:T(8,128)(2,1)S(1)} %copy-done.3, bf16[512,512]{1,0:T(8,128)(2,1)S(1)} %copy-done.14, ...), custom_call_target="tpu_custom_call" | custom-call | flops 10000000000 | bytes 6000000 | tf_op jit(solution)/shard_map/late/pallas_call | solution.py:374
  168.2 1.5 broadcast_select_fusion.ids_ref
  169.8 6.0 %collective-permute-done.10.refs_2_ = bf16[2,768,128]{2,1,0:T(8,128)(2,1)} collective-permute-done((bf16[2,768,128]{2,1,0:T(8,128)(2,1)}, bf16[2,768,128]{2,1,0:T(8,128)(2,1)}, u32[]{:S(2)}, u32[]{:S(2)}) %collective-permute-start.10) | collective-permute-done | bytes 393248 | tf_op jit(solution)/shard_map/ppermute | solution.py:86
  175.7 7.2 %collective-permute-done.11.refs_3_ = bf16[2,768,128]{2,1,0:T(8,128)(2,1)} collective-permute-done((bf16[2,768,128]{2,1,0:T(8,128)(2,1)}, bf16[2,768,128]{2,1,0:T(8,128)(2,1)}, u32[]{:S(2)}, u32[]{:S(2)}) %collective-permute-start.11) | collective-permute-done | bytes 393248 | tf_op jit(solution)/shard_map/ppermute | solution.py:86
  182.9 1.8 collective-permute-done.9.refs_1_
  186.1 3.4 %finish.1 = (bf16[3072,128]{1,0:T(8,128)(2,1)}, bf16[3072,128]{1,0:T(8,128)(2,1)}) custom-call(s32[1]{0:T(128)} %bitcast.me_ref, f32[24,128,128]{2,1,0:T(8,128)S(1)} %copy-done.1, bf16[2,768,128]{2,1,0:T(8,128)(2,1)S(1)} %get-tuple-element.49.refs_0_, bf16[2,768,128]{2,1,0:T(8,128)(2,1)} %collective-permute-done.9.refs_1_, ...), custom_call_target="tpu_custom_call" | custom-call | flops 1000000 | bytes 7000000 | tf_op jit(solution)/shard_map/finish/pallas_call | solution.py:408
  190.7 6.4 %all-to-all-done.1.val_ref = bf16[96,128,128]{2,1,0:T(8,128)(2,1)S(1)} async-done(((bf16[96,128,128]{2,1,0:T(8,128)(2,1)}), bf16[96,128,128]{2,1,0:T(8,128)(2,1)S(1)}, u32[]{:S(2)}, u32[]{:S(2)}) %all-to-all-start.1) | async-done | bytes 3145760 | tf_op jit(solution)/shard_map/all_to_all | solution.py:498
  197.1 13.7 %scatter_rows.1 = f32[3072,128]{1,0:T(8,128)} custom-call(s32[12,1,1024]{2,1,0:T(1,128)S(1)} %copy-done.4, bf16[96,128,128]{2,1,0:T(8,128)(2,1)S(1)} %all-to-all-done.1.val_ref), custom_call_target="tpu_custom_call" | custom-call | flops 9663676416 | bytes 4000000 | tf_op jit(solution)/shard_map/scatter_rows/pallas_call | solution.py:455
  (80 shorter events, 28.0 us)
Async XLA Ops:
  16.5 9.6 %copy-start.6 = (bf16[3072,128]{1,0:T(8,128)(2,1)S(1)}, bf16[3072,128]{1,0:T(8,128)(2,1)}, u32[]{:S(2)}) copy-start(bf16[3072,128]{1,0:T(8,128)(2,1)} %feat_ref.1) | copy-start | bytes 2359300
  16.5 9.6 %copy-start.7 = (bf16[3072,128]{1,0:T(8,128)(2,1)S(1)}, bf16[3072,128]{1,0:T(8,128)(2,1)}, u32[]{:S(2)}) copy-start(bf16[3072,128]{1,0:T(8,128)(2,1)} %up_ref.1) | copy-start | bytes 2359300
  16.5 9.6 %copy-start.8 = (bf16[512,512]{1,0:T(8,128)(2,1)S(1)}, bf16[512,512]{1,0:T(8,128)(2,1)}, u32[]{:S(2)}) copy-start(bf16[512,512]{1,0:T(8,128)(2,1)} %wn_ref.1) | copy-start | bytes 1572868
  16.5 48.8 %all-to-all-start = ((bf16[96,128,128]{2,1,0:T(8,128)(2,1)}), bf16[96,128,128]{2,1,0:T(8,128)(2,1)}, u32[]{:S(2)}, u32[]{:S(2)}) async-start(bf16[96,128,128]{2,1,0:T(8,128)(2,1)} %gather_rows.1.after_ref), calls=%async_computation | async-start | bytes 6291456 | tf_op jit(solution)/shard_map/all_to_all | solution.py:488
  30.7 50.7 %collective-permute-start.3 = (bf16[2,768,128]{2,1,0:T(8,128)(2,1)}, bf16[2,768,128]{2,1,0:T(8,128)(2,1)S(1)}, u32[]{:S(2)}, u32[]{:S(2)}) collective-permute-start(bf16[2,768,128]{2,1,0:T(8,128)(2,1)} %get-tuple-element.36), channel_id=1, source_target_pairs={{0,3},{1,0},{2,1},{3,2},{4,7},{5,4},{6,5},{7,6},{8,11},{9,8},{10,9... | collective-permute-start | bytes 1179656 | tf_op jit(solution)/shard_map/ppermute | solution.py:86
  33.5 48.6 %collective-permute-start.4 = (bf16[2,768,128]{2,1,0:T(8,128)(2,1)}, bf16[2,768,128]{2,1,0:T(8,128)(2,1)S(1)}, u32[]{:S(2)}, u32[]{:S(2)}) collective-permute-start(bf16[2,768,128]{2,1,0:T(8,128)(2,1)} %get-tuple-element.37), channel_id=1, source_target_pairs={{0,2},{1,3},{2,0},{3,1},{4,6},{5,7},{6,4},{7,5},{8,10},{9,11},{10,... | collective-permute-start | bytes 1179656 | tf_op jit(solution)/shard_map/ppermute | solution.py:86
  33.8 48.3 %collective-permute-start.5 = (bf16[2,768,128]{2,1,0:T(8,128)(2,1)}, bf16[2,768,128]{2,1,0:T(8,128)(2,1)S(1)}, u32[]{:S(2)}, u32[]{:S(2)}) collective-permute-start(bf16[2,768,128]{2,1,0:T(8,128)(2,1)} %get-tuple-element.38), channel_id=1, source_target_pairs={{0,1},{1,2},{2,3},{3,0},{4,5},{5,6},{6,7},{7,4},{8,9},{9,10},{10,1... | collective-permute-start | bytes 1179656 | tf_op jit(solution)/shard_map/ppermute | solution.py:86
  65.4 26.6 %copy-start.13 = (bf16[512,512]{1,0:T(8,128)(2,1)S(1)}, bf16[512,512]{1,0:T(8,128)(2,1)}, u32[]{:S(2)}) copy-start(bf16[512,512]{1,0:T(8,128)(2,1)} %copy-done.12) | copy-start | bytes 1572868
  65.4 26.6 %copy-start.16 = (bf16[512,512]{1,0:T(8,128)(2,1)S(1)}, bf16[512,512]{1,0:T(8,128)(2,1)}, u32[]{:S(2)}) copy-start(bf16[512,512]{1,0:T(8,128)(2,1)} %copy-done.15) | copy-start | bytes 1572868
  78.2 7.9 %collective-permute-start = (bf16[768,128]{1,0:T(8,128)(2,1)S(1)}, bf16[768,128]{1,0:T(8,128)(2,1)S(1)}, u32[]{:S(2)}, u32[]{:S(2)}) collective-permute-start(bf16[768,128]{1,0:T(8,128)(2,1)S(1)} %get-tuple-element.32), channel_id=1, source_target_pairs={{0,3},{1,0},{2,1},{3,2},{4,7},{5,4},{6,5},{7,6},{8,11},{9,8},{10,9... | collective-permute-start | bytes 589832 | tf_op jit(solution)/shard_map/ppermute | solution.py:86
  81.0 6.1 %collective-permute-start.1 = (bf16[768,128]{1,0:T(8,128)(2,1)S(1)}, bf16[768,128]{1,0:T(8,128)(2,1)S(1)}, u32[]{:S(2)}, u32[]{:S(2)}) collective-permute-start(bf16[768,128]{1,0:T(8,128)(2,1)S(1)} %get-tuple-element.33), channel_id=1, source_target_pairs={{0,2},{1,3},{2,0},{3,1},{4,6},{5,7},{6,4},{7,5},{8,10},{9,11},{10,... | collective-permute-start | bytes 589832 | tf_op jit(solution)/shard_map/ppermute | solution.py:86
  81.4 10.5 %collective-permute-start.2 = (bf16[768,128]{1,0:T(8,128)(2,1)S(1)}, bf16[768,128]{1,0:T(8,128)(2,1)S(1)}, u32[]{:S(2)}, u32[]{:S(2)}) collective-permute-start(bf16[768,128]{1,0:T(8,128)(2,1)S(1)} %get-tuple-element.34), channel_id=1, source_target_pairs={{0,1},{1,2},{2,3},{3,0},{4,5},{5,6},{6,7},{7,4},{8,9},{9,10},{10,1... | collective-permute-start | bytes 589832 | tf_op jit(solution)/shard_map/ppermute | solution.py:86
  121.5 5.1 %collective-permute-start.12 = (bf16[32,128]{1,0:T(8,128)(2,1)S(1)}, bf16[32,128]{1,0:T(8,128)(2,1)S(1)}, u32[]{:S(2)}, u32[]{:S(2)}) collective-permute-start(bf16[32,128]{1,0:T(8,128)(2,1)S(1)} %get-tuple-element.57), channel_id=1, source_target_pairs={{0,1},{1,2},{2,3},{3,0},{4,5},{5,6},{6,7},{7,4},{8,9},{9,10},{10,1... | collective-permute-start | bytes 24584 | tf_op jit(solution)/shard_map/ppermute | solution.py:86
  121.6 7.1 %collective-permute-start.13 = (bf16[32,128]{1,0:T(8,128)(2,1)S(1)}, bf16[32,128]{1,0:T(8,128)(2,1)S(1)}, u32[]{:S(2)}, u32[]{:S(2)}) collective-permute-start(bf16[32,128]{1,0:T(8,128)(2,1)S(1)} %get-tuple-element.59), channel_id=1, source_target_pairs={{0,2},{1,3},{2,0},{3,1},{4,6},{5,7},{6,4},{7,5},{8,10},{9,11},{10,... | collective-permute-start | bytes 24584 | tf_op jit(solution)/shard_map/ppermute | solution.py:86
  123.0 5.7 %collective-permute-start.14 = (bf16[32,128]{1,0:T(8,128)(2,1)S(1)}, bf16[32,128]{1,0:T(8,128)(2,1)S(1)}, u32[]{:S(2)}, u32[]{:S(2)}) collective-permute-start(bf16[32,128]{1,0:T(8,128)(2,1)S(1)} %get-tuple-element.58), channel_id=1, source_target_pairs={{0,3},{1,0},{2,1},{3,2},{4,7},{5,4},{6,5},{7,6},{8,11},{9,8},{10,9... | collective-permute-start | bytes 24584 | tf_op jit(solution)/shard_map/ppermute | solution.py:86
  124.2 10.8 %collective-permute-start.6 = (bf16[128,768]{1,0:T(8,128)(2,1)S(1)}, bf16[128,768]{1,0:T(8,128)(2,1)S(1)}, u32[]{:S(2)}, u32[]{:S(2)}) collective-permute-start(bf16[128,768]{1,0:T(8,128)(2,1)S(1)} %get-tuple-element.42), channel_id=1, source_target_pairs={{0,1},{1,2},{2,3},{3,0},{4,5},{5,6},{6,7},{7,4},{8,9},{9,10},{10,1... | collective-permute-start | bytes 589832 | tf_op jit(solution)/shard_map/ppermute | solution.py:86
  124.8 10.2 %collective-permute-start.7 = (bf16[128,768]{1,0:T(8,128)(2,1)S(1)}, bf16[128,768]{1,0:T(8,128)(2,1)S(1)}, u32[]{:S(2)}, u32[]{:S(2)}) collective-permute-start(bf16[128,768]{1,0:T(8,128)(2,1)S(1)} %get-tuple-element.43), channel_id=1, source_target_pairs={{0,2},{1,3},{2,0},{3,1},{4,6},{5,7},{6,4},{7,5},{8,10},{9,11},{10,... | collective-permute-start | bytes 589832 | tf_op jit(solution)/shard_map/ppermute | solution.py:86
  126.6 8.8 %collective-permute-start.8 = (bf16[128,768]{1,0:T(8,128)(2,1)S(1)}, bf16[128,768]{1,0:T(8,128)(2,1)S(1)}, u32[]{:S(2)}, u32[]{:S(2)}) collective-permute-start(bf16[128,768]{1,0:T(8,128)(2,1)S(1)} %get-tuple-element.44), channel_id=1, source_target_pairs={{0,3},{1,0},{2,1},{3,2},{4,7},{5,4},{6,5},{7,6},{8,11},{9,8},{10,9... | collective-permute-start | bytes 589832 | tf_op jit(solution)/shard_map/ppermute | solution.py:86
  129.4 20.6 %all-to-all-start.3 = ((bf16[32,32,128]{2,1,0:T(8,128)(2,1)}), bf16[32,32,128]{2,1,0:T(8,128)(2,1)S(1)}, u32[]{:S(2)}, u32[]{:S(2)}) async-start(bf16[32,32,128]{2,1,0:T(8,128)(2,1)} %broadcast_in_dim.15), calls=%async_computation.3 | async-start | bytes 524288 | tf_op jit(solution)/shard_map/all_to_all | solution.py:505
  150.8 46.3 %all-to-all-start.1 = ((bf16[96,128,128]{2,1,0:T(8,128)(2,1)}), bf16[96,128,128]{2,1,0:T(8,128)(2,1)S(1)}, u32[]{:S(2)}, u32[]{:S(2)}) async-start(bf16[96,128,128]{2,1,0:T(8,128)(2,1)} %get-tuple-element.48.after_ref), calls=%async_computation.1 | async-start | bytes 6291456 | tf_op jit(solution)/shard_map/all_to_all | solution.py:498
  163.4 12.3 %collective-permute-start.10 = (bf16[2,768,128]{2,1,0:T(8,128)(2,1)}, bf16[2,768,128]{2,1,0:T(8,128)(2,1)}, u32[]{:S(2)}, u32[]{:S(2)}) collective-permute-start(bf16[2,768,128]{2,1,0:T(8,128)(2,1)} %get-tuple-element.51), channel_id=1, source_target_pairs={{0,2},{1,3},{2,0},{3,1},{4,6},{5,7},{6,4},{7,5},{8,10},{9,11},{10,... | collective-permute-start | bytes 1179656 | tf_op jit(solution)/shard_map/ppermute | solution.py:86
  164.7 18.2 %collective-permute-start.11 = (bf16[2,768,128]{2,1,0:T(8,128)(2,1)}, bf16[2,768,128]{2,1,0:T(8,128)(2,1)}, u32[]{:S(2)}, u32[]{:S(2)}) collective-permute-start(bf16[2,768,128]{2,1,0:T(8,128)(2,1)} %get-tuple-element.52), channel_id=1, source_target_pairs={{0,3},{1,0},{2,1},{3,2},{4,7},{5,4},{6,5},{7,6},{8,11},{9,8},{10,9... | collective-permute-start | bytes 1179656 | tf_op jit(solution)/shard_map/ppermute | solution.py:86
  166.1 18.5 %collective-permute-start.9 = (bf16[2,768,128]{2,1,0:T(8,128)(2,1)}, bf16[2,768,128]{2,1,0:T(8,128)(2,1)}, u32[]{:S(2)}, u32[]{:S(2)}) collective-permute-start(bf16[2,768,128]{2,1,0:T(8,128)(2,1)} %get-tuple-element.50), channel_id=1, source_target_pairs={{0,1},{1,2},{2,3},{3,0},{4,5},{5,6},{6,7},{7,4},{8,9},{9,10},{10,1... | collective-permute-start | bytes 1179656 | tf_op jit(solution)/shard_map/ppermute | solution.py:86
  189.4 7.7 %copy-start.4 = (s32[12,1,1024]{2,1,0:T(1,128)S(1)}, s32[12,1,1024]{2,1,0:T(1,128)}, u32[]{:S(2)}) copy-start(s32[12,1,1024]{2,1,0:T(1,128)} %broadcast_select_fusion.ids_ref) | copy-start | bytes 147460
  (14 other events, 23.0 us)

commit v2 on v1

v2 whole, which is shorter than its diff:
```python
import functools

import jax
import jax.numpy as jnp
from jax import lax
from jax.experimental import pallas as pl
from jax.experimental.pallas import tpu as pltpu
from jax.sharding import PartitionSpec as P

TILE = 128
B = 384
CHUNKS = B // TILE
LOW = 512
F32 = jnp.float32
BF16 = jnp.bfloat16
NT = (((1,), (1,)), ((), ()))
TN = (((0,), (0,)), ((), ()))


def params(mib):
    return pltpu.CompilerParams(vmem_limit_bytes=mib * 1024 * 1024)


def cost(flops, nbytes, trans=0):
    return pl.CostEstimate(flops=int(flops), bytes_accessed=int(nbytes), transcendentals=int(trans))


def shape(dims, dtype):
    return jax.ShapeDtypeStruct(dims, dtype)


def turned(block):
    return jnp.transpose(block.astype(F32))


def masked_ids(ids_ref, counts_ref, first, peers):
    base = pl.program_id(0) * ids_ref.shape[0]
    slot = lax.broadcasted_iota(jnp.int32, (1, ids_ref.shape[1]), 1)
    rows = [
        jnp.where(slot < counts_ref[0, base + p], ids_ref[p : p + 1, :], -1)
        for p in range(first, first + peers)
    ]
    return jnp.concatenate(rows, axis=1)


def low_onehot(ids):
    spot = lax.broadcasted_iota(jnp.int32, (LOW, ids.shape[1]), 0)
    return jnp.where(spot == (ids & (LOW - 1)), 1.0, 0.0).astype(BF16)


def in_group(ids, g):
    return (ids >= g * LOW) & (ids < (g + 1) * LOW)


def gather_kernel(ids_ref, counts_ref, table_ref, out_ref, flipped):
    groups = table_ref.shape[0] // LOW

    @pl.when(pl.program_id(0) == 0)
    def _():
        for g in range(groups):
            for k in range(LOW // TILE):
                block = table_ref[g * LOW + k * TILE : g * LOW + (k + 1) * TILE, :]
                flipped[g * TILE : (g + 1) * TILE, k * TILE : (k + 1) * TILE] = turned(block).astype(
                    BF16
                )

    for p in range(0, ids_ref.shape[0], 2):
        ids = masked_ids(ids_ref, counts_ref, p, 2)
        found = jnp.dot(flipped[...], low_onehot(ids), preferred_element_type=F32)
        total = jnp.zeros((TILE, ids.shape[1]), F32)
        for g in range(groups):
            total = jnp.where(in_group(ids, g), found[g * TILE : (g + 1) * TILE, :], total)
        total = total.astype(BF16)
        for k in range(2 * CHUNKS):
            out_ref[p * CHUNKS + k] = total[:, k * TILE : (k + 1) * TILE]


def gather_rows(ids, counts, table):
    peers = ids.shape[0]
    size = 8
    rows, cols = table.shape
    return pl.pallas_call(
        gather_kernel,
        grid=(peers // size,),
        in_specs=[
            pl.BlockSpec((size, B), lambda i: (i, 0)),
            pl.BlockSpec(memory_space=pltpu.SMEM),
            pl.BlockSpec((rows, cols), lambda i: (0, 0)),
        ],
        out_specs=pl.BlockSpec((size * CHUNKS, TILE, TILE), lambda i: (i, 0, 0)),
        out_shape=shape((peers * CHUNKS, TILE, TILE), BF16),
        scratch_shapes=[pltpu.VMEM((rows // LOW * TILE, LOW), BF16)],
        compiler_params=params(48),
        cost_estimate=cost(2 * ids.size * rows * cols, 4e6),
        name="gather_rows",
    )(ids, counts, table)


def exchange(pieces):
    n = len(pieces)
    return [pieces[0]] + [
        lax.ppermute(pieces[s], "rep", [(i, (i + s) % n) for i in range(n)]) for s in range(1, n)
    ]


def relative(received):
    n = len(received)
    return [received[(n - j) % n] for j in range(n)]


def prep_kernel(
    me_ref, feat_ref, up_ref, wn_ref, ws_ref, adj_ref, after_ref, own_ref, wn_out, ws_out, adj_out, *refs
):
    del after_ref
    pieces, sems = refs[:-1], refs[-1]
    step = pl.program_id(0)
    n = len(pieces)
    part = adj_ref.shape[0] // sems.shape[0]
    copies = [
        pltpu.make_async_copy(
            adj_ref.at[pl.ds(k * part, part)], adj_out.at[pl.ds(k * part, part)], sems.at[k]
        )
        for k in range(sems.shape[0])
    ]

    @pl.when(step == 0)
    def _():
        for copy in copies:
            copy.start()

    for k in range(own_ref.shape[0]):
        own_ref[k] = turned(feat_ref[k * TILE : (k + 1) * TILE, :]).astype(BF16)
    for j, piece in enumerate(pieces):
        column = pl.multiple_of(lax.rem(me_ref[0] + j, n) * TILE, TILE)
        wn_out[:, j * TILE : (j + 1) * TILE] = wn_ref[:, pl.ds(column, TILE)]
        ws_out[:, j * TILE : (j + 1) * TILE] = ws_ref[:, pl.ds(column, TILE)]

        @pl.when(step == j)
        def _():
            piece[0] = feat_ref[...]
            piece[1] = up_ref[...]

    @pl.when(step == n - 1)
    def _():
        for copy in copies:
            copy.wait()


def prep(me, features, upstream, wn, ws, adj, after, n):
    rows, width = features.shape
    share = rows // n
    full = wn.shape[0]
    chunk = pl.BlockSpec((share, width), lambda i, me: (lax.rem(me[0] + i, n), 0))
    weight = pl.BlockSpec((width, full), lambda i, me: (lax.rem(me[0] + i, n), 0))
    placed = pl.BlockSpec((width, full), lambda i, me: (i, 0))
    own, wn, ws, adj, *pieces = pl.pallas_call(
        prep_kernel,
        grid_spec=pltpu.PrefetchScalarGridSpec(
            num_scalar_prefetch=1,
            grid=(n,),
            in_specs=[chunk, chunk, weight, weight] + [pl.BlockSpec(memory_space=pl.ANY)] * 2,
            out_specs=[
                pl.BlockSpec(
                    (share // TILE, TILE, TILE), lambda i, me: (lax.rem(me[0] + i, n), 0, 0)
                ),
                placed,
                placed,
                pl.BlockSpec(memory_space=pl.ANY),
            ]
            + [pl.BlockSpec((2, share, width), lambda i, me: (0, 0, 0))] * n,
            scratch_shapes=[pltpu.SemaphoreType.DMA((4,))],
        ),
        out_shape=[
            shape((rows // TILE, TILE, TILE), BF16),
            shape((full, full), BF16),
            shape((full, full), BF16),
            pltpu.VMEM(adj.shape, BF16),
        ]
        + [shape((2, share, width), BF16)] * n,
        compiler_params=params(16),
        cost_estimate=cost(1e10, 6e6),
        name="prep",
    )(me, features, upstream, wn, ws, adj, after)
    return own, wn, ws, adj, pieces


BLOCKS = 3


def adj_spec(per_row, inner, chunk_of):
    return pl.BlockSpec(
        (BLOCKS, per_row, TILE, TILE),
        lambda i, k, me, pos: (chunk_of(i, me) * inner + k, 0, 0, 0),
    )


def spmm_kernel(me_ref, pos_ref, *refs, n):
    adj, parts, outs, (ext, sems) = refs[0], refs[1 : -n - 2], refs[-n - 2 : -2], refs[-2:]
    chunk, part = pl.program_id(0), pl.program_id(1)
    per_row = adj.shape[1]

    @pl.when((chunk == 0) & (part == 0))
    def _():
        copies, start, at = [], 0, 0
        for source in parts:
            size = source.shape[0] // 4
            for k in range(4):
                copies.append(
                    pltpu.make_async_copy(
                        source.at[pl.ds(k * size, size)], ext.at[pl.ds(start, size)], sems.at[at]
                    )
                )
                start, at = start + size, at + 1
        for copy in copies:
            copy.start()
        for copy in copies:
            copy.wait()

    first = (lax.rem(me_ref[0] + chunk, n) * pl.num_programs(1) + part) * BLOCKS
    done = []
    for r in range(BLOCKS):
        base = (first + r) * per_row
        total = None
        for t in range(0, per_row, 2):
            left = jnp.concatenate([adj[r, t], adj[r, t + 1]], axis=1)
            right = jnp.concatenate([ext[pos_ref[base + t]], ext[pos_ref[base + t + 1]]], axis=1)
            term = lax.dot_general(left, right, NT, preferred_element_type=F32)
            total = term if total is None else total + term
        done.append(total.astype(BF16))
    done = jnp.concatenate(done, axis=0)
    size = BLOCKS * TILE
    place = pl.ds(pl.multiple_of(part * size, size), size)
    for j, out in enumerate(outs):

        @pl.when(chunk == j)
        def _():
            out[place, :] = done


def spmm(me, pos, adj, parts, n):
    row_tiles, per_row = adj.shape[:2]
    inner = row_tiles // n // BLOCKS
    share = row_tiles // n * TILE
    col_tiles = sum(p.shape[0] for p in parts)
    return pl.pallas_call(
        functools.partial(spmm_kernel, n=n),
        grid_spec=pltpu.PrefetchScalarGridSpec(
            num_scalar_prefetch=2,
            grid=(n, inner),
            in_specs=[adj_spec(per_row, inner, lambda i, me: lax.rem(me[0] + i, n))]
            + [pl.BlockSpec(memory_space=pl.ANY)] * len(parts),
            out_specs=[pl.BlockSpec((share, TILE), lambda i, k, me, pos: (0, 0))] * n,
            scratch_shapes=[
                pltpu.VMEM((col_tiles, TILE, TILE), BF16),
                pltpu.SemaphoreType.DMA((4 * len(parts),)),
            ],
        ),
        out_shape=[shape((share, TILE), BF16)] * n,
        compiler_params=params(20),
        cost_estimate=cost(2 * row_tiles * per_row * TILE**3 * 2, 2e7),
        name="spmm",
    )(me, pos, adj, *parts)


def joined(refs):
    return jnp.concatenate([ref[...] for ref in refs], axis=1)


def dense_kernel(*refs, n):
    agg, both, (wn_ref, ws_ref), rest = refs[:n], refs[n : 2 * n], refs[2 * n : 2 * n + 2], refs[2 * n + 2 :]
    ga, (act_ref, gp_ref) = rest[:n], rest[n:]
    wn = wn_ref[...]
    v = jnp.dot(joined(agg), wn, preferred_element_type=F32) + jnp.dot(
        joined([ref.at[0] for ref in both]), ws_ref[...], preferred_element_type=F32
    )
    root = 0.7978845608028654
    square = v * v
    t = jnp.tanh(root * v * (1.0 + 0.044715 * square))
    half = 0.5 * (1.0 + t)
    slope = half + 0.5 * v * (1.0 - t * t) * (root * (1.0 + 0.134145 * square))
    gp = (joined([ref.at[1] for ref in both]).astype(F32) * slope).astype(BF16)
    act_ref[...] = (v * half).astype(BF16)
    gp_ref[...] = gp
    back = lax.dot_general(wn, gp, NT, preferred_element_type=F32).astype(BF16)
    width = back.shape[0] // n
    for q in range(n):
        ga[q][...] = back[q * width : (q + 1) * width, :]


def dense(agg, both, wn, ws):
    n = len(agg)
    rows, width = agg[0].shape
    full = n * width
    size = 256
    weight = pl.BlockSpec((full, full), lambda i: (0, 0))
    whole = pl.BlockSpec((size, full), lambda i: (i, 0))
    results = pl.pallas_call(
        functools.partial(dense_kernel, n=n),
        grid=(rows // size,),
        in_specs=[pl.BlockSpec((size, width), lambda i: (i, 0))] * n
        + [pl.BlockSpec((2, size, width), lambda i: (0, i, 0))] * n
        + [weight, weight],
        out_specs=[pl.BlockSpec((width, size), lambda i: (0, i))] * n + [whole, whole],
        out_shape=[shape((width, rows), BF16)] * n + [pltpu.HBM((rows, full), BF16)] * 2,
        compiler_params=params(24),
        cost_estimate=cost(6 * rows * full * full, 7e6, rows * full),
        name="dense",
    )(*agg, *both, wn, ws)
    return results[:n], results[n], results[n + 1]


def wgrad_kernel(me_ref, *refs, n):
    agg, both, gp_ref, out_ref = refs[:n], refs[n : 2 * n], refs[2 * n], refs[-1]
    gp = gp_ref[...]
    rows = out_ref.shape[2]
    width = agg[0].shape[1]
    for j in range(n):
        for kind, left in enumerate((agg[j][...], both[j][0])):
            term = lax.dot_general(left, gp, TN, preferred_element_type=F32).astype(BF16)
            for i in range(n):
                q = lax.rem(me_ref[0] + i, n)
                for k in range(width // rows):
                    at = (kind * (width // rows) + k) * n + q
                    out_ref[at, j] = term[k * rows : (k + 1) * rows, i * TILE : (i + 1) * TILE]


def wgrad(me, agg, both, gp, after, dom_count):
    n = len(agg)
    rows, width = agg[0].shape
    size = 2 * width * n // dom_count
    vmem = pl.BlockSpec(memory_space=pltpu.VMEM)
    return pl.pallas_call(
        functools.partial(wgrad_kernel, n=n),
        in_specs=[pl.BlockSpec(memory_space=pltpu.SMEM)]
        + [vmem] * (2 * n + 1)
        + [pl.BlockSpec(memory_space=pl.ANY)],
        out_specs=vmem,
        out_shape=shape((dom_count, n, size, TILE), BF16),
        compiler_params=params(24),
        cost_estimate=cost(1e10, 4e6),
        name="wgrad",
    )(me, *agg, *both, gp, after)


PIECES = 6


def spmm_back_kernel(me_ref, pos_ref, *refs, n):
    adj, ga = refs[0], refs[1 : 1 + n]
    local_ref, away_ref, total, left_ref, stage, sems = refs[1 + n :]
    chunk, part = pl.program_id(0), pl.program_id(1)
    per_row = adj.shape[1]
    size = BLOCKS * TILE

    @pl.when((chunk == 0) & (part == 0))
    def _():
        total[...] = jnp.zeros_like(total)

    for s in range(n):

        @pl.when((chunk == s) & (part == 0))
        def _():
            for k in range(left_ref.shape[0]):
                left_ref[k] = ga[s][:, k * size : (k + 1) * size]

    first = (lax.rem(me_ref[0] + n - chunk, n) * pl.num_programs(1) + part) * BLOCKS
    for r in range(BLOCKS):
        base = (first + r) * per_row
        left = left_ref[part, :, r * TILE : (r + 1) * TILE]
        for t in range(0, per_row, 2):
            right = jnp.concatenate([adj[r, t], adj[r, t + 1]], axis=1)
            both = jnp.dot(left, right, preferred_element_type=F32)
            total[pos_ref[base + t]] += both[:, :TILE]
            total[pos_ref[base + t + 1]] += both[:, TILE:]

    @pl.when((chunk == n - 1) & (part == pl.num_programs(1) - 1))
    def _():
        own = local_ref.shape[0]
        step = away_ref.shape[0] // PIECES
        copies = [pltpu.make_async_copy(total.at[pl.ds(0, own)], local_ref, sems.at[PIECES])]
        copies[0].start()
        for k in range(PIECES):
            stage[k * step : (k + 1) * step] = total[own + k * step : own + (k + 1) * step].astype(BF16)
            copies.append(
                pltpu.make_async_copy(
                    stage.at[pl.ds(k * step, step)], away_ref.at[pl.ds(k * step, step)], sems.at[k]
                )
            )
            copies[-1].start()
        for copy in copies:
            copy.wait()


def spmm_back(me, pos, adj, ga, own, away):
    n = len(ga)
    row_tiles, per_row = adj.shape[:2]
    rows = ga[0].shape[1]
    inner = row_tiles // n // BLOCKS
    return pl.pallas_call(
        functools.partial(spmm_back_kernel, n=n),
        grid_spec=pltpu.PrefetchScalarGridSpec(
            num_scalar_prefetch=2,
            grid=(n, inner),
            in_specs=[adj_spec(per_row, inner, lambda i, me: lax.rem(me[0] + n - i, n))]
            + [pl.BlockSpec((TILE, rows), lambda i, k, me, pos: (0, 0))] * n,
            out_specs=[pl.BlockSpec(memory_space=pl.ANY)] * 2,
            scratch_shapes=[
                pltpu.VMEM((own + away, TILE, TILE), F32),
                pltpu.VMEM((inner, TILE, BLOCKS * TILE), BF16),
                pltpu.VMEM((away, TILE, TILE), BF16),
                pltpu.SemaphoreType.DMA((PIECES + 1,)),
            ],
        ),
        out_shape=[pltpu.HBM((own, TILE, TILE), F32), pltpu.HBM((away, TILE, TILE), BF16)],
        compiler_params=params(24),
        cost_estimate=cost(2 * row_tiles * per_row * TILE**3 * 2, 2.2e7),
        name="spmm_back",
    )(me, pos, adj, *ga)


def late_kernel(act_ref, gp_ref, ws_ref, after_ref, *pieces):
    del after_ref
    direct = lax.dot_general(gp_ref[...], ws_ref[...], NT, preferred_element_type=F32).astype(BF16)
    for j, piece in enumerate(pieces):
        piece[0] = act_ref[:, j * TILE : (j + 1) * TILE]
        piece[1] = direct[:, j * TILE : (j + 1) * TILE]


def late(act, gp, ws, after, n):
    rows, full = act.shape
    size = 256
    share = pl.BlockSpec((size, full), lambda i: (i, 0))
    return pl.pallas_call(
        late_kernel,
        grid=(rows // size,),
        in_specs=[
            share,
            share,
            pl.BlockSpec((full, full), lambda i: (0, 0)),
            pl.BlockSpec(memory_space=pl.ANY),
        ],
        out_specs=[pl.BlockSpec((2, size, TILE), lambda i: (0, i, 0))] * n,
        out_shape=[shape((2, rows, TILE), BF16)] * n,
        compiler_params=params(24),
        cost_estimate=cost(1e10, 6e6),
        name="late",
    )(act, gp, ws, after)


def finish_kernel(me_ref, ext_ref, *refs):
    pieces, (out_ref, grad_ref) = refs[:-2], refs[-2:]
    for s, piece in enumerate(pieces):

        @pl.when(pl.program_id(0) == s)
        def _():
            out_ref[...] = piece[0]
            for k in range(ext_ref.shape[0]):
                rows = slice(k * TILE, (k + 1) * TILE)
                total = piece[1, rows, :].astype(F32) + jnp.transpose(ext_ref[k])
                grad_ref[rows, :] = total.astype(BF16)


def finish(me, ext, pieces):
    n = len(pieces)
    share = pieces[0].shape[1]
    placed = pl.BlockSpec((share, TILE), lambda i, me: (lax.rem(me[0] + n - i, n), 0))
    return pl.pallas_call(
        finish_kernel,
        grid_spec=pltpu.PrefetchScalarGridSpec(
            num_scalar_prefetch=1,
            grid=(n,),
            in_specs=[
                pl.BlockSpec(
                    (share // TILE, TILE, TILE), lambda i, me: (lax.rem(me[0] + n - i, n), 0, 0)
                )
            ]
            + [pl.BlockSpec((2, share, TILE), lambda i, me: (0, 0, 0))] * n,
            out_specs=[placed, placed],
        ),
        out_shape=[shape((n * share, TILE), BF16)] * 2,
        compiler_params=params(24),
        cost_estimate=cost(1e6, 7e6),
        name="finish",
    )(me, ext, *pieces)


def scatter_kernel(ids_ref, counts_ref, val_ref, out_ref):
    groups = out_ref.shape[0] // LOW

    @pl.when(pl.program_id(0) == 0)
    def _():
        out_ref[...] = jnp.zeros_like(out_ref)

    for p in range(0, ids_ref.shape[0], 2):
        ids = masked_ids(ids_ref, counts_ref, p, 2)
        onehot = low_onehot(ids)
        values = jnp.concatenate([val_ref[p * CHUNKS + k] for k in range(2 * CHUNKS)], axis=1)
        zero = jnp.zeros_like(values)
        for g in range(0, groups, 2):
            pair = [jnp.where(in_group(ids, k), values, zero) for k in (g, g + 1)]
            both = lax.dot_general(
                onehot, jnp.concatenate(pair, axis=0), NT, preferred_element_type=F32
            )
            out_ref[g * LOW : (g + 1) * LOW, :] += both[:, :TILE]
            out_ref[(g + 1) * LOW : (g + 2) * LOW, :] += both[:, TILE:]


def scatter_rows(ids, counts, values, rows):
    peers = ids.shape[0]
    size = 8
    return pl.pallas_call(
        scatter_kernel,
        grid=(peers // size,),
        in_specs=[
            pl.BlockSpec((size, B), lambda i: (i, 0)),
            pl.BlockSpec(memory_space=pltpu.SMEM),
            pl.BlockSpec((size * CHUNKS, TILE, TILE), lambda i: (i, 0, 0)),
        ],
        out_specs=pl.BlockSpec((rows, TILE), lambda i: (0, 0)),
        out_shape=shape((rows, TILE), F32),
        compiler_params=params(40),
        cost_estimate=cost(2 * ids.size * rows * TILE, 4e6),
        name="scatter_rows",
    )(ids, counts, values)


def sum_kernel(terms_ref, after_ref, *outs):
    del after_ref
    total = jnp.sum(terms_ref[...].astype(F32), axis=0).astype(BF16)
    for j, out in enumerate(outs):
        out[...] = total[j]


def sum_terms(terms, after):
    n = terms.shape[1]
    return pl.pallas_call(
        sum_kernel,
        in_specs=[pl.BlockSpec(memory_space=pltpu.VMEM), pl.BlockSpec(memory_space=pl.ANY)],
        out_specs=[pl.BlockSpec(memory_space=pltpu.VMEM)] * n,
        out_shape=[shape(terms.shape[2:], BF16)] * n,
        compiler_params=params(16),
        cost_estimate=cost(1e9, 1e6),
        name="sum_terms",
    )(terms, after)


def spread_kernel(*refs):
    terms, out_ref = refs[:-2], refs[-1]
    total = terms[0][...].astype(F32)
    for term in terms[1:]:
        total = total + term[...].astype(F32)
    out_ref[...] = jnp.broadcast_to(total.astype(BF16)[None], out_ref.shape)


def spread_terms(terms, after, dom_count):
    return pl.pallas_call(
        spread_kernel,
        in_specs=[pl.BlockSpec(memory_space=pltpu.VMEM)] * len(terms)
        + [pl.BlockSpec(memory_space=pl.ANY)],
        out_specs=pl.BlockSpec(memory_space=pltpu.VMEM),
        out_shape=shape((dom_count, *terms[0].shape), BF16),
        compiler_params=params(8),
        cost_estimate=cost(1e5, 3e5),
        name="spread_terms",
    )(*terms, after)


def place_kernel(terms_ref, *outs):
    rows, width = terms_ref.shape[1:]
    n = outs[0].shape[1] // width
    for at in range(terms_ref.shape[0]):
        group, q = at // n, at % n
        per = outs[0].shape[0] // rows
        out = outs[group // per]
        first = group % per * rows
        out[first : first + rows, q * width : (q + 1) * width] = terms_ref[at].astype(F32)


def place_terms(terms, width, n):
    return pl.pallas_call(
        place_kernel,
        out_shape=[shape((width, n * width), F32)] * 2,
        compiler_params=params(8),
        cost_estimate=cost(1e5, 8e5),
        name="place_terms",
    )(terms)


def per_device(
    features, stale_features, grad_output, w_neigh, w_self, adj_tiles, tile_cols, send_idx, counts
):
    dom_count = lax.axis_size("dom")
    n = lax.axis_size("rep")
    row_count, width = features.shape
    row_tiles = row_count // TILE
    swap = functools.partial(
        lax.all_to_all, axis_name="dom", split_axis=0, concat_axis=0, tiled=True
    )
    me = lax.axis_index("rep").astype(jnp.int32).reshape(1)

    ids = send_idx[0]
    pos = tile_cols[0].reshape(-1)

    packed = gather_rows(ids, counts, stale_features)
    halo = swap(packed)
    own, wn, ws, adj, pieces = prep(
        me, features, grad_output, w_neigh, w_self, adj_tiles[0], packed, n
    )
    both = relative(exchange(pieces))

    agg = relative(exchange(spmm(me, pos, adj, [own, halo], n)))
    grad_agg, act, grad_pre = dense(agg, both, wn, ws)
    grad_agg = exchange(grad_agg)
    terms = swap(wgrad(me, agg, both, grad_pre, grad_agg[1], dom_count))

    local, away = spmm_back(me, pos, adj, grad_agg, row_tiles, dom_count * CHUNKS)
    returned = swap(away)
    pieces = exchange(late(act, grad_pre, ws, away, n))
    out, grad_input = finish(me, local, pieces)

    terms = exchange(sum_terms(terms, away))
    terms = swap(spread_terms(terms, returned, dom_count))
    grad_neigh, grad_self = place_terms(terms, width, n)

    grad_stale = scatter_rows(ids, counts, returned, row_count)
    return (out, grad_input, grad_stale, grad_neigh, grad_self)


def solution(mesh):
    in_specs = (
        P("dom", "rep"),
        P("dom", "rep"),
        P("dom", "rep"),
        P(),
        P(),
        P("dom", None, None, None, None),
        P("dom", None, None),
        P("dom", None, None),
        P("dom", None),
    )
    out_specs = (P("dom", "rep"), P("dom", "rep"), P("dom", "rep"), P("rep", None), P("rep", None))
    return jax.shard_map(
        per_device, mesh=mesh, in_specs=in_specs, out_specs=out_specs, check_vma=False
    )
```

time: 213 us -> 212 us (level)
  blocking collectives: 24.1 us -> 0 us
  local copies, waits for them, and re-layouts: 16.3 us -> 40.1 us
  starting transfers between devices: 39.9 us -> 50 us
  Pallas kernels: 65 us -> 60.3 us
  waiting for transfers between devices: 62.1 us -> 59 us
  other arithmetic: 2.51 us -> 0 us
    unnamed x41 -> x63, local copies, waits for them, and re-layouts: 11.3 us -> 40 us
    all_to_all x1 -> x0, blocking collectives: 24.1 us -> none  [per_device(): terms = swap(wgrad(me, agg, both, grad_pre, dom_count))]
    all_to_all x1, waiting for transfers between devices: 30.7 us -> 13 us  [per_device(): halo = swap(packed)]
    ppermute x15, waiting for transfers between devices: 25.1 us -> 36.6 us  [exchange(): lax.ppermute(pieces[s], 'rep', [(i, (i + s) % n) for i in range(n)])]
    all_to_all x1 -> x2, starting transfers between devices: 5.6 us -> 15.8 us  [the longest x1 9.46 us: per_device(): terms = swap(wgrad(me, agg, both, grad_pre, grad_agg[1], dom_count))]
    pallas_call x1, Pallas kernels: 12.9 us -> 7.63 us  [spmm(): pl.pallas_call(functools.partial(spmm_kernel, n=n), grid_spec=pltpu.Prefe...]
    pallas_call x1, Pallas kernels: 1.92 us -> 6.58 us  [prep(): pl.pallas_call(prep_kernel, grid_spec=pltpu.PrefetchScalarGridSpec(num_sc...]
    pallas_call x1, Pallas kernels: 13.5 us -> 9.4 us  [spmm_back(): pl.pallas_call(functools.partial(spmm_back_kernel, n=n), grid_spec=pltpu....]
  transfers between devices with their start and end apart: 18 -> 19, of which waited for: 9 -> 10; matrix products, arithmetic and copies ran while one was open for 3% -> 0% of each run, Pallas kernels for 16% -> 19%
where the time goes in v2:
time: 212 us; the launch traced here: 210 us
  Pallas kernels  60.3 us (28%)
  waiting for transfers between devices  59 us (28%)
  starting transfers between devices  50 us (24%)
  local copies, waits for them, and re-layouts  40.1 us (19%)
    unnamed x63, local copies, waits for them, and re-layouts  40 us
    ppermute x15, waiting for transfers between devices, exchange(): lax.ppermute(pieces[s], 'rep', [(i, (i + s) % n) for i in range(n)])  36.6 us
    ppermute x15, starting transfers between devices, exchange(): lax.ppermute(pieces[s], 'rep', [(i, (i + s) % n) for i in range(n)])  16.7 us
    all_to_all x1, waiting for transfers between devices, per_device(): halo = swap(packed)  13 us
    pallas_call x1, Pallas kernels, scatter_rows(): pl.pallas_call(scatter_kernel, grid=(peers // size,), in_specs=[pl.BlockS...  12.5 us
    pallas_call x1, Pallas kernels, gather_rows(): pl.pallas_call(gather_kernel, grid=(peers // size,), in_specs=[pl.BlockSp...  11.7 us
    all_to_all x1, starting transfers between devices, per_device(): terms = swap(wgrad(me, agg, both, grad_pre, grad_agg[1], dom_count))  9.46 us
    all_to_all x1, starting transfers between devices, per_device(): halo = swap(packed)  9.44 us
  transfers between devices with their start and end apart: 19, of which 10 were waited for; matrix products, arithmetic and copies ran while one was open for 0% of the time, Pallas kernels for 19%

profile of v2, /device:TPU:1, one launch (start us, length us, event | category | flops | bytes accessed | tf_op | source)
XLA Modules:
  0.0 210.3 jit_solution(15107509770909708931)
XLA Ops:
  3.2 11.7 %gather_rows.1.after_ref = bf16[96,128,128]{2,1,0:T(8,128)(2,1)S(1)} custom-call(s32[32,384]{1,0:T(8,128)S(1)} %bitcast.3, s32[1,32]{1,0:T(1,128)S(1)} %copy-done.19, bf16[3072,128]{1,0:T(8,128)(2,1)S(1)} %copy-done.12), custom_call_target="tpu_custom_call" | custom-call | flops 9663676416 | bytes 4000000 | tf_op jit(solution)/shard_map/gather_rows/pallas_call | solution.py:82
  16.6 9.4 %all-to-all-start = ((bf16[96,128,128]{2,1,0:T(8,128)(2,1)}), bf16[96,128,128]{2,1,0:T(8,128)(2,1)S(1)}, u32[]{:S(2)}, u32[]{:S(2)}) async-start(bf16[96,128,128]{2,1,0:T(8,128)(2,1)} %copy-done.6), calls=%async_computation | async-start | bytes 6291456 | tf_op jit(solution)/shard_map/all_to_all | solution.py:605
  32.4 6.6 %prep.1 = (bf16[24,128,128]{2,1,0:T(8,128)(2,1)S(1)}, bf16[512,512]{1,0:T(8,128)(2,1)S(1)}, bf16[512,512]{1,0:T(8,128)(2,1)S(1)}, bf16[24,20,128,128]{3,2,1,0:T(...) custom-call(s32[1]{0:T(128)} %bitcast.me_ref, ...), custom_call_target="tpu_custom_call" | custom-call | flops 10000000000 | bytes 6000000 | tf_op jit(solution)/shard_map/prep/pallas_call | solution.py:156
  39.0 5.4 %copy-done = bf16[24,20,128,128]{3,2,1,0:T(8,128)(2,1)} copy-done((bf16[24,20,128,128]{3,2,1,0:T(8,128)(2,1)}, bf16[24,20,128,128]{3,2,1,0:T(8,128)(2,1)S(1)}, u32[]{:S(2)}) %copy-start) | copy-done | bytes 15728664
  47.6 2.7 %collective-permute-start.3 = (bf16[2,768,128]{2,1,0:T(8,128)(2,1)}, bf16[2,768,128]{2,1,0:T(8,128)(2,1)S(1)}, u32[]{:S(2)}, u32[]{:S(2)}) collective-permute-start(bf16[2,768,128]{2,1,0:T(8,128)(2,1)} %get-tuple-element.44), channel_id=1, source_target_pairs={{0,3},{1,0},{2,1},{3,2},{4,7},{5,4},{6,5},{7,6},{8,11},{9,8},{10,9... | collective-permute-start | bytes 1179656 | tf_op jit(solution)/shard_map/ppermute | solution.py:102
  52.2 13.0 %all-to-all-done.refs_2_ = bf16[96,128,128]{2,1,0:T(8,128)(2,1)S(1)} async-done(((bf16[96,128,128]{2,1,0:T(8,128)(2,1)}), bf16[96,128,128]{2,1,0:T(8,128)(2,1)S(1)}, u32[]{:S(2)}, u32[]{:S(2)}) %all-to-all-start) | async-done | bytes 3145760 | tf_op jit(solution)/shard_map/all_to_all | solution.py:605
  65.3 5.5 %copy-done.1 = bf16[24,20,128,128]{3,2,1,0:T(8,128)(2,1)S(1)} copy-done((bf16[24,20,128,128]{3,2,1,0:T(8,128)(2,1)S(1)}, bf16[24,20,128,128]{3,2,1,0:T(8,128)(2,1)}, u32[]{:S(2)}) %copy-start.1) | copy-done | bytes 15728664
  71.9 7.6 %spmm.1 = (bf16[768,128]{1,0:T(8,128)(2,1)S(1)}, bf16[768,128]{1,0:T(8,128)(2,1)S(1)}, bf16[768,128]{1,0:T(8,128)(2,1)S(1)}, bf16[768,128]{1,0:T(8,128)(2,1)S(1)}) custom-call(s32[1]{0:T(128)} %bitcast.me_ref, s32[480]{0:T(512)S(1)} %reshape_squeeze.3.pos_ref, bf16[24,20,128,128]{3,2,1,0:T(8,128)(2,1)S(1)} %copy-done.1, ...), custom_call_target="tpu_custom_call" | custom-call | flops 4026531840 | bytes 20000000 | tf_op jit(solution)/shard_map/spmm/pallas_call | solution.py:245
  79.5 2.8 %collective-permute-start = (bf16[768,128]{1,0:T(8,128)(2,1)S(1)}, bf16[768,128]{1,0:T(8,128)(2,1)S(1)}, u32[]{:S(2)}, u32[]{:S(2)}) collective-permute-start(bf16[768,128]{1,0:T(8,128)(2,1)S(1)} %get-tuple-element.40), channel_id=1, source_target_pairs={{0,3},{1,0},{2,1},{3,2},{4,7},{5,4},{6,5},{7,6},{8,11},{9,8},{10,9... | collective-permute-start | bytes 589832 | tf_op jit(solution)/shard_map/ppermute | solution.py:102
  83.4 4.0 %collective-permute-done.refs_1_ = bf16[768,128]{1,0:T(8,128)(2,1)S(1)} collective-permute-done((bf16[768,128]{1,0:T(8,128)(2,1)S(1)}, bf16[768,128]{1,0:T(8,128)(2,1)S(1)}, u32[]{:S(2)}, u32[]{:S(2)}) %collective-permute-start) | collective-permute-done | bytes 196640 | tf_op jit(solution)/shard_map/ppermute | solution.py:102
  88.4 4.8 %collective-permute-done.2.refs_3_ = bf16[768,128]{1,0:T(8,128)(2,1)S(1)} collective-permute-done((bf16[768,128]{1,0:T(8,128)(2,1)S(1)}, bf16[768,128]{1,0:T(8,128)(2,1)S(1)}, u32[]{:S(2)}, u32[]{:S(2)}) %collective-permute-start.2) | collective-permute-done | bytes 196640 | tf_op jit(solution)/shard_map/ppermute | solution.py:102
  93.2 5.1 %dense.1 = (bf16[128,768]{1,0:T(8,128)(2,1)S(1)}, bf16[128,768]{1,0:T(8,128)(2,1)S(1)}, bf16[128,768]{1,0:T(8,128)(2,1)S(1)}, bf16[128,768]{1,0:T(8,128)(2,1)S(1...) custom-call(bf16[768,128]{1,0:T(8,128)(2,1)S(1)} %get-tuple-element.39.refs_0_, ...), custom_call_target="tpu_custom_call" | custom-call | flops 1207959552 | bytes 7000000 | tf_op jit(solution)/shard_map/dense/pallas_call | solution.py:297
  98.3 5.7 %collective-permute-done.6.refs_2_.refs_9_ = bf16[128,768]{1,0:T(8,128)(2,1)S(1)} collective-permute-done((bf16[128,768]{1,0:T(8,128)(2,1)S(1)}, bf16[128,768]{1,0:T(8,128)(2,1)S(1)}, u32[]{:S(2)}, u32[]{:S(2)}) %collective-permute-start.6) | collective-permute-done | bytes 196640 | tf_op jit(solution)/shard_map/ppermute | solution.py:102
  105.1 3.1 %wgrad.1 = bf16[32,4,32,128]{3,2,1,0:T(8,128)(2,1)} custom-call(s32[1]{0:T(128)} %bitcast.me_ref, bf16[768,128]{1,0:T(8,128)(2,1)S(1)} %get-tuple-element.39.refs_0_, bf16[768,128]{1,0:T(8,128)(2,1)S(1)} %collective-permute-done.refs_1_, bf16[768,128]{1,0:T(8,128)(2,1)S(1)} %collective-permute-done.1.refs_2_, ...), custom_call_target="tpu_custom_call" | custom-call | flops 10000000000 | bytes 4000000 | tf_op jit(solution)/shard_map/wgrad/pallas_call | solution.py:332
  108.3 9.5 %all-to-all-start.2 = ((bf16[32,4,32,128]{3,2,1,0:T(8,128)(2,1)}), bf16[32,4,32,128]{3,2,1,0:T(8,128)(2,1)S(1)}, u32[]{:S(2)}, u32[]{:S(2)}) async-start(bf16[32,4,32,128]{3,2,1,0:T(8,128)(2,1)} %wgrad.1), calls=%async_computation.2 | async-start | bytes 2097152 | tf_op jit(solution)/shard_map/all_to_all | solution.py:614
  119.0 6.6 %collective-permute-done.7.refs_3_ = bf16[128,768]{1,0:T(8,128)(2,1)S(1)} collective-permute-done((bf16[128,768]{1,0:T(8,128)(2,1)S(1)}, bf16[128,768]{1,0:T(8,128)(2,1)S(1)}, u32[]{:S(2)}, u32[]{:S(2)}) %collective-permute-start.7) | collective-permute-done | bytes 196640 | tf_op jit(solution)/shard_map/ppermute | solution.py:102
  126.8 5.5 %copy-done.2 = bf16[24,20,128,128]{3,2,1,0:T(8,128)(2,1)S(1)} copy-done((bf16[24,20,128,128]{3,2,1,0:T(8,128)(2,1)S(1)}, bf16[24,20,128,128]{3,2,1,0:T(8,128)(2,1)}, u32[]{:S(2)}) %copy-start.2) | copy-done | bytes 15728664
  132.2 9.4 %spmm_back.1 = (f32[24,128,128]{2,1,0:T(8,128)}, bf16[96,128,128]{2,1,0:T(8,128)(2,1)}) custom-call(s32[1]{0:T(128)} %bitcast.me_ref, s32[480]{0:T(512)S(1)} %reshape_squeeze.3.pos_ref, bf16[24,20,128,128]{3,2,1,0:T(8,128)(2,1)S(1)} %copy-done.2, bf16[128,768]{1,0:T(8,128)(2,1)S(1)} %get-tuple-element.49.refs_1_, ...), custom_call_target="tpu_custom_call" | custom-call | flops 4026531840 | bytes 22000000 | tf_op jit(solution)/shard_map/spmm_back/pallas_call | solution.py:399
  142.6 8.1 %all-to-all-start.1 = ((bf16[96,128,128]{2,1,0:T(8,128)(2,1)}), bf16[96,128,128]{2,1,0:T(8,128)(2,1)S(1)}, u32[]{:S(2)}, u32[]{:S(2)}) async-start(bf16[96,128,128]{2,1,0:T(8,128)(2,1)} %get-tuple-element.56.after_ref), calls=%async_computation.1 | async-start | bytes 6291456 | tf_op jit(solution)/shard_map/all_to_all | solution.py:617
  163.9 5.2 %collective-permute-done.9.refs_1_ = bf16[2,768,128]{2,1,0:T(8,128)(2,1)S(1)} collective-permute-done((bf16[2,768,128]{2,1,0:T(8,128)(2,1)S(1)}, bf16[2,768,128]{2,1,0:T(8,128)(2,1)S(1)}, u32[]{:S(2)}, u32[]{:S(2)}) %collective-permute-start.9) | collective-permute-done | bytes 393248 | tf_op jit(solution)/shard_map/ppermute | solution.py:102
  170.2 8.1 %collective-permute-done.10.refs_2_ = bf16[2,768,128]{2,1,0:T(8,128)(2,1)S(1)} collective-permute-done((bf16[2,768,128]{2,1,0:T(8,128)(2,1)S(1)}, bf16[2,768,128]{2,1,0:T(8,128)(2,1)S(1)}, u32[]{:S(2)}, u32[]{:S(2)}) %collective-permute-start.10) | collective-permute-done | bytes 393248 | tf_op jit(solution)/shard_map/ppermute | solution.py:102
  180.5 9.4 %all-to-all-done.1.val_ref.refs_4_ = bf16[96,128,128]{2,1,0:T(8,128)(2,1)S(1)} async-done(((bf16[96,128,128]{2,1,0:T(8,128)(2,1)}), bf16[96,128,128]{2,1,0:T(8,128)(2,1)S(1)}, u32[]{:S(2)}, u32[]{:S(2)}) %all-to-all-start.1) | async-done | bytes 3145760 | tf_op jit(solution)/shard_map/all_to_all | solution.py:617
  190.6 6.4 %all-to-all-start.3 = ((bf16[32,32,128]{2,1,0:T(8,128)(2,1)}), bf16[32,32,128]{2,1,0:T(8,128)(2,1)S(1)}, u32[]{:S(2)}, u32[]{:S(2)}) async-start(bf16[32,32,128]{2,1,0:T(8,128)(2,1)} %copy-done.9), calls=%async_computation.3 | async-start | bytes 524288 | tf_op jit(solution)/shard_map/all_to_all | solution.py:622
  197.0 12.5 %scatter_rows.1 = f32[3072,128]{1,0:T(8,128)} custom-call(s32[32,384]{1,0:T(8,128)S(1)} %bitcast.4, s32[1,32]{1,0:T(1,128)S(1)} %copy-done.20, bf16[96,128,128]{2,1,0:T(8,128)(2,1)S(1)} %all-to-all-done.1.val_ref.refs_4_), custom_call_target="tpu_custom_call" | custom-call | flops 9663676416 | bytes 4000000 | tf_op jit(solution)/shard_map/scatter_rows/pallas_call | solution.py:511
  (90 shorter events, 41.4 us)
Async XLA Ops:
  16.6 48.6 %all-to-all-start = ((bf16[96,128,128]{2,1,0:T(8,128)(2,1)}), bf16[96,128,128]{2,1,0:T(8,128)(2,1)S(1)}, u32[]{:S(2)}, u32[]{:S(2)}) async-start(bf16[96,128,128]{2,1,0:T(8,128)(2,1)} %copy-done.6), calls=%async_computation | async-start | bytes 6291456 | tf_op jit(solution)/shard_map/all_to_all | solution.py:605
  47.6 35.1 %collective-permute-start.3 = (bf16[2,768,128]{2,1,0:T(8,128)(2,1)}, bf16[2,768,128]{2,1,0:T(8,128)(2,1)S(1)}, u32[]{:S(2)}, u32[]{:S(2)}) collective-permute-start(bf16[2,768,128]{2,1,0:T(8,128)(2,1)} %get-tuple-element.44), channel_id=1, source_target_pairs={{0,3},{1,0},{2,1},{3,2},{4,7},{5,4},{6,5},{7,6},{8,11},{9,8},{10,9... | collective-permute-start | bytes 1179656 | tf_op jit(solution)/shard_map/ppermute | solution.py:102
  50.3 33.0 %collective-permute-start.4 = (bf16[2,768,128]{2,1,0:T(8,128)(2,1)}, bf16[2,768,128]{2,1,0:T(8,128)(2,1)}, u32[]{:S(2)}, u32[]{:S(2)}) collective-permute-start(bf16[2,768,128]{2,1,0:T(8,128)(2,1)} %get-tuple-element.45), channel_id=1, source_target_pairs={{0,2},{1,3},{2,0},{3,1},{4,6},{5,7},{6,4},{7,5},{8,10},{9,11},{10,... | collective-permute-start | bytes 1179656 | tf_op jit(solution)/shard_map/ppermute | solution.py:102
  50.7 32.7 %collective-permute-start.5 = (bf16[2,768,128]{2,1,0:T(8,128)(2,1)}, bf16[2,768,128]{2,1,0:T(8,128)(2,1)}, u32[]{:S(2)}, u32[]{:S(2)}) collective-permute-start(bf16[2,768,128]{2,1,0:T(8,128)(2,1)} %get-tuple-element.46), channel_id=1, source_target_pairs={{0,1},{1,2},{2,3},{3,0},{4,5},{5,6},{6,7},{7,4},{8,9},{9,10},{10,1... | collective-permute-start | bytes 1179656 | tf_op jit(solution)/shard_map/ppermute | solution.py:102
  71.9 21.3 %copy-start.25 = (bf16[512,512]{1,0:T(8,128)(2,1)S(1)}, bf16[512,512]{1,0:T(8,128)(2,1)}, u32[]{:S(2)}) copy-start(bf16[512,512]{1,0:T(8,128)(2,1)} %copy-done.24) | copy-start | bytes 1572868
  71.9 21.4 %copy-start.28 = (bf16[512,512]{1,0:T(8,128)(2,1)S(1)}, bf16[512,512]{1,0:T(8,128)(2,1)}, u32[]{:S(2)}) copy-start(bf16[512,512]{1,0:T(8,128)(2,1)} %copy-done.27) | copy-start | bytes 1572868
  71.9 21.4 %copy-start.30 = (bf16[2,768,128]{2,1,0:T(8,128)(2,1)S(1)}, bf16[2,768,128]{2,1,0:T(8,128)(2,1)}, u32[]{:S(2)}) copy-start(bf16[2,768,128]{2,1,0:T(8,128)(2,1)} %copy-done.29) | copy-start | bytes 1179652
  79.5 7.9 %collective-permute-start = (bf16[768,128]{1,0:T(8,128)(2,1)S(1)}, bf16[768,128]{1,0:T(8,128)(2,1)S(1)}, u32[]{:S(2)}, u32[]{:S(2)}) collective-permute-start(bf16[768,128]{1,0:T(8,128)(2,1)S(1)} %get-tuple-element.40), channel_id=1, source_target_pairs={{0,3},{1,0},{2,1},{3,2},{4,7},{5,4},{6,5},{7,6},{8,11},{9,8},{10,9... | collective-permute-start | bytes 589832 | tf_op jit(solution)/shard_map/ppermute | solution.py:102
  82.3 6.1 %collective-permute-start.1 = (bf16[768,128]{1,0:T(8,128)(2,1)S(1)}, bf16[768,128]{1,0:T(8,128)(2,1)S(1)}, u32[]{:S(2)}, u32[]{:S(2)}) collective-permute-start(bf16[768,128]{1,0:T(8,128)(2,1)S(1)} %get-tuple-element.41), channel_id=1, source_target_pairs={{0,2},{1,3},{2,0},{3,1},{4,6},{5,7},{6,4},{7,5},{8,10},{9,11},{10,... | collective-permute-start | bytes 589832 | tf_op jit(solution)/shard_map/ppermute | solution.py:102
  82.7 10.5 %collective-permute-start.2 = (bf16[768,128]{1,0:T(8,128)(2,1)S(1)}, bf16[768,128]{1,0:T(8,128)(2,1)S(1)}, u32[]{:S(2)}, u32[]{:S(2)}) collective-permute-start(bf16[768,128]{1,0:T(8,128)(2,1)S(1)} %get-tuple-element.42), channel_id=1, source_target_pairs={{0,1},{1,2},{2,3},{3,0},{4,5},{5,6},{6,7},{7,4},{8,9},{9,10},{10,1... | collective-permute-start | bytes 589832 | tf_op jit(solution)/shard_map/ppermute | solution.py:102
  98.3 5.7 %collective-permute-start.6 = (bf16[128,768]{1,0:T(8,128)(2,1)S(1)}, bf16[128,768]{1,0:T(8,128)(2,1)S(1)}, u32[]{:S(2)}, u32[]{:S(2)}) collective-permute-start(bf16[128,768]{1,0:T(8,128)(2,1)S(1)} %get-tuple-element.50), channel_id=1, source_target_pairs={{0,1},{1,2},{2,3},{3,0},{4,5},{5,6},{6,7},{7,4},{8,9},{9,10},{10,1... | collective-permute-start | bytes 589832 | tf_op jit(solution)/shard_map/ppermute | solution.py:102
  108.3 33.3 %all-to-all-start.2 = ((bf16[32,4,32,128]{3,2,1,0:T(8,128)(2,1)}), bf16[32,4,32,128]{3,2,1,0:T(8,128)(2,1)S(1)}, u32[]{:S(2)}, u32[]{:S(2)}) async-start(bf16[32,4,32,128]{3,2,1,0:T(8,128)(2,1)} %wgrad.1), calls=%async_computation.2 | async-start | bytes 2097152 | tf_op jit(solution)/shard_map/all_to_all | solution.py:614
  117.8 7.9 %collective-permute-start.7 = (bf16[128,768]{1,0:T(8,128)(2,1)S(1)}, bf16[128,768]{1,0:T(8,128)(2,1)S(1)}, u32[]{:S(2)}, u32[]{:S(2)}) collective-permute-start(bf16[128,768]{1,0:T(8,128)(2,1)S(1)} %get-tuple-element.51), channel_id=1, source_target_pairs={{0,2},{1,3},{2,0},{3,1},{4,6},{5,7},{6,4},{7,5},{8,10},{9,11},{10,... | collective-permute-start | bytes 589832 | tf_op jit(solution)/shard_map/ppermute | solution.py:102
  117.9 8.9 %collective-permute-start.8 = (bf16[128,768]{1,0:T(8,128)(2,1)S(1)}, bf16[128,768]{1,0:T(8,128)(2,1)S(1)}, u32[]{:S(2)}, u32[]{:S(2)}) collective-permute-start(bf16[128,768]{1,0:T(8,128)(2,1)S(1)} %get-tuple-element.52), channel_id=1, source_target_pairs={{0,3},{1,0},{2,1},{3,2},{4,7},{5,4},{6,5},{7,6},{8,11},{9,8},{10,9... | collective-permute-start | bytes 589832 | tf_op jit(solution)/shard_map/ppermute | solution.py:102
  142.6 47.2 %all-to-all-start.1 = ((bf16[96,128,128]{2,1,0:T(8,128)(2,1)}), bf16[96,128,128]{2,1,0:T(8,128)(2,1)S(1)}, u32[]{:S(2)}, u32[]{:S(2)}) async-start(bf16[96,128,128]{2,1,0:T(8,128)(2,1)} %get-tuple-element.56.after_ref), calls=%async_computation.1 | async-start | bytes 6291456 | tf_op jit(solution)/shard_map/all_to_all | solution.py:617
  157.1 21.3 %copy-start.8 = (f32[24,128,128]{2,1,0:T(8,128)S(1)}, f32[24,128,128]{2,1,0:T(8,128)}, u32[]{:S(2)}) copy-start(f32[24,128,128]{2,1,0:T(8,128)} %get-tuple-element.53.ext_ref) | copy-start | bytes 4718596
  157.1 11.9 %collective-permute-start.9 = (bf16[2,768,128]{2,1,0:T(8,128)(2,1)S(1)}, bf16[2,768,128]{2,1,0:T(8,128)(2,1)S(1)}, u32[]{:S(2)}, u32[]{:S(2)}) collective-permute-start(bf16[2,768,128]{2,1,0:T(8,128)(2,1)S(1)} %get-tuple-element.58), channel_id=1, source_target_pairs={{0,1},{1,2},{2,3},{3,0},{4,5},{5,6},{6,7},{7,4},{8,9},{9,10},{10,1... | collective-permute-start | bytes 1179656 | tf_op jit(solution)/shard_map/ppermute | solution.py:102
  159.2 19.1 %collective-permute-start.10 = (bf16[2,768,128]{2,1,0:T(8,128)(2,1)S(1)}, bf16[2,768,128]{2,1,0:T(8,128)(2,1)S(1)}, u32[]{:S(2)}, u32[]{:S(2)}) collective-permute-start(bf16[2,768,128]{2,1,0:T(8,128)(2,1)S(1)} %get-tuple-element.59), channel_id=1, source_target_pairs={{0,2},{1,3},{2,0},{3,1},{4,6},{5,7},{6,4},{7,5},{8,10},{9,11},{10,... | collective-permute-start | bytes 1179656 | tf_op jit(solution)/shard_map/ppermute | solution.py:102
  160.9 17.4 %collective-permute-start.11 = (bf16[2,768,128]{2,1,0:T(8,128)(2,1)S(1)}, bf16[2,768,128]{2,1,0:T(8,128)(2,1)S(1)}, u32[]{:S(2)}, u32[]{:S(2)}) collective-permute-start(bf16[2,768,128]{2,1,0:T(8,128)(2,1)S(1)} %get-tuple-element.60), channel_id=1, source_target_pairs={{0,3},{1,0},{2,1},{3,2},{4,7},{5,4},{6,5},{7,6},{8,11},{9,8},{10,9... | collective-permute-start | bytes 1179656 | tf_op jit(solution)/shard_map/ppermute | solution.py:102
  162.1 18.4 %collective-permute-start.12 = (bf16[32,128]{1,0:T(8,128)(2,1)S(1)}, bf16[32,128]{1,0:T(8,128)(2,1)S(1)}, u32[]{:S(2)}, u32[]{:S(2)}) collective-permute-start(bf16[32,128]{1,0:T(8,128)(2,1)S(1)} %get-tuple-element.64), channel_id=1, source_target_pairs={{0,1},{1,2},{2,3},{3,0},{4,5},{5,6},{6,7},{7,4},{8,9},{9,10},{10,1... | collective-permute-start | bytes 24584 | tf_op jit(solution)/shard_map/ppermute | solution.py:102
  162.6 17.9 %collective-permute-start.13 = (bf16[32,128]{1,0:T(8,128)(2,1)S(1)}, bf16[32,128]{1,0:T(8,128)(2,1)S(1)}, u32[]{:S(2)}, u32[]{:S(2)}) collective-permute-start(bf16[32,128]{1,0:T(8,128)(2,1)S(1)} %get-tuple-element.65), channel_id=1, source_target_pairs={{0,2},{1,3},{2,0},{3,1},{4,6},{5,7},{6,4},{7,5},{8,10},{9,11},{10,... | collective-permute-start | bytes 24584 | tf_op jit(solution)/shard_map/ppermute | solution.py:102
  169.0 11.4 %collective-permute-start.14 = (bf16[32,128]{1,0:T(8,128)(2,1)S(1)}, bf16[32,128]{1,0:T(8,128)(2,1)S(1)}, u32[]{:S(2)}, u32[]{:S(2)}) collective-permute-start(bf16[32,128]{1,0:T(8,128)(2,1)S(1)} %get-tuple-element.66), channel_id=1, source_target_pairs={{0,3},{1,0},{2,1},{3,2},{4,7},{5,4},{6,5},{7,6},{8,11},{9,8},{10,9... | collective-permute-start | bytes 24584 | tf_op jit(solution)/shard_map/ppermute | solution.py:102
  178.3 18.6 %copy-start.20 = (s32[1,32]{1,0:T(1,128)S(1)}, s32[1,32]{1,0:T(1,128)}, u32[]{:S(2)}) copy-start(s32[1,32]{1,0:T(1,128)} %counts_ref.3) | copy-start | bytes 388
  190.6 18.9 %all-to-all-start.3 = ((bf16[32,32,128]{2,1,0:T(8,128)(2,1)}), bf16[32,32,128]{2,1,0:T(8,128)(2,1)S(1)}, u32[]{:S(2)}, u32[]{:S(2)}) async-start(bf16[32,32,128]{2,1,0:T(8,128)(2,1)} %copy-done.9), calls=%async_computation.3 | async-start | bytes 524288 | tf_op jit(solution)/shard_map/all_to_all | solution.py:622
  (26 other events, 63.9 us)

commit v3 on v2

--- a/solution.py
+++ b/solution.py
@@ -33,8 +33,8 @@
     return jnp.transpose(block.astype(F32))
 
 
-def masked_ids(ids_ref, counts_ref, first, peers):
-    base = pl.program_id(0) * ids_ref.shape[0]
+def masked_ids(ids_ref, counts_ref, first, peers, skipped=0):
+    base = (pl.program_id(0) + skipped) * ids_ref.shape[0]
     slot = lax.broadcasted_iota(jnp.int32, (1, ids_ref.shape[1]), 1)
     rows = [
         jnp.where(slot < counts_ref[0, base + p], ids_ref[p : p + 1, :], -1)
@@ -90,7 +90,7 @@
         out_specs=pl.BlockSpec((size * CHUNKS, TILE, TILE), lambda i: (i, 0, 0)),
         out_shape=shape((peers * CHUNKS, TILE, TILE), BF16),
         scratch_shapes=[pltpu.VMEM((rows // LOW * TILE, LOW), BF16)],
-        compiler_params=params(48),
+        compiler_params=params(56),
         cost_estimate=cost(2 * ids.size * rows * cols, 4e6),
         name="gather_rows",
     )(ids, counts, table)
@@ -108,26 +108,10 @@
     return [received[(n - j) % n] for j in range(n)]
 
 
-def prep_kernel(
-    me_ref, feat_ref, up_ref, wn_ref, ws_ref, adj_ref, after_ref, own_ref, wn_out, ws_out, adj_out, *refs
-):
+def prep_kernel(me_ref, feat_ref, up_ref, wn_ref, ws_ref, after_ref, own_ref, wn_out, ws_out, *pieces):
     del after_ref
-    pieces, sems = refs[:-1], refs[-1]
     step = pl.program_id(0)
     n = len(pieces)
-    part = adj_ref.shape[0] // sems.shape[0]
-    copies = [
-        pltpu.make_async_copy(
-            adj_ref.at[pl.ds(k * part, part)], adj_out.at[pl.ds(k * part, part)], sems.at[k]
-        )
-        for k in range(sems.shape[0])
-    ]
-
-    @pl.when(step == 0)
-    def _():
-        for copy in copies:
-            copy.start()
-
     for k in range(own_ref.shape[0]):
         own_ref[k] = turned(feat_ref[k * TILE : (k + 1) * TILE, :]).astype(BF16)
     for j, piece in enumerate(pieces):
@@ -140,64 +124,67 @@
             piece[0] = feat_ref[...]
             piece[1] = up_ref[...]
 
-    @pl.when(step == n - 1)
-    def _():
-        for copy in copies:
-            copy.wait()
-
-
-def prep(me, features, upstream, wn, ws, adj, after, n):
+
+def prep(me, features, upstream, wn, ws, after, n):
     rows, width = features.shape
     share = rows // n
     full = wn.shape[0]
     chunk = pl.BlockSpec((share, width), lambda i, me: (lax.rem(me[0] + i, n), 0))
     weight = pl.BlockSpec((width, full), lambda i, me: (lax.rem(me[0] + i, n), 0))
     placed = pl.BlockSpec((width, full), lambda i, me: (i, 0))
-    own, wn, ws, adj, *pieces = pl.pallas_call(
+    own, wn, ws, *pieces = pl.pallas_call(
         prep_kernel,
         grid_spec=pltpu.PrefetchScalarGridSpec(
             num_scalar_prefetch=1,
             grid=(n,),
-            in_specs=[chunk, chunk, weight, weight] + [pl.BlockSpec(memory_space=pl.ANY)] * 2,
+            in_specs=[chunk, chunk, weight, weight, pl.BlockSpec(memory_space=pl.ANY)],
             out_specs=[
                 pl.BlockSpec(
                     (share // TILE, TILE, TILE), lambda i, me: (lax.rem(me[0] + i, n), 0, 0)
                 ),
                 placed,
                 placed,
-                pl.BlockSpec(memory_space=pl.ANY),
             ]
             + [pl.BlockSpec((2, share, width), lambda i, me: (0, 0, 0))] * n,
-            scratch_shapes=[pltpu.SemaphoreType.DMA((4,))],
         ),
         out_shape=[
-            shape((rows // TILE, TILE, TILE), BF16),
-            shape((full, full), BF16),
-            shape((full, full), BF16),
-            pltpu.VMEM(adj.shape, BF16),
+            pltpu.HBM((rows // TILE, TILE, TILE), BF16),
+            pltpu.HBM((full, full), BF16),
+            pltpu.HBM((full, full), BF16),
         ]
         + [shape((2, share, width), BF16)] * n,
-        compiler_params=params(16),
+        compiler_params=params(56),
         cost_estimate=cost(1e10, 6e6),
         name="prep",
-    )(me, features, upstream, wn, ws, adj, after)
-    return own, wn, ws, adj, pieces
+    )(me, features, upstream, wn, ws, after)
+    return own, wn, ws, pieces
 
 
 BLOCKS = 3
 
 
-def adj_spec(per_row, inner, chunk_of):
-    return pl.BlockSpec(
-        (BLOCKS, per_row, TILE, TILE),
-        lambda i, k, me, pos: (chunk_of(i, me) * inner + k, 0, 0, 0),
+def adj_copies(adj_ref, held, sems, inner, n, chunk_of):
+    def copy(step):
+        first = (chunk_of(step // inner) * inner + lax.rem(step, inner)) * BLOCKS
+        return pltpu.make_async_copy(
+            adj_ref.at[pl.ds(first, BLOCKS)], held.at[pl.ds(step * BLOCKS, BLOCKS)], sems.at[step]
+        )
+
+    return copy
+
+
+def spmm_kernel(me_ref, pos_ref, *refs, n):
+    adj_ref, parts, outs, (ext, sems, adj, adj_sems) = (
+        refs[0],
+        refs[1 : -n - 4],
+        refs[-n - 4 : -4],
+        refs[-4:],
     )
-
-
-def spmm_kernel(me_ref, pos_ref, *refs, n):
-    adj, parts, outs, (ext, sems) = refs[0], refs[1 : -n - 2], refs[-n - 2 : -2], refs[-2:]
     chunk, part = pl.program_id(0), pl.program_id(1)
+    inner = adj_sems.shape[0] // n
+    step = chunk * inner + part
     per_row = adj.shape[1]
+    copy_of = adj_copies(adj_ref, adj, adj_sems, inner, n, lambda c: lax.rem(me_ref[0] + c, n))
 
     @pl.when((chunk == 0) & (part == 0))
     def _():
@@ -213,16 +200,19 @@
                 start, at = start + size, at + 1
         for copy in copies:
             copy.start()
+        for k in range(adj_sems.shape[0]):
+            copy_of(k).start()
         for copy in copies:
             copy.wait()
 
+    copy_of(step).wait()
     first = (lax.rem(me_ref[0] + chunk, n) * pl.num_programs(1) + part) * BLOCKS
     done = []
     for r in range(BLOCKS):
         base = (first + r) * per_row
         total = None
         for t in range(0, per_row, 2):
-            left = jnp.concatenate([adj[r, t], adj[r, t + 1]], axis=1)
+            left = jnp.concatenate([adj[step * BLOCKS + r, t], adj[step * BLOCKS + r, t + 1]], axis=1)
             right = jnp.concatenate([ext[pos_ref[base + t]], ext[pos_ref[base + t + 1]]], axis=1)
             term = lax.dot_general(left, right, NT, preferred_element_type=F32)
             total = term if total is None else total + term
@@ -247,16 +237,17 @@
         grid_spec=pltpu.PrefetchScalarGridSpec(
             num_scalar_prefetch=2,
             grid=(n, inner),
-            in_specs=[adj_spec(per_row, inner, lambda i, me: lax.rem(me[0] + i, n))]
-            + [pl.BlockSpec(memory_space=pl.ANY)] * len(parts),
+            in_specs=[pl.BlockSpec(memory_space=pl.ANY)] * (1 + len(parts)),
             out_specs=[pl.BlockSpec((share, TILE), lambda i, k, me, pos: (0, 0))] * n,
             scratch_shapes=[
                 pltpu.VMEM((col_tiles, TILE, TILE), BF16),
                 pltpu.SemaphoreType.DMA((4 * len(parts),)),
+                pltpu.VMEM(adj.shape, BF16),
+                pltpu.SemaphoreType.DMA((n * inner,)),
             ],
         ),
         out_shape=[shape((share, TILE), BF16)] * n,
-        compiler_params=params(20),
+        compiler_params=params(52),
         cost_estimate=cost(2 * row_tiles * per_row * TILE**3 * 2, 2e7),
         name="spmm",
     )(me, pos, adj, *parts)
@@ -310,9 +301,9 @@
 
 
 def wgrad_kernel(me_ref, *refs, n):
-    agg, both, gp_ref, out_ref = refs[:n], refs[n : 2 * n], refs[2 * n], refs[-1]
+    agg, both, gp_ref, outs = refs[:n], refs[n : 2 * n], refs[2 * n], refs[-n:]
     gp = gp_ref[...]
-    rows = out_ref.shape[2]
+    rows = outs[0].shape[1]
     width = agg[0].shape[1]
     for j in range(n):
         for kind, left in enumerate((agg[j][...], both[j][0])):
@@ -321,7 +312,7 @@
                 q = lax.rem(me_ref[0] + i, n)
                 for k in range(width // rows):
                     at = (kind * (width // rows) + k) * n + q
-                    out_ref[at, j] = term[k * rows : (k + 1) * rows, i * TILE : (i + 1) * TILE]
+                    outs[j][at] = term[k * rows : (k + 1) * rows, i * TILE : (i + 1) * TILE]
 
 
 def wgrad(me, agg, both, gp, after, dom_count):
@@ -334,8 +325,8 @@
         in_specs=[pl.BlockSpec(memory_space=pltpu.SMEM)]
         + [vmem] * (2 * n + 1)
         + [pl.BlockSpec(memory_space=pl.ANY)],
-        out_specs=vmem,
-        out_shape=shape((dom_count, n, size, TILE), BF16),
+        out_specs=[vmem] * n,
+        out_shape=[shape((dom_count, size, TILE), BF16)] * n,
         compiler_params=params(24),
         cost_estimate=cost(1e10, 4e6),
         name="wgrad",
@@ -346,14 +337,19 @@
 
 
 def spmm_back_kernel(me_ref, pos_ref, *refs, n):
-    adj, ga = refs[0], refs[1 : 1 + n]
-    local_ref, away_ref, total, left_ref, stage, sems = refs[1 + n :]
+    adj_ref, ga = refs[0], refs[1 : 1 + n]
+    local_ref, away_ref, total, left_ref, stage, sems, adj, adj_sems = refs[1 + n :]
     chunk, part = pl.program_id(0), pl.program_id(1)
+    inner = adj_sems.shape[0] // n
+    step = chunk * inner + part
     per_row = adj.shape[1]
+    copy_of = adj_copies(adj_ref, adj, adj_sems, inner, n, lambda c: lax.rem(me_ref[0] + n - c, n))
     size = BLOCKS * TILE
 
     @pl.when((chunk == 0) & (part == 0))
     def _():
+        for k in range(adj_sems.shape[0]):
+            copy_of(k).start()
         total[...] = jnp.zeros_like(total)
 
     for s in range(n):
@@ -363,12 +359,13 @@
             for k in range(left_ref.shape[0]):
                 left_ref[k] = ga[s][:, k * size : (k + 1) * size]
 
+    copy_of(step).wait()
     first = (lax.rem(me_ref[0] + n - chunk, n) * pl.num_programs(1) + part) * BLOCKS
     for r in range(BLOCKS):
         base = (first + r) * per_row
         left = left_ref[part, :, r * TILE : (r + 1) * TILE]
         for t in range(0, per_row, 2):
-            right = jnp.concatenate([adj[r, t], adj[r, t + 1]], axis=1)
+            right = jnp.concatenate([adj[step * BLOCKS + r, t], adj[step * BLOCKS + r, t + 1]], axis=1)
             both = jnp.dot(left, right, preferred_element_type=F32)
             total[pos_ref[base + t]] += both[:, :TILE]
             total[pos_ref[base + t + 1]] += both[:, TILE:]
@@ -401,7 +398,7 @@
         grid_spec=pltpu.PrefetchScalarGridSpec(
             num_scalar_prefetch=2,
             grid=(n, inner),
-            in_specs=[adj_spec(per_row, inner, lambda i, me: lax.rem(me[0] + n - i, n))]
+            in_specs=[pl.BlockSpec(memory_space=pl.ANY)]
             + [pl.BlockSpec((TILE, rows), lambda i, k, me, pos: (0, 0))] * n,
             out_specs=[pl.BlockSpec(memory_space=pl.ANY)] * 2,
             scratch_shapes=[
@@ -409,10 +406,12 @@
                 pltpu.VMEM((inner, TILE, BLOCKS * TILE), BF16),
                 pltpu.VMEM((away, TILE, TILE), BF16),
                 pltpu.SemaphoreType.DMA((PIECES + 1,)),
+                pltpu.VMEM(adj.shape, BF16),
+                pltpu.SemaphoreType.DMA((n * inner,)),
             ],
         ),
         out_shape=[pltpu.HBM((own, TILE, TILE), F32), pltpu.HBM((away, TILE, TILE), BF16)],
-        compiler_params=params(24),
+        compiler_params=params(52),
         cost_estimate=cost(2 * row_tiles * per_row * TILE**3 * 2, 2.2e7),
         name="spmm_back",
     )(me, pos, adj, *ga)
@@ -484,15 +483,16 @@
     )(me, ext, *pieces)
 
 
-def scatter_kernel(ids_ref, counts_ref, val_ref, out_ref):
+def scatter_kernel(ids_ref, counts_ref, val_ref, *refs, first):
+    before, out_ref = refs[:-1], refs[-1]
     groups = out_ref.shape[0] // LOW
 
     @pl.when(pl.program_id(0) == 0)
     def _():
-        out_ref[...] = jnp.zeros_like(out_ref)
+        out_ref[...] = before[0][...] if before else jnp.zeros_like(out_ref)
 
     for p in range(0, ids_ref.shape[0], 2):
-        ids = masked_ids(ids_ref, counts_ref, p, 2)
+        ids = masked_ids(ids_ref, counts_ref, p, 2, first)
         onehot = low_onehot(ids)
         values = jnp.concatenate([val_ref[p * CHUNKS + k] for k in range(2 * CHUNKS)], axis=1)
         zero = jnp.zeros_like(values)
@@ -505,64 +505,65 @@
             out_ref[(g + 1) * LOW : (g + 2) * LOW, :] += both[:, TILE:]
 
 
-def scatter_rows(ids, counts, values, rows):
-    peers = ids.shape[0]
+def scatter_rows(ids, counts, values, rows, first, steps, before):
     size = 8
-    return pl.pallas_call(
-        scatter_kernel,
-        grid=(peers // size,),
+    whole = pl.BlockSpec((rows, TILE), lambda i: (0, 0))
+    extra = [] if before is None else [before]
+    return pl.pallas_call(
+        functools.partial(scatter_kernel, first=first),
+        grid=(steps,),
         in_specs=[
-            pl.BlockSpec((size, B), lambda i: (i, 0)),
+            pl.BlockSpec((size, B), lambda i: (i + first, 0)),
             pl.BlockSpec(memory_space=pltpu.SMEM),
-            pl.BlockSpec((size * CHUNKS, TILE, TILE), lambda i: (i, 0, 0)),
-        ],
-        out_specs=pl.BlockSpec((rows, TILE), lambda i: (0, 0)),
+            pl.BlockSpec((size * CHUNKS, TILE, TILE), lambda i: (i + first, 0, 0)),
+        ]
+        + [whole] * len(extra),
+        out_specs=whole,
         out_shape=shape((rows, TILE), F32),
         compiler_params=params(40),
-        cost_estimate=cost(2 * ids.size * rows * TILE, 4e6),
+        cost_estimate=cost(2 * steps * size * B * rows * TILE * 4, 4e6),
         name="scatter_rows",
-    )(ids, counts, values)
-
-
-def sum_kernel(terms_ref, after_ref, *outs):
-    del after_ref
-    total = jnp.sum(terms_ref[...].astype(F32), axis=0).astype(BF16)
-    for j, out in enumerate(outs):
-        out[...] = total[j]
-
-
-def sum_terms(terms, after):
-    n = terms.shape[1]
-    return pl.pallas_call(
-        sum_kernel,
-        in_specs=[pl.BlockSpec(memory_space=pltpu.VMEM), pl.BlockSpec(memory_space=pl.ANY)],
-        out_specs=[pl.BlockSpec(memory_space=pltpu.VMEM)] * n,
-        out_shape=[shape(terms.shape[2:], BF16)] * n,
-        compiler_params=params(16),
-        cost_estimate=cost(1e9, 1e6),
-        name="sum_terms",
-    )(terms, after)
-
-
-def spread_kernel(*refs):
+    )(ids, counts, values, *extra)
+
+
+def add_kernel(*refs):
     terms, out_ref = refs[:-2], refs[-1]
     total = terms[0][...].astype(F32)
     for term in terms[1:]:
         total = total + term[...].astype(F32)
-    out_ref[...] = jnp.broadcast_to(total.astype(BF16)[None], out_ref.shape)
-
-
-def spread_terms(terms, after, dom_count):
+    out_ref[...] = total.astype(BF16)
+
+
+def add_terms(terms, after):
+    vmem = pl.BlockSpec(memory_space=pltpu.VMEM)
+    return pl.pallas_call(
+        add_kernel,
+        in_specs=[vmem] * len(terms) + [pl.BlockSpec(memory_space=pl.ANY)],
+        out_specs=vmem,
+        out_shape=shape(terms[0].shape, BF16),
+        compiler_params=params(8),
+        cost_estimate=cost(1e6, 1e6),
+        name="add_terms",
+    )(*terms, after)
+
+
+def spread_kernel(terms_ref, after_ref, out_ref):
+    del after_ref
+    total = jnp.sum(terms_ref[...].astype(F32), axis=0).astype(BF16)
+    out_ref[...] = jnp.broadcast_to(total[None], out_ref.shape)
+
+
+def spread_terms(terms, after):
+    vmem = pl.BlockSpec(memory_space=pltpu.VMEM)
     return pl.pallas_call(
         spread_kernel,
-        in_specs=[pl.BlockSpec(memory_space=pltpu.VMEM)] * len(terms)
-        + [pl.BlockSpec(memory_space=pl.ANY)],
-        out_specs=pl.BlockSpec(memory_space=pltpu.VMEM),
-        out_shape=shape((dom_count, *terms[0].shape), BF16),
+        in_specs=[vmem, pl.BlockSpec(memory_space=pl.ANY)],
+        out_specs=vmem,
+        out_shape=shape(terms.shape, BF16),
         compiler_params=params(8),
-        cost_estimate=cost(1e5, 3e5),
+        cost_estimate=cost(1e6, 6e5),
         name="spread_terms",
-    )(*terms, after)
+    )(terms, after)
 
 
 def place_kernel(terms_ref, *outs):
@@ -600,29 +601,33 @@
 
     ids = send_idx[0]
     pos = tile_cols[0].reshape(-1)
+    adj = adj_tiles[0]
 
     packed = gather_rows(ids, counts, stale_features)
     halo = swap(packed)
-    own, wn, ws, adj, pieces = prep(
-        me, features, grad_output, w_neigh, w_self, adj_tiles[0], packed, n
-    )
+    own, wn, ws, pieces = prep(me, features, grad_output, w_neigh, w_self, packed, n)
     both = relative(exchange(pieces))
 
     agg = relative(exchange(spmm(me, pos, adj, [own, halo], n)))
     grad_agg, act, grad_pre = dense(agg, both, wn, ws)
     grad_agg = exchange(grad_agg)
-    terms = swap(wgrad(me, agg, both, grad_pre, grad_agg[1], dom_count))
 
     local, away = spmm_back(me, pos, adj, grad_agg, row_tiles, dom_count * CHUNKS)
     returned = swap(away)
     pieces = exchange(late(act, grad_pre, ws, away, n))
     out, grad_input = finish(me, local, pieces)
-
-    terms = exchange(sum_terms(terms, away))
-    terms = swap(spread_terms(terms, returned, dom_count))
+    terms = exchange(wgrad(me, agg, both, grad_pre, away, dom_count))
+
+    blocks = dom_count // 8
+    half = (blocks + 1) // 2
+    terms = swap(add_terms(terms, returned))
+    grad_stale = scatter_rows(ids, counts, returned, row_count, 0, half, None)
+    terms = swap(spread_terms(terms, grad_stale))
+    if blocks > half:
+        grad_stale = scatter_rows(
+            ids, counts, returned, row_count, half, blocks - half, grad_stale
+        )
     grad_neigh, grad_self = place_terms(terms, width, n)
-
-    grad_stale = scatter_rows(ids, counts, returned, row_count)
     return (out, grad_input, grad_stale, grad_neigh, grad_self)
 
 

time: 212 us -> 205 us (0.967)
  local copies, waits for them, and re-layouts: 40.1 us -> 16.2 us
  waiting for transfers between devices: 59 us -> 72.7 us
  Pallas kernels: 60.3 us -> 65.4 us
    unnamed x63 -> x77, local copies, waits for them, and re-layouts: 40 us -> 16.1 us
    all_to_all x1, waiting for transfers between devices: 13 us -> 30.3 us  [per_device(): halo = swap(packed)]
    all_to_all x1, waiting for transfers between devices: 9.37 us -> 0.01 us  [per_device(): returned = swap(away)]
    pallas_call x1, Pallas kernels: 7.63 us -> 13.5 us  [spmm(): pl.pallas_call(functools.partial(spmm_kernel, n=n), grid_spec=pltpu.Prefe...]
    ppermute x15, waiting for transfers between devices: 36.6 us -> 40.3 us  [exchange(): lax.ppermute(pieces[s], 'rep', [(i, (i + s) % n) for i in range(n)])]
    pallas_call x1, Pallas kernels: 3.14 us -> 1.02 us  [wgrad(): pl.pallas_call(functools.partial(wgrad_kernel, n=n), in_specs=[pl.BlockSp...]
    pallas_call x3 -> x4, Pallas kernels: 12.7 us -> 14 us  [the longest x2 13.1 us: scatter_rows(): pl.pallas_call(functools.partial(scatter_kernel, first=first), grid=(step...]
  transfers between devices with their start and end apart: 19 -> 19, of which waited for: 10 -> 11; matrix products, arithmetic and copies ran while one was open for 0% -> 0% of each run, Pallas kernels for 19% -> 18%
where the time goes in v3:
time: 205 us; the launch traced here: 204 us
  waiting for transfers between devices  72.7 us (35%)
  Pallas kernels  65.4 us (32%)
  starting transfers between devices  48.6 us (24%)
  local copies, waits for them, and re-layouts  16.2 us (8%)
    ppermute x15, waiting for transfers between devices, exchange(): lax.ppermute(pieces[s], 'rep', [(i, (i + s) % n) for i in range(n)])  40.3 us
    all_to_all x1, waiting for transfers between devices, per_device(): halo = swap(packed)  30.3 us
    ppermute x15, starting transfers between devices, exchange(): lax.ppermute(pieces[s], 'rep', [(i, (i + s) % n) for i in range(n)])  16.6 us
    unnamed x77, local copies, waits for them, and re-layouts  16.1 us
    pallas_call x1, Pallas kernels, spmm(): pl.pallas_call(functools.partial(spmm_kernel, n=n), grid_spec=pltpu.Prefe...  13.5 us
    pallas_call x1, Pallas kernels, gather_rows(): pl.pallas_call(gather_kernel, grid=(peers // size,), in_specs=[pl.BlockSp...  13.3 us
    pallas_call x2, Pallas kernels, scatter_rows(): pl.pallas_call(functools.partial(scatter_kernel, first=first), grid=(step...  13.1 us
    pallas_call x1, Pallas kernels, spmm_back(): pl.pallas_call(functools.partial(spmm_back_kernel, n=n), grid_spec=pltpu....  10.5 us
  transfers between devices with their start and end apart: 19, of which 11 were waited for; matrix products, arithmetic and copies ran while one was open for 0% of the time, Pallas kernels for 18%

profile of v3, /device:TPU:1, one launch (start us, length us, event | category | flops | bytes accessed | tf_op | source)
XLA Modules:
  0.0 203.9 jit_solution(284336144538534933)
XLA Ops:
  0.6 13.3 %gather_rows.1.after_ref = bf16[96,128,128]{2,1,0:T(8,128)(2,1)} custom-call(s32[32,384]{1,0:T(8,128)} %bitcast.3, s32[1,32]{1,0:T(1,128)} %counts_ref.5, bf16[3072,128]{1,0:T(8,128)(2,1)} %table_ref.1), custom_call_target="tpu_custom_call" | custom-call | flops 9663676416 | bytes 4000000 | tf_op jit(solution)/shard_map/gather_rows/pallas_call | solution.py:82
  13.9 9.5 %all-to-all-start = ((bf16[96,128,128]{2,1,0:T(8,128)(2,1)}), bf16[96,128,128]{2,1,0:T(8,128)(2,1)}, u32[]{:S(2)}, u32[]{:S(2)}) async-start(bf16[96,128,128]{2,1,0:T(8,128)(2,1)} %gather_rows.1.after_ref), calls=%async_computation | async-start | bytes 6291456 | tf_op jit(solution)/shard_map/all_to_all | solution.py:607
  23.4 4.9 %prep.1 = (bf16[24,128,128]{2,1,0:T(8,128)(2,1)}, bf16[512,512]{1,0:T(8,128)(2,1)}, bf16[512,512]{1,0:T(8,128)(2,1)}, bf16[2,768,128]{2,1,0:T(8,128)(2,1)}, bf16...) custom-call(s32[1]{0:T(128)} %bitcast.me_ref, bf16[3072,128]{1,0:T(8,128)(2,1)} %feat_ref.1, ...), custom_call_target="tpu_custom_call" | custom-call | flops 10000000000 | bytes 6000000 | tf_op jit(solution)/shard_map/prep/pallas_call | solution.py:135
  28.3 2.8 %collective-permute-start.3 = (bf16[2,768,128]{2,1,0:T(8,128)(2,1)}, bf16[2,768,128]{2,1,0:T(8,128)(2,1)S(1)}, u32[]{:S(2)}, u32[]{:S(2)}) collective-permute-start(bf16[2,768,128]{2,1,0:T(8,128)(2,1)} %get-tuple-element.42), channel_id=1, source_target_pairs={{0,3},{1,0},{2,1},{3,2},{4,7},{5,4},{6,5},{7,6},{8,11},{9,8},{10,9... | collective-permute-start | bytes 1179656 | tf_op jit(solution)/shard_map/ppermute | solution.py:102
  32.4 30.3 %all-to-all-done.refs_2_ = bf16[96,128,128]{2,1,0:T(8,128)(2,1)} async-done(((bf16[96,128,128]{2,1,0:T(8,128)(2,1)}), bf16[96,128,128]{2,1,0:T(8,128)(2,1)}, u32[]{:S(2)}, u32[]{:S(2)}) %all-to-all-start) | async-done | bytes 3145760 | tf_op jit(solution)/shard_map/all_to_all | solution.py:607
  63.8 13.5 %spmm.1 = (bf16[768,128]{1,0:T(8,128)(2,1)S(1)}, bf16[768,128]{1,0:T(8,128)(2,1)S(1)}, bf16[768,128]{1,0:T(8,128)(2,1)S(1)}, bf16[768,128]{1,0:T(8,128)(2,1)S(1)}) custom-call(s32[1]{0:T(128)} %bitcast.me_ref, s32[480]{0:T(512)S(1)} %reshape_squeeze.3.pos_ref, bf16[24,20,128,128]{3,2,1,0:T(8,128)(2,1)} %bitcast.6, bf16[24,128,128]{2,1,0:T(8,128)(2,1)S(1)} %copy-done.6, ...), custom_call_target="tpu_custom_call" | custom-call | flops 4026531840 | bytes 20000000 | tf_op jit(solution)/shard_map/spmm/pallas_call | solution.py:235
  77.3 2.8 %collective-permute-start = (bf16[768,128]{1,0:T(8,128)(2,1)S(1)}, bf16[768,128]{1,0:T(8,128)(2,1)S(1)}, u32[]{:S(2)}, u32[]{:S(2)}) collective-permute-start(bf16[768,128]{1,0:T(8,128)(2,1)S(1)} %get-tuple-element.38), channel_id=1, source_target_pairs={{0,3},{1,0},{2,1},{3,2},{4,7},{5,4},{6,5},{7,6},{8,11},{9,8},{10,9... | collective-permute-start | bytes 589832 | tf_op jit(solution)/shard_map/ppermute | solution.py:102
  81.1 4.0 %collective-permute-done.refs_1_ = bf16[768,128]{1,0:T(8,128)(2,1)S(1)} collective-permute-done((bf16[768,128]{1,0:T(8,128)(2,1)S(1)}, bf16[768,128]{1,0:T(8,128)(2,1)S(1)}, u32[]{:S(2)}, u32[]{:S(2)}) %collective-permute-start) | collective-permute-done | bytes 196640 | tf_op jit(solution)/shard_map/ppermute | solution.py:102
  86.2 4.8 %collective-permute-done.2.refs_3_ = bf16[768,128]{1,0:T(8,128)(2,1)S(1)} collective-permute-done((bf16[768,128]{1,0:T(8,128)(2,1)S(1)}, bf16[768,128]{1,0:T(8,128)(2,1)S(1)}, u32[]{:S(2)}, u32[]{:S(2)}) %collective-permute-start.2) | collective-permute-done | bytes 196640 | tf_op jit(solution)/shard_map/ppermute | solution.py:102
  91.0 4.2 %dense.1 = (bf16[128,768]{1,0:T(8,128)(2,1)S(1)}, bf16[128,768]{1,0:T(8,128)(2,1)S(1)}, bf16[128,768]{1,0:T(8,128)(2,1)S(1)}, bf16[128,768]{1,0:T(8,128)(2,1)S(1...) custom-call(bf16[768,128]{1,0:T(8,128)(2,1)S(1)} %get-tuple-element.37.refs_0_, ...), custom_call_target="tpu_custom_call" | custom-call | flops 1207959552 | bytes 7000000 | tf_op jit(solution)/shard_map/dense/pallas_call | solution.py:288
  95.2 2.6 %collective-permute-start.8 = (bf16[128,768]{1,0:T(8,128)(2,1)S(1)}, bf16[128,768]{1,0:T(8,128)(2,1)S(1)}, u32[]{:S(2)}, u32[]{:S(2)}) collective-permute-start(bf16[128,768]{1,0:T(8,128)(2,1)S(1)} %get-tuple-element.50), channel_id=1, source_target_pairs={{0,3},{1,0},{2,1},{3,2},{4,7},{5,4},{6,5},{7,6},{8,11},{9,8},{10,9... | collective-permute-start | bytes 589832 | tf_op jit(solution)/shard_map/ppermute | solution.py:102
  97.9 8.5 %collective-permute-done.6.refs_2_ = bf16[128,768]{1,0:T(8,128)(2,1)S(1)} collective-permute-done((bf16[128,768]{1,0:T(8,128)(2,1)S(1)}, bf16[128,768]{1,0:T(8,128)(2,1)S(1)}, u32[]{:S(2)}, u32[]{:S(2)}) %collective-permute-start.6) | collective-permute-done | bytes 196640 | tf_op jit(solution)/shard_map/ppermute | solution.py:102
  106.4 10.5 %spmm_back.1 = (f32[24,128,128]{2,1,0:T(8,128)}, bf16[96,128,128]{2,1,0:T(8,128)(2,1)}) custom-call(s32[1]{0:T(128)} %bitcast.me_ref, s32[480]{0:T(512)S(1)} %reshape_squeeze.3.pos_ref, bf16[24,20,128,128]{3,2,1,0:T(8,128)(2,1)} %bitcast.7, bf16[128,768]{1,0:T(8,128)(2,1)S(1)} %get-tuple-element.47.refs_1_, ...), custom_call_target="tpu_custom_call" | custom-call | flops 4026531840 | bytes 22000000 | tf_op jit(solution)/shard_map/spmm_back/pallas_call | solution.py:396
  116.9 8.8 %all-to-all-start.1 = ((bf16[96,128,128]{2,1,0:T(8,128)(2,1)}), bf16[96,128,128]{2,1,0:T(8,128)(2,1)S(1)}, u32[]{:S(2)}, u32[]{:S(2)}) async-start(bf16[96,128,128]{2,1,0:T(8,128)(2,1)} %get-tuple-element.54.after_ref.refs_9_), calls=%async_computation.1 | async-start | bytes 6291456 | tf_op jit(solution)/shard_map/all_to_all | solution.py:616
  132.3 3.3 %collective-permute-start.10 = (bf16[2,768,128]{2,1,0:T(8,128)(2,1)S(1)}, bf16[2,768,128]{2,1,0:T(8,128)(2,1)S(1)}, u32[]{:S(2)}, u32[]{:S(2)}) collective-permute-start(bf16[2,768,128]{2,1,0:T(8,128)(2,1)S(1)} %get-tuple-element.57), channel_id=1, source_target_pairs={{0,2},{1,3},{2,0},{3,1},{4,6},{5,7},{6,4},{7,5},{8,10},{9,11},{10,... | collective-permute-start | bytes 1179656 | tf_op jit(solution)/shard_map/ppermute | solution.py:102
  138.5 5.4 %collective-permute-done.9.refs_1_ = bf16[2,768,128]{2,1,0:T(8,128)(2,1)S(1)} collective-permute-done((bf16[2,768,128]{2,1,0:T(8,128)(2,1)S(1)}, bf16[2,768,128]{2,1,0:T(8,128)(2,1)S(1)}, u32[]{:S(2)}, u32[]{:S(2)}) %collective-permute-start.9) | collective-permute-done | bytes 393248 | tf_op jit(solution)/shard_map/ppermute | solution.py:102
  144.9 8.2 %collective-permute-done.10.refs_2_ = bf16[2,768,128]{2,1,0:T(8,128)(2,1)S(1)} collective-permute-done((bf16[2,768,128]{2,1,0:T(8,128)(2,1)S(1)}, bf16[2,768,128]{2,1,0:T(8,128)(2,1)S(1)}, u32[]{:S(2)}, u32[]{:S(2)}) %collective-permute-start.10) | collective-permute-done | bytes 393248 | tf_op jit(solution)/shard_map/ppermute | solution.py:102
  153.1 2.1 %finish.1 = (bf16[3072,128]{1,0:T(8,128)(2,1)}, bf16[3072,128]{1,0:T(8,128)(2,1)}) custom-call(s32[1]{0:T(128)} %bitcast.me_ref, f32[24,128,128]{2,1,0:T(8,128)S(1)} %copy-done.4, bf16[2,768,128]{2,1,0:T(8,128)(2,1)S(1)} %get-tuple-element.55.refs_0_, bf16[2,768,128]{2,1,0:T(8,128)(2,1)S(1)} %collective-permute-done.9.refs_1_, ...), custom_call_target="tpu_custom_call" | custom-call | flops 1000000 | bytes 7000000 | tf_op jit(solution)/shard_map/finish/pallas_call | solution.py:466
  155.2 2.8 %collective-permute-done.12.refs_1_ = bf16[32,32,128]{2,1,0:T(8,128)(2,1)S(1)} collective-permute-done((bf16[32,32,128]{2,1,0:T(8,128)(2,1)S(1)}, bf16[32,32,128]{2,1,0:T(8,128)(2,1)S(1)}, u32[]{:S(2)}, u32[]{:S(2)}) %collective-permute-start.12) | collective-permute-done | bytes 262176 | tf_op jit(solution)/shard_map/ppermute | solution.py:102
  158.7 5.6 %collective-permute-done.13.refs_2_ = bf16[32,32,128]{2,1,0:T(8,128)(2,1)S(1)} collective-permute-done((bf16[32,32,128]{2,1,0:T(8,128)(2,1)S(1)}, bf16[32,32,128]{2,1,0:T(8,128)(2,1)S(1)}, u32[]{:S(2)}, u32[]{:S(2)}) %collective-permute-start.13) | collective-permute-done | bytes 262176 | tf_op jit(solution)/shard_map/ppermute | solution.py:102
  169.4 8.1 %all-to-all-start.2 = ((bf16[32,32,128]{2,1,0:T(8,128)(2,1)}), bf16[32,32,128]{2,1,0:T(8,128)(2,1)S(1)}, u32[]{:S(2)}, u32[]{:S(2)}) async-start(bf16[32,32,128]{2,1,0:T(8,128)(2,1)} %add_terms.1), calls=%async_computation.2 | async-start | bytes 524288 | tf_op jit(solution)/shard_map/all_to_all | solution.py:623
  177.5 6.0 %scatter_rows.2.refs_0_.after_ref = f32[3072,128]{1,0:T(8,128)S(1)} custom-call(s32[32,384]{1,0:T(8,128)S(1)} %bitcast.4, s32[1,32]{1,0:T(1,128)S(1)} %copy-done.28, bf16[96,128,128]{2,1,0:T(8,128)(2,1)S(1)} %all-to-all-done.1.val_ref.refs_4_), custom_call_target="tpu_custom_call" | custom-call | flops 19327352832 | bytes 4000000 | tf_op jit(solution)/shard_map/scatter_rows/pallas_call | solution.py:512
  188.5 5.7 %all-to-all-start.3 = ((bf16[32,32,128]{2,1,0:T(8,128)(2,1)}), bf16[32,32,128]{2,1,0:T(8,128)(2,1)S(1)}, u32[]{:S(2)}, u32[]{:S(2)}) async-start(bf16[32,32,128]{2,1,0:T(8,128)(2,1)} %copy-done.5), calls=%async_computation.3 | async-start | bytes 524288 | tf_op jit(solution)/shard_map/all_to_all | solution.py:625
  195.6 7.1 %scatter_rows.3 = f32[3072,128]{1,0:T(8,128)} custom-call(s32[32,384]{1,0:T(8,128)S(1)} %bitcast.5, s32[1,32]{1,0:T(1,128)S(1)} %copy-done.28, bf16[96,128,128]{2,1,0:T(8,128)(2,1)S(1)} %all-to-all-done.1.val_ref.refs_4_, f32[3072,128]{1,0:T(8,128)S(1)} %copy-done.3), custom_call_target="tpu_custom_call" | custom-call | flops 19327352832 | bytes 4000000 | tf_op jit(solution)/shard_map/scatter_rows/pallas_call | solution.py:512
  (105 shorter events, 28.3 us)
Async XLA Ops:
  13.9 48.7 %all-to-all-start = ((bf16[96,128,128]{2,1,0:T(8,128)(2,1)}), bf16[96,128,128]{2,1,0:T(8,128)(2,1)}, u32[]{:S(2)}, u32[]{:S(2)}) async-start(bf16[96,128,128]{2,1,0:T(8,128)(2,1)} %gather_rows.1.after_ref), calls=%async_computation | async-start | bytes 6291456 | tf_op jit(solution)/shard_map/all_to_all | solution.py:607
  28.3 52.1 %collective-permute-start.3 = (bf16[2,768,128]{2,1,0:T(8,128)(2,1)}, bf16[2,768,128]{2,1,0:T(8,128)(2,1)S(1)}, u32[]{:S(2)}, u32[]{:S(2)}) collective-permute-start(bf16[2,768,128]{2,1,0:T(8,128)(2,1)} %get-tuple-element.42), channel_id=1, source_target_pairs={{0,3},{1,0},{2,1},{3,2},{4,7},{5,4},{6,5},{7,6},{8,11},{9,8},{10,9... | collective-permute-start | bytes 1179656 | tf_op jit(solution)/shard_map/ppermute | solution.py:102
  31.1 50.0 %collective-permute-start.4 = (bf16[2,768,128]{2,1,0:T(8,128)(2,1)}, bf16[2,768,128]{2,1,0:T(8,128)(2,1)S(1)}, u32[]{:S(2)}, u32[]{:S(2)}) collective-permute-start(bf16[2,768,128]{2,1,0:T(8,128)(2,1)} %get-tuple-element.43), channel_id=1, source_target_pairs={{0,2},{1,3},{2,0},{3,1},{4,6},{5,7},{6,4},{7,5},{8,10},{9,11},{10,... | collective-permute-start | bytes 1179656 | tf_op jit(solution)/shard_map/ppermute | solution.py:102
  31.5 49.7 %collective-permute-start.5 = (bf16[2,768,128]{2,1,0:T(8,128)(2,1)}, bf16[2,768,128]{2,1,0:T(8,128)(2,1)S(1)}, u32[]{:S(2)}, u32[]{:S(2)}) collective-permute-start(bf16[2,768,128]{2,1,0:T(8,128)(2,1)} %get-tuple-element.44), channel_id=1, source_target_pairs={{0,1},{1,2},{2,3},{3,0},{4,5},{5,6},{6,7},{7,4},{8,9},{9,10},{10,1... | collective-permute-start | bytes 1179656 | tf_op jit(solution)/shard_map/ppermute | solution.py:102
  63.8 27.2 %copy-start.34 = (bf16[512,512]{1,0:T(8,128)(2,1)S(1)}, bf16[512,512]{1,0:T(8,128)(2,1)}, u32[]{:S(2)}) copy-start(bf16[512,512]{1,0:T(8,128)(2,1)} %get-tuple-element.45.refs_8_) | copy-start | bytes 1572868
  63.8 27.2 %copy-start.35 = (bf16[2,768,128]{2,1,0:T(8,128)(2,1)S(1)}, bf16[2,768,128]{2,1,0:T(8,128)(2,1)}, u32[]{:S(2)}) copy-start(bf16[2,768,128]{2,1,0:T(8,128)(2,1)} %get-tuple-element.41.refs_4_) | copy-start | bytes 1179652
  77.3 7.9 %collective-permute-start = (bf16[768,128]{1,0:T(8,128)(2,1)S(1)}, bf16[768,128]{1,0:T(8,128)(2,1)S(1)}, u32[]{:S(2)}, u32[]{:S(2)}) collective-permute-start(bf16[768,128]{1,0:T(8,128)(2,1)S(1)} %get-tuple-element.38), channel_id=1, source_target_pairs={{0,3},{1,0},{2,1},{3,2},{4,7},{5,4},{6,5},{7,6},{8,11},{9,8},{10,9... | collective-permute-start | bytes 589832 | tf_op jit(solution)/shard_map/ppermute | solution.py:102
  80.1 6.1 %collective-permute-start.1 = (bf16[768,128]{1,0:T(8,128)(2,1)S(1)}, bf16[768,128]{1,0:T(8,128)(2,1)S(1)}, u32[]{:S(2)}, u32[]{:S(2)}) collective-permute-start(bf16[768,128]{1,0:T(8,128)(2,1)S(1)} %get-tuple-element.39), channel_id=1, source_target_pairs={{0,2},{1,3},{2,0},{3,1},{4,6},{5,7},{6,4},{7,5},{8,10},{9,11},{10,... | collective-permute-start | bytes 589832 | tf_op jit(solution)/shard_map/ppermute | solution.py:102
  80.4 36.5 %copy-start.13 = (bf16[2,768,128]{2,1,0:T(8,128)(2,1)}, bf16[2,768,128]{2,1,0:T(8,128)(2,1)S(1)}, u32[]{:S(2)}) copy-start(bf16[2,768,128]{2,1,0:T(8,128)(2,1)S(1)} %collective-permute-done.3.refs_5_) | copy-start | bytes 1179652
  80.4 10.5 %collective-permute-start.2 = (bf16[768,128]{1,0:T(8,128)(2,1)S(1)}, bf16[768,128]{1,0:T(8,128)(2,1)S(1)}, u32[]{:S(2)}, u32[]{:S(2)}) collective-permute-start(bf16[768,128]{1,0:T(8,128)(2,1)S(1)} %get-tuple-element.40), channel_id=1, source_target_pairs={{0,1},{1,2},{2,3},{3,0},{4,5},{5,6},{6,7},{7,4},{8,9},{9,10},{10,1... | collective-permute-start | bytes 589832 | tf_op jit(solution)/shard_map/ppermute | solution.py:102
  81.1 35.8 %copy-start.15 = (bf16[2,768,128]{2,1,0:T(8,128)(2,1)}, bf16[2,768,128]{2,1,0:T(8,128)(2,1)S(1)}, u32[]{:S(2)}) copy-start(bf16[2,768,128]{2,1,0:T(8,128)(2,1)S(1)} %collective-permute-done.4.refs_6_) | copy-start | bytes 1179652
  81.1 35.8 %copy-start.17 = (bf16[2,768,128]{2,1,0:T(8,128)(2,1)}, bf16[2,768,128]{2,1,0:T(8,128)(2,1)S(1)}, u32[]{:S(2)}) copy-start(bf16[2,768,128]{2,1,0:T(8,128)(2,1)S(1)} %collective-permute-done.5.refs_7_) | copy-start | bytes 1179652
  95.1 11.3 %collective-permute-start.6 = (bf16[128,768]{1,0:T(8,128)(2,1)S(1)}, bf16[128,768]{1,0:T(8,128)(2,1)S(1)}, u32[]{:S(2)}, u32[]{:S(2)}) collective-permute-start(bf16[128,768]{1,0:T(8,128)(2,1)S(1)} %get-tuple-element.48), channel_id=1, source_target_pairs={{0,1},{1,2},{2,3},{3,0},{4,5},{5,6},{6,7},{7,4},{8,9},{9,10},{10,1... | collective-permute-start | bytes 589832 | tf_op jit(solution)/shard_map/ppermute | solution.py:102
  95.1 11.3 %collective-permute-start.7 = (bf16[128,768]{1,0:T(8,128)(2,1)S(1)}, bf16[128,768]{1,0:T(8,128)(2,1)S(1)}, u32[]{:S(2)}, u32[]{:S(2)}) collective-permute-start(bf16[128,768]{1,0:T(8,128)(2,1)S(1)} %get-tuple-element.49), channel_id=1, source_target_pairs={{0,2},{1,3},{2,0},{3,1},{4,6},{5,7},{6,4},{7,5},{8,10},{9,11},{10,... | collective-permute-start | bytes 589832 | tf_op jit(solution)/shard_map/ppermute | solution.py:102
  95.2 11.2 %collective-permute-start.8 = (bf16[128,768]{1,0:T(8,128)(2,1)S(1)}, bf16[128,768]{1,0:T(8,128)(2,1)S(1)}, u32[]{:S(2)}, u32[]{:S(2)}) collective-permute-start(bf16[128,768]{1,0:T(8,128)(2,1)S(1)} %get-tuple-element.50), channel_id=1, source_target_pairs={{0,3},{1,0},{2,1},{3,2},{4,7},{5,4},{6,5},{7,6},{8,11},{9,8},{10,9... | collective-permute-start | bytes 589832 | tf_op jit(solution)/shard_map/ppermute | solution.py:102
  116.9 48.8 %all-to-all-start.1 = ((bf16[96,128,128]{2,1,0:T(8,128)(2,1)}), bf16[96,128,128]{2,1,0:T(8,128)(2,1)S(1)}, u32[]{:S(2)}, u32[]{:S(2)}) async-start(bf16[96,128,128]{2,1,0:T(8,128)(2,1)} %get-tuple-element.54.after_ref.refs_9_), calls=%async_computation.1 | async-start | bytes 6291456 | tf_op jit(solution)/shard_map/all_to_all | solution.py:616
  132.2 11.8 %collective-permute-start.9 = (bf16[2,768,128]{2,1,0:T(8,128)(2,1)S(1)}, bf16[2,768,128]{2,1,0:T(8,128)(2,1)S(1)}, u32[]{:S(2)}, u32[]{:S(2)}) collective-permute-start(bf16[2,768,128]{2,1,0:T(8,128)(2,1)S(1)} %get-tuple-element.56), channel_id=1, source_target_pairs={{0,1},{1,2},{2,3},{3,0},{4,5},{5,6},{6,7},{7,4},{8,9},{9,10},{10,1... | collective-permute-start | bytes 1179656 | tf_op jit(solution)/shard_map/ppermute | solution.py:102
  132.3 20.8 %collective-permute-start.10 = (bf16[2,768,128]{2,1,0:T(8,128)(2,1)S(1)}, bf16[2,768,128]{2,1,0:T(8,128)(2,1)S(1)}, u32[]{:S(2)}, u32[]{:S(2)}) collective-permute-start(bf16[2,768,128]{2,1,0:T(8,128)(2,1)S(1)} %get-tuple-element.57), channel_id=1, source_target_pairs={{0,2},{1,3},{2,0},{3,1},{4,6},{5,7},{6,4},{7,5},{8,10},{9,11},{10,... | collective-permute-start | bytes 1179656 | tf_op jit(solution)/shard_map/ppermute | solution.py:102
  135.6 17.5 %collective-permute-start.11 = (bf16[2,768,128]{2,1,0:T(8,128)(2,1)S(1)}, bf16[2,768,128]{2,1,0:T(8,128)(2,1)S(1)}, u32[]{:S(2)}, u32[]{:S(2)}) collective-permute-start(bf16[2,768,128]{2,1,0:T(8,128)(2,1)S(1)} %get-tuple-element.58), channel_id=1, source_target_pairs={{0,3},{1,0},{2,1},{3,2},{4,7},{5,4},{6,5},{7,6},{8,11},{9,8},{10,9... | collective-permute-start | bytes 1179656 | tf_op jit(solution)/shard_map/ppermute | solution.py:102
  136.7 21.3 %collective-permute-start.12 = (bf16[32,32,128]{2,1,0:T(8,128)(2,1)S(1)}, bf16[32,32,128]{2,1,0:T(8,128)(2,1)S(1)}, u32[]{:S(2)}, u32[]{:S(2)}) collective-permute-start(bf16[32,32,128]{2,1,0:T(8,128)(2,1)S(1)} %get-tuple-element.62), channel_id=1, source_target_pairs={{0,1},{1,2},{2,3},{3,0},{4,5},{5,6},{6,7},{7,4},{8,9},{9,10},{10,1... | collective-permute-start | bytes 786440 | tf_op jit(solution)/shard_map/ppermute | solution.py:102
  138.2 26.1 %collective-permute-start.13 = (bf16[32,32,128]{2,1,0:T(8,128)(2,1)S(1)}, bf16[32,32,128]{2,1,0:T(8,128)(2,1)S(1)}, u32[]{:S(2)}, u32[]{:S(2)}) collective-permute-start(bf16[32,32,128]{2,1,0:T(8,128)(2,1)S(1)} %get-tuple-element.63), channel_id=1, source_target_pairs={{0,2},{1,3},{2,0},{3,1},{4,6},{5,7},{6,4},{7,5},{8,10},{9,11},{10,... | collective-permute-start | bytes 786440 | tf_op jit(solution)/shard_map/ppermute | solution.py:102
  143.9 21.0 %collective-permute-start.14 = (bf16[32,32,128]{2,1,0:T(8,128)(2,1)S(1)}, bf16[32,32,128]{2,1,0:T(8,128)(2,1)S(1)}, u32[]{:S(2)}, u32[]{:S(2)}) collective-permute-start(bf16[32,32,128]{2,1,0:T(8,128)(2,1)S(1)} %get-tuple-element.64), channel_id=1, source_target_pairs={{0,3},{1,0},{2,1},{3,2},{4,7},{5,4},{6,5},{7,6},{8,11},{9,8},{10,9... | collective-permute-start | bytes 786440 | tf_op jit(solution)/shard_map/ppermute | solution.py:102
  169.4 17.0 %all-to-all-start.2 = ((bf16[32,32,128]{2,1,0:T(8,128)(2,1)}), bf16[32,32,128]{2,1,0:T(8,128)(2,1)S(1)}, u32[]{:S(2)}, u32[]{:S(2)}) async-start(bf16[32,32,128]{2,1,0:T(8,128)(2,1)} %add_terms.1), calls=%async_computation.2 | async-start | bytes 524288 | tf_op jit(solution)/shard_map/all_to_all | solution.py:623
  188.5 14.6 %all-to-all-start.3 = ((bf16[32,32,128]{2,1,0:T(8,128)(2,1)}), bf16[32,32,128]{2,1,0:T(8,128)(2,1)S(1)}, u32[]{:S(2)}, u32[]{:S(2)}) async-start(bf16[32,32,128]{2,1,0:T(8,128)(2,1)} %copy-done.5), calls=%async_computation.3 | async-start | bytes 524288 | tf_op jit(solution)/shard_map/all_to_all | solution.py:625
  (33 other events, 210.3 us)

commit v4 on v3

--- a/solution.py
+++ b/solution.py
@@ -163,17 +163,27 @@
 BLOCKS = 3
 
 
-def adj_copies(adj_ref, held, sems, inner, n, chunk_of):
+def span(index, size):
+    return pl.ds(pl.multiple_of(index * size, size), size)
+
+
+def adj_copies(adj_ref, held, sems, inner, chunk_of):
+    size = held.shape[0] // sems.shape[0]
+
     def copy(step):
-        first = (chunk_of(step // inner) * inner + lax.rem(step, inner)) * BLOCKS
+        source = chunk_of(step // inner) * inner + lax.rem(step, inner)
         return pltpu.make_async_copy(
-            adj_ref.at[pl.ds(first, BLOCKS)], held.at[pl.ds(step * BLOCKS, BLOCKS)], sems.at[step]
+            adj_ref.at[span(source, size), :], held.at[span(step, size), :], sems.at[step]
         )
 
     return copy
 
 
-def spmm_kernel(me_ref, pos_ref, *refs, n):
+def tile_pair(adj, at):
+    return jnp.concatenate([adj[span(at, TILE), :], adj[span(at + 1, TILE), :]], axis=1)
+
+
+def spmm_kernel(me_ref, pos_ref, *refs, n, per_row):
     adj_ref, parts, outs, (ext, sems, adj, adj_sems) = (
         refs[0],
         refs[1 : -n - 4],
@@ -183,8 +193,7 @@
     chunk, part = pl.program_id(0), pl.program_id(1)
     inner = adj_sems.shape[0] // n
     step = chunk * inner + part
-    per_row = adj.shape[1]
-    copy_of = adj_copies(adj_ref, adj, adj_sems, inner, n, lambda c: lax.rem(me_ref[0] + c, n))
+    copy_of = adj_copies(adj_ref, adj, adj_sems, inner, lambda c: lax.rem(me_ref[0] + c, n))
 
     @pl.when((chunk == 0) & (part == 0))
     def _():
@@ -194,7 +203,7 @@
             for k in range(4):
                 copies.append(
                     pltpu.make_async_copy(
-                        source.at[pl.ds(k * size, size)], ext.at[pl.ds(start, size)], sems.at[at]
+                        source.at[pl.ds(k * size, size), :], ext.at[pl.ds(start, size), :], sems.at[at]
                     )
                 )
                 start, at = start + size, at + 1
@@ -212,8 +221,11 @@
         base = (first + r) * per_row
         total = None
         for t in range(0, per_row, 2):
-            left = jnp.concatenate([adj[step * BLOCKS + r, t], adj[step * BLOCKS + r, t + 1]], axis=1)
-            right = jnp.concatenate([ext[pos_ref[base + t]], ext[pos_ref[base + t + 1]]], axis=1)
+            left = tile_pair(adj, (step * BLOCKS + r) * per_row + t)
+            right = jnp.concatenate(
+                [ext[span(pos_ref[base + t], TILE), :], ext[span(pos_ref[base + t + 1], TILE), :]],
+                axis=1,
+            )
             term = lax.dot_general(left, right, NT, preferred_element_type=F32)
             total = term if total is None else total + term
         done.append(total.astype(BF16))
@@ -227,27 +239,27 @@
             out[place, :] = done
 
 
-def spmm(me, pos, adj, parts, n):
-    row_tiles, per_row = adj.shape[:2]
+def spmm(me, pos, adj, parts, n, row_tiles):
+    per_row = pos.shape[0] // row_tiles
     inner = row_tiles // n // BLOCKS
     share = row_tiles // n * TILE
-    col_tiles = sum(p.shape[0] for p in parts)
-    return pl.pallas_call(
-        functools.partial(spmm_kernel, n=n),
+    col_rows = sum(p.shape[0] for p in parts)
+    return pl.pallas_call(
+        functools.partial(spmm_kernel, n=n, per_row=per_row),
         grid_spec=pltpu.PrefetchScalarGridSpec(
             num_scalar_prefetch=2,
             grid=(n, inner),
             in_specs=[pl.BlockSpec(memory_space=pl.ANY)] * (1 + len(parts)),
             out_specs=[pl.BlockSpec((share, TILE), lambda i, k, me, pos: (0, 0))] * n,
             scratch_shapes=[
-                pltpu.VMEM((col_tiles, TILE, TILE), BF16),
+                pltpu.VMEM((col_rows, TILE), BF16),
                 pltpu.SemaphoreType.DMA((4 * len(parts),)),
                 pltpu.VMEM(adj.shape, BF16),
                 pltpu.SemaphoreType.DMA((n * inner,)),
             ],
         ),
         out_shape=[shape((share, TILE), BF16)] * n,
-        compiler_params=params(52),
+        compiler_params=params(56),
         cost_estimate=cost(2 * row_tiles * per_row * TILE**3 * 2, 2e7),
         name="spmm",
     )(me, pos, adj, *parts)
@@ -336,14 +348,13 @@
 PIECES = 6
 
 
-def spmm_back_kernel(me_ref, pos_ref, *refs, n):
+def spmm_back_kernel(me_ref, pos_ref, *refs, n, per_row):
     adj_ref, ga = refs[0], refs[1 : 1 + n]
     local_ref, away_ref, total, left_ref, stage, sems, adj, adj_sems = refs[1 + n :]
     chunk, part = pl.program_id(0), pl.program_id(1)
     inner = adj_sems.shape[0] // n
     step = chunk * inner + part
-    per_row = adj.shape[1]
-    copy_of = adj_copies(adj_ref, adj, adj_sems, inner, n, lambda c: lax.rem(me_ref[0] + n - c, n))
+    copy_of = adj_copies(adj_ref, adj, adj_sems, inner, lambda c: lax.rem(me_ref[0] + n - c, n))
     size = BLOCKS * TILE
 
     @pl.when((chunk == 0) & (part == 0))
@@ -365,7 +376,7 @@
         base = (first + r) * per_row
         left = left_ref[part, :, r * TILE : (r + 1) * TILE]
         for t in range(0, per_row, 2):
-            right = jnp.concatenate([adj[step * BLOCKS + r, t], adj[step * BLOCKS + r, t + 1]], axis=1)
+            right = tile_pair(adj, (step * BLOCKS + r) * per_row + t)
             both = jnp.dot(left, right, preferred_element_type=F32)
             total[pos_ref[base + t]] += both[:, :TILE]
             total[pos_ref[base + t + 1]] += both[:, TILE:]
@@ -390,11 +401,12 @@
 
 def spmm_back(me, pos, adj, ga, own, away):
     n = len(ga)
-    row_tiles, per_row = adj.shape[:2]
     rows = ga[0].shape[1]
+    row_tiles = n * rows // TILE
+    per_row = pos.shape[0] // row_tiles
     inner = row_tiles // n // BLOCKS
     return pl.pallas_call(
-        functools.partial(spmm_back_kernel, n=n),
+        functools.partial(spmm_back_kernel, n=n, per_row=per_row),
         grid_spec=pltpu.PrefetchScalarGridSpec(
             num_scalar_prefetch=2,
             grid=(n, inner),
@@ -411,7 +423,7 @@
             ],
         ),
         out_shape=[pltpu.HBM((own, TILE, TILE), F32), pltpu.HBM((away, TILE, TILE), BF16)],
-        compiler_params=params(52),
+        compiler_params=params(56),
         cost_estimate=cost(2 * row_tiles * per_row * TILE**3 * 2, 2.2e7),
         name="spmm_back",
     )(me, pos, adj, *ga)
@@ -520,31 +532,48 @@
         + [whole] * len(extra),
         out_specs=whole,
         out_shape=shape((rows, TILE), F32),
-        compiler_params=params(40),
+        compiler_params=params(56),
         cost_estimate=cost(2 * steps * size * B * rows * TILE * 4, 4e6),
         name="scatter_rows",
     )(ids, counts, values, *extra)
 
 
 def add_kernel(*refs):
-    terms, out_ref = refs[:-2], refs[-1]
+    terms, out_ref = refs[:-1], refs[-1]
     total = terms[0][...].astype(F32)
     for term in terms[1:]:
         total = total + term[...].astype(F32)
     out_ref[...] = total.astype(BF16)
 
 
-def add_terms(terms, after):
+def add_terms(terms):
     vmem = pl.BlockSpec(memory_space=pltpu.VMEM)
     return pl.pallas_call(
         add_kernel,
-        in_specs=[vmem] * len(terms) + [pl.BlockSpec(memory_space=pl.ANY)],
+        in_specs=[vmem] * len(terms),
         out_specs=vmem,
         out_shape=shape(terms[0].shape, BF16),
         compiler_params=params(8),
         cost_estimate=cost(1e6, 1e6),
         name="add_terms",
-    )(*terms, after)
+    )(*terms)
+
+
+def tie_kernel(value_ref, after_ref, out_ref):
+    del value_ref, after_ref, out_ref
+
+
+def tie(value, after):
+    anywhere = pl.BlockSpec(memory_space=pl.ANY)
+    return pl.pallas_call(
+        tie_kernel,
+        in_specs=[anywhere, anywhere],
+        out_specs=anywhere,
+        out_shape=shape(value.shape, value.dtype),
+        input_output_aliases={0: 0},
+        compiler_params=params(56),
+        name="tie",
+    )(value, after)
 
 
 def spread_kernel(terms_ref, after_ref, out_ref):
@@ -601,14 +630,14 @@
 
     ids = send_idx[0]
     pos = tile_cols[0].reshape(-1)
-    adj = adj_tiles[0]
+    adj = adj_tiles.reshape(-1, TILE)
 
     packed = gather_rows(ids, counts, stale_features)
     halo = swap(packed)
     own, wn, ws, pieces = prep(me, features, grad_output, w_neigh, w_self, packed, n)
     both = relative(exchange(pieces))
 
-    agg = relative(exchange(spmm(me, pos, adj, [own, halo], n)))
+    agg = relative(exchange(spmm(me, pos, adj, [own.reshape(-1, TILE), halo.reshape(-1, TILE)], n, row_tiles)))
     grad_agg, act, grad_pre = dense(agg, both, wn, ws)
     grad_agg = exchange(grad_agg)
 
@@ -620,7 +649,7 @@
 
     blocks = dom_count // 8
     half = (blocks + 1) // 2
-    terms = swap(add_terms(terms, returned))
+    terms = swap(tie(add_terms(terms), returned))
     grad_stale = scatter_rows(ids, counts, returned, row_count, 0, half, None)
     terms = swap(spread_terms(terms, grad_stale))
     if blocks > half:

time: 205 us -> 211 us (1.029)
  Pallas kernels: 65.4 us -> 70.1 us
  local copies, waits for them, and re-layouts: 16.2 us -> 13.2 us
  waiting for transfers between devices: 72.7 us -> 75.4 us
    ppermute x15, waiting for transfers between devices: 40.3 us -> 44 us  [exchange(): lax.ppermute(pieces[s], 'rep', [(i, (i + s) % n) for i in range(n)])]
    unnamed x77 -> x57, local copies, waits for them, and re-layouts: 16.1 us -> 12.5 us
    pallas_call x2, Pallas kernels: 13.1 us -> 16.1 us  [scatter_rows(): pl.pallas_call(functools.partial(scatter_kernel, first=first), grid=(step...]
    pallas_call x3 -> x4, Pallas kernels: 24.8 us -> 25.8 us  [the longest x1 13.8 us: spmm(): pl.pallas_call(functools.partial(spmm_kernel, n=n, per_row=per_row), grid...]
  transfers between devices with their start and end apart: 19 -> 19, of which waited for: 11 -> 10; matrix products, arithmetic and copies ran while one was open for 0% -> 0% of each run, Pallas kernels for 18% -> 19%
where the time goes in v4:
time: 211 us; the launch traced here: 210 us
  waiting for transfers between devices  75.4 us (36%)
  Pallas kernels  70.1 us (33%)
  starting transfers between devices  50.1 us (24%)
  local copies, waits for them, and re-layouts  13.2 us (6%)
    ppermute x15, waiting for transfers between devices, exchange(): lax.ppermute(pieces[s], 'rep', [(i, (i + s) % n) for i in range(n)])  44 us
    all_to_all x1, waiting for transfers between devices, per_device(): halo = swap(packed)  29.7 us
    ppermute x15, starting transfers between devices, exchange(): lax.ppermute(pieces[s], 'rep', [(i, (i + s) % n) for i in range(n)])  16.8 us
    pallas_call x2, Pallas kernels, scatter_rows(): pl.pallas_call(functools.partial(scatter_kernel, first=first), grid=(step...  16.1 us
    pallas_call x1, Pallas kernels, spmm(): pl.pallas_call(functools.partial(spmm_kernel, n=n, per_row=per_row), grid...  13.8 us
    pallas_call x1, Pallas kernels, gather_rows(): pl.pallas_call(gather_kernel, grid=(peers // size,), in_specs=[pl.BlockSp...  13.3 us
    unnamed x57, local copies, waits for them, and re-layouts  12.5 us
    pallas_call x1, Pallas kernels, spmm_back(): pl.pallas_call(functools.partial(spmm_back_kernel, n=n, per_row=per_row),...  11.9 us
  transfers between devices with their start and end apart: 19, of which 10 were waited for; matrix products, arithmetic and copies ran while one was open for 0% of the time, Pallas kernels for 19%

profile of v4, /device:TPU:1, one launch (start us, length us, event | category | flops | bytes accessed | tf_op | source)
XLA Modules:
  0.0 209.8 jit_solution(3116873249123629187)
XLA Ops:
  0.6 13.3 %gather_rows.1.after_ref = bf16[96,128,128]{2,1,0:T(8,128)(2,1)} custom-call(s32[32,384]{1,0:T(8,128)} %bitcast.8, s32[1,32]{1,0:T(1,128)} %counts_ref.5, bf16[3072,128]{1,0:T(8,128)(2,1)} %table_ref.1), custom_call_target="tpu_custom_call" | custom-call | flops 9663676416 | bytes 4000000 | tf_op jit(solution)/shard_map/gather_rows/pallas_call | solution.py:82
  13.9 9.5 %all-to-all-start = ((bf16[96,128,128]{2,1,0:T(8,128)(2,1)}), bf16[96,128,128]{2,1,0:T(8,128)(2,1)}, u32[]{:S(2)}, u32[]{:S(2)}) async-start(bf16[96,128,128]{2,1,0:T(8,128)(2,1)} %gather_rows.1.after_ref), calls=%async_computation | async-start | bytes 6291456 | tf_op jit(solution)/shard_map/all_to_all | solution.py:636
  23.4 4.9 %prep.1 = (bf16[24,128,128]{2,1,0:T(8,128)(2,1)}, bf16[512,512]{1,0:T(8,128)(2,1)}, bf16[512,512]{1,0:T(8,128)(2,1)}, bf16[2,768,128]{2,1,0:T(8,128)(2,1)}, bf16...) custom-call(s32[1]{0:T(128)} %bitcast.me_ref, bf16[3072,128]{1,0:T(8,128)(2,1)} %feat_ref.1, ...), custom_call_target="tpu_custom_call" | custom-call | flops 10000000000 | bytes 6000000 | tf_op jit(solution)/shard_map/prep/pallas_call | solution.py:135
  28.3 2.8 %collective-permute-start.3 = (bf16[2,768,128]{2,1,0:T(8,128)(2,1)}, bf16[2,768,128]{2,1,0:T(8,128)(2,1)S(1)}, u32[]{:S(2)}, u32[]{:S(2)}) collective-permute-start(bf16[2,768,128]{2,1,0:T(8,128)(2,1)} %get-tuple-element.42), channel_id=1, source_target_pairs={{0,3},{1,0},{2,1},{3,2},{4,7},{5,4},{6,5},{7,6},{8,11},{9,8},{10,9... | collective-permute-start | bytes 1179656 | tf_op jit(solution)/shard_map/ppermute | solution.py:102
  32.9 29.7 %all-to-all-done = bf16[96,128,128]{2,1,0:T(8,128)(2,1)} async-done(((bf16[96,128,128]{2,1,0:T(8,128)(2,1)}), bf16[96,128,128]{2,1,0:T(8,128)(2,1)}, u32[]{:S(2)}, u32[]{:S(2)}) %all-to-all-start) | async-done | bytes 3145760 | tf_op jit(solution)/shard_map/all_to_all | solution.py:636
  62.6 13.8 %spmm.1 = (bf16[768,128]{1,0:T(8,128)(2,1)}, bf16[768,128]{1,0:T(8,128)(2,1)}, bf16[768,128]{1,0:T(8,128)(2,1)}, bf16[768,128]{1,0:T(8,128)(2,1)}) custom-call(s32[1]{0:T(128)} %bitcast.me_ref, s32[480]{0:T(512)} %reshape_squeeze.3.pos_ref, bf16[61440,128]{1,0:T(8,128)(2,1)} %bitcast.5, bf16[3072,128]{1,0:T(8,128)(2,1)} %bitcast.7, ...), custom_call_target="tpu_custom_call" | custom-call | flops 4026531840 | bytes 20000000 | tf_op jit(solution)/shard_map/spmm/pallas_call | solution.py:247
  76.5 2.8 %collective-permute-start = (bf16[768,128]{1,0:T(8,128)(2,1)}, bf16[768,128]{1,0:T(8,128)(2,1)S(1)}, u32[]{:S(2)}, u32[]{:S(2)}) collective-permute-start(bf16[768,128]{1,0:T(8,128)(2,1)} %get-tuple-element.38), channel_id=1, source_target_pairs={{0,3},{1,0},{2,1},{3,2},{4,7},{5,4},{6,5},{7,6},{8,11},{9,8},{10,9... | collective-permute-start | bytes 589832 | tf_op jit(solution)/shard_map/ppermute | solution.py:102
  80.4 4.3 %collective-permute-done.refs_1_ = bf16[768,128]{1,0:T(8,128)(2,1)S(1)} collective-permute-done((bf16[768,128]{1,0:T(8,128)(2,1)}, bf16[768,128]{1,0:T(8,128)(2,1)S(1)}, u32[]{:S(2)}, u32[]{:S(2)}) %collective-permute-start) | collective-permute-done | bytes 196640 | tf_op jit(solution)/shard_map/ppermute | solution.py:102
  85.6 4.8 %collective-permute-done.2.refs_3_ = bf16[768,128]{1,0:T(8,128)(2,1)S(1)} collective-permute-done((bf16[768,128]{1,0:T(8,128)(2,1)}, bf16[768,128]{1,0:T(8,128)(2,1)S(1)}, u32[]{:S(2)}, u32[]{:S(2)}) %collective-permute-start.2) | collective-permute-done | bytes 196640 | tf_op jit(solution)/shard_map/ppermute | solution.py:102
  91.4 4.1 %dense.1 = (bf16[128,768]{1,0:T(8,128)(2,1)S(1)}, bf16[128,768]{1,0:T(8,128)(2,1)S(1)}, bf16[128,768]{1,0:T(8,128)(2,1)S(1)}, bf16[128,768]{1,0:T(8,128)(2,1)S(1...) custom-call(bf16[768,128]{1,0:T(8,128)(2,1)S(1)} %copy-done.9, bf16[768,128]{1,0:T(8,128)(2,1)S(1)} %collective-permute-done.refs_1_, ...), custom_call_target="tpu_custom_call" | custom-call | flops 1207959552 | bytes 7000000 | tf_op jit(solution)/shard_map/dense/pallas_call | solution.py:300
  96.3 2.6 %collective-permute-start.8 = (bf16[128,768]{1,0:T(8,128)(2,1)S(1)}, bf16[128,768]{1,0:T(8,128)(2,1)S(1)}, u32[]{:S(2)}, u32[]{:S(2)}) collective-permute-start(bf16[128,768]{1,0:T(8,128)(2,1)S(1)} %get-tuple-element.50), channel_id=1, source_target_pairs={{0,3},{1,0},{2,1},{3,2},{4,7},{5,4},{6,5},{7,6},{8,11},{9,8},{10,9... | collective-permute-start | bytes 589832 | tf_op jit(solution)/shard_map/ppermute | solution.py:102
  98.9 8.6 %collective-permute-done.6.refs_2_ = bf16[128,768]{1,0:T(8,128)(2,1)S(1)} collective-permute-done((bf16[128,768]{1,0:T(8,128)(2,1)S(1)}, bf16[128,768]{1,0:T(8,128)(2,1)S(1)}, u32[]{:S(2)}, u32[]{:S(2)}) %collective-permute-start.6) | collective-permute-done | bytes 196640 | tf_op jit(solution)/shard_map/ppermute | solution.py:102
  108.3 11.9 %spmm_back.1 = (f32[24,128,128]{2,1,0:T(8,128)}, bf16[96,128,128]{2,1,0:T(8,128)(2,1)}) custom-call(s32[1]{0:T(128)} %bitcast.me_ref, s32[480]{0:T(512)} %reshape_squeeze.3.pos_ref, bf16[61440,128]{1,0:T(8,128)(2,1)} %bitcast.6, bf16[128,768]{1,0:T(8,128)(2,1)} %copy-done.4, bf16[128,768]{1,0:T(8,128)(2,1)} %copy-done.24, bf16[128,768]{1,0:T(8,128)(2,1)} %copy-done.25, ...), custom_call_target="tpu_custom_call" | custom-call | flops 4026531840 | bytes 22000000 | tf_op jit(solution)/shard_map/spmm_back/pallas_call | solution.py:408
  120.3 8.9 %all-to-all-start.1 = ((bf16[96,128,128]{2,1,0:T(8,128)(2,1)}), bf16[96,128,128]{2,1,0:T(8,128)(2,1)}, u32[]{:S(2)}, u32[]{:S(2)}) async-start(bf16[96,128,128]{2,1,0:T(8,128)(2,1)} %get-tuple-element.54.after_ref.refs_9_), calls=%async_computation.1 | async-start | bytes 6291456 | tf_op jit(solution)/shard_map/all_to_all | solution.py:645
  139.8 3.6 %collective-permute-start.10 = (bf16[2,768,128]{2,1,0:T(8,128)(2,1)S(1)}, bf16[2,768,128]{2,1,0:T(8,128)(2,1)S(1)}, u32[]{:S(2)}, u32[]{:S(2)}) collective-permute-start(bf16[2,768,128]{2,1,0:T(8,128)(2,1)S(1)} %get-tuple-element.57), channel_id=1, source_target_pairs={{0,2},{1,3},{2,0},{3,1},{4,6},{5,7},{6,4},{7,5},{8,10},{9,11},{10,... | collective-permute-start | bytes 1179656 | tf_op jit(solution)/shard_map/ppermute | solution.py:102
  143.4 1.5 collective-permute-start.11
  144.9 2.4 %collective-permute-done.12.refs_1_ = bf16[32,32,128]{2,1,0:T(8,128)(2,1)S(1)} collective-permute-done((bf16[32,32,128]{2,1,0:T(8,128)(2,1)S(1)}, bf16[32,32,128]{2,1,0:T(8,128)(2,1)S(1)}, u32[]{:S(2)}, u32[]{:S(2)}) %collective-permute-start.12) | collective-permute-done | bytes 262176 | tf_op jit(solution)/shard_map/ppermute | solution.py:102
  148.1 22.2 %collective-permute-done.13.refs_2_ = bf16[32,32,128]{2,1,0:T(8,128)(2,1)S(1)} collective-permute-done((bf16[32,32,128]{2,1,0:T(8,128)(2,1)S(1)}, bf16[32,32,128]{2,1,0:T(8,128)(2,1)S(1)}, u32[]{:S(2)}, u32[]{:S(2)}) %collective-permute-start.13) | collective-permute-done | bytes 262176 | tf_op jit(solution)/shard_map/ppermute | solution.py:102
  172.0 2.1 %finish.1 = (bf16[3072,128]{1,0:T(8,128)(2,1)}, bf16[3072,128]{1,0:T(8,128)(2,1)}) custom-call(s32[1]{0:T(128)} %bitcast.me_ref, f32[24,128,128]{2,1,0:T(8,128)S(1)} %copy-done.3, bf16[2,768,128]{2,1,0:T(8,128)(2,1)S(1)} %get-tuple-element.55.refs_0_, bf16[2,768,128]{2,1,0:T(8,128)(2,1)S(1)} %collective-permute-done.9.refs_1_, ...), custom_call_target="tpu_custom_call" | custom-call | flops 1000000 | bytes 7000000 | tf_op jit(solution)/shard_map/finish/pallas_call | solution.py:478
  174.1 8.6 %all-to-all-start.2 = ((bf16[32,32,128]{2,1,0:T(8,128)(2,1)}), bf16[32,32,128]{2,1,0:T(8,128)(2,1)S(1)}, u32[]{:S(2)}, u32[]{:S(2)}) async-start(bf16[32,32,128]{2,1,0:T(8,128)(2,1)} %tie.1), calls=%async_computation.2 | async-start | bytes 524288 | tf_op jit(solution)/shard_map/all_to_all | solution.py:652
  182.7 7.8 %scatter_rows.2.refs_0_.after_ref = f32[3072,128]{1,0:T(8,128)} custom-call(s32[32,384]{1,0:T(8,128)} %bitcast.9, s32[1,32]{1,0:T(1,128)} %counts_ref.5, bf16[96,128,128]{2,1,0:T(8,128)(2,1)} %all-to-all-done.1.val_ref.after_ref), custom_call_target="tpu_custom_call" | custom-call | flops 19327352832 | bytes 4000000 | tf_op jit(solution)/shard_map/scatter_rows/pallas_call | solution.py:524
  191.6 1.4 copy-done.2
  193.8 6.3 %all-to-all-start.3 = ((bf16[32,32,128]{2,1,0:T(8,128)(2,1)}), bf16[32,32,128]{2,1,0:T(8,128)(2,1)S(1)}, u32[]{:S(2)}, u32[]{:S(2)}) async-start(bf16[32,32,128]{2,1,0:T(8,128)(2,1)} %spread_terms.1), calls=%async_computation.3 | async-start | bytes 524288 | tf_op jit(solution)/shard_map/all_to_all | solution.py:654
  200.1 8.3 %scatter_rows.3 = f32[3072,128]{1,0:T(8,128)} custom-call(s32[32,384]{1,0:T(8,128)} %bitcast.10, s32[1,32]{1,0:T(1,128)} %counts_ref.5, bf16[96,128,128]{2,1,0:T(8,128)(2,1)} %all-to-all-done.1.val_ref.after_ref, f32[3072,128]{1,0:T(8,128)} %scatter_rows.2.refs_0_.after_ref), custom_call_target="tpu_custom_call" | custom-call | flops 19327352832 | bytes 4000000 | tf_op jit(solution)/shard_map/scatter_rows/pallas_call | solution.py:524
  (86 shorter events, 22.8 us)
Async XLA Ops:
  13.9 48.7 %all-to-all-start = ((bf16[96,128,128]{2,1,0:T(8,128)(2,1)}), bf16[96,128,128]{2,1,0:T(8,128)(2,1)}, u32[]{:S(2)}, u32[]{:S(2)}) async-start(bf16[96,128,128]{2,1,0:T(8,128)(2,1)} %gather_rows.1.after_ref), calls=%async_computation | async-start | bytes 6291456 | tf_op jit(solution)/shard_map/all_to_all | solution.py:636
  28.3 51.3 %collective-permute-start.3 = (bf16[2,768,128]{2,1,0:T(8,128)(2,1)}, bf16[2,768,128]{2,1,0:T(8,128)(2,1)S(1)}, u32[]{:S(2)}, u32[]{:S(2)}) collective-permute-start(bf16[2,768,128]{2,1,0:T(8,128)(2,1)} %get-tuple-element.42), channel_id=1, source_target_pairs={{0,3},{1,0},{2,1},{3,2},{4,7},{5,4},{6,5},{7,6},{8,11},{9,8},{10,9... | collective-permute-start | bytes 1179656 | tf_op jit(solution)/shard_map/ppermute | solution.py:102
  31.1 49.2 %collective-permute-start.4 = (bf16[2,768,128]{2,1,0:T(8,128)(2,1)}, bf16[2,768,128]{2,1,0:T(8,128)(2,1)S(1)}, u32[]{:S(2)}, u32[]{:S(2)}) collective-permute-start(bf16[2,768,128]{2,1,0:T(8,128)(2,1)} %get-tuple-element.43), channel_id=1, source_target_pairs={{0,2},{1,3},{2,0},{3,1},{4,6},{5,7},{6,4},{7,5},{8,10},{9,11},{10,... | collective-permute-start | bytes 1179656 | tf_op jit(solution)/shard_map/ppermute | solution.py:102
  31.5 48.9 %collective-permute-start.5 = (bf16[2,768,128]{2,1,0:T(8,128)(2,1)}, bf16[2,768,128]{2,1,0:T(8,128)(2,1)S(1)}, u32[]{:S(2)}, u32[]{:S(2)}) collective-permute-start(bf16[2,768,128]{2,1,0:T(8,128)(2,1)} %get-tuple-element.44), channel_id=1, source_target_pairs={{0,1},{1,2},{2,3},{3,0},{4,5},{5,6},{6,7},{7,4},{8,9},{9,10},{10,1... | collective-permute-start | bytes 1179656 | tf_op jit(solution)/shard_map/ppermute | solution.py:102
  62.6 27.8 %copy-start.21 = (bf16[512,512]{1,0:T(8,128)(2,1)S(1)}, bf16[512,512]{1,0:T(8,128)(2,1)}, u32[]{:S(2)}) copy-start(bf16[512,512]{1,0:T(8,128)(2,1)} %get-tuple-element.45.refs_8_) | copy-start | bytes 1572868
  62.6 27.8 %copy-start.22 = (bf16[2,768,128]{2,1,0:T(8,128)(2,1)S(1)}, bf16[2,768,128]{2,1,0:T(8,128)(2,1)}, u32[]{:S(2)}) copy-start(bf16[2,768,128]{2,1,0:T(8,128)(2,1)} %get-tuple-element.41.refs_4_) | copy-start | bytes 1179652
  76.5 8.2 %collective-permute-start = (bf16[768,128]{1,0:T(8,128)(2,1)}, bf16[768,128]{1,0:T(8,128)(2,1)S(1)}, u32[]{:S(2)}, u32[]{:S(2)}) collective-permute-start(bf16[768,128]{1,0:T(8,128)(2,1)} %get-tuple-element.38), channel_id=1, source_target_pairs={{0,3},{1,0},{2,1},{3,2},{4,7},{5,4},{6,5},{7,6},{8,11},{9,8},{10,9... | collective-permute-start | bytes 589832 | tf_op jit(solution)/shard_map/ppermute | solution.py:102
  79.3 6.3 %collective-permute-start.1 = (bf16[768,128]{1,0:T(8,128)(2,1)}, bf16[768,128]{1,0:T(8,128)(2,1)S(1)}, u32[]{:S(2)}, u32[]{:S(2)}) collective-permute-start(bf16[768,128]{1,0:T(8,128)(2,1)} %get-tuple-element.39), channel_id=1, source_target_pairs={{0,2},{1,3},{2,0},{3,1},{4,6},{5,7},{6,4},{7,5},{8,10},{9,11},{10,... | collective-permute-start | bytes 589832 | tf_op jit(solution)/shard_map/ppermute | solution.py:102
  79.6 10.8 %collective-permute-start.2 = (bf16[768,128]{1,0:T(8,128)(2,1)}, bf16[768,128]{1,0:T(8,128)(2,1)S(1)}, u32[]{:S(2)}, u32[]{:S(2)}) collective-permute-start(bf16[768,128]{1,0:T(8,128)(2,1)} %get-tuple-element.40), channel_id=1, source_target_pairs={{0,1},{1,2},{2,3},{3,0},{4,5},{5,6},{6,7},{7,4},{8,9},{9,10},{10,1... | collective-permute-start | bytes 589832 | tf_op jit(solution)/shard_map/ppermute | solution.py:102
  80.3 39.9 %copy-start.5 = (bf16[2,768,128]{2,1,0:T(8,128)(2,1)}, bf16[2,768,128]{2,1,0:T(8,128)(2,1)S(1)}, u32[]{:S(2)}) copy-start(bf16[2,768,128]{2,1,0:T(8,128)(2,1)S(1)} %collective-permute-done.4.refs_6_) | copy-start | bytes 1179652
  80.3 39.9 %copy-start.7 = (bf16[2,768,128]{2,1,0:T(8,128)(2,1)}, bf16[2,768,128]{2,1,0:T(8,128)(2,1)S(1)}, u32[]{:S(2)}) copy-start(bf16[2,768,128]{2,1,0:T(8,128)(2,1)S(1)} %collective-permute-done.5.refs_7_) | copy-start | bytes 1179652
  96.2 11.3 %collective-permute-start.6 = (bf16[128,768]{1,0:T(8,128)(2,1)S(1)}, bf16[128,768]{1,0:T(8,128)(2,1)S(1)}, u32[]{:S(2)}, u32[]{:S(2)}) collective-permute-start(bf16[128,768]{1,0:T(8,128)(2,1)S(1)} %get-tuple-element.48), channel_id=1, source_target_pairs={{0,1},{1,2},{2,3},{3,0},{4,5},{5,6},{6,7},{7,4},{8,9},{9,10},{10,1... | collective-permute-start | bytes 589832 | tf_op jit(solution)/shard_map/ppermute | solution.py:102
  96.2 11.3 %collective-permute-start.7 = (bf16[128,768]{1,0:T(8,128)(2,1)S(1)}, bf16[128,768]{1,0:T(8,128)(2,1)S(1)}, u32[]{:S(2)}, u32[]{:S(2)}) collective-permute-start(bf16[128,768]{1,0:T(8,128)(2,1)S(1)} %get-tuple-element.49), channel_id=1, source_target_pairs={{0,2},{1,3},{2,0},{3,1},{4,6},{5,7},{6,4},{7,5},{8,10},{9,11},{10,... | collective-permute-start | bytes 589832 | tf_op jit(solution)/shard_map/ppermute | solution.py:102
  96.3 11.2 %collective-permute-start.8 = (bf16[128,768]{1,0:T(8,128)(2,1)S(1)}, bf16[128,768]{1,0:T(8,128)(2,1)S(1)}, u32[]{:S(2)}, u32[]{:S(2)}) collective-permute-start(bf16[128,768]{1,0:T(8,128)(2,1)S(1)} %get-tuple-element.50), channel_id=1, source_target_pairs={{0,3},{1,0},{2,1},{3,2},{4,7},{5,4},{6,5},{7,6},{8,11},{9,8},{10,9... | collective-permute-start | bytes 589832 | tf_op jit(solution)/shard_map/ppermute | solution.py:102
  120.3 53.8 %all-to-all-start.1 = ((bf16[96,128,128]{2,1,0:T(8,128)(2,1)}), bf16[96,128,128]{2,1,0:T(8,128)(2,1)}, u32[]{:S(2)}, u32[]{:S(2)}) async-start(bf16[96,128,128]{2,1,0:T(8,128)(2,1)} %get-tuple-element.54.after_ref.refs_9_), calls=%async_computation.1 | async-start | bytes 6291456 | tf_op jit(solution)/shard_map/all_to_all | solution.py:645
  138.1 9.2 %collective-permute-start.12 = (bf16[32,32,128]{2,1,0:T(8,128)(2,1)S(1)}, bf16[32,32,128]{2,1,0:T(8,128)(2,1)S(1)}, u32[]{:S(2)}, u32[]{:S(2)}) collective-permute-start(bf16[32,32,128]{2,1,0:T(8,128)(2,1)S(1)} %get-tuple-element.62), channel_id=1, source_target_pairs={{0,1},{1,2},{2,3},{3,0},{4,5},{5,6},{6,7},{7,4},{8,9},{9,10},{10,1... | collective-permute-start | bytes 786440 | tf_op jit(solution)/shard_map/ppermute | solution.py:102
  138.4 33.6 %copy-start.3 = (f32[24,128,128]{2,1,0:T(8,128)S(1)}, f32[24,128,128]{2,1,0:T(8,128)}, u32[]{:S(2)}) copy-start(f32[24,128,128]{2,1,0:T(8,128)} %get-tuple-element.51.ext_ref) | copy-start | bytes 4718596
  139.6 32.4 %collective-permute-start.9 = (bf16[2,768,128]{2,1,0:T(8,128)(2,1)S(1)}, bf16[2,768,128]{2,1,0:T(8,128)(2,1)S(1)}, u32[]{:S(2)}, u32[]{:S(2)}) collective-permute-start(bf16[2,768,128]{2,1,0:T(8,128)(2,1)S(1)} %get-tuple-element.56), channel_id=1, source_target_pairs={{0,1},{1,2},{2,3},{3,0},{4,5},{5,6},{6,7},{7,4},{8,9},{9,10},{10,1... | collective-permute-start | bytes 1179656 | tf_op jit(solution)/shard_map/ppermute | solution.py:102
  139.8 32.1 %collective-permute-start.10 = (bf16[2,768,128]{2,1,0:T(8,128)(2,1)S(1)}, bf16[2,768,128]{2,1,0:T(8,128)(2,1)S(1)}, u32[]{:S(2)}, u32[]{:S(2)}) collective-permute-start(bf16[2,768,128]{2,1,0:T(8,128)(2,1)S(1)} %get-tuple-element.57), channel_id=1, source_target_pairs={{0,2},{1,3},{2,0},{3,1},{4,6},{5,7},{6,4},{7,5},{8,10},{9,11},{10,... | collective-permute-start | bytes 1179656 | tf_op jit(solution)/shard_map/ppermute | solution.py:102
  143.4 28.6 %collective-permute-start.11 = (bf16[2,768,128]{2,1,0:T(8,128)(2,1)S(1)}, bf16[2,768,128]{2,1,0:T(8,128)(2,1)S(1)}, u32[]{:S(2)}, u32[]{:S(2)}) collective-permute-start(bf16[2,768,128]{2,1,0:T(8,128)(2,1)S(1)} %get-tuple-element.58), channel_id=1, source_target_pairs={{0,3},{1,0},{2,1},{3,2},{4,7},{5,4},{6,5},{7,6},{8,11},{9,8},{10,9... | collective-permute-start | bytes 1179656 | tf_op jit(solution)/shard_map/ppermute | solution.py:102
  144.9 25.4 %collective-permute-start.13 = (bf16[32,32,128]{2,1,0:T(8,128)(2,1)S(1)}, bf16[32,32,128]{2,1,0:T(8,128)(2,1)S(1)}, u32[]{:S(2)}, u32[]{:S(2)}) collective-permute-start(bf16[32,32,128]{2,1,0:T(8,128)(2,1)S(1)} %get-tuple-element.63), channel_id=1, source_target_pairs={{0,2},{1,3},{2,0},{3,1},{4,6},{5,7},{6,4},{7,5},{8,10},{9,11},{10,... | collective-permute-start | bytes 786440 | tf_op jit(solution)/shard_map/ppermute | solution.py:102
  147.3 23.9 %collective-permute-start.14 = (bf16[32,32,128]{2,1,0:T(8,128)(2,1)S(1)}, bf16[32,32,128]{2,1,0:T(8,128)(2,1)S(1)}, u32[]{:S(2)}, u32[]{:S(2)}) collective-permute-start(bf16[32,32,128]{2,1,0:T(8,128)(2,1)S(1)} %get-tuple-element.64), channel_id=1, source_target_pairs={{0,3},{1,0},{2,1},{3,2},{4,7},{5,4},{6,5},{7,6},{8,11},{9,8},{10,9... | collective-permute-start | bytes 786440 | tf_op jit(solution)/shard_map/ppermute | solution.py:102
  174.1 17.5 %all-to-all-start.2 = ((bf16[32,32,128]{2,1,0:T(8,128)(2,1)}), bf16[32,32,128]{2,1,0:T(8,128)(2,1)S(1)}, u32[]{:S(2)}, u32[]{:S(2)}) async-start(bf16[32,32,128]{2,1,0:T(8,128)(2,1)} %tie.1), calls=%async_computation.2 | async-start | bytes 524288 | tf_op jit(solution)/shard_map/all_to_all | solution.py:652
  193.8 15.2 %all-to-all-start.3 = ((bf16[32,32,128]{2,1,0:T(8,128)(2,1)}), bf16[32,32,128]{2,1,0:T(8,128)(2,1)S(1)}, u32[]{:S(2)}, u32[]{:S(2)}) async-start(bf16[32,32,128]{2,1,0:T(8,128)(2,1)} %spread_terms.1), calls=%async_computation.3 | async-start | bytes 524288 | tf_op jit(solution)/shard_map/all_to_all | solution.py:654
  (23 other events, 89.2 us)

commit v5 on v3

--- a/solution.py
+++ b/solution.py
@@ -163,14 +163,30 @@
 BLOCKS = 3
 
 
-def adj_copies(adj_ref, held, sems, inner, n, chunk_of):
-    def copy(step):
-        first = (chunk_of(step // inner) * inner + lax.rem(step, inner)) * BLOCKS
-        return pltpu.make_async_copy(
-            adj_ref.at[pl.ds(first, BLOCKS)], held.at[pl.ds(step * BLOCKS, BLOCKS)], sems.at[step]
-        )
-
-    return copy
+SLOTS = 3 * BLOCKS
+
+
+def adj_stream(adj_ref, held, sems, chunk, part, n, inner, chunk_of):
+    step = chunk * inner + part
+
+    def copy(at, r):
+        source = (chunk_of(at // inner) * inner + lax.rem(at, inner)) * BLOCKS + r
+        slot = lax.rem(at, 3) * BLOCKS + r
+        return pltpu.make_async_copy(adj_ref.at[source], held.at[slot], sems.at[slot])
+
+    def start(at):
+        for r in range(BLOCKS):
+            copy(at, r).start()
+
+    def wait(r):
+        copy(step, r).wait()
+
+    def ahead():
+        @pl.when(step + 2 < n * inner)
+        def _():
+            start(step + 2)
+
+    return lax.rem(step, 3) * BLOCKS, start, wait, ahead
 
 
 def spmm_kernel(me_ref, pos_ref, *refs, n):
@@ -181,10 +197,11 @@
         refs[-4:],
     )
     chunk, part = pl.program_id(0), pl.program_id(1)
-    inner = adj_sems.shape[0] // n
-    step = chunk * inner + part
+    inner = pl.num_programs(1)
     per_row = adj.shape[1]
-    copy_of = adj_copies(adj_ref, adj, adj_sems, inner, n, lambda c: lax.rem(me_ref[0] + c, n))
+    slot, start_adj, wait_adj, ahead = adj_stream(
+        adj_ref, adj, adj_sems, chunk, part, n, inner, lambda c: lax.rem(me_ref[0] + c, n)
+    )
 
     @pl.when((chunk == 0) & (part == 0))
     def _():
@@ -200,19 +217,20 @@
                 start, at = start + size, at + 1
         for copy in copies:
             copy.start()
-        for k in range(adj_sems.shape[0]):
-            copy_of(k).start()
+        start_adj(0)
         for copy in copies:
             copy.wait()
-
-    copy_of(step).wait()
+        start_adj(1)
+
+    ahead()
     first = (lax.rem(me_ref[0] + chunk, n) * pl.num_programs(1) + part) * BLOCKS
     done = []
     for r in range(BLOCKS):
         base = (first + r) * per_row
+        wait_adj(r)
         total = None
         for t in range(0, per_row, 2):
-            left = jnp.concatenate([adj[step * BLOCKS + r, t], adj[step * BLOCKS + r, t + 1]], axis=1)
+            left = jnp.concatenate([adj[slot + r, t], adj[slot + r, t + 1]], axis=1)
             right = jnp.concatenate([ext[pos_ref[base + t]], ext[pos_ref[base + t + 1]]], axis=1)
             term = lax.dot_general(left, right, NT, preferred_element_type=F32)
             total = term if total is None else total + term
@@ -242,8 +260,8 @@
             scratch_shapes=[
                 pltpu.VMEM((col_tiles, TILE, TILE), BF16),
                 pltpu.SemaphoreType.DMA((4 * len(parts),)),
-                pltpu.VMEM(adj.shape, BF16),
-                pltpu.SemaphoreType.DMA((n * inner,)),
+                pltpu.VMEM((SLOTS, *adj.shape[1:]), BF16),
+                pltpu.SemaphoreType.DMA((SLOTS,)),
             ],
         ),
         out_shape=[shape((share, TILE), BF16)] * n,
@@ -340,16 +358,17 @@
     adj_ref, ga = refs[0], refs[1 : 1 + n]
     local_ref, away_ref, total, left_ref, stage, sems, adj, adj_sems = refs[1 + n :]
     chunk, part = pl.program_id(0), pl.program_id(1)
-    inner = adj_sems.shape[0] // n
-    step = chunk * inner + part
+    inner = pl.num_programs(1)
     per_row = adj.shape[1]
-    copy_of = adj_copies(adj_ref, adj, adj_sems, inner, n, lambda c: lax.rem(me_ref[0] + n - c, n))
+    slot, start_adj, wait_adj, ahead = adj_stream(
+        adj_ref, adj, adj_sems, chunk, part, n, inner, lambda c: lax.rem(me_ref[0] + n - c, n)
+    )
     size = BLOCKS * TILE
 
     @pl.when((chunk == 0) & (part == 0))
     def _():
-        for k in range(adj_sems.shape[0]):
-            copy_of(k).start()
+        start_adj(0)
+        start_adj(1)
         total[...] = jnp.zeros_like(total)
 
     for s in range(n):
@@ -359,13 +378,14 @@
             for k in range(left_ref.shape[0]):
                 left_ref[k] = ga[s][:, k * size : (k + 1) * size]
 
-    copy_of(step).wait()
+    ahead()
     first = (lax.rem(me_ref[0] + n - chunk, n) * pl.num_programs(1) + part) * BLOCKS
     for r in range(BLOCKS):
         base = (first + r) * per_row
+        wait_adj(r)
         left = left_ref[part, :, r * TILE : (r + 1) * TILE]
         for t in range(0, per_row, 2):
-            right = jnp.concatenate([adj[step * BLOCKS + r, t], adj[step * BLOCKS + r, t + 1]], axis=1)
+            right = jnp.concatenate([adj[slot + r, t], adj[slot + r, t + 1]], axis=1)
             both = jnp.dot(left, right, preferred_element_type=F32)
             total[pos_ref[base + t]] += both[:, :TILE]
             total[pos_ref[base + t + 1]] += both[:, TILE:]
@@ -406,8 +426,8 @@
                 pltpu.VMEM((inner, TILE, BLOCKS * TILE), BF16),
                 pltpu.VMEM((away, TILE, TILE), BF16),
                 pltpu.SemaphoreType.DMA((PIECES + 1,)),
-                pltpu.VMEM(adj.shape, BF16),
-                pltpu.SemaphoreType.DMA((n * inner,)),
+                pltpu.VMEM((SLOTS, *adj.shape[1:]), BF16),
+                pltpu.SemaphoreType.DMA((SLOTS,)),
             ],
         ),
         out_shape=[pltpu.HBM((own, TILE, TILE), F32), pltpu.HBM((away, TILE, TILE), BF16)],
@@ -484,12 +504,13 @@
 
 
 def scatter_kernel(ids_ref, counts_ref, val_ref, *refs, first):
-    before, out_ref = refs[:-1], refs[-1]
+    before, (out_ref, mark_ref) = refs[:-2], refs[-2:]
     groups = out_ref.shape[0] // LOW
 
     @pl.when(pl.program_id(0) == 0)
     def _():
         out_ref[...] = before[0][...] if before else jnp.zeros_like(out_ref)
+        mark_ref[...] = jnp.zeros_like(mark_ref)
 
     for p in range(0, ids_ref.shape[0], 2):
         ids = masked_ids(ids_ref, counts_ref, p, 2, first)
@@ -518,33 +539,50 @@
             pl.BlockSpec((size * CHUNKS, TILE, TILE), lambda i: (i + first, 0, 0)),
         ]
         + [whole] * len(extra),
-        out_specs=whole,
-        out_shape=shape((rows, TILE), F32),
-        compiler_params=params(40),
+        out_specs=[whole, pl.BlockSpec((8, TILE), lambda i: (0, 0))],
+        out_shape=[shape((rows, TILE), F32), shape((8, TILE), F32)],
+        compiler_params=params(24),
         cost_estimate=cost(2 * steps * size * B * rows * TILE * 4, 4e6),
         name="scatter_rows",
     )(ids, counts, values, *extra)
 
 
 def add_kernel(*refs):
-    terms, out_ref = refs[:-2], refs[-1]
+    terms, out_ref = refs[:-1], refs[-1]
     total = terms[0][...].astype(F32)
     for term in terms[1:]:
         total = total + term[...].astype(F32)
     out_ref[...] = total.astype(BF16)
 
 
-def add_terms(terms, after):
+def add_terms(terms):
     vmem = pl.BlockSpec(memory_space=pltpu.VMEM)
     return pl.pallas_call(
         add_kernel,
-        in_specs=[vmem] * len(terms) + [pl.BlockSpec(memory_space=pl.ANY)],
+        in_specs=[vmem] * len(terms),
         out_specs=vmem,
         out_shape=shape(terms[0].shape, BF16),
         compiler_params=params(8),
         cost_estimate=cost(1e6, 1e6),
         name="add_terms",
-    )(*terms, after)
+    )(*terms)
+
+
+def tie_kernel(value_ref, after_ref, out_ref):
+    del value_ref, after_ref, out_ref
+
+
+def tie(value, after):
+    anywhere = pl.BlockSpec(memory_space=pl.ANY)
+    return pl.pallas_call(
+        tie_kernel,
+        in_specs=[anywhere, anywhere],
+        out_specs=anywhere,
+        out_shape=shape(value.shape, value.dtype),
+        input_output_aliases={0: 0},
+        compiler_params=params(8),
+        name="tie",
+    )(value, after)
 
 
 def spread_kernel(terms_ref, after_ref, out_ref):
@@ -620,11 +658,11 @@
 
     blocks = dom_count // 8
     half = (blocks + 1) // 2
-    terms = swap(add_terms(terms, returned))
-    grad_stale = scatter_rows(ids, counts, returned, row_count, 0, half, None)
-    terms = swap(spread_terms(terms, grad_stale))
+    terms = swap(tie(add_terms(terms), returned[0]))
+    grad_stale, mark = scatter_rows(ids, counts, returned, row_count, 0, half, None)
+    terms = swap(spread_terms(terms, mark))
     if blocks > half:
-        grad_stale = scatter_rows(
+        grad_stale, _ = scatter_rows(
             ids, counts, returned, row_count, half, blocks - half, grad_stale
         )
     grad_neigh, grad_self = place_terms(terms, width, n)

time: 205 us -> 211 us (1.029)
  waiting for transfers between devices: 72.7 us -> 76.3 us
  Pallas kernels: 65.4 us -> 68.8 us
    ppermute x15, waiting for transfers between devices: 40.3 us -> 43.9 us  [exchange(): lax.ppermute(pieces[s], 'rep', [(i, (i + s) % n) for i in range(n)])]
    unnamed x77 -> x59, local copies, waits for them, and re-layouts: 16.1 us -> 14.5 us
  transfers between devices with their start and end apart: 19 -> 19, of which waited for: 11 -> 10; matrix products, arithmetic and copies ran while one was open for 0% -> 0% of each run, Pallas kernels for 18% -> 18%
where the time goes in v5:
time: 211 us; the launch traced here: 210 us
  waiting for transfers between devices  76.3 us (36%)
  Pallas kernels  68.8 us (33%)
  starting transfers between devices  49.2 us (23%)
  local copies, waits for them, and re-layouts  14.6 us (7%)
    ppermute x15, waiting for transfers between devices, exchange(): lax.ppermute(pieces[s], 'rep', [(i, (i + s) % n) for i in range(n)])  43.9 us
    all_to_all x1, waiting for transfers between devices, per_device(): halo = swap(packed)  30.3 us
    ppermute x15, starting transfers between devices, exchange(): lax.ppermute(pieces[s], 'rep', [(i, (i + s) % n) for i in range(n)])  16.9 us
    pallas_call x1, Pallas kernels, spmm(): pl.pallas_call(functools.partial(spmm_kernel, n=n), grid_spec=pltpu.Prefe...  14.8 us
    unnamed x59, local copies, waits for them, and re-layouts  14.5 us
    pallas_call x1, Pallas kernels, gather_rows(): pl.pallas_call(gather_kernel, grid=(peers // size,), in_specs=[pl.BlockSp...  13.3 us
    pallas_call x2, Pallas kernels, scatter_rows(): pl.pallas_call(functools.partial(scatter_kernel, first=first), grid=(step...  13.1 us
    pallas_call x1, Pallas kernels, spmm_back(): pl.pallas_call(functools.partial(spmm_back_kernel, n=n), grid_spec=pltpu....  12.6 us
  transfers between devices with their start and end apart: 19, of which 10 were waited for; matrix products, arithmetic and copies ran while one was open for 0% of the time, Pallas kernels for 18%

profile of v5, /device:TPU:1, one launch (start us, length us, event | category | flops | bytes accessed | tf_op | source)
XLA Modules:
  0.0 209.8 jit_solution(13952288842168743629)
XLA Ops:
  0.6 13.3 %gather_rows.1.after_ref = bf16[96,128,128]{2,1,0:T(8,128)(2,1)} custom-call(s32[32,384]{1,0:T(8,128)} %bitcast.5, s32[1,32]{1,0:T(1,128)} %counts_ref.5, bf16[3072,128]{1,0:T(8,128)(2,1)} %table_ref.1), custom_call_target="tpu_custom_call" | custom-call | flops 9663676416 | bytes 4000000 | tf_op jit(solution)/shard_map/gather_rows/pallas_call | solution.py:82
  13.9 9.5 %all-to-all-start = ((bf16[96,128,128]{2,1,0:T(8,128)(2,1)}), bf16[96,128,128]{2,1,0:T(8,128)(2,1)}, u32[]{:S(2)}, u32[]{:S(2)}) async-start(bf16[96,128,128]{2,1,0:T(8,128)(2,1)} %gather_rows.1.after_ref), calls=%async_computation | async-start | bytes 6291456 | tf_op jit(solution)/shard_map/all_to_all | solution.py:645
  23.4 4.9 %prep.1 = (bf16[24,128,128]{2,1,0:T(8,128)(2,1)}, bf16[512,512]{1,0:T(8,128)(2,1)}, bf16[512,512]{1,0:T(8,128)(2,1)}, bf16[2,768,128]{2,1,0:T(8,128)(2,1)}, bf16...) custom-call(s32[1]{0:T(128)} %bitcast.me_ref, bf16[3072,128]{1,0:T(8,128)(2,1)} %feat_ref.1, ...), custom_call_target="tpu_custom_call" | custom-call | flops 10000000000 | bytes 6000000 | tf_op jit(solution)/shard_map/prep/pallas_call | solution.py:135
  28.3 2.8 %collective-permute-start.3 = (bf16[2,768,128]{2,1,0:T(8,128)(2,1)}, bf16[2,768,128]{2,1,0:T(8,128)(2,1)S(1)}, u32[]{:S(2)}, u32[]{:S(2)}) collective-permute-start(bf16[2,768,128]{2,1,0:T(8,128)(2,1)} %get-tuple-element.45), channel_id=1, source_target_pairs={{0,3},{1,0},{2,1},{3,2},{4,7},{5,4},{6,5},{7,6},{8,11},{9,8},{10,9... | collective-permute-start | bytes 1179656 | tf_op jit(solution)/shard_map/ppermute | solution.py:102
  32.3 30.3 %all-to-all-done.refs_2_ = bf16[96,128,128]{2,1,0:T(8,128)(2,1)} async-done(((bf16[96,128,128]{2,1,0:T(8,128)(2,1)}), bf16[96,128,128]{2,1,0:T(8,128)(2,1)}, u32[]{:S(2)}, u32[]{:S(2)}) %all-to-all-start) | async-done | bytes 3145760 | tf_op jit(solution)/shard_map/all_to_all | solution.py:645
  63.8 14.8 %spmm.1 = (bf16[768,128]{1,0:T(8,128)(2,1)S(1)}, bf16[768,128]{1,0:T(8,128)(2,1)S(1)}, bf16[768,128]{1,0:T(8,128)(2,1)S(1)}, bf16[768,128]{1,0:T(8,128)(2,1)S(1)}) custom-call(s32[1]{0:T(128)} %bitcast.me_ref, s32[480]{0:T(512)S(1)} %reshape_squeeze.3.pos_ref, bf16[24,20,128,128]{3,2,1,0:T(8,128)(2,1)} %bitcast.8, bf16[24,128,128]{2,1,0:T(8,128)(2,1)S(1)} %copy-done.3, ...), custom_call_target="tpu_custom_call" | custom-call | flops 4026531840 | bytes 20000000 | tf_op jit(solution)/shard_map/spmm/pallas_call | solution.py:253
  78.6 2.8 %collective-permute-start = (bf16[768,128]{1,0:T(8,128)(2,1)S(1)}, bf16[768,128]{1,0:T(8,128)(2,1)S(1)}, u32[]{:S(2)}, u32[]{:S(2)}) collective-permute-start(bf16[768,128]{1,0:T(8,128)(2,1)S(1)} %get-tuple-element.41), channel_id=1, source_target_pairs={{0,3},{1,0},{2,1},{3,2},{4,7},{5,4},{6,5},{7,6},{8,11},{9,8},{10,9... | collective-permute-start | bytes 589832 | tf_op jit(solution)/shard_map/ppermute | solution.py:102
  82.5 4.0 %collective-permute-done.refs_1_ = bf16[768,128]{1,0:T(8,128)(2,1)S(1)} collective-permute-done((bf16[768,128]{1,0:T(8,128)(2,1)S(1)}, bf16[768,128]{1,0:T(8,128)(2,1)S(1)}, u32[]{:S(2)}, u32[]{:S(2)}) %collective-permute-start) | collective-permute-done | bytes 196640 | tf_op jit(solution)/shard_map/ppermute | solution.py:102
  87.5 4.8 %collective-permute-done.2.refs_3_ = bf16[768,128]{1,0:T(8,128)(2,1)S(1)} collective-permute-done((bf16[768,128]{1,0:T(8,128)(2,1)S(1)}, bf16[768,128]{1,0:T(8,128)(2,1)S(1)}, u32[]{:S(2)}, u32[]{:S(2)}) %collective-permute-start.2) | collective-permute-done | bytes 196640 | tf_op jit(solution)/shard_map/ppermute | solution.py:102
  92.3 4.2 %dense.1 = (bf16[128,768]{1,0:T(8,128)(2,1)S(1)}, bf16[128,768]{1,0:T(8,128)(2,1)S(1)}, bf16[128,768]{1,0:T(8,128)(2,1)S(1)}, bf16[128,768]{1,0:T(8,128)(2,1)S(1...) custom-call(bf16[768,128]{1,0:T(8,128)(2,1)S(1)} %get-tuple-element.40.refs_0_, ...), custom_call_target="tpu_custom_call" | custom-call | flops 1207959552 | bytes 7000000 | tf_op jit(solution)/shard_map/dense/pallas_call | solution.py:306
  96.6 2.6 %collective-permute-start.8 = (bf16[128,768]{1,0:T(8,128)(2,1)S(1)}, bf16[128,768]{1,0:T(8,128)(2,1)S(1)}, u32[]{:S(2)}, u32[]{:S(2)}) collective-permute-start(bf16[128,768]{1,0:T(8,128)(2,1)S(1)} %get-tuple-element.53), channel_id=1, source_target_pairs={{0,3},{1,0},{2,1},{3,2},{4,7},{5,4},{6,5},{7,6},{8,11},{9,8},{10,9... | collective-permute-start | bytes 589832 | tf_op jit(solution)/shard_map/ppermute | solution.py:102
  99.2 8.5 %collective-permute-done.6.refs_2_ = bf16[128,768]{1,0:T(8,128)(2,1)S(1)} collective-permute-done((bf16[128,768]{1,0:T(8,128)(2,1)S(1)}, bf16[128,768]{1,0:T(8,128)(2,1)S(1)}, u32[]{:S(2)}, u32[]{:S(2)}) %collective-permute-start.6) | collective-permute-done | bytes 196640 | tf_op jit(solution)/shard_map/ppermute | solution.py:102
  107.8 12.6 %spmm_back.1 = (f32[24,128,128]{2,1,0:T(8,128)}, bf16[96,128,128]{2,1,0:T(8,128)(2,1)}) custom-call(s32[1]{0:T(128)} %bitcast.me_ref, s32[480]{0:T(512)S(1)} %reshape_squeeze.3.pos_ref, bf16[24,20,128,128]{3,2,1,0:T(8,128)(2,1)} %bitcast.9, bf16[128,768]{1,0:T(8,128)(2,1)S(1)} %get-tuple-element.50.refs_1_, ...), custom_call_target="tpu_custom_call" | custom-call | flops 4026531840 | bytes 22000000 | tf_op jit(solution)/shard_map/spmm_back/pallas_call | solution.py:416
  120.4 8.8 %all-to-all-start.1 = ((bf16[96,128,128]{2,1,0:T(8,128)(2,1)}), bf16[96,128,128]{2,1,0:T(8,128)(2,1)S(1)}, u32[]{:S(2)}, u32[]{:S(2)}) async-start(bf16[96,128,128]{2,1,0:T(8,128)(2,1)} %get-tuple-element.57.after_ref.refs_9_), calls=%async_computation.1 | async-start | bytes 6291456 | tf_op jit(solution)/shard_map/all_to_all | solution.py:654
  129.1 1.9 copy-done
  141.8 3.6 %collective-permute-start.10 = (bf16[2,768,128]{2,1,0:T(8,128)(2,1)S(1)}, bf16[2,768,128]{2,1,0:T(8,128)(2,1)S(1)}, u32[]{:S(2)}, u32[]{:S(2)}) collective-permute-start(bf16[2,768,128]{2,1,0:T(8,128)(2,1)S(1)} %get-tuple-element.60), channel_id=1, source_target_pairs={{0,2},{1,3},{2,0},{3,1},{4,6},{5,7},{6,4},{7,5},{8,10},{9,11},{10,... | collective-permute-start | bytes 1179656 | tf_op jit(solution)/shard_map/ppermute | solution.py:102
  146.9 2.2 %collective-permute-done.12.refs_1_ = bf16[32,32,128]{2,1,0:T(8,128)(2,1)S(1)} collective-permute-done((bf16[32,32,128]{2,1,0:T(8,128)(2,1)S(1)}, bf16[32,32,128]{2,1,0:T(8,128)(2,1)S(1)}, u32[]{:S(2)}, u32[]{:S(2)}) %collective-permute-start.12) | collective-permute-done | bytes 262176 | tf_op jit(solution)/shard_map/ppermute | solution.py:102
  150.0 22.2 %collective-permute-done.13.refs_2_ = bf16[32,32,128]{2,1,0:T(8,128)(2,1)S(1)} collective-permute-done((bf16[32,32,128]{2,1,0:T(8,128)(2,1)S(1)}, bf16[32,32,128]{2,1,0:T(8,128)(2,1)S(1)}, u32[]{:S(2)}, u32[]{:S(2)}) %collective-permute-start.13) | collective-permute-done | bytes 262176 | tf_op jit(solution)/shard_map/ppermute | solution.py:102
  174.2 2.1 %finish.1 = (bf16[3072,128]{1,0:T(8,128)(2,1)}, bf16[3072,128]{1,0:T(8,128)(2,1)}) custom-call(s32[1]{0:T(128)} %bitcast.me_ref, f32[24,128,128]{2,1,0:T(8,128)S(1)} %copy-done.1, bf16[2,768,128]{2,1,0:T(8,128)(2,1)S(1)} %get-tuple-element.58.refs_0_, bf16[2,768,128]{2,1,0:T(8,128)(2,1)S(1)} %collective-permute-done.9.refs_1_, ...), custom_call_target="tpu_custom_call" | custom-call | flops 1000000 | bytes 7000000 | tf_op jit(solution)/shard_map/finish/pallas_call | solution.py:486
  176.3 8.4 %all-to-all-start.2 = ((bf16[32,32,128]{2,1,0:T(8,128)(2,1)}), bf16[32,32,128]{2,1,0:T(8,128)(2,1)S(1)}, u32[]{:S(2)}, u32[]{:S(2)}) async-start(bf16[32,32,128]{2,1,0:T(8,128)(2,1)} %tie.1), calls=%async_computation.2 | async-start | bytes 524288 | tf_op jit(solution)/shard_map/all_to_all | solution.py:661
  184.8 6.0 %scatter_rows.2 = (f32[3072,128]{1,0:T(8,128)S(1)}, f32[8,128]{1,0:T(8,128)S(1)}) custom-call(s32[32,384]{1,0:T(8,128)S(1)} %bitcast.6, s32[1,32]{1,0:T(1,128)S(1)} %copy-done.17, bf16[96,128,128]{2,1,0:T(8,128)(2,1)S(1)} %all-to-all-done.1.val_ref), custom_call_target="tpu_custom_call" | custom-call | flops 19327352832 | bytes 4000000 | tf_op jit(solution)/shard_map/scatter_rows/pallas_call | solution.py:533
  191.9 1.7 all-to-all-done.2.terms_ref
  194.4 5.7 %all-to-all-start.3 = ((bf16[32,32,128]{2,1,0:T(8,128)(2,1)}), bf16[32,32,128]{2,1,0:T(8,128)(2,1)S(1)}, u32[]{:S(2)}, u32[]{:S(2)}) async-start(bf16[32,32,128]{2,1,0:T(8,128)(2,1)} %copy-done.2), calls=%async_computation.3 | async-start | bytes 524288 | tf_op jit(solution)/shard_map/all_to_all | solution.py:663
  201.5 7.1 %scatter_rows.3 = (f32[3072,128]{1,0:T(8,128)}, f32[8,128]{1,0:T(8,128)}) custom-call(s32[32,384]{1,0:T(8,128)S(1)} %bitcast.7, s32[1,32]{1,0:T(1,128)S(1)} %copy-done.17, bf16[96,128,128]{2,1,0:T(8,128)(2,1)S(1)} %all-to-all-done.1.val_ref, f32[3072,128]{1,0:T(8,128)S(1)} %copy-done.27), custom_call_target="tpu_custom_call" | custom-call | flops 19327352832 | bytes 4000000 | tf_op jit(solution)/shard_map/scatter_rows/pallas_call | solution.py:533
  (89 shorter events, 24.2 us)
Async XLA Ops:
  13.9 48.7 %all-to-all-start = ((bf16[96,128,128]{2,1,0:T(8,128)(2,1)}), bf16[96,128,128]{2,1,0:T(8,128)(2,1)}, u32[]{:S(2)}, u32[]{:S(2)}) async-start(bf16[96,128,128]{2,1,0:T(8,128)(2,1)} %gather_rows.1.after_ref), calls=%async_computation | async-start | bytes 6291456 | tf_op jit(solution)/shard_map/all_to_all | solution.py:645
  28.3 53.5 %collective-permute-start.3 = (bf16[2,768,128]{2,1,0:T(8,128)(2,1)}, bf16[2,768,128]{2,1,0:T(8,128)(2,1)S(1)}, u32[]{:S(2)}, u32[]{:S(2)}) collective-permute-start(bf16[2,768,128]{2,1,0:T(8,128)(2,1)} %get-tuple-element.45), channel_id=1, source_target_pairs={{0,3},{1,0},{2,1},{3,2},{4,7},{5,4},{6,5},{7,6},{8,11},{9,8},{10,9... | collective-permute-start | bytes 1179656 | tf_op jit(solution)/shard_map/ppermute | solution.py:102
  31.1 51.4 %collective-permute-start.4 = (bf16[2,768,128]{2,1,0:T(8,128)(2,1)}, bf16[2,768,128]{2,1,0:T(8,128)(2,1)S(1)}, u32[]{:S(2)}, u32[]{:S(2)}) collective-permute-start(bf16[2,768,128]{2,1,0:T(8,128)(2,1)} %get-tuple-element.46), channel_id=1, source_target_pairs={{0,2},{1,3},{2,0},{3,1},{4,6},{5,7},{6,4},{7,5},{8,10},{9,11},{10,... | collective-permute-start | bytes 1179656 | tf_op jit(solution)/shard_map/ppermute | solution.py:102
  31.4 51.0 %collective-permute-start.5 = (bf16[2,768,128]{2,1,0:T(8,128)(2,1)}, bf16[2,768,128]{2,1,0:T(8,128)(2,1)S(1)}, u32[]{:S(2)}, u32[]{:S(2)}) collective-permute-start(bf16[2,768,128]{2,1,0:T(8,128)(2,1)} %get-tuple-element.47), channel_id=1, source_target_pairs={{0,1},{1,2},{2,3},{3,0},{4,5},{5,6},{6,7},{7,4},{8,9},{9,10},{10,1... | collective-permute-start | bytes 1179656 | tf_op jit(solution)/shard_map/ppermute | solution.py:102
  78.6 7.8 %collective-permute-start = (bf16[768,128]{1,0:T(8,128)(2,1)S(1)}, bf16[768,128]{1,0:T(8,128)(2,1)S(1)}, u32[]{:S(2)}, u32[]{:S(2)}) collective-permute-start(bf16[768,128]{1,0:T(8,128)(2,1)S(1)} %get-tuple-element.41), channel_id=1, source_target_pairs={{0,3},{1,0},{2,1},{3,2},{4,7},{5,4},{6,5},{7,6},{8,11},{9,8},{10,9... | collective-permute-start | bytes 589832 | tf_op jit(solution)/shard_map/ppermute | solution.py:102
  81.4 6.1 %collective-permute-start.1 = (bf16[768,128]{1,0:T(8,128)(2,1)S(1)}, bf16[768,128]{1,0:T(8,128)(2,1)S(1)}, u32[]{:S(2)}, u32[]{:S(2)}) collective-permute-start(bf16[768,128]{1,0:T(8,128)(2,1)S(1)} %get-tuple-element.42), channel_id=1, source_target_pairs={{0,2},{1,3},{2,0},{3,1},{4,6},{5,7},{6,4},{7,5},{8,10},{9,11},{10,... | collective-permute-start | bytes 589832 | tf_op jit(solution)/shard_map/ppermute | solution.py:102
  81.8 10.5 %collective-permute-start.2 = (bf16[768,128]{1,0:T(8,128)(2,1)S(1)}, bf16[768,128]{1,0:T(8,128)(2,1)S(1)}, u32[]{:S(2)}, u32[]{:S(2)}) collective-permute-start(bf16[768,128]{1,0:T(8,128)(2,1)S(1)} %get-tuple-element.43), channel_id=1, source_target_pairs={{0,1},{1,2},{2,3},{3,0},{4,5},{5,6},{6,7},{7,4},{8,9},{9,10},{10,1... | collective-permute-start | bytes 589832 | tf_op jit(solution)/shard_map/ppermute | solution.py:102
  82.5 37.9 %copy-start.4 = (bf16[2,768,128]{2,1,0:T(8,128)(2,1)}, bf16[2,768,128]{2,1,0:T(8,128)(2,1)S(1)}, u32[]{:S(2)}) copy-start(bf16[2,768,128]{2,1,0:T(8,128)(2,1)S(1)} %collective-permute-done.4.refs_6_) | copy-start | bytes 1179652
  82.5 37.9 %copy-start.6 = (bf16[2,768,128]{2,1,0:T(8,128)(2,1)}, bf16[2,768,128]{2,1,0:T(8,128)(2,1)S(1)}, u32[]{:S(2)}) copy-start(bf16[2,768,128]{2,1,0:T(8,128)(2,1)S(1)} %collective-permute-done.5.refs_7_) | copy-start | bytes 1179652
  96.5 11.3 %collective-permute-start.6 = (bf16[128,768]{1,0:T(8,128)(2,1)S(1)}, bf16[128,768]{1,0:T(8,128)(2,1)S(1)}, u32[]{:S(2)}, u32[]{:S(2)}) collective-permute-start(bf16[128,768]{1,0:T(8,128)(2,1)S(1)} %get-tuple-element.51), channel_id=1, source_target_pairs={{0,1},{1,2},{2,3},{3,0},{4,5},{5,6},{6,7},{7,4},{8,9},{9,10},{10,1... | collective-permute-start | bytes 589832 | tf_op jit(solution)/shard_map/ppermute | solution.py:102
  96.5 11.3 %collective-permute-start.7 = (bf16[128,768]{1,0:T(8,128)(2,1)S(1)}, bf16[128,768]{1,0:T(8,128)(2,1)S(1)}, u32[]{:S(2)}, u32[]{:S(2)}) collective-permute-start(bf16[128,768]{1,0:T(8,128)(2,1)S(1)} %get-tuple-element.52), channel_id=1, source_target_pairs={{0,2},{1,3},{2,0},{3,1},{4,6},{5,7},{6,4},{7,5},{8,10},{9,11},{10,... | collective-permute-start | bytes 589832 | tf_op jit(solution)/shard_map/ppermute | solution.py:102
  96.6 11.2 %collective-permute-start.8 = (bf16[128,768]{1,0:T(8,128)(2,1)S(1)}, bf16[128,768]{1,0:T(8,128)(2,1)S(1)}, u32[]{:S(2)}, u32[]{:S(2)}) collective-permute-start(bf16[128,768]{1,0:T(8,128)(2,1)S(1)} %get-tuple-element.53), channel_id=1, source_target_pairs={{0,3},{1,0},{2,1},{3,2},{4,7},{5,4},{6,5},{7,6},{8,11},{9,8},{10,9... | collective-permute-start | bytes 589832 | tf_op jit(solution)/shard_map/ppermute | solution.py:102
  120.4 55.9 %all-to-all-start.1 = ((bf16[96,128,128]{2,1,0:T(8,128)(2,1)}), bf16[96,128,128]{2,1,0:T(8,128)(2,1)S(1)}, u32[]{:S(2)}, u32[]{:S(2)}) async-start(bf16[96,128,128]{2,1,0:T(8,128)(2,1)} %get-tuple-element.57.after_ref.refs_9_), calls=%async_computation.1 | async-start | bytes 6291456 | tf_op jit(solution)/shard_map/all_to_all | solution.py:654
  139.9 9.1 %collective-permute-start.12 = (bf16[32,32,128]{2,1,0:T(8,128)(2,1)S(1)}, bf16[32,32,128]{2,1,0:T(8,128)(2,1)S(1)}, u32[]{:S(2)}, u32[]{:S(2)}) collective-permute-start(bf16[32,32,128]{2,1,0:T(8,128)(2,1)S(1)} %get-tuple-element.67), channel_id=1, source_target_pairs={{0,1},{1,2},{2,3},{3,0},{4,5},{5,6},{6,7},{7,4},{8,9},{9,10},{10,1... | collective-permute-start | bytes 786440 | tf_op jit(solution)/shard_map/ppermute | solution.py:102
  140.4 33.8 %copy-start.1 = (f32[24,128,128]{2,1,0:T(8,128)S(1)}, f32[24,128,128]{2,1,0:T(8,128)}, u32[]{:S(2)}) copy-start(f32[24,128,128]{2,1,0:T(8,128)} %get-tuple-element.54.ext_ref) | copy-start | bytes 4718596
  141.6 43.2 %copy-start.16 = (s32[1,32,384]{2,1,0:T(8,128)S(1)}, s32[1,32,384]{2,1,0:T(8,128)}, u32[]{:S(2)}) copy-start(s32[1,32,384]{2,1,0:T(8,128)} %param.16) | copy-start | bytes 147460
  141.6 43.2 %copy-start.17 = (s32[1,32]{1,0:T(1,128)S(1)}, s32[1,32]{1,0:T(1,128)}, u32[]{:S(2)}) copy-start(s32[1,32]{1,0:T(1,128)} %counts_ref.5) | copy-start | bytes 388
  141.6 32.6 %collective-permute-start.9 = (bf16[2,768,128]{2,1,0:T(8,128)(2,1)S(1)}, bf16[2,768,128]{2,1,0:T(8,128)(2,1)S(1)}, u32[]{:S(2)}, u32[]{:S(2)}) collective-permute-start(bf16[2,768,128]{2,1,0:T(8,128)(2,1)S(1)} %get-tuple-element.59), channel_id=1, source_target_pairs={{0,1},{1,2},{2,3},{3,0},{4,5},{5,6},{6,7},{7,4},{8,9},{9,10},{10,1... | collective-permute-start | bytes 1179656 | tf_op jit(solution)/shard_map/ppermute | solution.py:102
  141.8 32.4 %collective-permute-start.10 = (bf16[2,768,128]{2,1,0:T(8,128)(2,1)S(1)}, bf16[2,768,128]{2,1,0:T(8,128)(2,1)S(1)}, u32[]{:S(2)}, u32[]{:S(2)}) collective-permute-start(bf16[2,768,128]{2,1,0:T(8,128)(2,1)S(1)} %get-tuple-element.60), channel_id=1, source_target_pairs={{0,2},{1,3},{2,0},{3,1},{4,6},{5,7},{6,4},{7,5},{8,10},{9,11},{10,... | collective-permute-start | bytes 1179656 | tf_op jit(solution)/shard_map/ppermute | solution.py:102
  145.3 28.8 %collective-permute-start.11 = (bf16[2,768,128]{2,1,0:T(8,128)(2,1)S(1)}, bf16[2,768,128]{2,1,0:T(8,128)(2,1)S(1)}, u32[]{:S(2)}, u32[]{:S(2)}) collective-permute-start(bf16[2,768,128]{2,1,0:T(8,128)(2,1)S(1)} %get-tuple-element.61), channel_id=1, source_target_pairs={{0,3},{1,0},{2,1},{3,2},{4,7},{5,4},{6,5},{7,6},{8,11},{9,8},{10,9... | collective-permute-start | bytes 1179656 | tf_op jit(solution)/shard_map/ppermute | solution.py:102
  146.8 25.3 %collective-permute-start.13 = (bf16[32,32,128]{2,1,0:T(8,128)(2,1)S(1)}, bf16[32,32,128]{2,1,0:T(8,128)(2,1)S(1)}, u32[]{:S(2)}, u32[]{:S(2)}) collective-permute-start(bf16[32,32,128]{2,1,0:T(8,128)(2,1)S(1)} %get-tuple-element.68), channel_id=1, source_target_pairs={{0,2},{1,3},{2,0},{3,1},{4,6},{5,7},{6,4},{7,5},{8,10},{9,11},{10,... | collective-permute-start | bytes 786440 | tf_op jit(solution)/shard_map/ppermute | solution.py:102
  149.0 24.3 %collective-permute-start.14 = (bf16[32,32,128]{2,1,0:T(8,128)(2,1)S(1)}, bf16[32,32,128]{2,1,0:T(8,128)(2,1)S(1)}, u32[]{:S(2)}, u32[]{:S(2)}) collective-permute-start(bf16[32,32,128]{2,1,0:T(8,128)(2,1)S(1)} %get-tuple-element.69), channel_id=1, source_target_pairs={{0,3},{1,0},{2,1},{3,2},{4,7},{5,4},{6,5},{7,6},{8,11},{9,8},{10,9... | collective-permute-start | bytes 786440 | tf_op jit(solution)/shard_map/ppermute | solution.py:102
  176.3 17.3 %all-to-all-start.2 = ((bf16[32,32,128]{2,1,0:T(8,128)(2,1)}), bf16[32,32,128]{2,1,0:T(8,128)(2,1)S(1)}, u32[]{:S(2)}, u32[]{:S(2)}) async-start(bf16[32,32,128]{2,1,0:T(8,128)(2,1)} %tie.1), calls=%async_computation.2 | async-start | bytes 524288 | tf_op jit(solution)/shard_map/all_to_all | solution.py:661
  194.4 14.6 %all-to-all-start.3 = ((bf16[32,32,128]{2,1,0:T(8,128)(2,1)}), bf16[32,32,128]{2,1,0:T(8,128)(2,1)S(1)}, u32[]{:S(2)}, u32[]{:S(2)}) async-start(bf16[32,32,128]{2,1,0:T(8,128)(2,1)} %copy-done.2), calls=%async_computation.3 | async-start | bytes 524288 | tf_op jit(solution)/shard_map/all_to_all | solution.py:663
  (24 other events, 165.0 us)

commit v6 on v2

--- a/solution.py
+++ b/solution.py
@@ -90,7 +90,7 @@
         out_specs=pl.BlockSpec((size * CHUNKS, TILE, TILE), lambda i: (i, 0, 0)),
         out_shape=shape((peers * CHUNKS, TILE, TILE), BF16),
         scratch_shapes=[pltpu.VMEM((rows // LOW * TILE, LOW), BF16)],
-        compiler_params=params(48),
+        compiler_params=params(56),
         cost_estimate=cost(2 * ids.size * rows * cols, 4e6),
         name="gather_rows",
     )(ids, counts, table)
@@ -108,26 +108,10 @@
     return [received[(n - j) % n] for j in range(n)]
 
 
-def prep_kernel(
-    me_ref, feat_ref, up_ref, wn_ref, ws_ref, adj_ref, after_ref, own_ref, wn_out, ws_out, adj_out, *refs
-):
+def prep_kernel(me_ref, feat_ref, up_ref, wn_ref, ws_ref, after_ref, own_ref, wn_out, ws_out, *pieces):
     del after_ref
-    pieces, sems = refs[:-1], refs[-1]
     step = pl.program_id(0)
     n = len(pieces)
-    part = adj_ref.shape[0] // sems.shape[0]
-    copies = [
-        pltpu.make_async_copy(
-            adj_ref.at[pl.ds(k * part, part)], adj_out.at[pl.ds(k * part, part)], sems.at[k]
-        )
-        for k in range(sems.shape[0])
-    ]
-
-    @pl.when(step == 0)
-    def _():
-        for copy in copies:
-            copy.start()
-
     for k in range(own_ref.shape[0]):
         own_ref[k] = turned(feat_ref[k * TILE : (k + 1) * TILE, :]).astype(BF16)
     for j, piece in enumerate(pieces):
@@ -140,64 +124,69 @@
             piece[0] = feat_ref[...]
             piece[1] = up_ref[...]
 
-    @pl.when(step == n - 1)
-    def _():
-        for copy in copies:
-            copy.wait()
-
-
-def prep(me, features, upstream, wn, ws, adj, after, n):
+
+def prep(me, features, upstream, wn, ws, after, n):
     rows, width = features.shape
     share = rows // n
     full = wn.shape[0]
     chunk = pl.BlockSpec((share, width), lambda i, me: (lax.rem(me[0] + i, n), 0))
     weight = pl.BlockSpec((width, full), lambda i, me: (lax.rem(me[0] + i, n), 0))
     placed = pl.BlockSpec((width, full), lambda i, me: (i, 0))
-    own, wn, ws, adj, *pieces = pl.pallas_call(
+    own, wn, ws, *pieces = pl.pallas_call(
         prep_kernel,
         grid_spec=pltpu.PrefetchScalarGridSpec(
             num_scalar_prefetch=1,
             grid=(n,),
-            in_specs=[chunk, chunk, weight, weight] + [pl.BlockSpec(memory_space=pl.ANY)] * 2,
+            in_specs=[chunk, chunk, weight, weight, pl.BlockSpec(memory_space=pl.ANY)],
             out_specs=[
                 pl.BlockSpec(
                     (share // TILE, TILE, TILE), lambda i, me: (lax.rem(me[0] + i, n), 0, 0)
                 ),
                 placed,
                 placed,
-                pl.BlockSpec(memory_space=pl.ANY),
             ]
             + [pl.BlockSpec((2, share, width), lambda i, me: (0, 0, 0))] * n,
-            scratch_shapes=[pltpu.SemaphoreType.DMA((4,))],
         ),
         out_shape=[
-            shape((rows // TILE, TILE, TILE), BF16),
-            shape((full, full), BF16),
-            shape((full, full), BF16),
-            pltpu.VMEM(adj.shape, BF16),
+            pltpu.HBM((rows // TILE, TILE, TILE), BF16),
+            pltpu.HBM((full, full), BF16),
+            pltpu.HBM((full, full), BF16),
         ]
         + [shape((2, share, width), BF16)] * n,
-        compiler_params=params(16),
+        compiler_params=params(56),
         cost_estimate=cost(1e10, 6e6),
         name="prep",
-    )(me, features, upstream, wn, ws, adj, after)
-    return own, wn, ws, adj, pieces
+    )(me, features, upstream, wn, ws, after)
+    return own, wn, ws, pieces
 
 
 BLOCKS = 3
 
 
-def adj_spec(per_row, inner, chunk_of):
-    return pl.BlockSpec(
-        (BLOCKS, per_row, TILE, TILE),
-        lambda i, k, me, pos: (chunk_of(i, me) * inner + k, 0, 0, 0),
+def adj_copies(adj_ref, held, sems, inner, chunk_of):
+    def copy(step):
+        first = (chunk_of(step // inner) * inner + lax.rem(step, inner)) * BLOCKS
+        return pltpu.make_async_copy(
+            adj_ref.at[pl.ds(first, BLOCKS)], held.at[pl.ds(step * BLOCKS, BLOCKS)], sems.at[step]
+        )
+
+    return copy
+
+
+def spmm_kernel(me_ref, pos_ref, *refs, n, start_chunk, extras):
+    adj_ref, parts, outs, (ext, sems, adj, adj_sems) = (
+        refs[0],
+        refs[1 : 3],
+        refs[3 + extras : -4],
+        refs[-4:],
     )
-
-
-def spmm_kernel(me_ref, pos_ref, *refs, n):
-    adj, parts, outs, (ext, sems) = refs[0], refs[1 : -n - 2], refs[-n - 2 : -2], refs[-2:]
     chunk, part = pl.program_id(0), pl.program_id(1)
+    inner = adj_sems.shape[0] // len(outs)
+    step = chunk * inner + part
     per_row = adj.shape[1]
+    copy_of = adj_copies(
+        adj_ref, adj, adj_sems, inner, lambda c: lax.rem(me_ref[0] + start_chunk + c, n)
+    )
 
     @pl.when((chunk == 0) & (part == 0))
     def _():
@@ -213,16 +202,20 @@
                 start, at = start + size, at + 1
         for copy in copies:
             copy.start()
+        copy_of(0).start()
         for copy in copies:
             copy.wait()
-
-    first = (lax.rem(me_ref[0] + chunk, n) * pl.num_programs(1) + part) * BLOCKS
+        for k in range(1, adj_sems.shape[0]):
+            copy_of(k).start()
+
+    copy_of(step).wait()
+    first = (lax.rem(me_ref[0] + start_chunk + chunk, n) * inner + part) * BLOCKS
     done = []
     for r in range(BLOCKS):
         base = (first + r) * per_row
         total = None
         for t in range(0, per_row, 2):
-            left = jnp.concatenate([adj[r, t], adj[r, t + 1]], axis=1)
+            left = jnp.concatenate([adj[step * BLOCKS + r, t], adj[step * BLOCKS + r, t + 1]], axis=1)
             right = jnp.concatenate([ext[pos_ref[base + t]], ext[pos_ref[base + t + 1]]], axis=1)
             term = lax.dot_general(left, right, NT, preferred_element_type=F32)
             total = term if total is None else total + term
@@ -237,29 +230,30 @@
             out[place, :] = done
 
 
-def spmm(me, pos, adj, parts, n):
+def spmm(me, pos, adj, parts, n, start_chunk, count, after):
     row_tiles, per_row = adj.shape[:2]
     inner = row_tiles // n // BLOCKS
     share = row_tiles // n * TILE
     col_tiles = sum(p.shape[0] for p in parts)
     return pl.pallas_call(
-        functools.partial(spmm_kernel, n=n),
+        functools.partial(spmm_kernel, n=n, start_chunk=start_chunk, extras=len(after)),
         grid_spec=pltpu.PrefetchScalarGridSpec(
             num_scalar_prefetch=2,
-            grid=(n, inner),
-            in_specs=[adj_spec(per_row, inner, lambda i, me: lax.rem(me[0] + i, n))]
-            + [pl.BlockSpec(memory_space=pl.ANY)] * len(parts),
-            out_specs=[pl.BlockSpec((share, TILE), lambda i, k, me, pos: (0, 0))] * n,
+            grid=(count, inner),
+            in_specs=[pl.BlockSpec(memory_space=pl.ANY)] * (1 + len(parts) + len(after)),
+            out_specs=[pl.BlockSpec((share, TILE), lambda i, k, me, pos: (0, 0))] * count,
             scratch_shapes=[
                 pltpu.VMEM((col_tiles, TILE, TILE), BF16),
                 pltpu.SemaphoreType.DMA((4 * len(parts),)),
+                pltpu.VMEM((count * inner * BLOCKS, *adj.shape[1:]), BF16),
+                pltpu.SemaphoreType.DMA((count * inner,)),
             ],
         ),
-        out_shape=[shape((share, TILE), BF16)] * n,
-        compiler_params=params(20),
-        cost_estimate=cost(2 * row_tiles * per_row * TILE**3 * 2, 2e7),
+        out_shape=[shape((share, TILE), BF16)] * count,
+        compiler_params=params(52),
+        cost_estimate=cost(2 * count * share * per_row * TILE**2 * 8, 1e7),
         name="spmm",
-    )(me, pos, adj, *parts)
+    )(me, pos, adj, *parts, *after)
 
 
 def joined(refs):
@@ -324,7 +318,7 @@
                     out_ref[at, j] = term[k * rows : (k + 1) * rows, i * TILE : (i + 1) * TILE]
 
 
-def wgrad(me, agg, both, gp, after, dom_count):
+def wgrad(me, agg, both, gp, dom_count):
     n = len(agg)
     rows, width = agg[0].shape
     size = 2 * width * n // dom_count
@@ -332,28 +326,32 @@
     return pl.pallas_call(
         functools.partial(wgrad_kernel, n=n),
         in_specs=[pl.BlockSpec(memory_space=pltpu.SMEM)]
-        + [vmem] * (2 * n + 1)
-        + [pl.BlockSpec(memory_space=pl.ANY)],
+        + [vmem] * (2 * n + 1),
         out_specs=vmem,
         out_shape=shape((dom_count, n, size, TILE), BF16),
         compiler_params=params(24),
         cost_estimate=cost(1e10, 4e6),
         name="wgrad",
-    )(me, *agg, *both, gp, after)
+    )(me, *agg, *both, gp)
 
 
 PIECES = 6
 
 
 def spmm_back_kernel(me_ref, pos_ref, *refs, n):
-    adj, ga = refs[0], refs[1 : 1 + n]
-    local_ref, away_ref, total, left_ref, stage, sems = refs[1 + n :]
+    adj_ref, ga = refs[0], refs[1 : 1 + n]
+    local_ref, away_ref, total, left_ref, stage, sems, adj, adj_sems = refs[1 + n :]
     chunk, part = pl.program_id(0), pl.program_id(1)
+    inner = adj_sems.shape[0] // n
+    step = chunk * inner + part
     per_row = adj.shape[1]
+    copy_of = adj_copies(adj_ref, adj, adj_sems, inner, lambda c: lax.rem(me_ref[0] + n - c, n))
     size = BLOCKS * TILE
 
     @pl.when((chunk == 0) & (part == 0))
     def _():
+        for k in range(adj_sems.shape[0]):
+            copy_of(k).start()
         total[...] = jnp.zeros_like(total)
 
     for s in range(n):
@@ -363,12 +361,13 @@
             for k in range(left_ref.shape[0]):
                 left_ref[k] = ga[s][:, k * size : (k + 1) * size]
 
+    copy_of(step).wait()
     first = (lax.rem(me_ref[0] + n - chunk, n) * pl.num_programs(1) + part) * BLOCKS
     for r in range(BLOCKS):
         base = (first + r) * per_row
         left = left_ref[part, :, r * TILE : (r + 1) * TILE]
         for t in range(0, per_row, 2):
-            right = jnp.concatenate([adj[r, t], adj[r, t + 1]], axis=1)
+            right = jnp.concatenate([adj[step * BLOCKS + r, t], adj[step * BLOCKS + r, t + 1]], axis=1)
             both = jnp.dot(left, right, preferred_element_type=F32)
             total[pos_ref[base + t]] += both[:, :TILE]
             total[pos_ref[base + t + 1]] += both[:, TILE:]
@@ -401,7 +400,7 @@
         grid_spec=pltpu.PrefetchScalarGridSpec(
             num_scalar_prefetch=2,
             grid=(n, inner),
-            in_specs=[adj_spec(per_row, inner, lambda i, me: lax.rem(me[0] + n - i, n))]
+            in_specs=[pl.BlockSpec(memory_space=pl.ANY)]
             + [pl.BlockSpec((TILE, rows), lambda i, k, me, pos: (0, 0))] * n,
             out_specs=[pl.BlockSpec(memory_space=pl.ANY)] * 2,
             scratch_shapes=[
@@ -409,10 +408,12 @@
                 pltpu.VMEM((inner, TILE, BLOCKS * TILE), BF16),
                 pltpu.VMEM((away, TILE, TILE), BF16),
                 pltpu.SemaphoreType.DMA((PIECES + 1,)),
+                pltpu.VMEM(adj.shape, BF16),
+                pltpu.SemaphoreType.DMA((n * inner,)),
             ],
         ),
         out_shape=[pltpu.HBM((own, TILE, TILE), F32), pltpu.HBM((away, TILE, TILE), BF16)],
-        compiler_params=params(24),
+        compiler_params=params(52),
         cost_estimate=cost(2 * row_tiles * per_row * TILE**3 * 2, 2.2e7),
         name="spmm_back",
     )(me, pos, adj, *ga)
@@ -519,7 +520,7 @@
         out_specs=pl.BlockSpec((rows, TILE), lambda i: (0, 0)),
         out_shape=shape((rows, TILE), F32),
         compiler_params=params(40),
-        cost_estimate=cost(2 * ids.size * rows * TILE, 4e6),
+        cost_estimate=cost(8 * ids.size * rows * TILE, 4e6),
         name="scatter_rows",
     )(ids, counts, values)
 
@@ -600,29 +601,30 @@
 
     ids = send_idx[0]
     pos = tile_cols[0].reshape(-1)
+    adj = adj_tiles[0]
 
     packed = gather_rows(ids, counts, stale_features)
     halo = swap(packed)
-    own, wn, ws, adj, pieces = prep(
-        me, features, grad_output, w_neigh, w_self, adj_tiles[0], packed, n
-    )
+    own, wn, ws, pieces = prep(me, features, grad_output, w_neigh, w_self, packed, n)
     both = relative(exchange(pieces))
 
-    agg = relative(exchange(spmm(me, pos, adj, [own, halo], n)))
+    half = n // 2
+    early = spmm(me, pos, adj, [own, halo], n, 1, half, [])
+    rest = spmm(me, pos, adj, [own, halo], n, 1 + half, n - half, [early[-1]])
+    agg = relative(exchange([rest[-1], *early, *rest[:-1]]))
     grad_agg, act, grad_pre = dense(agg, both, wn, ws)
     grad_agg = exchange(grad_agg)
-    terms = swap(wgrad(me, agg, both, grad_pre, grad_agg[1], dom_count))
+    terms = swap(wgrad(me, agg, both, grad_pre, dom_count))
 
     local, away = spmm_back(me, pos, adj, grad_agg, row_tiles, dom_count * CHUNKS)
     returned = swap(away)
     pieces = exchange(late(act, grad_pre, ws, away, n))
     out, grad_input = finish(me, local, pieces)
-
     terms = exchange(sum_terms(terms, away))
-    terms = swap(spread_terms(terms, returned, dom_count))
+
+    terms = swap(spread_terms(terms, returned[0], dom_count))
+    grad_stale = scatter_rows(ids, counts, returned, row_count)
     grad_neigh, grad_self = place_terms(terms, width, n)
-
-    grad_stale = scatter_rows(ids, counts, returned, row_count)
     return (out, grad_input, grad_stale, grad_neigh, grad_self)
 
 

time: 212 us -> 200 us (0.943)
  local copies, waits for them, and re-layouts: 40.1 us -> 7.55 us
  waiting for transfers between devices: 59 us -> 71.4 us
  Pallas kernels: 60.3 us -> 67.5 us
  starting transfers between devices: 50 us -> 52.2 us
    unnamed x63 -> x31, local copies, waits for them, and re-layouts: 40 us -> 6.7 us
    all_to_all x1, waiting for transfers between devices: 13 us -> 30.3 us  [per_device(): halo = swap(packed)]
    pallas_call x1 -> x2, Pallas kernels: 7.63 us -> 14.7 us  [spmm(): pl.pallas_call(functools.partial(spmm_kernel, n=n, start_chunk=start_chun...]
    ppermute x15, waiting for transfers between devices: 36.6 us -> 33.7 us  [exchange(): lax.ppermute(pieces[s], 'rep', [(i, (i + s) % n) for i in range(n)])]
  transfers between devices with their start and end apart: 19 -> 19, of which waited for: 10 -> 8; matrix products, arithmetic and copies ran while one was open for 0% -> 0% of each run, Pallas kernels for 19% -> 23%
where the time goes in v6:
time: 200 us
  waiting for transfers between devices  71.4 us (36%)
  Pallas kernels  67.5 us (34%)
  starting transfers between devices  52.2 us (26%)
  local copies, waits for them, and re-layouts  7.55 us (4%)
    ppermute x15, waiting for transfers between devices, exchange(): lax.ppermute(pieces[s], 'rep', [(i, (i + s) % n) for i in range(n)])  33.7 us
    all_to_all x1, waiting for transfers between devices, per_device(): halo = swap(packed)  30.3 us
    ppermute x15, starting transfers between devices, exchange(): lax.ppermute(pieces[s], 'rep', [(i, (i + s) % n) for i in range(n)])  18.6 us
    pallas_call x2, Pallas kernels, spmm(): pl.pallas_call(functools.partial(spmm_kernel, n=n, start_chunk=start_chun...  14.7 us
    pallas_call x1, Pallas kernels, gather_rows(): pl.pallas_call(gather_kernel, grid=(peers // size,), in_specs=[pl.BlockSp...  13.3 us
    pallas_call x1, Pallas kernels, scatter_rows(): pl.pallas_call(scatter_kernel, grid=(peers // size,), in_specs=[pl.BlockS...  13.1 us
    pallas_call x1, Pallas kernels, spmm_back(): pl.pallas_call(functools.partial(spmm_back_kernel, n=n), grid_spec=pltpu....  10.5 us
    all_to_all x1, starting transfers between devices, per_device(): halo = swap(packed)  9.48 us
  transfers between devices with their start and end apart: 19, of which 8 were waited for; matrix products, arithmetic and copies ran while one was open for 0% of the time, Pallas kernels for 23%

profile of v6, /device:TPU:1, one launch (start us, length us, event | category | flops | bytes accessed | tf_op | source)
XLA Modules:
  0.0 199.6 jit_solution(10039313593158897231)
XLA Ops:
  0.6 13.3 %gather_rows.1.after_ref = bf16[96,128,128]{2,1,0:T(8,128)(2,1)} custom-call(s32[32,384]{1,0:T(8,128)} %bitcast.5, s32[1,32]{1,0:T(1,128)} %counts_ref.3, bf16[3072,128]{1,0:T(8,128)(2,1)} %table_ref.1), custom_call_target="tpu_custom_call" | custom-call | flops 9663676416 | bytes 4000000 | tf_op jit(solution)/shard_map/gather_rows/pallas_call | solution.py:82
  13.9 9.5 %all-to-all-start = ((bf16[96,128,128]{2,1,0:T(8,128)(2,1)}), bf16[96,128,128]{2,1,0:T(8,128)(2,1)}, u32[]{:S(2)}, u32[]{:S(2)}) async-start(bf16[96,128,128]{2,1,0:T(8,128)(2,1)} %gather_rows.1.after_ref), calls=%async_computation | async-start | bytes 6291456 | tf_op jit(solution)/shard_map/all_to_all | solution.py:607
  23.4 4.9 %prep.1 = (bf16[24,128,128]{2,1,0:T(8,128)(2,1)}, bf16[512,512]{1,0:T(8,128)(2,1)}, bf16[512,512]{1,0:T(8,128)(2,1)}, bf16[2,768,128]{2,1,0:T(8,128)(2,1)}, bf16...) custom-call(s32[1]{0:T(128)} %bitcast.me_ref, bf16[3072,128]{1,0:T(8,128)(2,1)} %feat_ref.1, ...), custom_call_target="tpu_custom_call" | custom-call | flops 10000000000 | bytes 6000000 | tf_op jit(solution)/shard_map/prep/pallas_call | solution.py:135
  28.3 2.8 %collective-permute-start.3 = (bf16[2,768,128]{2,1,0:T(8,128)(2,1)}, bf16[2,768,128]{2,1,0:T(8,128)(2,1)S(1)}, u32[]{:S(2)}, u32[]{:S(2)}) collective-permute-start(bf16[2,768,128]{2,1,0:T(8,128)(2,1)} %get-tuple-element.42), channel_id=1, source_target_pairs={{0,3},{1,0},{2,1},{3,2},{4,7},{5,4},{6,5},{7,6},{8,11},{9,8},{10,9... | collective-permute-start | bytes 1179656 | tf_op jit(solution)/shard_map/ppermute | solution.py:102
  32.3 30.3 %all-to-all-done.refs_2_ = bf16[96,128,128]{2,1,0:T(8,128)(2,1)} async-done(((bf16[96,128,128]{2,1,0:T(8,128)(2,1)}), bf16[96,128,128]{2,1,0:T(8,128)(2,1)}, u32[]{:S(2)}, u32[]{:S(2)}) %all-to-all-start) | async-done | bytes 3145760 | tf_op jit(solution)/shard_map/all_to_all | solution.py:607
  63.8 7.3 %spmm.2 = (bf16[768,128]{1,0:T(8,128)(2,1)S(1)}, bf16[768,128]{1,0:T(8,128)(2,1)S(1)}) custom-call(s32[1]{0:T(128)} %bitcast.me_ref, s32[480]{0:T(512)S(1)} %reshape_squeeze.3.pos_ref, bf16[24,20,128,128]{3,2,1,0:T(8,128)(2,1)} %bitcast.7, bf16[24,128,128]{2,1,0:T(8,128)(2,1)S(1)} %copy-done.13, bf16[96,128,128]{2,1,0:T(8,128)(2,1)} %all-to-all-done.refs_2_), custom_call_target="tpu_custom_call" | custom-call | flops 8053063680 | bytes 10000000 | tf_op jit(solution)/shard_map/spmm/pallas_call | solution.py:238
  71.1 7.3 %spmm.3 = (bf16[768,128]{1,0:T(8,128)(2,1)S(1)}, bf16[768,128]{1,0:T(8,128)(2,1)S(1)}) custom-call(s32[1]{0:T(128)} %bitcast.me_ref, s32[480]{0:T(512)S(1)} %reshape_squeeze.3.pos_ref, bf16[24,20,128,128]{3,2,1,0:T(8,128)(2,1)} %bitcast.8, bf16[24,128,128]{2,1,0:T(8,128)(2,1)S(1)} %copy-done.13, bf16[96,128,128]{2,1,0:T(8,128)(2,1)} %all-to-all-done.refs_2_, ...), custom_call_target="tpu_custom_call" | custom-call | flops 8053063680 | bytes 10000000 | tf_op jit(solution)/shard_map/spmm/pallas_call | solution.py:238
  78.5 2.8 %collective-permute-start = (bf16[768,128]{1,0:T(8,128)(2,1)S(1)}, bf16[768,128]{1,0:T(8,128)(2,1)S(1)}, u32[]{:S(2)}, u32[]{:S(2)}) collective-permute-start(bf16[768,128]{1,0:T(8,128)(2,1)S(1)} %get-tuple-element.39), channel_id=1, source_target_pairs={{0,3},{1,0},{2,1},{3,2},{4,7},{5,4},{6,5},{7,6},{8,11},{9,8},{10,9... | collective-permute-start | bytes 589832 | tf_op jit(solution)/shard_map/ppermute | solution.py:102
  83.9 6.0 %collective-permute-done.2.refs_3_ = bf16[768,128]{1,0:T(8,128)(2,1)S(1)} collective-permute-done((bf16[768,128]{1,0:T(8,128)(2,1)S(1)}, bf16[768,128]{1,0:T(8,128)(2,1)S(1)}, u32[]{:S(2)}, u32[]{:S(2)}) %collective-permute-start.2) | collective-permute-done | bytes 196640 | tf_op jit(solution)/shard_map/ppermute | solution.py:102
  89.8 4.2 %dense.1 = (bf16[128,768]{1,0:T(8,128)(2,1)S(1)}, bf16[128,768]{1,0:T(8,128)(2,1)S(1)}, bf16[128,768]{1,0:T(8,128)(2,1)S(1)}, bf16[128,768]{1,0:T(8,128)(2,1)S(1...) custom-call(bf16[768,128]{1,0:T(8,128)(2,1)S(1)} %get-tuple-element.38.refs_0_, ...), custom_call_target="tpu_custom_call" | custom-call | flops 1207959552 | bytes 7000000 | tf_op jit(solution)/shard_map/dense/pallas_call | solution.py:291
  95.1 2.0 %wgrad.1 = bf16[32,4,32,128]{3,2,1,0:T(8,128)(2,1)} custom-call(s32[1]{0:T(128)} %bitcast.me_ref, bf16[768,128]{1,0:T(8,128)(2,1)S(1)} %get-tuple-element.38.refs_0_, bf16[768,128]{1,0:T(8,128)(2,1)S(1)} %collective-permute-done.refs_1_, bf16[768,128]{1,0:T(8,128)(2,1)S(1)} %collective-permute-done.1.refs_2_, ...), custom_call_target="tpu_custom_call" | custom-call | flops 10000000000 | bytes 4000000 | tf_op jit(solution)/shard_map/wgrad/pallas_call | solution.py:326
  97.2 9.1 %all-to-all-start.2 = ((bf16[32,4,32,128]{3,2,1,0:T(8,128)(2,1)}), bf16[32,4,32,128]{3,2,1,0:T(8,128)(2,1)S(1)}, u32[]{:S(2)}, u32[]{:S(2)}) async-start(bf16[32,4,32,128]{3,2,1,0:T(8,128)(2,1)} %wgrad.1), calls=%async_computation.2 | async-start | bytes 2097152 | tf_op jit(solution)/shard_map/all_to_all | solution.py:617
  107.2 1.8 collective-permute-start.8
  109.0 9.0 %collective-permute-done.6.refs_2_ = bf16[128,768]{1,0:T(8,128)(2,1)S(1)} collective-permute-done((bf16[128,768]{1,0:T(8,128)(2,1)S(1)}, bf16[128,768]{1,0:T(8,128)(2,1)S(1)}, u32[]{:S(2)}, u32[]{:S(2)}) %collective-permute-start.6) | collective-permute-done | bytes 196640 | tf_op jit(solution)/shard_map/ppermute | solution.py:102
  118.3 10.5 %spmm_back.1 = (f32[24,128,128]{2,1,0:T(8,128)}, bf16[96,128,128]{2,1,0:T(8,128)(2,1)}) custom-call(s32[1]{0:T(128)} %bitcast.me_ref, s32[480]{0:T(512)S(1)} %reshape_squeeze.3.pos_ref, bf16[24,20,128,128]{3,2,1,0:T(8,128)(2,1)} %bitcast.9, bf16[128,768]{1,0:T(8,128)(2,1)S(1)} %get-tuple-element.47.refs_1_, ...), custom_call_target="tpu_custom_call" | custom-call | flops 4026531840 | bytes 22000000 | tf_op jit(solution)/shard_map/spmm_back/pallas_call | solution.py:398
  129.8 8.7 %all-to-all-start.1 = ((bf16[96,128,128]{2,1,0:T(8,128)(2,1)}), bf16[96,128,128]{2,1,0:T(8,128)(2,1)}, u32[]{:S(2)}, u32[]{:S(2)}) async-start(bf16[96,128,128]{2,1,0:T(8,128)(2,1)} %get-tuple-element.54.after_ref), calls=%async_computation.1 | async-start | bytes 6291456 | tf_op jit(solution)/shard_map/all_to_all | solution.py:620
  143.1 3.2 %collective-permute-start.10 = (bf16[2,768,128]{2,1,0:T(8,128)(2,1)S(1)}, bf16[2,768,128]{2,1,0:T(8,128)(2,1)S(1)}, u32[]{:S(2)}, u32[]{:S(2)}) collective-permute-start(bf16[2,768,128]{2,1,0:T(8,128)(2,1)S(1)} %get-tuple-element.57), channel_id=1, source_target_pairs={{0,2},{1,3},{2,0},{3,1},{4,6},{5,7},{6,4},{7,5},{8,10},{9,11},{10,... | collective-permute-start | bytes 1179656 | tf_op jit(solution)/shard_map/ppermute | solution.py:102
  146.3 8.5 %collective-permute-done.9.refs_1_ = bf16[2,768,128]{2,1,0:T(8,128)(2,1)S(1)} collective-permute-done((bf16[2,768,128]{2,1,0:T(8,128)(2,1)S(1)}, bf16[2,768,128]{2,1,0:T(8,128)(2,1)S(1)}, u32[]{:S(2)}, u32[]{:S(2)}) %collective-permute-start.9) | collective-permute-done | bytes 393248 | tf_op jit(solution)/shard_map/ppermute | solution.py:102
  154.8 9.0 %collective-permute-done.10.refs_2_ = bf16[2,768,128]{2,1,0:T(8,128)(2,1)S(1)} collective-permute-done((bf16[2,768,128]{2,1,0:T(8,128)(2,1)S(1)}, bf16[2,768,128]{2,1,0:T(8,128)(2,1)S(1)}, u32[]{:S(2)}, u32[]{:S(2)}) %collective-permute-start.10) | collective-permute-done | bytes 393248 | tf_op jit(solution)/shard_map/ppermute | solution.py:102
  163.8 2.1 %finish.1 = (bf16[3072,128]{1,0:T(8,128)(2,1)}, bf16[3072,128]{1,0:T(8,128)(2,1)}) custom-call(s32[1]{0:T(128)} %bitcast.me_ref, f32[24,128,128]{2,1,0:T(8,128)S(1)} %copy-done.3, bf16[2,768,128]{2,1,0:T(8,128)(2,1)S(1)} %get-tuple-element.55.refs_0_, bf16[2,768,128]{2,1,0:T(8,128)(2,1)S(1)} %collective-permute-done.9.refs_1_, ...), custom_call_target="tpu_custom_call" | custom-call | flops 1000000 | bytes 7000000 | tf_op jit(solution)/shard_map/finish/pallas_call | solution.py:468
  166.7 3.6 %collective-permute-start.13 = (bf16[32,128]{1,0:T(8,128)(2,1)S(1)}, bf16[32,128]{1,0:T(8,128)(2,1)S(1)}, u32[]{:S(2)}, u32[]{:S(2)}) collective-permute-start(bf16[32,128]{1,0:T(8,128)(2,1)S(1)} %get-tuple-element.63), channel_id=1, source_target_pairs={{0,2},{1,3},{2,0},{3,1},{4,6},{5,7},{6,4},{7,5},{8,10},{9,11},{10,... | collective-permute-start | bytes 24584 | tf_op jit(solution)/shard_map/ppermute | solution.py:102
  170.3 7.4 %all-to-all-done.1.val_ref = bf16[96,128,128]{2,1,0:T(8,128)(2,1)} async-done(((bf16[96,128,128]{2,1,0:T(8,128)(2,1)}), bf16[96,128,128]{2,1,0:T(8,128)(2,1)}, u32[]{:S(2)}, u32[]{:S(2)}) %all-to-all-start.1) | async-done | bytes 3145760 | tf_op jit(solution)/shard_map/all_to_all | solution.py:620
  179.2 6.4 %all-to-all-start.3 = ((bf16[32,32,128]{2,1,0:T(8,128)(2,1)}), bf16[32,32,128]{2,1,0:T(8,128)(2,1)S(1)}, u32[]{:S(2)}, u32[]{:S(2)}) async-start(bf16[32,32,128]{2,1,0:T(8,128)(2,1)} %spread_terms.1), calls=%async_computation.3 | async-start | bytes 524288 | tf_op jit(solution)/shard_map/all_to_all | solution.py:625
  185.6 13.1 %scatter_rows.1 = f32[3072,128]{1,0:T(8,128)} custom-call(s32[32,384]{1,0:T(8,128)S(1)} %bitcast.6, s32[1,32]{1,0:T(1,128)S(1)} %copy-done.5, bf16[96,128,128]{2,1,0:T(8,128)(2,1)} %all-to-all-done.1.val_ref), custom_call_target="tpu_custom_call" | custom-call | flops 38654705664 | bytes 4000000 | tf_op jit(solution)/shard_map/scatter_rows/pallas_call | solution.py:512
  (60 shorter events, 16.1 us)
Async XLA Ops:
  13.9 48.7 %all-to-all-start = ((bf16[96,128,128]{2,1,0:T(8,128)(2,1)}), bf16[96,128,128]{2,1,0:T(8,128)(2,1)}, u32[]{:S(2)}, u32[]{:S(2)}) async-start(bf16[96,128,128]{2,1,0:T(8,128)(2,1)} %gather_rows.1.after_ref), calls=%async_computation | async-start | bytes 6291456 | tf_op jit(solution)/shard_map/all_to_all | solution.py:607
  28.3 53.0 %collective-permute-start.3 = (bf16[2,768,128]{2,1,0:T(8,128)(2,1)}, bf16[2,768,128]{2,1,0:T(8,128)(2,1)S(1)}, u32[]{:S(2)}, u32[]{:S(2)}) collective-permute-start(bf16[2,768,128]{2,1,0:T(8,128)(2,1)} %get-tuple-element.42), channel_id=1, source_target_pairs={{0,3},{1,0},{2,1},{3,2},{4,7},{5,4},{6,5},{7,6},{8,11},{9,8},{10,9... | collective-permute-start | bytes 1179656 | tf_op jit(solution)/shard_map/ppermute | solution.py:102
  31.1 51.8 %collective-permute-start.4 = (bf16[2,768,128]{2,1,0:T(8,128)(2,1)}, bf16[2,768,128]{2,1,0:T(8,128)(2,1)S(1)}, u32[]{:S(2)}, u32[]{:S(2)}) collective-permute-start(bf16[2,768,128]{2,1,0:T(8,128)(2,1)} %get-tuple-element.43), channel_id=1, source_target_pairs={{0,2},{1,3},{2,0},{3,1},{4,6},{5,7},{6,4},{7,5},{8,10},{9,11},{10,... | collective-permute-start | bytes 1179656 | tf_op jit(solution)/shard_map/ppermute | solution.py:102
  31.4 51.5 %collective-permute-start.5 = (bf16[2,768,128]{2,1,0:T(8,128)(2,1)}, bf16[2,768,128]{2,1,0:T(8,128)(2,1)S(1)}, u32[]{:S(2)}, u32[]{:S(2)}) collective-permute-start(bf16[2,768,128]{2,1,0:T(8,128)(2,1)} %get-tuple-element.44), channel_id=1, source_target_pairs={{0,1},{1,2},{2,3},{3,0},{4,5},{5,6},{6,7},{7,4},{8,9},{9,10},{10,1... | collective-permute-start | bytes 1179656 | tf_op jit(solution)/shard_map/ppermute | solution.py:102
  71.1 18.7 %copy-start.9 = (bf16[512,512]{1,0:T(8,128)(2,1)S(1)}, bf16[512,512]{1,0:T(8,128)(2,1)}, u32[]{:S(2)}) copy-start(bf16[512,512]{1,0:T(8,128)(2,1)} %get-tuple-element.46.refs_9_.ws_ref) | copy-start | bytes 1572868
  78.5 5.4 %collective-permute-start = (bf16[768,128]{1,0:T(8,128)(2,1)S(1)}, bf16[768,128]{1,0:T(8,128)(2,1)S(1)}, u32[]{:S(2)}, u32[]{:S(2)}) collective-permute-start(bf16[768,128]{1,0:T(8,128)(2,1)S(1)} %get-tuple-element.39), channel_id=1, source_target_pairs={{0,3},{1,0},{2,1},{3,2},{4,7},{5,4},{6,5},{7,6},{8,11},{9,8},{10,9... | collective-permute-start | bytes 589832 | tf_op jit(solution)/shard_map/ppermute | solution.py:102
  81.3 8.6 %collective-permute-start.2 = (bf16[768,128]{1,0:T(8,128)(2,1)S(1)}, bf16[768,128]{1,0:T(8,128)(2,1)S(1)}, u32[]{:S(2)}, u32[]{:S(2)}) collective-permute-start(bf16[768,128]{1,0:T(8,128)(2,1)S(1)} %get-tuple-element.40), channel_id=1, source_target_pairs={{0,1},{1,2},{2,3},{3,0},{4,5},{5,6},{6,7},{7,4},{8,9},{9,10},{10,1... | collective-permute-start | bytes 589832 | tf_op jit(solution)/shard_map/ppermute | solution.py:102
  81.3 8.6 %collective-permute-start.1 = (bf16[768,128]{1,0:T(8,128)(2,1)S(1)}, bf16[768,128]{1,0:T(8,128)(2,1)S(1)}, u32[]{:S(2)}, u32[]{:S(2)}) collective-permute-start(bf16[768,128]{1,0:T(8,128)(2,1)S(1)} %get-tuple-element.37.refs_3_), channel_id=1, source_target_pairs={{0,2},{1,3},{2,0},{3,1},{4,6},{5,7},{6,4},{7,5},{8,10},{9,11},{10,... | collective-permute-start | bytes 589832 | tf_op jit(solution)/shard_map/ppermute | solution.py:102
  97.2 31.6 %all-to-all-start.2 = ((bf16[32,4,32,128]{3,2,1,0:T(8,128)(2,1)}), bf16[32,4,32,128]{3,2,1,0:T(8,128)(2,1)S(1)}, u32[]{:S(2)}, u32[]{:S(2)}) async-start(bf16[32,4,32,128]{3,2,1,0:T(8,128)(2,1)} %wgrad.1), calls=%async_computation.2 | async-start | bytes 2097152 | tf_op jit(solution)/shard_map/all_to_all | solution.py:617
  106.2 11.8 %collective-permute-start.6 = (bf16[128,768]{1,0:T(8,128)(2,1)S(1)}, bf16[128,768]{1,0:T(8,128)(2,1)S(1)}, u32[]{:S(2)}, u32[]{:S(2)}) collective-permute-start(bf16[128,768]{1,0:T(8,128)(2,1)S(1)} %get-tuple-element.48), channel_id=1, source_target_pairs={{0,1},{1,2},{2,3},{3,0},{4,5},{5,6},{6,7},{7,4},{8,9},{9,10},{10,1... | collective-permute-start | bytes 589832 | tf_op jit(solution)/shard_map/ppermute | solution.py:102
  106.3 11.7 %collective-permute-start.7 = (bf16[128,768]{1,0:T(8,128)(2,1)S(1)}, bf16[128,768]{1,0:T(8,128)(2,1)S(1)}, u32[]{:S(2)}, u32[]{:S(2)}) collective-permute-start(bf16[128,768]{1,0:T(8,128)(2,1)S(1)} %get-tuple-element.49), channel_id=1, source_target_pairs={{0,2},{1,3},{2,0},{3,1},{4,6},{5,7},{6,4},{7,5},{8,10},{9,11},{10,... | collective-permute-start | bytes 589832 | tf_op jit(solution)/shard_map/ppermute | solution.py:102
  107.2 11.1 %collective-permute-start.8 = (bf16[128,768]{1,0:T(8,128)(2,1)S(1)}, bf16[128,768]{1,0:T(8,128)(2,1)S(1)}, u32[]{:S(2)}, u32[]{:S(2)}) collective-permute-start(bf16[128,768]{1,0:T(8,128)(2,1)S(1)} %get-tuple-element.50), channel_id=1, source_target_pairs={{0,3},{1,0},{2,1},{3,2},{4,7},{5,4},{6,5},{7,6},{8,11},{9,8},{10,9... | collective-permute-start | bytes 589832 | tf_op jit(solution)/shard_map/ppermute | solution.py:102
  129.8 47.9 %all-to-all-start.1 = ((bf16[96,128,128]{2,1,0:T(8,128)(2,1)}), bf16[96,128,128]{2,1,0:T(8,128)(2,1)}, u32[]{:S(2)}, u32[]{:S(2)}) async-start(bf16[96,128,128]{2,1,0:T(8,128)(2,1)} %get-tuple-element.54.after_ref), calls=%async_computation.1 | async-start | bytes 6291456 | tf_op jit(solution)/shard_map/all_to_all | solution.py:620
  141.8 22.0 %copy-start.3 = (f32[24,128,128]{2,1,0:T(8,128)S(1)}, f32[24,128,128]{2,1,0:T(8,128)}, u32[]{:S(2)}) copy-start(f32[24,128,128]{2,1,0:T(8,128)} %get-tuple-element.51.ext_ref) | copy-start | bytes 4718596
  143.0 22.9 %copy-start.2 = (bf16[32,4,32,128]{3,2,1,0:T(8,128)(2,1)S(1)}, bf16[32,4,32,128]{3,2,1,0:T(8,128)(2,1)}, u32[]{:S(2)}) copy-start(bf16[32,4,32,128]{3,2,1,0:T(8,128)(2,1)} %copy-done.1) | copy-start | bytes 3145732
  143.0 11.8 %collective-permute-start.9 = (bf16[2,768,128]{2,1,0:T(8,128)(2,1)S(1)}, bf16[2,768,128]{2,1,0:T(8,128)(2,1)S(1)}, u32[]{:S(2)}, u32[]{:S(2)}) collective-permute-start(bf16[2,768,128]{2,1,0:T(8,128)(2,1)S(1)} %get-tuple-element.56), channel_id=1, source_target_pairs={{0,1},{1,2},{2,3},{3,0},{4,5},{5,6},{6,7},{7,4},{8,9},{9,10},{10,1... | collective-permute-start | bytes 1179656 | tf_op jit(solution)/shard_map/ppermute | solution.py:102
  143.1 20.7 %collective-permute-start.10 = (bf16[2,768,128]{2,1,0:T(8,128)(2,1)S(1)}, bf16[2,768,128]{2,1,0:T(8,128)(2,1)S(1)}, u32[]{:S(2)}, u32[]{:S(2)}) collective-permute-start(bf16[2,768,128]{2,1,0:T(8,128)(2,1)S(1)} %get-tuple-element.57), channel_id=1, source_target_pairs={{0,2},{1,3},{2,0},{3,1},{4,6},{5,7},{6,4},{7,5},{8,10},{9,11},{10,... | collective-permute-start | bytes 1179656 | tf_op jit(solution)/shard_map/ppermute | solution.py:102
  146.3 17.5 %collective-permute-start.11 = (bf16[2,768,128]{2,1,0:T(8,128)(2,1)S(1)}, bf16[2,768,128]{2,1,0:T(8,128)(2,1)S(1)}, u32[]{:S(2)}, u32[]{:S(2)}) collective-permute-start(bf16[2,768,128]{2,1,0:T(8,128)(2,1)S(1)} %get-tuple-element.58), channel_id=1, source_target_pairs={{0,3},{1,0},{2,1},{3,2},{4,7},{5,4},{6,5},{7,6},{8,11},{9,8},{10,9... | collective-permute-start | bytes 1179656 | tf_op jit(solution)/shard_map/ppermute | solution.py:102
  165.9 19.7 %copy-start.4 = (s32[1,32,384]{2,1,0:T(8,128)S(1)}, s32[1,32,384]{2,1,0:T(8,128)}, u32[]{:S(2)}) copy-start(s32[1,32,384]{2,1,0:T(8,128)} %param.16) | copy-start | bytes 147460
  165.9 19.7 %copy-start.5 = (s32[1,32]{1,0:T(1,128)S(1)}, s32[1,32]{1,0:T(1,128)}, u32[]{:S(2)}) copy-start(s32[1,32]{1,0:T(1,128)} %counts_ref.3) | copy-start | bytes 388
  166.1 12.4 %collective-permute-start.12 = (bf16[32,128]{1,0:T(8,128)(2,1)S(1)}, bf16[32,128]{1,0:T(8,128)(2,1)S(1)}, u32[]{:S(2)}, u32[]{:S(2)}) collective-permute-start(bf16[32,128]{1,0:T(8,128)(2,1)S(1)} %get-tuple-element.62), channel_id=1, source_target_pairs={{0,1},{1,2},{2,3},{3,0},{4,5},{5,6},{6,7},{7,4},{8,9},{9,10},{10,1... | collective-permute-start | bytes 24584 | tf_op jit(solution)/shard_map/ppermute | solution.py:102
  166.7 11.8 %collective-permute-start.13 = (bf16[32,128]{1,0:T(8,128)(2,1)S(1)}, bf16[32,128]{1,0:T(8,128)(2,1)S(1)}, u32[]{:S(2)}, u32[]{:S(2)}) collective-permute-start(bf16[32,128]{1,0:T(8,128)(2,1)S(1)} %get-tuple-element.63), channel_id=1, source_target_pairs={{0,2},{1,3},{2,0},{3,1},{4,6},{5,7},{6,4},{7,5},{8,10},{9,11},{10,... | collective-permute-start | bytes 24584 | tf_op jit(solution)/shard_map/ppermute | solution.py:102
  170.3 8.2 %collective-permute-start.14 = (bf16[32,128]{1,0:T(8,128)(2,1)S(1)}, bf16[32,128]{1,0:T(8,128)(2,1)S(1)}, u32[]{:S(2)}, u32[]{:S(2)}) collective-permute-start(bf16[32,128]{1,0:T(8,128)(2,1)S(1)} %get-tuple-element.64), channel_id=1, source_target_pairs={{0,3},{1,0},{2,1},{3,2},{4,7},{5,4},{6,5},{7,6},{8,11},{9,8},{10,9... | collective-permute-start | bytes 24584 | tf_op jit(solution)/shard_map/ppermute | solution.py:102
  179.2 19.5 %all-to-all-start.3 = ((bf16[32,32,128]{2,1,0:T(8,128)(2,1)}), bf16[32,32,128]{2,1,0:T(8,128)(2,1)S(1)}, u32[]{:S(2)}, u32[]{:S(2)}) async-start(bf16[32,32,128]{2,1,0:T(8,128)(2,1)} %spread_terms.1), calls=%async_computation.3 | async-start | bytes 524288 | tf_op jit(solution)/shard_map/all_to_all | solution.py:625
  (10 other events, 61.5 us)

commit v7 on v6

--- a/solution.py
+++ b/solution.py
@@ -10,7 +10,8 @@
 TILE = 128
 B = 384
 CHUNKS = B // TILE
-LOW = 512
+LOW_BITS = 9
+LOW = 1 << LOW_BITS
 F32 = jnp.float32
 BF16 = jnp.bfloat16
 NT = (((1,), (1,)), ((), ()))
@@ -44,8 +45,9 @@
 
 
 def low_onehot(ids):
-    spot = lax.broadcasted_iota(jnp.int32, (LOW, ids.shape[1]), 0)
-    return jnp.where(spot == (ids & (LOW - 1)), 1.0, 0.0).astype(BF16)
+    spot = lax.broadcasted_iota(jnp.int32, (LOW, ids.shape[1]), 0).astype(jnp.int16)
+    low = jnp.broadcast_to((ids & (LOW - 1)).astype(jnp.int16), spot.shape)
+    return jnp.where(spot == low, jnp.ones(spot.shape, BF16), jnp.zeros(spot.shape, BF16))
 
 
 def in_group(ids, g):
@@ -250,7 +252,7 @@
             ],
         ),
         out_shape=[shape((share, TILE), BF16)] * count,
-        compiler_params=params(52),
+        compiler_params=params(56),
         cost_estimate=cost(2 * count * share * per_row * TILE**2 * 8, 1e7),
         name="spmm",
     )(me, pos, adj, *parts, *after)
@@ -260,12 +262,14 @@
     return jnp.concatenate([ref[...] for ref in refs], axis=1)
 
 
-def dense_kernel(*refs, n):
+def dense_kernel(me_ref, *refs, n):
     agg, both, (wn_ref, ws_ref), rest = refs[:n], refs[n : 2 * n], refs[2 * n : 2 * n + 2], refs[2 * n + 2 :]
-    ga, (act_ref, gp_ref) = rest[:n], rest[n:]
+    ga, (act_ref, gp_ref, terms_ref, total) = rest[:n], rest[n:]
+    step = pl.program_id(0)
     wn = wn_ref[...]
+    feat = [ref[0] for ref in both]
     v = jnp.dot(joined(agg), wn, preferred_element_type=F32) + jnp.dot(
-        joined([ref.at[0] for ref in both]), ws_ref[...], preferred_element_type=F32
+        jnp.concatenate(feat, axis=1), ws_ref[...], preferred_element_type=F32
     )
     root = 0.7978845608028654
     square = v * v
@@ -280,59 +284,55 @@
     for q in range(n):
         ga[q][...] = back[q * width : (q + 1) * width, :]
 
-
-def dense(agg, both, wn, ws):
+    @pl.when(step == 0)
+    def _():
+        total[...] = jnp.zeros_like(total)
+
+    for j in range(n):
+        for kind, left in enumerate((agg[j][...], feat[j])):
+            total[2 * j + kind] += lax.dot_general(left, gp, TN, preferred_element_type=F32)
+
+    @pl.when(step == pl.num_programs(0) - 1)
+    def _():
+        rows = terms_ref.shape[2]
+        for j in range(n):
+            for kind in range(2):
+                term = total[2 * j + kind].astype(BF16)
+                for i in range(n):
+                    q = lax.rem(me_ref[0] + i, n)
+                    for k in range(width // rows):
+                        at = (kind * (width // rows) + k) * n + q
+                        terms_ref[at, j] = term[k * rows : (k + 1) * rows, i * width : (i + 1) * width]
+
+
+def dense(me, agg, both, wn, ws, dom_count):
     n = len(agg)
     rows, width = agg[0].shape
     full = n * width
     size = 256
-    weight = pl.BlockSpec((full, full), lambda i: (0, 0))
-    whole = pl.BlockSpec((size, full), lambda i: (i, 0))
+    piece = (dom_count, n, 2 * width * n // dom_count, width)
+    weight = pl.BlockSpec((full, full), lambda i, me: (0, 0))
+    whole = pl.BlockSpec((size, full), lambda i, me: (i, 0))
     results = pl.pallas_call(
         functools.partial(dense_kernel, n=n),
-        grid=(rows // size,),
-        in_specs=[pl.BlockSpec((size, width), lambda i: (i, 0))] * n
-        + [pl.BlockSpec((2, size, width), lambda i: (0, i, 0))] * n
-        + [weight, weight],
-        out_specs=[pl.BlockSpec((width, size), lambda i: (0, i))] * n + [whole, whole],
-        out_shape=[shape((width, rows), BF16)] * n + [pltpu.HBM((rows, full), BF16)] * 2,
+        grid_spec=pltpu.PrefetchScalarGridSpec(
+            num_scalar_prefetch=1,
+            grid=(rows // size,),
+            in_specs=[pl.BlockSpec((size, width), lambda i, me: (i, 0))] * n
+            + [pl.BlockSpec((2, size, width), lambda i, me: (0, i, 0))] * n
+            + [weight, weight],
+            out_specs=[pl.BlockSpec((width, size), lambda i, me: (0, i))] * n
+            + [whole, whole, pl.BlockSpec(piece, lambda i, me: (0, 0, 0, 0))],
+            scratch_shapes=[pltpu.VMEM((2 * n, width, full), F32)],
+        ),
+        out_shape=[shape((width, rows), BF16)] * n
+        + [pltpu.HBM((rows, full), BF16)] * 2
+        + [pltpu.HBM(piece, BF16)],
         compiler_params=params(24),
-        cost_estimate=cost(6 * rows * full * full, 7e6, rows * full),
+        cost_estimate=cost(10 * rows * full * full, 9e6, rows * full),
         name="dense",
-    )(*agg, *both, wn, ws)
-    return results[:n], results[n], results[n + 1]
-
-
-def wgrad_kernel(me_ref, *refs, n):
-    agg, both, gp_ref, out_ref = refs[:n], refs[n : 2 * n], refs[2 * n], refs[-1]
-    gp = gp_ref[...]
-    rows = out_ref.shape[2]
-    width = agg[0].shape[1]
-    for j in range(n):
-        for kind, left in enumerate((agg[j][...], both[j][0])):
-            term = lax.dot_general(left, gp, TN, preferred_element_type=F32).astype(BF16)
-            for i in range(n):
-                q = lax.rem(me_ref[0] + i, n)
-                for k in range(width // rows):
-                    at = (kind * (width // rows) + k) * n + q
-                    out_ref[at, j] = term[k * rows : (k + 1) * rows, i * TILE : (i + 1) * TILE]
-
-
-def wgrad(me, agg, both, gp, dom_count):
-    n = len(agg)
-    rows, width = agg[0].shape
-    size = 2 * width * n // dom_count
-    vmem = pl.BlockSpec(memory_space=pltpu.VMEM)
-    return pl.pallas_call(
-        functools.partial(wgrad_kernel, n=n),
-        in_specs=[pl.BlockSpec(memory_space=pltpu.SMEM)]
-        + [vmem] * (2 * n + 1),
-        out_specs=vmem,
-        out_shape=shape((dom_count, n, size, TILE), BF16),
-        compiler_params=params(24),
-        cost_estimate=cost(1e10, 4e6),
-        name="wgrad",
-    )(me, *agg, *both, gp)
+    )(me, *agg, *both, wn, ws)
+    return results[:n], *results[n:]
 
 
 PIECES = 6
@@ -497,8 +497,9 @@
         onehot = low_onehot(ids)
         values = jnp.concatenate([val_ref[p * CHUNKS + k] for k in range(2 * CHUNKS)], axis=1)
         zero = jnp.zeros_like(values)
+        which = jnp.broadcast_to((ids >> LOW_BITS).astype(jnp.int16), values.shape)
         for g in range(0, groups, 2):
-            pair = [jnp.where(in_group(ids, k), values, zero) for k in (g, g + 1)]
+            pair = [jnp.where(which == jnp.int16(k), values, zero) for k in (g, g + 1)]
             both = lax.dot_general(
                 onehot, jnp.concatenate(pair, axis=0), NT, preferred_element_type=F32
             )
@@ -546,24 +547,41 @@
 
 
 def spread_kernel(*refs):
-    terms, out_ref = refs[:-2], refs[-1]
+    terms, out_ref = refs[:-1], refs[-1]
     total = terms[0][...].astype(F32)
     for term in terms[1:]:
         total = total + term[...].astype(F32)
     out_ref[...] = jnp.broadcast_to(total.astype(BF16)[None], out_ref.shape)
 
 
-def spread_terms(terms, after, dom_count):
+def spread_terms(terms, dom_count):
+    vmem = pl.BlockSpec(memory_space=pltpu.VMEM)
     return pl.pallas_call(
         spread_kernel,
-        in_specs=[pl.BlockSpec(memory_space=pltpu.VMEM)] * len(terms)
-        + [pl.BlockSpec(memory_space=pl.ANY)],
-        out_specs=pl.BlockSpec(memory_space=pltpu.VMEM),
+        in_specs=[vmem] * len(terms),
+        out_specs=vmem,
         out_shape=shape((dom_count, *terms[0].shape), BF16),
         compiler_params=params(8),
         cost_estimate=cost(1e5, 3e5),
         name="spread_terms",
-    )(*terms, after)
+    )(*terms)
+
+
+def tie_kernel(value_ref, after_ref, out_ref):
+    del value_ref, after_ref, out_ref
+
+
+def tie(value, after):
+    anywhere = pl.BlockSpec(memory_space=pl.ANY)
+    return pl.pallas_call(
+        tie_kernel,
+        in_specs=[anywhere, anywhere],
+        out_specs=anywhere,
+        out_shape=shape(value.shape, value.dtype),
+        input_output_aliases={0: 0},
+        compiler_params=params(8),
+        name="tie",
+    )(value, after)
 
 
 def place_kernel(terms_ref, *outs):
@@ -608,13 +626,10 @@
     own, wn, ws, pieces = prep(me, features, grad_output, w_neigh, w_self, packed, n)
     both = relative(exchange(pieces))
 
-    half = n // 2
-    early = spmm(me, pos, adj, [own, halo], n, 1, half, [])
-    rest = spmm(me, pos, adj, [own, halo], n, 1 + half, n - half, [early[-1]])
-    agg = relative(exchange([rest[-1], *early, *rest[:-1]]))
-    grad_agg, act, grad_pre = dense(agg, both, wn, ws)
+    agg = relative(exchange(spmm(me, pos, adj, [own, halo], n, 0, n, [])))
+    grad_agg, act, grad_pre, terms = dense(me, agg, both, wn, ws, dom_count)
     grad_agg = exchange(grad_agg)
-    terms = swap(wgrad(me, agg, both, grad_pre, dom_count))
+    terms = swap(terms)
 
     local, away = spmm_back(me, pos, adj, grad_agg, row_tiles, dom_count * CHUNKS)
     returned = swap(away)
@@ -622,7 +637,7 @@
     out, grad_input = finish(me, local, pieces)
     terms = exchange(sum_terms(terms, away))
 
-    terms = swap(spread_terms(terms, returned[0], dom_count))
+    terms = swap(tie(spread_terms(terms, dom_count), returned[0, :16]))
     grad_stale = scatter_rows(ids, counts, returned, row_count)
     grad_neigh, grad_self = place_terms(terms, width, n)
     return (out, grad_input, grad_stale, grad_neigh, grad_self)

time: 200 us -> 195 us (0.975)
  starting transfers between devices: 52.2 us -> 48.4 us
  Pallas kernels: 67.5 us -> 64 us
  waiting for transfers between devices: 71.4 us -> 74.5 us
    pallas_call x2 -> x1, Pallas kernels: 14.7 us -> 10.8 us  [spmm(): pl.pallas_call(functools.partial(spmm_kernel, n=n, start_chunk=start_chun...]
    all_to_all x1, waiting for transfers between devices: 7.42 us -> 10.9 us  [per_device(): returned = swap(away)]
  transfers between devices with their start and end apart: 19 -> 19, of which waited for: 8 -> 9; matrix products, arithmetic and copies ran while one was open for 0% -> 0% of each run, Pallas kernels for 23% -> 22%
where the time goes in v7:
time: 195 us; the launch traced here: 194 us
  waiting for transfers between devices  74.5 us (38%)
  Pallas kernels  64 us (33%)
  starting transfers between devices  48.4 us (25%)
  local copies, waits for them, and re-layouts  6.72 us (3%)
    ppermute x15, waiting for transfers between devices, exchange(): lax.ppermute(pieces[s], 'rep', [(i, (i + s) % n) for i in range(n)])  33.9 us
    all_to_all x1, waiting for transfers between devices, per_device(): halo = swap(packed)  29.7 us
    ppermute x15, starting transfers between devices, exchange(): lax.ppermute(pieces[s], 'rep', [(i, (i + s) % n) for i in range(n)])  16.7 us
    pallas_call x1, Pallas kernels, gather_rows(): pl.pallas_call(gather_kernel, grid=(peers // size,), in_specs=[pl.BlockSp...  13.1 us
    pallas_call x1, Pallas kernels, scatter_rows(): pl.pallas_call(scatter_kernel, grid=(peers // size,), in_specs=[pl.BlockS...  13.1 us
    all_to_all x1, waiting for transfers between devices, per_device(): returned = swap(away)  10.9 us
    pallas_call x1, Pallas kernels, spmm(): pl.pallas_call(functools.partial(spmm_kernel, n=n, start_chunk=start_chun...  10.8 us
    pallas_call x1, Pallas kernels, spmm_back(): pl.pallas_call(functools.partial(spmm_back_kernel, n=n), grid_spec=pltpu....  10.5 us
  transfers between devices with their start and end apart: 19, of which 9 were waited for; matrix products, arithmetic and copies ran while one was open for 0% of the time, Pallas kernels for 22%

profile of v7, /device:TPU:1, one launch (start us, length us, event | category | flops | bytes accessed | tf_op | source)
XLA Modules:
  0.0 194.4 jit_solution(17425102450194143230)
XLA Ops:
  0.6 13.1 %gather_rows.1.after_ref = bf16[96,128,128]{2,1,0:T(8,128)(2,1)} custom-call(s32[32,384]{1,0:T(8,128)} %bitcast.5, s32[1,32]{1,0:T(1,128)} %counts_ref.3, bf16[3072,128]{1,0:T(8,128)(2,1)} %table_ref.1), custom_call_target="tpu_custom_call" | custom-call | flops 9663676416 | bytes 4000000 | tf_op jit(solution)/shard_map/gather_rows/pallas_call | solution.py:84
  13.7 9.5 %all-to-all-start = ((bf16[96,128,128]{2,1,0:T(8,128)(2,1)}), bf16[96,128,128]{2,1,0:T(8,128)(2,1)}, u32[]{:S(2)}, u32[]{:S(2)}) async-start(bf16[96,128,128]{2,1,0:T(8,128)(2,1)} %gather_rows.1.after_ref), calls=%async_computation | async-start | bytes 6291456 | tf_op jit(solution)/shard_map/all_to_all | solution.py:625
  23.2 4.8 %prep.1 = (bf16[24,128,128]{2,1,0:T(8,128)(2,1)}, bf16[512,512]{1,0:T(8,128)(2,1)}, bf16[512,512]{1,0:T(8,128)(2,1)}, bf16[2,768,128]{2,1,0:T(8,128)(2,1)}, bf16...) custom-call(s32[1]{0:T(128)} %bitcast.me_ref, bf16[3072,128]{1,0:T(8,128)(2,1)} %feat_ref.1, ...), custom_call_target="tpu_custom_call" | custom-call | flops 10000000000 | bytes 6000000 | tf_op jit(solution)/shard_map/prep/pallas_call | solution.py:137
  28.1 2.8 %collective-permute-start.3 = (bf16[2,768,128]{2,1,0:T(8,128)(2,1)}, bf16[2,768,128]{2,1,0:T(8,128)(2,1)S(1)}, u32[]{:S(2)}, u32[]{:S(2)}) collective-permute-start(bf16[2,768,128]{2,1,0:T(8,128)(2,1)} %get-tuple-element.43), channel_id=1, source_target_pairs={{0,3},{1,0},{2,1},{3,2},{4,7},{5,4},{6,5},{7,6},{8,11},{9,8},{10,9... | collective-permute-start | bytes 1179656 | tf_op jit(solution)/shard_map/ppermute | solution.py:104
  32.7 29.7 %all-to-all-done.refs_2_ = bf16[96,128,128]{2,1,0:T(8,128)(2,1)} async-done(((bf16[96,128,128]{2,1,0:T(8,128)(2,1)}), bf16[96,128,128]{2,1,0:T(8,128)(2,1)}, u32[]{:S(2)}, u32[]{:S(2)}) %all-to-all-start) | async-done | bytes 3145760 | tf_op jit(solution)/shard_map/all_to_all | solution.py:625
  62.4 10.8 %spmm.1 = (bf16[768,128]{1,0:T(8,128)(2,1)}, bf16[768,128]{1,0:T(8,128)(2,1)}, bf16[768,128]{1,0:T(8,128)(2,1)}, bf16[768,128]{1,0:T(8,128)(2,1)}) custom-call(s32[1]{0:T(128)} %bitcast.me_ref, s32[480]{0:T(512)} %reshape_squeeze.3.pos_ref, bf16[24,20,128,128]{3,2,1,0:T(8,128)(2,1)} %bitcast.7, bf16[24,128,128]{2,1,0:T(8,128)(2,1)} %get-tuple-element.37.refs_1_, ...), custom_call_target="tpu_custom_call" | custom-call | flops 16106127360 | bytes 10000000 | tf_op jit(solution)/shard_map/spmm/pallas_call | solution.py:240
  73.2 2.8 %collective-permute-start = (bf16[768,128]{1,0:T(8,128)(2,1)}, bf16[768,128]{1,0:T(8,128)(2,1)S(1)}, u32[]{:S(2)}, u32[]{:S(2)}) collective-permute-start(bf16[768,128]{1,0:T(8,128)(2,1)} %get-tuple-element.39), channel_id=1, source_target_pairs={{0,3},{1,0},{2,1},{3,2},{4,7},{5,4},{6,5},{7,6},{8,11},{9,8},{10,9... | collective-permute-start | bytes 589832 | tf_op jit(solution)/shard_map/ppermute | solution.py:104
  77.1 4.3 %collective-permute-done.refs_1_ = bf16[768,128]{1,0:T(8,128)(2,1)S(1)} collective-permute-done((bf16[768,128]{1,0:T(8,128)(2,1)}, bf16[768,128]{1,0:T(8,128)(2,1)S(1)}, u32[]{:S(2)}, u32[]{:S(2)}) %collective-permute-start) | collective-permute-done | bytes 196640 | tf_op jit(solution)/shard_map/ppermute | solution.py:104
  82.3 4.8 %collective-permute-done.2.refs_3_ = bf16[768,128]{1,0:T(8,128)(2,1)S(1)} collective-permute-done((bf16[768,128]{1,0:T(8,128)(2,1)}, bf16[768,128]{1,0:T(8,128)(2,1)S(1)}, u32[]{:S(2)}, u32[]{:S(2)}) %collective-permute-start.2) | collective-permute-done | bytes 196640 | tf_op jit(solution)/shard_map/ppermute | solution.py:104
  88.1 6.8 %dense.1 = (bf16[128,768]{1,0:T(8,128)(2,1)S(1)}, bf16[128,768]{1,0:T(8,128)(2,1)S(1)}, bf16[128,768]{1,0:T(8,128)(2,1)S(1)}, bf16[128,768]{1,0:T(8,128)(2,1)S(1...) custom-call(s32[1]{0:T(128)} %bitcast.me_ref, ...), custom_call_target="tpu_custom_call" | custom-call | flops 2013265920 | bytes 9000000 | tf_op jit(solution)/shard_map/dense/pallas_call | solution.py:316
  94.8 7.1 %all-to-all-start.2 = ((bf16[32,4,32,128]{3,2,1,0:T(8,128)(2,1)}), bf16[32,4,32,128]{3,2,1,0:T(8,128)(2,1)S(1)}, u32[]{:S(2)}, u32[]{:S(2)}) async-start(bf16[32,4,32,128]{3,2,1,0:T(8,128)(2,1)} %get-tuple-element.62), calls=%async_computation.2 | async-start | bytes 2097152 | tf_op jit(solution)/shard_map/all_to_all | solution.py:632
  102.0 1.4 collective-permute-start.7
  103.5 1.2 collective-permute-start.8
  104.7 9.0 %collective-permute-done.6.refs_2_ = bf16[128,768]{1,0:T(8,128)(2,1)S(1)} collective-permute-done((bf16[128,768]{1,0:T(8,128)(2,1)S(1)}, bf16[128,768]{1,0:T(8,128)(2,1)S(1)}, u32[]{:S(2)}, u32[]{:S(2)}) %collective-permute-start.6) | collective-permute-done | bytes 196640 | tf_op jit(solution)/shard_map/ppermute | solution.py:104
  114.0 10.5 %spmm_back.1 = (f32[24,128,128]{2,1,0:T(8,128)}, bf16[96,128,128]{2,1,0:T(8,128)(2,1)}) custom-call(s32[1]{0:T(128)} %bitcast.me_ref, s32[480]{0:T(512)S(1)} %copy-done.4, bf16[24,20,128,128]{3,2,1,0:T(8,128)(2,1)} %bitcast.8, bf16[128,768]{1,0:T(8,128)(2,1)S(1)} %get-tuple-element.48.refs_1_, bf16[128,768]{1,0:T(8,128)(2,1)S(1)} %collective-permute-done.6.refs_2_, ...), custom_call_target="tpu_custom_call" | custom-call | flops 4026531840 | bytes 22000000 | tf_op jit(solution)/shard_map/spmm_back/pallas_call | solution.py:398
  125.5 8.7 %all-to-all-start.1 = ((bf16[96,128,128]{2,1,0:T(8,128)(2,1)}), bf16[96,128,128]{2,1,0:T(8,128)(2,1)}, u32[]{:S(2)}, u32[]{:S(2)}) async-start(bf16[96,128,128]{2,1,0:T(8,128)(2,1)} %get-tuple-element.55.after_ref), calls=%async_computation.1 | async-start | bytes 6291456 | tf_op jit(solution)/shard_map/all_to_all | solution.py:635
  139.0 3.2 %collective-permute-start.10 = (bf16[2,768,128]{2,1,0:T(8,128)(2,1)S(1)}, bf16[2,768,128]{2,1,0:T(8,128)(2,1)S(1)}, u32[]{:S(2)}, u32[]{:S(2)}) collective-permute-start(bf16[2,768,128]{2,1,0:T(8,128)(2,1)S(1)} %get-tuple-element.58), channel_id=1, source_target_pairs={{0,2},{1,3},{2,0},{3,1},{4,6},{5,7},{6,4},{7,5},{8,10},{9,11},{10,... | collective-permute-start | bytes 1179656 | tf_op jit(solution)/shard_map/ppermute | solution.py:104
  142.4 1.5 collective-permute-start.12
  144.4 6.3 %collective-permute-done.9.refs_1_ = bf16[2,768,128]{2,1,0:T(8,128)(2,1)S(1)} collective-permute-done((bf16[2,768,128]{2,1,0:T(8,128)(2,1)S(1)}, bf16[2,768,128]{2,1,0:T(8,128)(2,1)S(1)}, u32[]{:S(2)}, u32[]{:S(2)}) %collective-permute-start.9) | collective-permute-done | bytes 393248 | tf_op jit(solution)/shard_map/ppermute | solution.py:104
  151.5 8.1 %collective-permute-done.10.refs_2_ = bf16[2,768,128]{2,1,0:T(8,128)(2,1)S(1)} collective-permute-done((bf16[2,768,128]{2,1,0:T(8,128)(2,1)S(1)}, bf16[2,768,128]{2,1,0:T(8,128)(2,1)S(1)}, u32[]{:S(2)}, u32[]{:S(2)}) %collective-permute-start.10) | collective-permute-done | bytes 393248 | tf_op jit(solution)/shard_map/ppermute | solution.py:104
  159.7 2.1 %finish.1 = (bf16[3072,128]{1,0:T(8,128)(2,1)}, bf16[3072,128]{1,0:T(8,128)(2,1)}) custom-call(s32[1]{0:T(128)} %bitcast.me_ref, f32[24,128,128]{2,1,0:T(8,128)S(1)} %copy-done.3, bf16[2,768,128]{2,1,0:T(8,128)(2,1)S(1)} %get-tuple-element.56.refs_0_, bf16[2,768,128]{2,1,0:T(8,128)(2,1)S(1)} %collective-permute-done.9.refs_1_, ...), custom_call_target="tpu_custom_call" | custom-call | flops 1000000 | bytes 7000000 | tf_op jit(solution)/shard_map/finish/pallas_call | solution.py:468
  162.5 10.9 %all-to-all-done.1.val_ref = bf16[96,128,128]{2,1,0:T(8,128)(2,1)} async-done(((bf16[96,128,128]{2,1,0:T(8,128)(2,1)}), bf16[96,128,128]{2,1,0:T(8,128)(2,1)}, u32[]{:S(2)}, u32[]{:S(2)}) %all-to-all-start.1) | async-done | bytes 3145760 | tf_op jit(solution)/shard_map/all_to_all | solution.py:635
  174.1 6.4 %all-to-all-start.3 = ((bf16[32,32,128]{2,1,0:T(8,128)(2,1)}), bf16[32,32,128]{2,1,0:T(8,128)(2,1)S(1)}, u32[]{:S(2)}, u32[]{:S(2)}) async-start(bf16[32,32,128]{2,1,0:T(8,128)(2,1)} %tie.1), calls=%async_computation.3 | async-start | bytes 524288 | tf_op jit(solution)/shard_map/all_to_all | solution.py:640
  180.5 13.1 %scatter_rows.1 = f32[3072,128]{1,0:T(8,128)} custom-call(s32[32,384]{1,0:T(8,128)S(1)} %bitcast.6, s32[1,32]{1,0:T(1,128)S(1)} %copy-done.6, bf16[96,128,128]{2,1,0:T(8,128)(2,1)} %all-to-all-done.1.val_ref), custom_call_target="tpu_custom_call" | custom-call | flops 38654705664 | bytes 4000000 | tf_op jit(solution)/shard_map/scatter_rows/pallas_call | solution.py:513
  (59 shorter events, 14.6 us)
Async XLA Ops:
  13.7 48.7 %all-to-all-start = ((bf16[96,128,128]{2,1,0:T(8,128)(2,1)}), bf16[96,128,128]{2,1,0:T(8,128)(2,1)}, u32[]{:S(2)}, u32[]{:S(2)}) async-start(bf16[96,128,128]{2,1,0:T(8,128)(2,1)} %gather_rows.1.after_ref), calls=%async_computation | async-start | bytes 6291456 | tf_op jit(solution)/shard_map/all_to_all | solution.py:625
  28.1 48.3 %collective-permute-start.3 = (bf16[2,768,128]{2,1,0:T(8,128)(2,1)}, bf16[2,768,128]{2,1,0:T(8,128)(2,1)S(1)}, u32[]{:S(2)}, u32[]{:S(2)}) collective-permute-start(bf16[2,768,128]{2,1,0:T(8,128)(2,1)} %get-tuple-element.43), channel_id=1, source_target_pairs={{0,3},{1,0},{2,1},{3,2},{4,7},{5,4},{6,5},{7,6},{8,11},{9,8},{10,9... | collective-permute-start | bytes 1179656 | tf_op jit(solution)/shard_map/ppermute | solution.py:104
  30.9 46.2 %collective-permute-start.4 = (bf16[2,768,128]{2,1,0:T(8,128)(2,1)}, bf16[2,768,128]{2,1,0:T(8,128)(2,1)S(1)}, u32[]{:S(2)}, u32[]{:S(2)}) collective-permute-start(bf16[2,768,128]{2,1,0:T(8,128)(2,1)} %get-tuple-element.44), channel_id=1, source_target_pairs={{0,2},{1,3},{2,0},{3,1},{4,6},{5,7},{6,4},{7,5},{8,10},{9,11},{10,... | collective-permute-start | bytes 1179656 | tf_op jit(solution)/shard_map/ppermute | solution.py:104
  31.2 45.8 %collective-permute-start.5 = (bf16[2,768,128]{2,1,0:T(8,128)(2,1)}, bf16[2,768,128]{2,1,0:T(8,128)(2,1)S(1)}, u32[]{:S(2)}, u32[]{:S(2)}) collective-permute-start(bf16[2,768,128]{2,1,0:T(8,128)(2,1)} %get-tuple-element.45), channel_id=1, source_target_pairs={{0,1},{1,2},{2,3},{3,0},{4,5},{5,6},{6,7},{7,4},{8,9},{9,10},{10,1... | collective-permute-start | bytes 1179656 | tf_op jit(solution)/shard_map/ppermute | solution.py:104
  62.4 24.7 %copy-start.11 = (bf16[512,512]{1,0:T(8,128)(2,1)S(1)}, bf16[512,512]{1,0:T(8,128)(2,1)}, u32[]{:S(2)}) copy-start(bf16[512,512]{1,0:T(8,128)(2,1)} %get-tuple-element.46.refs_8_) | copy-start | bytes 1572868
  62.4 24.7 %copy-start.12 = (bf16[2,768,128]{2,1,0:T(8,128)(2,1)S(1)}, bf16[2,768,128]{2,1,0:T(8,128)(2,1)}, u32[]{:S(2)}) copy-start(bf16[2,768,128]{2,1,0:T(8,128)(2,1)} %get-tuple-element.42.refs_4_) | copy-start | bytes 1179652
  73.2 8.2 %collective-permute-start = (bf16[768,128]{1,0:T(8,128)(2,1)}, bf16[768,128]{1,0:T(8,128)(2,1)S(1)}, u32[]{:S(2)}, u32[]{:S(2)}) collective-permute-start(bf16[768,128]{1,0:T(8,128)(2,1)} %get-tuple-element.39), channel_id=1, source_target_pairs={{0,3},{1,0},{2,1},{3,2},{4,7},{5,4},{6,5},{7,6},{8,11},{9,8},{10,9... | collective-permute-start | bytes 589832 | tf_op jit(solution)/shard_map/ppermute | solution.py:104
  76.0 6.3 %collective-permute-start.1 = (bf16[768,128]{1,0:T(8,128)(2,1)}, bf16[768,128]{1,0:T(8,128)(2,1)S(1)}, u32[]{:S(2)}, u32[]{:S(2)}) collective-permute-start(bf16[768,128]{1,0:T(8,128)(2,1)} %get-tuple-element.40), channel_id=1, source_target_pairs={{0,2},{1,3},{2,0},{3,1},{4,6},{5,7},{6,4},{7,5},{8,10},{9,11},{10,... | collective-permute-start | bytes 589832 | tf_op jit(solution)/shard_map/ppermute | solution.py:104
  76.4 10.7 %collective-permute-start.2 = (bf16[768,128]{1,0:T(8,128)(2,1)}, bf16[768,128]{1,0:T(8,128)(2,1)S(1)}, u32[]{:S(2)}, u32[]{:S(2)}) collective-permute-start(bf16[768,128]{1,0:T(8,128)(2,1)} %get-tuple-element.41), channel_id=1, source_target_pairs={{0,1},{1,2},{2,3},{3,0},{4,5},{5,6},{6,7},{7,4},{8,9},{9,10},{10,1... | collective-permute-start | bytes 589832 | tf_op jit(solution)/shard_map/ppermute | solution.py:104
  88.1 26.0 %copy-start.4 = (s32[480]{0:T(512)S(1)}, s32[480]{0:T(512)}, u32[]{:S(2)}) copy-start(s32[480]{0:T(512)} %reshape_squeeze.3.pos_ref) | copy-start | bytes 5764
  94.8 29.7 %all-to-all-start.2 = ((bf16[32,4,32,128]{3,2,1,0:T(8,128)(2,1)}), bf16[32,4,32,128]{3,2,1,0:T(8,128)(2,1)S(1)}, u32[]{:S(2)}, u32[]{:S(2)}) async-start(bf16[32,4,32,128]{3,2,1,0:T(8,128)(2,1)} %get-tuple-element.62), calls=%async_computation.2 | async-start | bytes 2097152 | tf_op jit(solution)/shard_map/all_to_all | solution.py:632
  102.0 11.8 %collective-permute-start.6 = (bf16[128,768]{1,0:T(8,128)(2,1)S(1)}, bf16[128,768]{1,0:T(8,128)(2,1)S(1)}, u32[]{:S(2)}, u32[]{:S(2)}) collective-permute-start(bf16[128,768]{1,0:T(8,128)(2,1)S(1)} %get-tuple-element.49), channel_id=1, source_target_pairs={{0,1},{1,2},{2,3},{3,0},{4,5},{5,6},{6,7},{7,4},{8,9},{9,10},{10,1... | collective-permute-start | bytes 589832 | tf_op jit(solution)/shard_map/ppermute | solution.py:104
  102.0 11.7 %collective-permute-start.7 = (bf16[128,768]{1,0:T(8,128)(2,1)S(1)}, bf16[128,768]{1,0:T(8,128)(2,1)S(1)}, u32[]{:S(2)}, u32[]{:S(2)}) collective-permute-start(bf16[128,768]{1,0:T(8,128)(2,1)S(1)} %get-tuple-element.50), channel_id=1, source_target_pairs={{0,2},{1,3},{2,0},{3,1},{4,6},{5,7},{6,4},{7,5},{8,10},{9,11},{10,... | collective-permute-start | bytes 589832 | tf_op jit(solution)/shard_map/ppermute | solution.py:104
  103.5 10.6 %collective-permute-start.8 = (bf16[128,768]{1,0:T(8,128)(2,1)S(1)}, bf16[128,768]{1,0:T(8,128)(2,1)S(1)}, u32[]{:S(2)}, u32[]{:S(2)}) collective-permute-start(bf16[128,768]{1,0:T(8,128)(2,1)S(1)} %get-tuple-element.51), channel_id=1, source_target_pairs={{0,3},{1,0},{2,1},{3,2},{4,7},{5,4},{6,5},{7,6},{8,11},{9,8},{10,9... | collective-permute-start | bytes 589832 | tf_op jit(solution)/shard_map/ppermute | solution.py:104
  125.5 47.9 %all-to-all-start.1 = ((bf16[96,128,128]{2,1,0:T(8,128)(2,1)}), bf16[96,128,128]{2,1,0:T(8,128)(2,1)}, u32[]{:S(2)}, u32[]{:S(2)}) async-start(bf16[96,128,128]{2,1,0:T(8,128)(2,1)} %get-tuple-element.55.after_ref), calls=%async_computation.1 | async-start | bytes 6291456 | tf_op jit(solution)/shard_map/all_to_all | solution.py:635
  138.7 12.0 %collective-permute-start.9 = (bf16[2,768,128]{2,1,0:T(8,128)(2,1)S(1)}, bf16[2,768,128]{2,1,0:T(8,128)(2,1)S(1)}, u32[]{:S(2)}, u32[]{:S(2)}) collective-permute-start(bf16[2,768,128]{2,1,0:T(8,128)(2,1)S(1)} %get-tuple-element.57), channel_id=1, source_target_pairs={{0,1},{1,2},{2,3},{3,0},{4,5},{5,6},{6,7},{7,4},{8,9},{9,10},{10,1... | collective-permute-start | bytes 1179656 | tf_op jit(solution)/shard_map/ppermute | solution.py:104
  139.0 20.7 %collective-permute-start.10 = (bf16[2,768,128]{2,1,0:T(8,128)(2,1)S(1)}, bf16[2,768,128]{2,1,0:T(8,128)(2,1)S(1)}, u32[]{:S(2)}, u32[]{:S(2)}) collective-permute-start(bf16[2,768,128]{2,1,0:T(8,128)(2,1)S(1)} %get-tuple-element.58), channel_id=1, source_target_pairs={{0,2},{1,3},{2,0},{3,1},{4,6},{5,7},{6,4},{7,5},{8,10},{9,11},{10,... | collective-permute-start | bytes 1179656 | tf_op jit(solution)/shard_map/ppermute | solution.py:104
  142.2 17.5 %collective-permute-start.11 = (bf16[2,768,128]{2,1,0:T(8,128)(2,1)S(1)}, bf16[2,768,128]{2,1,0:T(8,128)(2,1)S(1)}, u32[]{:S(2)}, u32[]{:S(2)}) collective-permute-start(bf16[2,768,128]{2,1,0:T(8,128)(2,1)S(1)} %get-tuple-element.59), channel_id=1, source_target_pairs={{0,3},{1,0},{2,1},{3,2},{4,7},{5,4},{6,5},{7,6},{8,11},{9,8},{10,9... | collective-permute-start | bytes 1179656 | tf_op jit(solution)/shard_map/ppermute | solution.py:104
  142.4 38.1 %copy-start.5 = (s32[1,32,384]{2,1,0:T(8,128)S(1)}, s32[1,32,384]{2,1,0:T(8,128)}, u32[]{:S(2)}) copy-start(s32[1,32,384]{2,1,0:T(8,128)} %param.16) | copy-start | bytes 147460
  142.4 38.1 %copy-start.6 = (s32[1,32]{1,0:T(1,128)S(1)}, s32[1,32]{1,0:T(1,128)}, u32[]{:S(2)}) copy-start(s32[1,32]{1,0:T(1,128)} %counts_ref.3) | copy-start | bytes 388
  142.4 19.4 %collective-permute-start.12 = (bf16[32,128]{1,0:T(8,128)(2,1)S(1)}, bf16[32,128]{1,0:T(8,128)(2,1)S(1)}, u32[]{:S(2)}, u32[]{:S(2)}) collective-permute-start(bf16[32,128]{1,0:T(8,128)(2,1)S(1)} %get-tuple-element.64), channel_id=1, source_target_pairs={{0,1},{1,2},{2,3},{3,0},{4,5},{5,6},{6,7},{7,4},{8,9},{9,10},{10,1... | collective-permute-start | bytes 24584 | tf_op jit(solution)/shard_map/ppermute | solution.py:104
  143.9 17.9 %collective-permute-start.13 = (bf16[32,128]{1,0:T(8,128)(2,1)S(1)}, bf16[32,128]{1,0:T(8,128)(2,1)S(1)}, u32[]{:S(2)}, u32[]{:S(2)}) collective-permute-start(bf16[32,128]{1,0:T(8,128)(2,1)S(1)} %get-tuple-element.65), channel_id=1, source_target_pairs={{0,2},{1,3},{2,0},{3,1},{4,6},{5,7},{6,4},{7,5},{8,10},{9,11},{10,... | collective-permute-start | bytes 24584 | tf_op jit(solution)/shard_map/ppermute | solution.py:104
  150.7 11.1 %collective-permute-start.14 = (bf16[32,128]{1,0:T(8,128)(2,1)S(1)}, bf16[32,128]{1,0:T(8,128)(2,1)S(1)}, u32[]{:S(2)}, u32[]{:S(2)}) collective-permute-start(bf16[32,128]{1,0:T(8,128)(2,1)S(1)} %get-tuple-element.66), channel_id=1, source_target_pairs={{0,3},{1,0},{2,1},{3,2},{4,7},{5,4},{6,5},{7,6},{8,11},{9,8},{10,9... | collective-permute-start | bytes 24584 | tf_op jit(solution)/shard_map/ppermute | solution.py:104
  174.1 19.5 %all-to-all-start.3 = ((bf16[32,32,128]{2,1,0:T(8,128)(2,1)}), bf16[32,32,128]{2,1,0:T(8,128)(2,1)S(1)}, u32[]{:S(2)}, u32[]{:S(2)}) async-start(bf16[32,32,128]{2,1,0:T(8,128)(2,1)} %tie.1), calls=%async_computation.3 | async-start | bytes 524288 | tf_op jit(solution)/shard_map/all_to_all | solution.py:640
  (10 other events, 73.0 us)

commit v8 on v7

--- a/solution.py
+++ b/solution.py
@@ -163,6 +163,7 @@
 
 
 BLOCKS = 3
+AHEAD = 4
 
 
 def adj_copies(adj_ref, held, sems, inner, chunk_of):
@@ -207,8 +208,12 @@
         copy_of(0).start()
         for copy in copies:
             copy.wait()
-        for k in range(1, adj_sems.shape[0]):
+        for k in range(1, AHEAD):
             copy_of(k).start()
+
+    @pl.when(step + AHEAD < adj_sems.shape[0])
+    def _():
+        copy_of(step + AHEAD).start()
 
     copy_of(step).wait()
     first = (lax.rem(me_ref[0] + start_chunk + chunk, n) * inner + part) * BLOCKS
@@ -284,13 +289,21 @@
     for q in range(n):
         ga[q][...] = back[q * width : (q + 1) * width, :]
 
+    terms = [
+        lax.dot_general(left, gp, TN, preferred_element_type=F32)
+        for j in range(n)
+        for left in (agg[j][...], feat[j])
+    ]
+
     @pl.when(step == 0)
     def _():
-        total[...] = jnp.zeros_like(total)
-
-    for j in range(n):
-        for kind, left in enumerate((agg[j][...], feat[j])):
-            total[2 * j + kind] += lax.dot_general(left, gp, TN, preferred_element_type=F32)
+        for k, term in enumerate(terms):
+            total[k] = term
+
+    @pl.when(step > 0)
+    def _():
+        for k, term in enumerate(terms):
+            total[k] += term
 
     @pl.when(step == pl.num_programs(0) - 1)
     def _():
@@ -350,9 +363,11 @@
 
     @pl.when((chunk == 0) & (part == 0))
     def _():
-        for k in range(adj_sems.shape[0]):
+        copy_of(0).start()
+        copy_of(1).start()
+        total[...] = jnp.zeros_like(total)
+        for k in range(2, AHEAD):
             copy_of(k).start()
-        total[...] = jnp.zeros_like(total)
 
     for s in range(n):
 
@@ -360,6 +375,10 @@
         def _():
             for k in range(left_ref.shape[0]):
                 left_ref[k] = ga[s][:, k * size : (k + 1) * size]
+
+    @pl.when(step + AHEAD < adj_sems.shape[0])
+    def _():
+        copy_of(step + AHEAD).start()
 
     copy_of(step).wait()
     first = (lax.rem(me_ref[0] + n - chunk, n) * pl.num_programs(1) + part) * BLOCKS
@@ -637,7 +656,7 @@
     out, grad_input = finish(me, local, pieces)
     terms = exchange(sum_terms(terms, away))
 
-    terms = swap(tie(spread_terms(terms, dom_count), returned[0, :16]))
+    terms = swap(tie(spread_terms(terms, dom_count), returned))
     grad_stale = scatter_rows(ids, counts, returned, row_count)
     grad_neigh, grad_self = place_terms(terms, width, n)
     return (out, grad_input, grad_stale, grad_neigh, grad_self)

time: 195 us -> 193 us (0.990)
  waiting for transfers between devices: 74.5 us -> 72.5 us
    all_to_all x1, waiting for transfers between devices: 10.9 us -> 8.94 us  [per_device(): returned = swap(away)]
where the time goes in v8:
time: 193 us; the launch traced here: 192 us
  waiting for transfers between devices  72.5 us (38%)
  Pallas kernels  62.9 us (33%)
  starting transfers between devices  48 us (25%)
  local copies, waits for them, and re-layouts  7.93 us (4%)
    ppermute x15, waiting for transfers between devices, exchange(): lax.ppermute(pieces[s], 'rep', [(i, (i + s) % n) for i in range(n)])  33.9 us
    all_to_all x1, waiting for transfers between devices, per_device(): halo = swap(packed)  29.7 us
    ppermute x15, starting transfers between devices, exchange(): lax.ppermute(pieces[s], 'rep', [(i, (i + s) % n) for i in range(n)])  16.7 us
    pallas_call x1, Pallas kernels, gather_rows(): pl.pallas_call(gather_kernel, grid=(peers // size,), in_specs=[pl.BlockSp...  13 us
    pallas_call x1, Pallas kernels, scatter_rows(): pl.pallas_call(scatter_kernel, grid=(peers // size,), in_specs=[pl.BlockS...  12.5 us
    pallas_call x1, Pallas kernels, spmm(): pl.pallas_call(functools.partial(spmm_kernel, n=n, start_chunk=start_chun...  11 us
    pallas_call x1, Pallas kernels, spmm_back(): pl.pallas_call(functools.partial(spmm_back_kernel, n=n), grid_spec=pltpu....  10.6 us
    all_to_all x1, starting transfers between devices, per_device(): halo = swap(packed)  9.48 us
  transfers between devices with their start and end apart: 19, of which 9 were waited for; matrix products, arithmetic and copies ran while one was open for 0% of the time, Pallas kernels for 22%

profile of v8, /device:TPU:1, one launch (start us, length us, event | category | flops | bytes accessed | tf_op | source)
XLA Modules:
  0.0 192.2 jit_solution(13768822203303468174)
XLA Ops:
  0.6 13.0 %gather_rows.1.after_ref = bf16[96,128,128]{2,1,0:T(8,128)(2,1)} custom-call(s32[32,384]{1,0:T(8,128)} %bitcast.3, s32[1,32]{1,0:T(1,128)} %counts_ref.3, bf16[3072,128]{1,0:T(8,128)(2,1)} %table_ref.1), custom_call_target="tpu_custom_call" | custom-call | flops 9663676416 | bytes 4000000 | tf_op jit(solution)/shard_map/gather_rows/pallas_call | solution.py:84
  13.6 9.5 %all-to-all-start = ((bf16[96,128,128]{2,1,0:T(8,128)(2,1)}), bf16[96,128,128]{2,1,0:T(8,128)(2,1)}, u32[]{:S(2)}, u32[]{:S(2)}) async-start(bf16[96,128,128]{2,1,0:T(8,128)(2,1)} %gather_rows.1.after_ref), calls=%async_computation | async-start | bytes 6291456 | tf_op jit(solution)/shard_map/all_to_all | solution.py:644
  23.1 4.9 %prep.1 = (bf16[24,128,128]{2,1,0:T(8,128)(2,1)}, bf16[512,512]{1,0:T(8,128)(2,1)}, bf16[512,512]{1,0:T(8,128)(2,1)}, bf16[2,768,128]{2,1,0:T(8,128)(2,1)}, bf16...) custom-call(s32[1]{0:T(128)} %bitcast.me_ref, bf16[3072,128]{1,0:T(8,128)(2,1)} %feat_ref.1, ...), custom_call_target="tpu_custom_call" | custom-call | flops 10000000000 | bytes 6000000 | tf_op jit(solution)/shard_map/prep/pallas_call | solution.py:137
  28.0 2.8 %collective-permute-start.3 = (bf16[2,768,128]{2,1,0:T(8,128)(2,1)}, bf16[2,768,128]{2,1,0:T(8,128)(2,1)S(1)}, u32[]{:S(2)}, u32[]{:S(2)}) collective-permute-start(bf16[2,768,128]{2,1,0:T(8,128)(2,1)} %get-tuple-element.43), channel_id=1, source_target_pairs={{0,3},{1,0},{2,1},{3,2},{4,7},{5,4},{6,5},{7,6},{8,11},{9,8},{10,9... | collective-permute-start | bytes 1179656 | tf_op jit(solution)/shard_map/ppermute | solution.py:104
  32.6 29.7 %all-to-all-done.refs_2_ = bf16[96,128,128]{2,1,0:T(8,128)(2,1)} async-done(((bf16[96,128,128]{2,1,0:T(8,128)(2,1)}), bf16[96,128,128]{2,1,0:T(8,128)(2,1)}, u32[]{:S(2)}, u32[]{:S(2)}) %all-to-all-start) | async-done | bytes 3145760 | tf_op jit(solution)/shard_map/all_to_all | solution.py:644
  62.3 11.0 %spmm.1 = (bf16[768,128]{1,0:T(8,128)(2,1)}, bf16[768,128]{1,0:T(8,128)(2,1)}, bf16[768,128]{1,0:T(8,128)(2,1)}, bf16[768,128]{1,0:T(8,128)(2,1)}) custom-call(s32[1]{0:T(128)} %bitcast.me_ref, s32[480]{0:T(512)} %reshape_squeeze.3.pos_ref, bf16[24,20,128,128]{3,2,1,0:T(8,128)(2,1)} %bitcast.5, bf16[24,128,128]{2,1,0:T(8,128)(2,1)} %get-tuple-element.37.refs_1_, ...), custom_call_target="tpu_custom_call" | custom-call | flops 16106127360 | bytes 10000000 | tf_op jit(solution)/shard_map/spmm/pallas_call | solution.py:245
  73.3 2.8 %collective-permute-start = (bf16[768,128]{1,0:T(8,128)(2,1)}, bf16[768,128]{1,0:T(8,128)(2,1)S(1)}, u32[]{:S(2)}, u32[]{:S(2)}) collective-permute-start(bf16[768,128]{1,0:T(8,128)(2,1)} %get-tuple-element.39), channel_id=1, source_target_pairs={{0,3},{1,0},{2,1},{3,2},{4,7},{5,4},{6,5},{7,6},{8,11},{9,8},{10,9... | collective-permute-start | bytes 589832 | tf_op jit(solution)/shard_map/ppermute | solution.py:104
  77.2 4.3 %collective-permute-done.refs_1_ = bf16[768,128]{1,0:T(8,128)(2,1)S(1)} collective-permute-done((bf16[768,128]{1,0:T(8,128)(2,1)}, bf16[768,128]{1,0:T(8,128)(2,1)S(1)}, u32[]{:S(2)}, u32[]{:S(2)}) %collective-permute-start) | collective-permute-done | bytes 196640 | tf_op jit(solution)/shard_map/ppermute | solution.py:104
  82.5 4.8 %collective-permute-done.2.refs_3_ = bf16[768,128]{1,0:T(8,128)(2,1)S(1)} collective-permute-done((bf16[768,128]{1,0:T(8,128)(2,1)}, bf16[768,128]{1,0:T(8,128)(2,1)S(1)}, u32[]{:S(2)}, u32[]{:S(2)}) %collective-permute-start.2) | collective-permute-done | bytes 196640 | tf_op jit(solution)/shard_map/ppermute | solution.py:104
  88.2 6.0 %dense.1 = (bf16[128,768]{1,0:T(8,128)(2,1)S(1)}, bf16[128,768]{1,0:T(8,128)(2,1)S(1)}, bf16[128,768]{1,0:T(8,128)(2,1)S(1)}, bf16[128,768]{1,0:T(8,128)(2,1)S(1...) custom-call(s32[1]{0:T(128)} %bitcast.me_ref, ...), custom_call_target="tpu_custom_call" | custom-call | flops 2013265920 | bytes 9000000 | tf_op jit(solution)/shard_map/dense/pallas_call | solution.py:329
  94.2 7.1 %all-to-all-start.2 = ((bf16[32,4,32,128]{3,2,1,0:T(8,128)(2,1)}), bf16[32,4,32,128]{3,2,1,0:T(8,128)(2,1)S(1)}, u32[]{:S(2)}, u32[]{:S(2)}) async-start(bf16[32,4,32,128]{3,2,1,0:T(8,128)(2,1)} %get-tuple-element.62), calls=%async_computation.2 | async-start | bytes 2097152 | tf_op jit(solution)/shard_map/all_to_all | solution.py:651
  101.4 1.4 collective-permute-start.7
  104.1 9.0 %collective-permute-done.6.refs_2_ = bf16[128,768]{1,0:T(8,128)(2,1)S(1)} collective-permute-done((bf16[128,768]{1,0:T(8,128)(2,1)S(1)}, bf16[128,768]{1,0:T(8,128)(2,1)S(1)}, u32[]{:S(2)}, u32[]{:S(2)}) %collective-permute-start.6) | collective-permute-done | bytes 196640 | tf_op jit(solution)/shard_map/ppermute | solution.py:104
  113.4 10.6 %spmm_back.1 = (f32[24,128,128]{2,1,0:T(8,128)}, bf16[96,128,128]{2,1,0:T(8,128)(2,1)}) custom-call(s32[1]{0:T(128)} %bitcast.me_ref, s32[480]{0:T(512)S(1)} %copy-done.4, bf16[24,20,128,128]{3,2,1,0:T(8,128)(2,1)} %bitcast.6, bf16[128,768]{1,0:T(8,128)(2,1)S(1)} %get-tuple-element.48.refs_1_, bf16[128,768]{1,0:T(8,128)(2,1)S(1)} %collective-permute-done.6.refs_2_, ...), custom_call_target="tpu_custom_call" | custom-call | flops 4026531840 | bytes 22000000 | tf_op jit(solution)/shard_map/spmm_back/pallas_call | solution.py:417
  125.0 8.4 %all-to-all-start.1 = ((bf16[96,128,128]{2,1,0:T(8,128)(2,1)}), bf16[96,128,128]{2,1,0:T(8,128)(2,1)S(1)}, u32[]{:S(2)}, u32[]{:S(2)}) async-start(bf16[96,128,128]{2,1,0:T(8,128)(2,1)} %get-tuple-element.55.after_ref), calls=%async_computation.1 | async-start | bytes 6291456 | tf_op jit(solution)/shard_map/all_to_all | solution.py:654
  133.4 1.9 copy-done
  140.0 3.2 %collective-permute-start.10 = (bf16[2,768,128]{2,1,0:T(8,128)(2,1)S(1)}, bf16[2,768,128]{2,1,0:T(8,128)(2,1)S(1)}, u32[]{:S(2)}, u32[]{:S(2)}) collective-permute-start(bf16[2,768,128]{2,1,0:T(8,128)(2,1)S(1)} %get-tuple-element.58), channel_id=1, source_target_pairs={{0,2},{1,3},{2,0},{3,1},{4,6},{5,7},{6,4},{7,5},{8,10},{9,11},{10,... | collective-permute-start | bytes 1179656 | tf_op jit(solution)/shard_map/ppermute | solution.py:104
  143.4 1.5 collective-permute-start.12
  145.4 6.3 %collective-permute-done.9.refs_1_ = bf16[2,768,128]{2,1,0:T(8,128)(2,1)S(1)} collective-permute-done((bf16[2,768,128]{2,1,0:T(8,128)(2,1)S(1)}, bf16[2,768,128]{2,1,0:T(8,128)(2,1)S(1)}, u32[]{:S(2)}, u32[]{:S(2)}) %collective-permute-start.9) | collective-permute-done | bytes 393248 | tf_op jit(solution)/shard_map/ppermute | solution.py:104
  152.6 8.1 %collective-permute-done.10.refs_2_ = bf16[2,768,128]{2,1,0:T(8,128)(2,1)S(1)} collective-permute-done((bf16[2,768,128]{2,1,0:T(8,128)(2,1)S(1)}, bf16[2,768,128]{2,1,0:T(8,128)(2,1)S(1)}, u32[]{:S(2)}, u32[]{:S(2)}) %collective-permute-start.10) | collective-permute-done | bytes 393248 | tf_op jit(solution)/shard_map/ppermute | solution.py:104
  160.7 2.1 %finish.1 = (bf16[3072,128]{1,0:T(8,128)(2,1)}, bf16[3072,128]{1,0:T(8,128)(2,1)}) custom-call(s32[1]{0:T(128)} %bitcast.me_ref, f32[24,128,128]{2,1,0:T(8,128)S(1)} %copy-done.3, bf16[2,768,128]{2,1,0:T(8,128)(2,1)S(1)} %get-tuple-element.56.refs_0_, bf16[2,768,128]{2,1,0:T(8,128)(2,1)S(1)} %collective-permute-done.9.refs_1_, ...), custom_call_target="tpu_custom_call" | custom-call | flops 1000000 | bytes 7000000 | tf_op jit(solution)/shard_map/finish/pallas_call | solution.py:487
  163.6 8.9 %all-to-all-done.1.val_ref.after_ref = bf16[96,128,128]{2,1,0:T(8,128)(2,1)S(1)} async-done(((bf16[96,128,128]{2,1,0:T(8,128)(2,1)}), bf16[96,128,128]{2,1,0:T(8,128)(2,1)S(1)}, u32[]{:S(2)}, u32[]{:S(2)}) %all-to-all-start.1) | async-done | bytes 3145760 | tf_op jit(solution)/shard_map/all_to_all | solution.py:654
  172.5 6.4 %all-to-all-start.3 = ((bf16[32,32,128]{2,1,0:T(8,128)(2,1)}), bf16[32,32,128]{2,1,0:T(8,128)(2,1)S(1)}, u32[]{:S(2)}, u32[]{:S(2)}) async-start(bf16[32,32,128]{2,1,0:T(8,128)(2,1)} %tie.1), calls=%async_computation.3 | async-start | bytes 524288 | tf_op jit(solution)/shard_map/all_to_all | solution.py:659
  178.9 12.5 %scatter_rows.1 = f32[3072,128]{1,0:T(8,128)} custom-call(s32[32,384]{1,0:T(8,128)S(1)} %bitcast.4, s32[1,32]{1,0:T(1,128)S(1)} %copy-done.6, bf16[96,128,128]{2,1,0:T(8,128)(2,1)S(1)} %all-to-all-done.1.val_ref.after_ref), custom_call_target="tpu_custom_call" | custom-call | flops 38654705664 | bytes 4000000 | tf_op jit(solution)/shard_map/scatter_rows/pallas_call | solution.py:532
  (58 shorter events, 15.1 us)
Async XLA Ops:
  13.6 48.7 %all-to-all-start = ((bf16[96,128,128]{2,1,0:T(8,128)(2,1)}), bf16[96,128,128]{2,1,0:T(8,128)(2,1)}, u32[]{:S(2)}, u32[]{:S(2)}) async-start(bf16[96,128,128]{2,1,0:T(8,128)(2,1)} %gather_rows.1.after_ref), calls=%async_computation | async-start | bytes 6291456 | tf_op jit(solution)/shard_map/all_to_all | solution.py:644
  28.0 48.5 %collective-permute-start.3 = (bf16[2,768,128]{2,1,0:T(8,128)(2,1)}, bf16[2,768,128]{2,1,0:T(8,128)(2,1)S(1)}, u32[]{:S(2)}, u32[]{:S(2)}) collective-permute-start(bf16[2,768,128]{2,1,0:T(8,128)(2,1)} %get-tuple-element.43), channel_id=1, source_target_pairs={{0,3},{1,0},{2,1},{3,2},{4,7},{5,4},{6,5},{7,6},{8,11},{9,8},{10,9... | collective-permute-start | bytes 1179656 | tf_op jit(solution)/shard_map/ppermute | solution.py:104
  30.8 46.4 %collective-permute-start.4 = (bf16[2,768,128]{2,1,0:T(8,128)(2,1)}, bf16[2,768,128]{2,1,0:T(8,128)(2,1)S(1)}, u32[]{:S(2)}, u32[]{:S(2)}) collective-permute-start(bf16[2,768,128]{2,1,0:T(8,128)(2,1)} %get-tuple-element.44), channel_id=1, source_target_pairs={{0,2},{1,3},{2,0},{3,1},{4,6},{5,7},{6,4},{7,5},{8,10},{9,11},{10,... | collective-permute-start | bytes 1179656 | tf_op jit(solution)/shard_map/ppermute | solution.py:104
  31.2 46.0 %collective-permute-start.5 = (bf16[2,768,128]{2,1,0:T(8,128)(2,1)}, bf16[2,768,128]{2,1,0:T(8,128)(2,1)S(1)}, u32[]{:S(2)}, u32[]{:S(2)}) collective-permute-start(bf16[2,768,128]{2,1,0:T(8,128)(2,1)} %get-tuple-element.45), channel_id=1, source_target_pairs={{0,1},{1,2},{2,3},{3,0},{4,5},{5,6},{6,7},{7,4},{8,9},{9,10},{10,1... | collective-permute-start | bytes 1179656 | tf_op jit(solution)/shard_map/ppermute | solution.py:104
  62.3 24.9 %copy-start.9 = (bf16[512,512]{1,0:T(8,128)(2,1)S(1)}, bf16[512,512]{1,0:T(8,128)(2,1)}, u32[]{:S(2)}) copy-start(bf16[512,512]{1,0:T(8,128)(2,1)} %get-tuple-element.47.refs_9_.ws_ref) | copy-start | bytes 1572868
  62.3 24.9 %copy-start.11 = (bf16[512,512]{1,0:T(8,128)(2,1)S(1)}, bf16[512,512]{1,0:T(8,128)(2,1)}, u32[]{:S(2)}) copy-start(bf16[512,512]{1,0:T(8,128)(2,1)} %get-tuple-element.46.refs_8_) | copy-start | bytes 1572868
  62.3 24.9 %copy-start.12 = (bf16[2,768,128]{2,1,0:T(8,128)(2,1)S(1)}, bf16[2,768,128]{2,1,0:T(8,128)(2,1)}, u32[]{:S(2)}) copy-start(bf16[2,768,128]{2,1,0:T(8,128)(2,1)} %get-tuple-element.42.refs_4_) | copy-start | bytes 1179652
  73.3 8.2 %collective-permute-start = (bf16[768,128]{1,0:T(8,128)(2,1)}, bf16[768,128]{1,0:T(8,128)(2,1)S(1)}, u32[]{:S(2)}, u32[]{:S(2)}) collective-permute-start(bf16[768,128]{1,0:T(8,128)(2,1)} %get-tuple-element.39), channel_id=1, source_target_pairs={{0,3},{1,0},{2,1},{3,2},{4,7},{5,4},{6,5},{7,6},{8,11},{9,8},{10,9... | collective-permute-start | bytes 589832 | tf_op jit(solution)/shard_map/ppermute | solution.py:104
  76.2 6.3 %collective-permute-start.1 = (bf16[768,128]{1,0:T(8,128)(2,1)}, bf16[768,128]{1,0:T(8,128)(2,1)S(1)}, u32[]{:S(2)}, u32[]{:S(2)}) collective-permute-start(bf16[768,128]{1,0:T(8,128)(2,1)} %get-tuple-element.40), channel_id=1, source_target_pairs={{0,2},{1,3},{2,0},{3,1},{4,6},{5,7},{6,4},{7,5},{8,10},{9,11},{10,... | collective-permute-start | bytes 589832 | tf_op jit(solution)/shard_map/ppermute | solution.py:104
  76.5 10.8 %collective-permute-start.2 = (bf16[768,128]{1,0:T(8,128)(2,1)}, bf16[768,128]{1,0:T(8,128)(2,1)S(1)}, u32[]{:S(2)}, u32[]{:S(2)}) collective-permute-start(bf16[768,128]{1,0:T(8,128)(2,1)} %get-tuple-element.41), channel_id=1, source_target_pairs={{0,1},{1,2},{2,3},{3,0},{4,5},{5,6},{6,7},{7,4},{8,9},{9,10},{10,1... | collective-permute-start | bytes 589832 | tf_op jit(solution)/shard_map/ppermute | solution.py:104
  88.2 25.2 %copy-start.4 = (s32[480]{0:T(512)S(1)}, s32[480]{0:T(512)}, u32[]{:S(2)}) copy-start(s32[480]{0:T(512)} %reshape_squeeze.3.pos_ref) | copy-start | bytes 5764
  94.2 29.8 %all-to-all-start.2 = ((bf16[32,4,32,128]{3,2,1,0:T(8,128)(2,1)}), bf16[32,4,32,128]{3,2,1,0:T(8,128)(2,1)S(1)}, u32[]{:S(2)}, u32[]{:S(2)}) async-start(bf16[32,4,32,128]{3,2,1,0:T(8,128)(2,1)} %get-tuple-element.62), calls=%async_computation.2 | async-start | bytes 2097152 | tf_op jit(solution)/shard_map/all_to_all | solution.py:651
  101.3 11.8 %collective-permute-start.6 = (bf16[128,768]{1,0:T(8,128)(2,1)S(1)}, bf16[128,768]{1,0:T(8,128)(2,1)S(1)}, u32[]{:S(2)}, u32[]{:S(2)}) collective-permute-start(bf16[128,768]{1,0:T(8,128)(2,1)S(1)} %get-tuple-element.49), channel_id=1, source_target_pairs={{0,1},{1,2},{2,3},{3,0},{4,5},{5,6},{6,7},{7,4},{8,9},{9,10},{10,1... | collective-permute-start | bytes 589832 | tf_op jit(solution)/shard_map/ppermute | solution.py:104
  101.4 11.7 %collective-permute-start.7 = (bf16[128,768]{1,0:T(8,128)(2,1)S(1)}, bf16[128,768]{1,0:T(8,128)(2,1)S(1)}, u32[]{:S(2)}, u32[]{:S(2)}) collective-permute-start(bf16[128,768]{1,0:T(8,128)(2,1)S(1)} %get-tuple-element.50), channel_id=1, source_target_pairs={{0,2},{1,3},{2,0},{3,1},{4,6},{5,7},{6,4},{7,5},{8,10},{9,11},{10,... | collective-permute-start | bytes 589832 | tf_op jit(solution)/shard_map/ppermute | solution.py:104
  102.8 10.6 %collective-permute-start.8 = (bf16[128,768]{1,0:T(8,128)(2,1)S(1)}, bf16[128,768]{1,0:T(8,128)(2,1)S(1)}, u32[]{:S(2)}, u32[]{:S(2)}) collective-permute-start(bf16[128,768]{1,0:T(8,128)(2,1)S(1)} %get-tuple-element.51), channel_id=1, source_target_pairs={{0,3},{1,0},{2,1},{3,2},{4,7},{5,4},{6,5},{7,6},{8,11},{9,8},{10,9... | collective-permute-start | bytes 589832 | tf_op jit(solution)/shard_map/ppermute | solution.py:104
  125.0 47.5 %all-to-all-start.1 = ((bf16[96,128,128]{2,1,0:T(8,128)(2,1)}), bf16[96,128,128]{2,1,0:T(8,128)(2,1)S(1)}, u32[]{:S(2)}, u32[]{:S(2)}) async-start(bf16[96,128,128]{2,1,0:T(8,128)(2,1)} %get-tuple-element.55.after_ref), calls=%async_computation.1 | async-start | bytes 6291456 | tf_op jit(solution)/shard_map/all_to_all | solution.py:654
  139.8 20.9 %copy-start.3 = (f32[24,128,128]{2,1,0:T(8,128)S(1)}, f32[24,128,128]{2,1,0:T(8,128)}, u32[]{:S(2)}) copy-start(f32[24,128,128]{2,1,0:T(8,128)} %get-tuple-element.52.ext_ref) | copy-start | bytes 4718596
  139.8 11.9 %collective-permute-start.9 = (bf16[2,768,128]{2,1,0:T(8,128)(2,1)S(1)}, bf16[2,768,128]{2,1,0:T(8,128)(2,1)S(1)}, u32[]{:S(2)}, u32[]{:S(2)}) collective-permute-start(bf16[2,768,128]{2,1,0:T(8,128)(2,1)S(1)} %get-tuple-element.57), channel_id=1, source_target_pairs={{0,1},{1,2},{2,3},{3,0},{4,5},{5,6},{6,7},{7,4},{8,9},{9,10},{10,1... | collective-permute-start | bytes 1179656 | tf_op jit(solution)/shard_map/ppermute | solution.py:104
  140.0 20.7 %collective-permute-start.10 = (bf16[2,768,128]{2,1,0:T(8,128)(2,1)S(1)}, bf16[2,768,128]{2,1,0:T(8,128)(2,1)S(1)}, u32[]{:S(2)}, u32[]{:S(2)}) collective-permute-start(bf16[2,768,128]{2,1,0:T(8,128)(2,1)S(1)} %get-tuple-element.58), channel_id=1, source_target_pairs={{0,2},{1,3},{2,0},{3,1},{4,6},{5,7},{6,4},{7,5},{8,10},{9,11},{10,... | collective-permute-start | bytes 1179656 | tf_op jit(solution)/shard_map/ppermute | solution.py:104
  143.3 17.4 %collective-permute-start.11 = (bf16[2,768,128]{2,1,0:T(8,128)(2,1)S(1)}, bf16[2,768,128]{2,1,0:T(8,128)(2,1)S(1)}, u32[]{:S(2)}, u32[]{:S(2)}) collective-permute-start(bf16[2,768,128]{2,1,0:T(8,128)(2,1)S(1)} %get-tuple-element.59), channel_id=1, source_target_pairs={{0,3},{1,0},{2,1},{3,2},{4,7},{5,4},{6,5},{7,6},{8,11},{9,8},{10,9... | collective-permute-start | bytes 1179656 | tf_op jit(solution)/shard_map/ppermute | solution.py:104
  143.4 19.4 %collective-permute-start.12 = (bf16[32,128]{1,0:T(8,128)(2,1)S(1)}, bf16[32,128]{1,0:T(8,128)(2,1)S(1)}, u32[]{:S(2)}, u32[]{:S(2)}) collective-permute-start(bf16[32,128]{1,0:T(8,128)(2,1)S(1)} %get-tuple-element.64), channel_id=1, source_target_pairs={{0,1},{1,2},{2,3},{3,0},{4,5},{5,6},{6,7},{7,4},{8,9},{9,10},{10,1... | collective-permute-start | bytes 24584 | tf_op jit(solution)/shard_map/ppermute | solution.py:104
  144.9 17.9 %collective-permute-start.13 = (bf16[32,128]{1,0:T(8,128)(2,1)S(1)}, bf16[32,128]{1,0:T(8,128)(2,1)S(1)}, u32[]{:S(2)}, u32[]{:S(2)}) collective-permute-start(bf16[32,128]{1,0:T(8,128)(2,1)S(1)} %get-tuple-element.65), channel_id=1, source_target_pairs={{0,2},{1,3},{2,0},{3,1},{4,6},{5,7},{6,4},{7,5},{8,10},{9,11},{10,... | collective-permute-start | bytes 24584 | tf_op jit(solution)/shard_map/ppermute | solution.py:104
  151.7 11.1 %collective-permute-start.14 = (bf16[32,128]{1,0:T(8,128)(2,1)S(1)}, bf16[32,128]{1,0:T(8,128)(2,1)S(1)}, u32[]{:S(2)}, u32[]{:S(2)}) collective-permute-start(bf16[32,128]{1,0:T(8,128)(2,1)S(1)} %get-tuple-element.66), channel_id=1, source_target_pairs={{0,3},{1,0},{2,1},{3,2},{4,7},{5,4},{6,5},{7,6},{8,11},{9,8},{10,9... | collective-permute-start | bytes 24584 | tf_op jit(solution)/shard_map/ppermute | solution.py:104
  172.5 18.8 %all-to-all-start.3 = ((bf16[32,32,128]{2,1,0:T(8,128)(2,1)}), bf16[32,32,128]{2,1,0:T(8,128)(2,1)S(1)}, u32[]{:S(2)}, u32[]{:S(2)}) async-start(bf16[32,32,128]{2,1,0:T(8,128)(2,1)} %tie.1), calls=%async_computation.3 | async-start | bytes 524288 | tf_op jit(solution)/shard_map/all_to_all | solution.py:659
  (10 other events, 56.9 us)

commit v9 on v8

--- a/solution.py
+++ b/solution.py
@@ -163,7 +163,6 @@
 
 
 BLOCKS = 3
-AHEAD = 4
 
 
 def adj_copies(adj_ref, held, sems, inner, chunk_of):
@@ -208,12 +207,8 @@
         copy_of(0).start()
         for copy in copies:
             copy.wait()
-        for k in range(1, AHEAD):
+        for k in range(1, adj_sems.shape[0]):
             copy_of(k).start()
-
-    @pl.when(step + AHEAD < adj_sems.shape[0])
-    def _():
-        copy_of(step + AHEAD).start()
 
     copy_of(step).wait()
     first = (lax.rem(me_ref[0] + start_chunk + chunk, n) * inner + part) * BLOCKS
@@ -363,11 +358,9 @@
 
     @pl.when((chunk == 0) & (part == 0))
     def _():
-        copy_of(0).start()
-        copy_of(1).start()
+        for k in range(adj_sems.shape[0]):
+            copy_of(k).start()
         total[...] = jnp.zeros_like(total)
-        for k in range(2, AHEAD):
-            copy_of(k).start()
 
     for s in range(n):
 
@@ -375,10 +368,6 @@
         def _():
             for k in range(left_ref.shape[0]):
                 left_ref[k] = ga[s][:, k * size : (k + 1) * size]
-
-    @pl.when(step + AHEAD < adj_sems.shape[0])
-    def _():
-        copy_of(step + AHEAD).start()
 
     copy_of(step).wait()
     first = (lax.rem(me_ref[0] + n - chunk, n) * pl.num_programs(1) + part) * BLOCKS
@@ -433,7 +422,7 @@
         ),
         out_shape=[pltpu.HBM((own, TILE, TILE), F32), pltpu.HBM((away, TILE, TILE), BF16)],
         compiler_params=params(52),
-        cost_estimate=cost(2 * row_tiles * per_row * TILE**3 * 2, 2.2e7),
+        cost_estimate=cost(24 * row_tiles * per_row * TILE**3, 2.2e7),
         name="spmm_back",
     )(me, pos, adj, *ga)
 

time: 193 us -> 186 us (0.964)
  starting transfers between devices: 48 us -> 44.7 us
  waiting for transfers between devices: 72.5 us -> 69.5 us
    ppermute x15, waiting for transfers between devices: 33.9 us -> 24.7 us  [exchange(): lax.ppermute(pieces[s], 'rep', [(i, (i + s) % n) for i in range(n)])]
    all_to_all x1, waiting for transfers between devices: 0.01 us -> 5.74 us  [per_device(): terms = swap(terms)]
    all_to_all x1, starting transfers between devices: 8.37 us -> 4.11 us  [per_device(): returned = swap(away)]
  transfers between devices with their start and end apart: 19 -> 19, of which waited for: 9 -> 9; matrix products, arithmetic and copies ran while one was open for 0% -> 0% of each run, Pallas kernels for 22% -> 23%
where the time goes in v9:
time: 186 us
  waiting for transfers between devices  69.5 us (37%)
  Pallas kernels  62.6 us (34%)
  starting transfers between devices  44.7 us (24%)
  local copies, waits for them, and re-layouts  7.94 us (4%)
    all_to_all x1, waiting for transfers between devices, per_device(): halo = swap(packed)  29.7 us
    ppermute x15, waiting for transfers between devices, exchange(): lax.ppermute(pieces[s], 'rep', [(i, (i + s) % n) for i in range(n)])  24.7 us
    ppermute x15, starting transfers between devices, exchange(): lax.ppermute(pieces[s], 'rep', [(i, (i + s) % n) for i in range(n)])  17.1 us
    pallas_call x1, Pallas kernels, gather_rows(): pl.pallas_call(gather_kernel, grid=(peers // size,), in_specs=[pl.BlockSp...  13 us
    pallas_call x1, Pallas kernels, scatter_rows(): pl.pallas_call(scatter_kernel, grid=(peers // size,), in_specs=[pl.BlockS...  12.5 us
    pallas_call x1, Pallas kernels, spmm(): pl.pallas_call(functools.partial(spmm_kernel, n=n, start_chunk=start_chun...  10.7 us
    pallas_call x1, Pallas kernels, spmm_back(): pl.pallas_call(functools.partial(spmm_back_kernel, n=n), grid_spec=pltpu....  10.5 us
    all_to_all x1, starting transfers between devices, per_device(): halo = swap(packed)  9.48 us
  transfers between devices with their start and end apart: 19, of which 9 were waited for; matrix products, arithmetic and copies ran while one was open for 0% of the time, Pallas kernels for 23%

profile of v9, /device:TPU:1, one launch (start us, length us, event | category | flops | bytes accessed | tf_op | source)
XLA Modules:
  0.0 185.6 jit_solution(5410831831957699415)
XLA Ops:
  0.6 13.0 %gather_rows.1.after_ref = bf16[96,128,128]{2,1,0:T(8,128)(2,1)} custom-call(s32[32,384]{1,0:T(8,128)} %bitcast.3, s32[1,32]{1,0:T(1,128)} %counts_ref.3, bf16[3072,128]{1,0:T(8,128)(2,1)} %table_ref.1), custom_call_target="tpu_custom_call" | custom-call | flops 9663676416 | bytes 4000000 | tf_op jit(solution)/shard_map/gather_rows/pallas_call | solution.py:84
  13.6 9.5 %all-to-all-start = ((bf16[96,128,128]{2,1,0:T(8,128)(2,1)}), bf16[96,128,128]{2,1,0:T(8,128)(2,1)}, u32[]{:S(2)}, u32[]{:S(2)}) async-start(bf16[96,128,128]{2,1,0:T(8,128)(2,1)} %gather_rows.1.after_ref), calls=%async_computation | async-start | bytes 6291456 | tf_op jit(solution)/shard_map/all_to_all | solution.py:633
  23.1 4.9 %prep.1 = (bf16[24,128,128]{2,1,0:T(8,128)(2,1)}, bf16[512,512]{1,0:T(8,128)(2,1)}, bf16[512,512]{1,0:T(8,128)(2,1)}, bf16[2,768,128]{2,1,0:T(8,128)(2,1)}, bf16...) custom-call(s32[1]{0:T(128)} %bitcast.me_ref, bf16[3072,128]{1,0:T(8,128)(2,1)} %feat_ref.1, ...), custom_call_target="tpu_custom_call" | custom-call | flops 10000000000 | bytes 6000000 | tf_op jit(solution)/shard_map/prep/pallas_call | solution.py:137
  28.0 2.8 %collective-permute-start.3 = (bf16[2,768,128]{2,1,0:T(8,128)(2,1)}, bf16[2,768,128]{2,1,0:T(8,128)(2,1)S(1)}, u32[]{:S(2)}, u32[]{:S(2)}) collective-permute-start(bf16[2,768,128]{2,1,0:T(8,128)(2,1)} %get-tuple-element.43), channel_id=1, source_target_pairs={{0,3},{1,0},{2,1},{3,2},{4,7},{5,4},{6,5},{7,6},{8,11},{9,8},{10,9... | collective-permute-start | bytes 1179656 | tf_op jit(solution)/shard_map/ppermute | solution.py:104
  32.6 29.7 %all-to-all-done.refs_2_ = bf16[96,128,128]{2,1,0:T(8,128)(2,1)} async-done(((bf16[96,128,128]{2,1,0:T(8,128)(2,1)}), bf16[96,128,128]{2,1,0:T(8,128)(2,1)}, u32[]{:S(2)}, u32[]{:S(2)}) %all-to-all-start) | async-done | bytes 3145760 | tf_op jit(solution)/shard_map/all_to_all | solution.py:633
  62.3 10.7 %spmm.1 = (bf16[768,128]{1,0:T(8,128)(2,1)}, bf16[768,128]{1,0:T(8,128)(2,1)}, bf16[768,128]{1,0:T(8,128)(2,1)}, bf16[768,128]{1,0:T(8,128)(2,1)}) custom-call(s32[1]{0:T(128)} %bitcast.me_ref, s32[480]{0:T(512)} %reshape_squeeze.3.pos_ref, bf16[24,20,128,128]{3,2,1,0:T(8,128)(2,1)} %bitcast.5, bf16[24,128,128]{2,1,0:T(8,128)(2,1)} %get-tuple-element.37.refs_1_, ...), custom_call_target="tpu_custom_call" | custom-call | flops 16106127360 | bytes 10000000 | tf_op jit(solution)/shard_map/spmm/pallas_call | solution.py:240
  73.1 2.8 %collective-permute-start = (bf16[768,128]{1,0:T(8,128)(2,1)}, bf16[768,128]{1,0:T(8,128)(2,1)S(1)}, u32[]{:S(2)}, u32[]{:S(2)}) collective-permute-start(bf16[768,128]{1,0:T(8,128)(2,1)} %get-tuple-element.39), channel_id=1, source_target_pairs={{0,3},{1,0},{2,1},{3,2},{4,7},{5,4},{6,5},{7,6},{8,11},{9,8},{10,9... | collective-permute-start | bytes 589832 | tf_op jit(solution)/shard_map/ppermute | solution.py:104
  77.0 4.3 %collective-permute-done.refs_1_ = bf16[768,128]{1,0:T(8,128)(2,1)S(1)} collective-permute-done((bf16[768,128]{1,0:T(8,128)(2,1)}, bf16[768,128]{1,0:T(8,128)(2,1)S(1)}, u32[]{:S(2)}, u32[]{:S(2)}) %collective-permute-start) | collective-permute-done | bytes 196640 | tf_op jit(solution)/shard_map/ppermute | solution.py:104
  82.2 4.8 %collective-permute-done.2.refs_3_ = bf16[768,128]{1,0:T(8,128)(2,1)S(1)} collective-permute-done((bf16[768,128]{1,0:T(8,128)(2,1)}, bf16[768,128]{1,0:T(8,128)(2,1)S(1)}, u32[]{:S(2)}, u32[]{:S(2)}) %collective-permute-start.2) | collective-permute-done | bytes 196640 | tf_op jit(solution)/shard_map/ppermute | solution.py:104
  88.0 6.0 %dense.1 = (bf16[128,768]{1,0:T(8,128)(2,1)S(1)}, bf16[128,768]{1,0:T(8,128)(2,1)S(1)}, bf16[128,768]{1,0:T(8,128)(2,1)S(1)}, bf16[128,768]{1,0:T(8,128)(2,1)S(1...) custom-call(s32[1]{0:T(128)} %bitcast.me_ref, ...), custom_call_target="tpu_custom_call" | custom-call | flops 2013265920 | bytes 9000000 | tf_op jit(solution)/shard_map/dense/pallas_call | solution.py:324
  94.1 2.6 %collective-permute-start.8 = (bf16[128,768]{1,0:T(8,128)(2,1)S(1)}, bf16[128,768]{1,0:T(8,128)(2,1)S(1)}, u32[]{:S(2)}, u32[]{:S(2)}) collective-permute-start(bf16[128,768]{1,0:T(8,128)(2,1)S(1)} %get-tuple-element.51), channel_id=1, source_target_pairs={{0,3},{1,0},{2,1},{3,2},{4,7},{5,4},{6,5},{7,6},{8,11},{9,8},{10,9... | collective-permute-start | bytes 589832 | tf_op jit(solution)/shard_map/ppermute | solution.py:104
  96.7 7.7 %all-to-all-start.2 = ((bf16[32,4,32,128]{3,2,1,0:T(8,128)(2,1)}), bf16[32,4,32,128]{3,2,1,0:T(8,128)(2,1)S(1)}, u32[]{:S(2)}, u32[]{:S(2)}) async-start(bf16[32,4,32,128]{3,2,1,0:T(8,128)(2,1)} %get-tuple-element.62), calls=%async_computation.2 | async-start | bytes 2097152 | tf_op jit(solution)/shard_map/all_to_all | solution.py:640
  105.3 10.5 %spmm_back.1 = (f32[24,128,128]{2,1,0:T(8,128)}, bf16[96,128,128]{2,1,0:T(8,128)(2,1)}) custom-call(s32[1]{0:T(128)} %bitcast.me_ref, s32[480]{0:T(512)S(1)} %copy-done.4, bf16[24,20,128,128]{3,2,1,0:T(8,128)(2,1)} %bitcast.6, bf16[128,768]{1,0:T(8,128)(2,1)S(1)} %get-tuple-element.48.refs_1_, bf16[128,768]{1,0:T(8,128)(2,1)S(1)} %collective-permute-done.6.refs_2_, ...), custom_call_target="tpu_custom_call" | custom-call | flops 24159191040 | bytes 22000000 | tf_op jit(solution)/shard_map/spmm_back/pallas_call | solution.py:406
  115.8 5.7 %all-to-all-done.2.terms_ref = bf16[32,4,32,128]{3,2,1,0:T(8,128)(2,1)S(1)} async-done(((bf16[32,4,32,128]{3,2,1,0:T(8,128)(2,1)}), bf16[32,4,32,128]{3,2,1,0:T(8,128)(2,1)S(1)}, u32[]{:S(2)}, u32[]{:S(2)}) %all-to-all-start.2) | async-done | bytes 1048608 | tf_op jit(solution)/shard_map/all_to_all | solution.py:640
  122.5 4.1 %all-to-all-start.1 = ((bf16[96,128,128]{2,1,0:T(8,128)(2,1)}), bf16[96,128,128]{2,1,0:T(8,128)(2,1)S(1)}, u32[]{:S(2)}, u32[]{:S(2)}) async-start(bf16[96,128,128]{2,1,0:T(8,128)(2,1)} %get-tuple-element.55.after_ref), calls=%async_computation.1 | async-start | bytes 6291456 | tf_op jit(solution)/shard_map/all_to_all | solution.py:643
  126.6 1.9 %copy-done = bf16[96,128,128]{2,1,0:T(8,128)(2,1)S(1)} copy-done((bf16[96,128,128]{2,1,0:T(8,128)(2,1)S(1)}, bf16[96,128,128]{2,1,0:T(8,128)(2,1)}, u32[]{:S(2)}) %copy-start) | copy-done | bytes 3145752
  133.8 2.2 %collective-permute-start.10 = (bf16[2,768,128]{2,1,0:T(8,128)(2,1)S(1)}, bf16[2,768,128]{2,1,0:T(8,128)(2,1)S(1)}, u32[]{:S(2)}, u32[]{:S(2)}) collective-permute-start(bf16[2,768,128]{2,1,0:T(8,128)(2,1)S(1)} %get-tuple-element.58), channel_id=1, source_target_pairs={{0,2},{1,3},{2,0},{3,1},{4,6},{5,7},{6,4},{7,5},{8,10},{9,11},{10,... | collective-permute-start | bytes 1179656 | tf_op jit(solution)/shard_map/ppermute | solution.py:104
  136.0 2.0 %collective-permute-start.11 = (bf16[2,768,128]{2,1,0:T(8,128)(2,1)S(1)}, bf16[2,768,128]{2,1,0:T(8,128)(2,1)S(1)}, u32[]{:S(2)}, u32[]{:S(2)}) collective-permute-start(bf16[2,768,128]{2,1,0:T(8,128)(2,1)S(1)} %get-tuple-element.59), channel_id=1, source_target_pairs={{0,3},{1,0},{2,1},{3,2},{4,7},{5,4},{6,5},{7,6},{8,11},{9,8},{10,9... | collective-permute-start | bytes 1179656 | tf_op jit(solution)/shard_map/ppermute | solution.py:104
  139.4 5.5 %collective-permute-done.9.refs_1_ = bf16[2,768,128]{2,1,0:T(8,128)(2,1)S(1)} collective-permute-done((bf16[2,768,128]{2,1,0:T(8,128)(2,1)S(1)}, bf16[2,768,128]{2,1,0:T(8,128)(2,1)S(1)}, u32[]{:S(2)}, u32[]{:S(2)}) %collective-permute-start.9) | collective-permute-done | bytes 393248 | tf_op jit(solution)/shard_map/ppermute | solution.py:104
  145.4 8.2 %collective-permute-done.10.refs_2_ = bf16[2,768,128]{2,1,0:T(8,128)(2,1)S(1)} collective-permute-done((bf16[2,768,128]{2,1,0:T(8,128)(2,1)S(1)}, bf16[2,768,128]{2,1,0:T(8,128)(2,1)S(1)}, u32[]{:S(2)}, u32[]{:S(2)}) %collective-permute-start.10) | collective-permute-done | bytes 393248 | tf_op jit(solution)/shard_map/ppermute | solution.py:104
  153.6 2.1 %finish.1 = (bf16[3072,128]{1,0:T(8,128)(2,1)}, bf16[3072,128]{1,0:T(8,128)(2,1)}) custom-call(s32[1]{0:T(128)} %bitcast.me_ref, f32[24,128,128]{2,1,0:T(8,128)S(1)} %copy-done.3, bf16[2,768,128]{2,1,0:T(8,128)(2,1)S(1)} %get-tuple-element.56.refs_0_, bf16[2,768,128]{2,1,0:T(8,128)(2,1)S(1)} %collective-permute-done.9.refs_1_, ...), custom_call_target="tpu_custom_call" | custom-call | flops 1000000 | bytes 7000000 | tf_op jit(solution)/shard_map/finish/pallas_call | solution.py:476
  156.5 9.4 %all-to-all-done.1.val_ref.after_ref = bf16[96,128,128]{2,1,0:T(8,128)(2,1)S(1)} async-done(((bf16[96,128,128]{2,1,0:T(8,128)(2,1)}), bf16[96,128,128]{2,1,0:T(8,128)(2,1)S(1)}, u32[]{:S(2)}, u32[]{:S(2)}) %all-to-all-start.1) | async-done | bytes 3145760 | tf_op jit(solution)/shard_map/all_to_all | solution.py:643
  165.9 6.4 %all-to-all-start.3 = ((bf16[32,32,128]{2,1,0:T(8,128)(2,1)}), bf16[32,32,128]{2,1,0:T(8,128)(2,1)S(1)}, u32[]{:S(2)}, u32[]{:S(2)}) async-start(bf16[32,32,128]{2,1,0:T(8,128)(2,1)} %tie.1), calls=%async_computation.3 | async-start | bytes 524288 | tf_op jit(solution)/shard_map/all_to_all | solution.py:648
  172.3 12.5 %scatter_rows.1 = f32[3072,128]{1,0:T(8,128)} custom-call(s32[32,384]{1,0:T(8,128)S(1)} %bitcast.4, s32[1,32]{1,0:T(1,128)S(1)} %copy-done.6, bf16[96,128,128]{2,1,0:T(8,128)(2,1)S(1)} %all-to-all-done.1.val_ref.after_ref), custom_call_target="tpu_custom_call" | custom-call | flops 38654705664 | bytes 4000000 | tf_op jit(solution)/shard_map/scatter_rows/pallas_call | solution.py:521
  (58 shorter events, 15.6 us)
Async XLA Ops:
  13.6 48.7 %all-to-all-start = ((bf16[96,128,128]{2,1,0:T(8,128)(2,1)}), bf16[96,128,128]{2,1,0:T(8,128)(2,1)}, u32[]{:S(2)}, u32[]{:S(2)}) async-start(bf16[96,128,128]{2,1,0:T(8,128)(2,1)} %gather_rows.1.after_ref), calls=%async_computation | async-start | bytes 6291456 | tf_op jit(solution)/shard_map/all_to_all | solution.py:633
  28.0 48.2 %collective-permute-start.3 = (bf16[2,768,128]{2,1,0:T(8,128)(2,1)}, bf16[2,768,128]{2,1,0:T(8,128)(2,1)S(1)}, u32[]{:S(2)}, u32[]{:S(2)}) collective-permute-start(bf16[2,768,128]{2,1,0:T(8,128)(2,1)} %get-tuple-element.43), channel_id=1, source_target_pairs={{0,3},{1,0},{2,1},{3,2},{4,7},{5,4},{6,5},{7,6},{8,11},{9,8},{10,9... | collective-permute-start | bytes 1179656 | tf_op jit(solution)/shard_map/ppermute | solution.py:104
  30.8 46.1 %collective-permute-start.4 = (bf16[2,768,128]{2,1,0:T(8,128)(2,1)}, bf16[2,768,128]{2,1,0:T(8,128)(2,1)S(1)}, u32[]{:S(2)}, u32[]{:S(2)}) collective-permute-start(bf16[2,768,128]{2,1,0:T(8,128)(2,1)} %get-tuple-element.44), channel_id=1, source_target_pairs={{0,2},{1,3},{2,0},{3,1},{4,6},{5,7},{6,4},{7,5},{8,10},{9,11},{10,... | collective-permute-start | bytes 1179656 | tf_op jit(solution)/shard_map/ppermute | solution.py:104
  31.2 45.8 %collective-permute-start.5 = (bf16[2,768,128]{2,1,0:T(8,128)(2,1)}, bf16[2,768,128]{2,1,0:T(8,128)(2,1)S(1)}, u32[]{:S(2)}, u32[]{:S(2)}) collective-permute-start(bf16[2,768,128]{2,1,0:T(8,128)(2,1)} %get-tuple-element.45), channel_id=1, source_target_pairs={{0,1},{1,2},{2,3},{3,0},{4,5},{5,6},{6,7},{7,4},{8,9},{9,10},{10,1... | collective-permute-start | bytes 1179656 | tf_op jit(solution)/shard_map/ppermute | solution.py:104
  62.3 24.7 %copy-start.9 = (bf16[512,512]{1,0:T(8,128)(2,1)S(1)}, bf16[512,512]{1,0:T(8,128)(2,1)}, u32[]{:S(2)}) copy-start(bf16[512,512]{1,0:T(8,128)(2,1)} %get-tuple-element.47.refs_9_.ws_ref) | copy-start | bytes 1572868
  62.3 24.7 %copy-start.11 = (bf16[512,512]{1,0:T(8,128)(2,1)S(1)}, bf16[512,512]{1,0:T(8,128)(2,1)}, u32[]{:S(2)}) copy-start(bf16[512,512]{1,0:T(8,128)(2,1)} %get-tuple-element.46.refs_8_) | copy-start | bytes 1572868
  62.3 24.7 %copy-start.12 = (bf16[2,768,128]{2,1,0:T(8,128)(2,1)S(1)}, bf16[2,768,128]{2,1,0:T(8,128)(2,1)}, u32[]{:S(2)}) copy-start(bf16[2,768,128]{2,1,0:T(8,128)(2,1)} %get-tuple-element.42.refs_4_) | copy-start | bytes 1179652
  73.1 8.2 %collective-permute-start = (bf16[768,128]{1,0:T(8,128)(2,1)}, bf16[768,128]{1,0:T(8,128)(2,1)S(1)}, u32[]{:S(2)}, u32[]{:S(2)}) collective-permute-start(bf16[768,128]{1,0:T(8,128)(2,1)} %get-tuple-element.39), channel_id=1, source_target_pairs={{0,3},{1,0},{2,1},{3,2},{4,7},{5,4},{6,5},{7,6},{8,11},{9,8},{10,9... | collective-permute-start | bytes 589832 | tf_op jit(solution)/shard_map/ppermute | solution.py:104
  75.9 6.3 %collective-permute-start.1 = (bf16[768,128]{1,0:T(8,128)(2,1)}, bf16[768,128]{1,0:T(8,128)(2,1)S(1)}, u32[]{:S(2)}, u32[]{:S(2)}) collective-permute-start(bf16[768,128]{1,0:T(8,128)(2,1)} %get-tuple-element.40), channel_id=1, source_target_pairs={{0,2},{1,3},{2,0},{3,1},{4,6},{5,7},{6,4},{7,5},{8,10},{9,11},{10,... | collective-permute-start | bytes 589832 | tf_op jit(solution)/shard_map/ppermute | solution.py:104
  76.3 10.8 %collective-permute-start.2 = (bf16[768,128]{1,0:T(8,128)(2,1)}, bf16[768,128]{1,0:T(8,128)(2,1)S(1)}, u32[]{:S(2)}, u32[]{:S(2)}) collective-permute-start(bf16[768,128]{1,0:T(8,128)(2,1)} %get-tuple-element.41), channel_id=1, source_target_pairs={{0,1},{1,2},{2,3},{3,0},{4,5},{5,6},{6,7},{7,4},{8,9},{9,10},{10,1... | collective-permute-start | bytes 589832 | tf_op jit(solution)/shard_map/ppermute | solution.py:104
  94.0 11.3 %collective-permute-start.6 = (bf16[128,768]{1,0:T(8,128)(2,1)S(1)}, bf16[128,768]{1,0:T(8,128)(2,1)S(1)}, u32[]{:S(2)}, u32[]{:S(2)}) collective-permute-start(bf16[128,768]{1,0:T(8,128)(2,1)S(1)} %get-tuple-element.49), channel_id=1, source_target_pairs={{0,1},{1,2},{2,3},{3,0},{4,5},{5,6},{6,7},{7,4},{8,9},{9,10},{10,1... | collective-permute-start | bytes 589832 | tf_op jit(solution)/shard_map/ppermute | solution.py:104
  94.0 11.3 %collective-permute-start.7 = (bf16[128,768]{1,0:T(8,128)(2,1)S(1)}, bf16[128,768]{1,0:T(8,128)(2,1)S(1)}, u32[]{:S(2)}, u32[]{:S(2)}) collective-permute-start(bf16[128,768]{1,0:T(8,128)(2,1)S(1)} %get-tuple-element.50), channel_id=1, source_target_pairs={{0,2},{1,3},{2,0},{3,1},{4,6},{5,7},{6,4},{7,5},{8,10},{9,11},{10,... | collective-permute-start | bytes 589832 | tf_op jit(solution)/shard_map/ppermute | solution.py:104
  94.1 11.2 %collective-permute-start.8 = (bf16[128,768]{1,0:T(8,128)(2,1)S(1)}, bf16[128,768]{1,0:T(8,128)(2,1)S(1)}, u32[]{:S(2)}, u32[]{:S(2)}) collective-permute-start(bf16[128,768]{1,0:T(8,128)(2,1)S(1)} %get-tuple-element.51), channel_id=1, source_target_pairs={{0,3},{1,0},{2,1},{3,2},{4,7},{5,4},{6,5},{7,6},{8,11},{9,8},{10,9... | collective-permute-start | bytes 589832 | tf_op jit(solution)/shard_map/ppermute | solution.py:104
  96.7 24.9 %all-to-all-start.2 = ((bf16[32,4,32,128]{3,2,1,0:T(8,128)(2,1)}), bf16[32,4,32,128]{3,2,1,0:T(8,128)(2,1)S(1)}, u32[]{:S(2)}, u32[]{:S(2)}) async-start(bf16[32,4,32,128]{3,2,1,0:T(8,128)(2,1)} %get-tuple-element.62), calls=%async_computation.2 | async-start | bytes 2097152 | tf_op jit(solution)/shard_map/all_to_all | solution.py:640
  122.5 43.4 %all-to-all-start.1 = ((bf16[96,128,128]{2,1,0:T(8,128)(2,1)}), bf16[96,128,128]{2,1,0:T(8,128)(2,1)S(1)}, u32[]{:S(2)}, u32[]{:S(2)}) async-start(bf16[96,128,128]{2,1,0:T(8,128)(2,1)} %get-tuple-element.55.after_ref), calls=%async_computation.1 | async-start | bytes 6291456 | tf_op jit(solution)/shard_map/all_to_all | solution.py:643
  133.0 20.6 %copy-start.3 = (f32[24,128,128]{2,1,0:T(8,128)S(1)}, f32[24,128,128]{2,1,0:T(8,128)}, u32[]{:S(2)}) copy-start(f32[24,128,128]{2,1,0:T(8,128)} %get-tuple-element.52.ext_ref) | copy-start | bytes 4718596
  133.0 11.8 %collective-permute-start.9 = (bf16[2,768,128]{2,1,0:T(8,128)(2,1)S(1)}, bf16[2,768,128]{2,1,0:T(8,128)(2,1)S(1)}, u32[]{:S(2)}, u32[]{:S(2)}) collective-permute-start(bf16[2,768,128]{2,1,0:T(8,128)(2,1)S(1)} %get-tuple-element.57), channel_id=1, source_target_pairs={{0,1},{1,2},{2,3},{3,0},{4,5},{5,6},{6,7},{7,4},{8,9},{9,10},{10,1... | collective-permute-start | bytes 1179656 | tf_op jit(solution)/shard_map/ppermute | solution.py:104
  133.8 19.7 %collective-permute-start.10 = (bf16[2,768,128]{2,1,0:T(8,128)(2,1)S(1)}, bf16[2,768,128]{2,1,0:T(8,128)(2,1)S(1)}, u32[]{:S(2)}, u32[]{:S(2)}) collective-permute-start(bf16[2,768,128]{2,1,0:T(8,128)(2,1)S(1)} %get-tuple-element.58), channel_id=1, source_target_pairs={{0,2},{1,3},{2,0},{3,1},{4,6},{5,7},{6,4},{7,5},{8,10},{9,11},{10,... | collective-permute-start | bytes 1179656 | tf_op jit(solution)/shard_map/ppermute | solution.py:104
  136.0 17.6 %collective-permute-start.11 = (bf16[2,768,128]{2,1,0:T(8,128)(2,1)S(1)}, bf16[2,768,128]{2,1,0:T(8,128)(2,1)S(1)}, u32[]{:S(2)}, u32[]{:S(2)}) collective-permute-start(bf16[2,768,128]{2,1,0:T(8,128)(2,1)S(1)} %get-tuple-element.59), channel_id=1, source_target_pairs={{0,3},{1,0},{2,1},{3,2},{4,7},{5,4},{6,5},{7,6},{8,11},{9,8},{10,9... | collective-permute-start | bytes 1179656 | tf_op jit(solution)/shard_map/ppermute | solution.py:104
  138.1 17.6 %collective-permute-start.12 = (bf16[32,128]{1,0:T(8,128)(2,1)S(1)}, bf16[32,128]{1,0:T(8,128)(2,1)S(1)}, u32[]{:S(2)}, u32[]{:S(2)}) collective-permute-start(bf16[32,128]{1,0:T(8,128)(2,1)S(1)} %get-tuple-element.64), channel_id=1, source_target_pairs={{0,1},{1,2},{2,3},{3,0},{4,5},{5,6},{6,7},{7,4},{8,9},{9,10},{10,1... | collective-permute-start | bytes 24584 | tf_op jit(solution)/shard_map/ppermute | solution.py:104
  138.2 17.5 %collective-permute-start.13 = (bf16[32,128]{1,0:T(8,128)(2,1)S(1)}, bf16[32,128]{1,0:T(8,128)(2,1)S(1)}, u32[]{:S(2)}, u32[]{:S(2)}) collective-permute-start(bf16[32,128]{1,0:T(8,128)(2,1)S(1)} %get-tuple-element.65), channel_id=1, source_target_pairs={{0,2},{1,3},{2,0},{3,1},{4,6},{5,7},{6,4},{7,5},{8,10},{9,11},{10,... | collective-permute-start | bytes 24584 | tf_op jit(solution)/shard_map/ppermute | solution.py:104
  144.8 10.9 %collective-permute-start.14 = (bf16[32,128]{1,0:T(8,128)(2,1)S(1)}, bf16[32,128]{1,0:T(8,128)(2,1)S(1)}, u32[]{:S(2)}, u32[]{:S(2)}) collective-permute-start(bf16[32,128]{1,0:T(8,128)(2,1)S(1)} %get-tuple-element.66), channel_id=1, source_target_pairs={{0,3},{1,0},{2,1},{3,2},{4,7},{5,4},{6,5},{7,6},{8,11},{9,8},{10,9... | collective-permute-start | bytes 24584 | tf_op jit(solution)/shard_map/ppermute | solution.py:104
  153.6 18.7 %copy-start.6 = (s32[1,32]{1,0:T(1,128)S(1)}, s32[1,32]{1,0:T(1,128)}, u32[]{:S(2)}) copy-start(s32[1,32]{1,0:T(1,128)} %counts_ref.3) | copy-start | bytes 388
  165.9 18.9 %all-to-all-start.3 = ((bf16[32,32,128]{2,1,0:T(8,128)(2,1)}), bf16[32,32,128]{2,1,0:T(8,128)(2,1)S(1)}, u32[]{:S(2)}, u32[]{:S(2)}) async-start(bf16[32,32,128]{2,1,0:T(8,128)(2,1)} %tie.1), calls=%async_computation.3 | async-start | bytes 524288 | tf_op jit(solution)/shard_map/all_to_all | solution.py:648
  (10 other events, 58.0 us)

commit v10 on v9

--- a/solution.py
+++ b/solution.py
@@ -336,7 +336,7 @@
         out_shape=[shape((width, rows), BF16)] * n
         + [pltpu.HBM((rows, full), BF16)] * 2
         + [pltpu.HBM(piece, BF16)],
-        compiler_params=params(24),
+        compiler_params=params(52),
         cost_estimate=cost(10 * rows * full * full, 9e6, rows * full),
         name="dense",
     )(me, *agg, *both, wn, ws)

time: 186 us -> 189 us (1.016)
    unnamed x31 -> x29, local copies, waits for them, and re-layouts: 7.24 us -> 8.89 us
where the time goes in v10:
time: 189 us; the launch traced here: 188 us
  waiting for transfers between devices  69.6 us (37%)
  Pallas kernels  63.8 us (34%)
  starting transfers between devices  44.7 us (24%)
  local copies, waits for them, and re-layouts  9.56 us (5%)
    all_to_all x1, waiting for transfers between devices, per_device(): halo = swap(packed)  29.7 us
    ppermute x15, waiting for transfers between devices, exchange(): lax.ppermute(pieces[s], 'rep', [(i, (i + s) % n) for i in range(n)])  24.7 us
    ppermute x15, starting transfers between devices, exchange(): lax.ppermute(pieces[s], 'rep', [(i, (i + s) % n) for i in range(n)])  17.2 us
    pallas_call x1, Pallas kernels, gather_rows(): pl.pallas_call(gather_kernel, grid=(peers // size,), in_specs=[pl.BlockSp...  13 us
    pallas_call x1, Pallas kernels, scatter_rows(): pl.pallas_call(scatter_kernel, grid=(peers // size,), in_specs=[pl.BlockS...  12.5 us
    pallas_call x1, Pallas kernels, spmm(): pl.pallas_call(functools.partial(spmm_kernel, n=n, start_chunk=start_chun...  10.7 us
    pallas_call x1, Pallas kernels, spmm_back(): pl.pallas_call(functools.partial(spmm_back_kernel, n=n), grid_spec=pltpu....  10.5 us
    all_to_all x1, starting transfers between devices, per_device(): halo = swap(packed)  9.43 us
  transfers between devices with their start and end apart: 19, of which 9 were waited for; matrix products, arithmetic and copies ran while one was open for 0% of the time, Pallas kernels for 23%

profile of v10, /device:TPU:1, one launch (start us, length us, event | category | flops | bytes accessed | tf_op | source)
XLA Modules:
  0.0 188.5 jit_solution(9582484363187850630)
XLA Ops:
  0.6 13.0 %gather_rows.1.after_ref = bf16[96,128,128]{2,1,0:T(8,128)(2,1)} custom-call(s32[32,384]{1,0:T(8,128)} %bitcast.3, s32[1,32]{1,0:T(1,128)} %counts_ref.3, bf16[3072,128]{1,0:T(8,128)(2,1)} %table_ref.1), custom_call_target="tpu_custom_call" | custom-call | flops 9663676416 | bytes 4000000 | tf_op jit(solution)/shard_map/gather_rows/pallas_call | solution.py:84
  13.7 9.4 %all-to-all-start = ((bf16[96,128,128]{2,1,0:T(8,128)(2,1)}), bf16[96,128,128]{2,1,0:T(8,128)(2,1)S(1)}, u32[]{:S(2)}, u32[]{:S(2)}) async-start(bf16[96,128,128]{2,1,0:T(8,128)(2,1)} %gather_rows.1.after_ref), calls=%async_computation | async-start | bytes 6291456 | tf_op jit(solution)/shard_map/all_to_all | solution.py:633
  23.1 4.8 %prep.1 = (bf16[24,128,128]{2,1,0:T(8,128)(2,1)}, bf16[512,512]{1,0:T(8,128)(2,1)}, bf16[512,512]{1,0:T(8,128)(2,1)}, bf16[2,768,128]{2,1,0:T(8,128)(2,1)}, bf16...) custom-call(s32[1]{0:T(128)} %bitcast.me_ref, bf16[3072,128]{1,0:T(8,128)(2,1)} %feat_ref.1, ...), custom_call_target="tpu_custom_call" | custom-call | flops 10000000000 | bytes 6000000 | tf_op jit(solution)/shard_map/prep/pallas_call | solution.py:137
  27.9 2.8 %collective-permute-start.3 = (bf16[2,768,128]{2,1,0:T(8,128)(2,1)}, bf16[2,768,128]{2,1,0:T(8,128)(2,1)}, u32[]{:S(2)}, u32[]{:S(2)}) collective-permute-start(bf16[2,768,128]{2,1,0:T(8,128)(2,1)} %get-tuple-element.43), channel_id=1, source_target_pairs={{0,3},{1,0},{2,1},{3,2},{4,7},{5,4},{6,5},{7,6},{8,11},{9,8},{10,9... | collective-permute-start | bytes 1179656 | tf_op jit(solution)/shard_map/ppermute | solution.py:104
  32.5 29.7 %all-to-all-done.refs_2_ = bf16[96,128,128]{2,1,0:T(8,128)(2,1)S(1)} async-done(((bf16[96,128,128]{2,1,0:T(8,128)(2,1)}), bf16[96,128,128]{2,1,0:T(8,128)(2,1)S(1)}, u32[]{:S(2)}, u32[]{:S(2)}) %all-to-all-start) | async-done | bytes 3145760 | tf_op jit(solution)/shard_map/all_to_all | solution.py:633
  63.9 10.7 %spmm.1 = (bf16[768,128]{1,0:T(8,128)(2,1)}, bf16[768,128]{1,0:T(8,128)(2,1)}, bf16[768,128]{1,0:T(8,128)(2,1)}, bf16[768,128]{1,0:T(8,128)(2,1)}) custom-call(s32[1]{0:T(128)} %bitcast.me_ref, s32[480]{0:T(512)} %reshape_squeeze.3.pos_ref, bf16[24,20,128,128]{3,2,1,0:T(8,128)(2,1)} %bitcast.5, bf16[24,128,128]{2,1,0:T(8,128)(2,1)} %get-tuple-element.37.refs_1_, ...), custom_call_target="tpu_custom_call" | custom-call | flops 16106127360 | bytes 10000000 | tf_op jit(solution)/shard_map/spmm/pallas_call | solution.py:240
  74.7 2.8 %collective-permute-start = (bf16[768,128]{1,0:T(8,128)(2,1)}, bf16[768,128]{1,0:T(8,128)(2,1)S(1)}, u32[]{:S(2)}, u32[]{:S(2)}) collective-permute-start(bf16[768,128]{1,0:T(8,128)(2,1)} %get-tuple-element.39), channel_id=1, source_target_pairs={{0,3},{1,0},{2,1},{3,2},{4,7},{5,4},{6,5},{7,6},{8,11},{9,8},{10,9... | collective-permute-start | bytes 589832 | tf_op jit(solution)/shard_map/ppermute | solution.py:104
  78.5 4.3 %collective-permute-done.refs_1_ = bf16[768,128]{1,0:T(8,128)(2,1)S(1)} collective-permute-done((bf16[768,128]{1,0:T(8,128)(2,1)}, bf16[768,128]{1,0:T(8,128)(2,1)S(1)}, u32[]{:S(2)}, u32[]{:S(2)}) %collective-permute-start) | collective-permute-done | bytes 196640 | tf_op jit(solution)/shard_map/ppermute | solution.py:104
  83.8 4.8 %collective-permute-done.2.refs_3_ = bf16[768,128]{1,0:T(8,128)(2,1)S(1)} collective-permute-done((bf16[768,128]{1,0:T(8,128)(2,1)}, bf16[768,128]{1,0:T(8,128)(2,1)S(1)}, u32[]{:S(2)}, u32[]{:S(2)}) %collective-permute-start.2) | collective-permute-done | bytes 196640 | tf_op jit(solution)/shard_map/ppermute | solution.py:104
  89.5 7.3 %dense.1 = (bf16[128,768]{1,0:T(8,128)(2,1)S(1)}, bf16[128,768]{1,0:T(8,128)(2,1)S(1)}, bf16[128,768]{1,0:T(8,128)(2,1)S(1)}, bf16[128,768]{1,0:T(8,128)(2,1)S(1...) custom-call(s32[1]{0:T(128)} %bitcast.me_ref, ...), custom_call_target="tpu_custom_call" | custom-call | flops 2013265920 | bytes 9000000 | tf_op jit(solution)/shard_map/dense/pallas_call | solution.py:324
  97.0 2.6 %collective-permute-start.8 = (bf16[128,768]{1,0:T(8,128)(2,1)S(1)}, bf16[128,768]{1,0:T(8,128)(2,1)S(1)}, u32[]{:S(2)}, u32[]{:S(2)}) collective-permute-start(bf16[128,768]{1,0:T(8,128)(2,1)S(1)} %get-tuple-element.51), channel_id=1, source_target_pairs={{0,3},{1,0},{2,1},{3,2},{4,7},{5,4},{6,5},{7,6},{8,11},{9,8},{10,9... | collective-permute-start | bytes 589832 | tf_op jit(solution)/shard_map/ppermute | solution.py:104
  99.6 7.7 %all-to-all-start.2 = ((bf16[32,4,32,128]{3,2,1,0:T(8,128)(2,1)}), bf16[32,4,32,128]{3,2,1,0:T(8,128)(2,1)S(1)}, u32[]{:S(2)}, u32[]{:S(2)}) async-start(bf16[32,4,32,128]{3,2,1,0:T(8,128)(2,1)} %get-tuple-element.62), calls=%async_computation.2 | async-start | bytes 2097152 | tf_op jit(solution)/shard_map/all_to_all | solution.py:640
  108.2 10.5 %spmm_back.1 = (f32[24,128,128]{2,1,0:T(8,128)}, bf16[96,128,128]{2,1,0:T(8,128)(2,1)}) custom-call(s32[1]{0:T(128)} %bitcast.me_ref, s32[480]{0:T(512)S(1)} %copy-done.4, bf16[24,20,128,128]{3,2,1,0:T(8,128)(2,1)} %bitcast.6, bf16[128,768]{1,0:T(8,128)(2,1)S(1)} %get-tuple-element.48.refs_1_, bf16[128,768]{1,0:T(8,128)(2,1)S(1)} %collective-permute-done.6.refs_2_, ...), custom_call_target="tpu_custom_call" | custom-call | flops 24159191040 | bytes 22000000 | tf_op jit(solution)/shard_map/spmm_back/pallas_call | solution.py:406
  118.7 5.7 %all-to-all-done.2.terms_ref = bf16[32,4,32,128]{3,2,1,0:T(8,128)(2,1)S(1)} async-done(((bf16[32,4,32,128]{3,2,1,0:T(8,128)(2,1)}), bf16[32,4,32,128]{3,2,1,0:T(8,128)(2,1)S(1)}, u32[]{:S(2)}, u32[]{:S(2)}) %all-to-all-start.2) | async-done | bytes 1048608 | tf_op jit(solution)/shard_map/all_to_all | solution.py:640
  125.4 4.1 %all-to-all-start.1 = ((bf16[96,128,128]{2,1,0:T(8,128)(2,1)}), bf16[96,128,128]{2,1,0:T(8,128)(2,1)S(1)}, u32[]{:S(2)}, u32[]{:S(2)}) async-start(bf16[96,128,128]{2,1,0:T(8,128)(2,1)} %get-tuple-element.55.after_ref), calls=%async_computation.1 | async-start | bytes 6291456 | tf_op jit(solution)/shard_map/all_to_all | solution.py:643
  129.6 1.9 %copy-done = bf16[96,128,128]{2,1,0:T(8,128)(2,1)S(1)} copy-done((bf16[96,128,128]{2,1,0:T(8,128)(2,1)S(1)}, bf16[96,128,128]{2,1,0:T(8,128)(2,1)}, u32[]{:S(2)}) %copy-start) | copy-done | bytes 3145752
  136.7 2.2 %collective-permute-start.10 = (bf16[2,768,128]{2,1,0:T(8,128)(2,1)S(1)}, bf16[2,768,128]{2,1,0:T(8,128)(2,1)S(1)}, u32[]{:S(2)}, u32[]{:S(2)}) collective-permute-start(bf16[2,768,128]{2,1,0:T(8,128)(2,1)S(1)} %get-tuple-element.58), channel_id=1, source_target_pairs={{0,2},{1,3},{2,0},{3,1},{4,6},{5,7},{6,4},{7,5},{8,10},{9,11},{10,... | collective-permute-start | bytes 1179656 | tf_op jit(solution)/shard_map/ppermute | solution.py:104
  138.9 2.0 %collective-permute-start.11 = (bf16[2,768,128]{2,1,0:T(8,128)(2,1)S(1)}, bf16[2,768,128]{2,1,0:T(8,128)(2,1)S(1)}, u32[]{:S(2)}, u32[]{:S(2)}) collective-permute-start(bf16[2,768,128]{2,1,0:T(8,128)(2,1)S(1)} %get-tuple-element.59), channel_id=1, source_target_pairs={{0,3},{1,0},{2,1},{3,2},{4,7},{5,4},{6,5},{7,6},{8,11},{9,8},{10,9... | collective-permute-start | bytes 1179656 | tf_op jit(solution)/shard_map/ppermute | solution.py:104
  142.3 5.5 %collective-permute-done.9.refs_1_ = bf16[2,768,128]{2,1,0:T(8,128)(2,1)S(1)} collective-permute-done((bf16[2,768,128]{2,1,0:T(8,128)(2,1)S(1)}, bf16[2,768,128]{2,1,0:T(8,128)(2,1)S(1)}, u32[]{:S(2)}, u32[]{:S(2)}) %collective-permute-start.9) | collective-permute-done | bytes 393248 | tf_op jit(solution)/shard_map/ppermute | solution.py:104
  148.3 8.2 %collective-permute-done.10.refs_2_ = bf16[2,768,128]{2,1,0:T(8,128)(2,1)S(1)} collective-permute-done((bf16[2,768,128]{2,1,0:T(8,128)(2,1)S(1)}, bf16[2,768,128]{2,1,0:T(8,128)(2,1)S(1)}, u32[]{:S(2)}, u32[]{:S(2)}) %collective-permute-start.10) | collective-permute-done | bytes 393248 | tf_op jit(solution)/shard_map/ppermute | solution.py:104
  156.5 2.1 %finish.1 = (bf16[3072,128]{1,0:T(8,128)(2,1)}, bf16[3072,128]{1,0:T(8,128)(2,1)}) custom-call(s32[1]{0:T(128)} %bitcast.me_ref, f32[24,128,128]{2,1,0:T(8,128)S(1)} %copy-done.3, bf16[2,768,128]{2,1,0:T(8,128)(2,1)S(1)} %get-tuple-element.56.refs_0_, bf16[2,768,128]{2,1,0:T(8,128)(2,1)S(1)} %collective-permute-done.9.refs_1_, ...), custom_call_target="tpu_custom_call" | custom-call | flops 1000000 | bytes 7000000 | tf_op jit(solution)/shard_map/finish/pallas_call | solution.py:476
  159.4 9.4 %all-to-all-done.1.val_ref.after_ref = bf16[96,128,128]{2,1,0:T(8,128)(2,1)S(1)} async-done(((bf16[96,128,128]{2,1,0:T(8,128)(2,1)}), bf16[96,128,128]{2,1,0:T(8,128)(2,1)S(1)}, u32[]{:S(2)}, u32[]{:S(2)}) %all-to-all-start.1) | async-done | bytes 3145760 | tf_op jit(solution)/shard_map/all_to_all | solution.py:643
  168.8 6.4 %all-to-all-start.3 = ((bf16[32,32,128]{2,1,0:T(8,128)(2,1)}), bf16[32,32,128]{2,1,0:T(8,128)(2,1)S(1)}, u32[]{:S(2)}, u32[]{:S(2)}) async-start(bf16[32,32,128]{2,1,0:T(8,128)(2,1)} %tie.1), calls=%async_computation.3 | async-start | bytes 524288 | tf_op jit(solution)/shard_map/all_to_all | solution.py:648
  175.2 12.5 %scatter_rows.1 = f32[3072,128]{1,0:T(8,128)} custom-call(s32[32,384]{1,0:T(8,128)S(1)} %bitcast.4, s32[1,32]{1,0:T(1,128)S(1)} %copy-done.6, bf16[96,128,128]{2,1,0:T(8,128)(2,1)S(1)} %all-to-all-done.1.val_ref.after_ref), custom_call_target="tpu_custom_call" | custom-call | flops 38654705664 | bytes 4000000 | tf_op jit(solution)/shard_map/scatter_rows/pallas_call | solution.py:521
  (56 shorter events, 17.3 us)
Async XLA Ops:
  13.7 48.6 %all-to-all-start = ((bf16[96,128,128]{2,1,0:T(8,128)(2,1)}), bf16[96,128,128]{2,1,0:T(8,128)(2,1)S(1)}, u32[]{:S(2)}, u32[]{:S(2)}) async-start(bf16[96,128,128]{2,1,0:T(8,128)(2,1)} %gather_rows.1.after_ref), calls=%async_computation | async-start | bytes 6291456 | tf_op jit(solution)/shard_map/all_to_all | solution.py:633
  27.9 49.9 %collective-permute-start.3 = (bf16[2,768,128]{2,1,0:T(8,128)(2,1)}, bf16[2,768,128]{2,1,0:T(8,128)(2,1)}, u32[]{:S(2)}, u32[]{:S(2)}) collective-permute-start(bf16[2,768,128]{2,1,0:T(8,128)(2,1)} %get-tuple-element.43), channel_id=1, source_target_pairs={{0,3},{1,0},{2,1},{3,2},{4,7},{5,4},{6,5},{7,6},{8,11},{9,8},{10,9... | collective-permute-start | bytes 1179656 | tf_op jit(solution)/shard_map/ppermute | solution.py:104
  30.7 47.8 %collective-permute-start.4 = (bf16[2,768,128]{2,1,0:T(8,128)(2,1)}, bf16[2,768,128]{2,1,0:T(8,128)(2,1)}, u32[]{:S(2)}, u32[]{:S(2)}) collective-permute-start(bf16[2,768,128]{2,1,0:T(8,128)(2,1)} %get-tuple-element.44), channel_id=1, source_target_pairs={{0,2},{1,3},{2,0},{3,1},{4,6},{5,7},{6,4},{7,5},{8,10},{9,11},{10,... | collective-permute-start | bytes 1179656 | tf_op jit(solution)/shard_map/ppermute | solution.py:104
  31.1 47.4 %collective-permute-start.5 = (bf16[2,768,128]{2,1,0:T(8,128)(2,1)}, bf16[2,768,128]{2,1,0:T(8,128)(2,1)}, u32[]{:S(2)}, u32[]{:S(2)}) collective-permute-start(bf16[2,768,128]{2,1,0:T(8,128)(2,1)} %get-tuple-element.45), channel_id=1, source_target_pairs={{0,1},{1,2},{2,3},{3,0},{4,5},{5,6},{6,7},{7,4},{8,9},{9,10},{10,1... | collective-permute-start | bytes 1179656 | tf_op jit(solution)/shard_map/ppermute | solution.py:104
  63.9 24.7 %copy-start.10 = (bf16[2,768,128]{2,1,0:T(8,128)(2,1)S(1)}, bf16[2,768,128]{2,1,0:T(8,128)(2,1)}, u32[]{:S(2)}) copy-start(bf16[2,768,128]{2,1,0:T(8,128)(2,1)} %get-tuple-element.42.refs_4_) | copy-start | bytes 1179652
  74.7 8.2 %collective-permute-start = (bf16[768,128]{1,0:T(8,128)(2,1)}, bf16[768,128]{1,0:T(8,128)(2,1)S(1)}, u32[]{:S(2)}, u32[]{:S(2)}) collective-permute-start(bf16[768,128]{1,0:T(8,128)(2,1)} %get-tuple-element.39), channel_id=1, source_target_pairs={{0,3},{1,0},{2,1},{3,2},{4,7},{5,4},{6,5},{7,6},{8,11},{9,8},{10,9... | collective-permute-start | bytes 589832 | tf_op jit(solution)/shard_map/ppermute | solution.py:104
  77.5 6.3 %collective-permute-start.1 = (bf16[768,128]{1,0:T(8,128)(2,1)}, bf16[768,128]{1,0:T(8,128)(2,1)S(1)}, u32[]{:S(2)}, u32[]{:S(2)}) collective-permute-start(bf16[768,128]{1,0:T(8,128)(2,1)} %get-tuple-element.40), channel_id=1, source_target_pairs={{0,2},{1,3},{2,0},{3,1},{4,6},{5,7},{6,4},{7,5},{8,10},{9,11},{10,... | collective-permute-start | bytes 589832 | tf_op jit(solution)/shard_map/ppermute | solution.py:104
  77.8 10.8 %collective-permute-start.2 = (bf16[768,128]{1,0:T(8,128)(2,1)}, bf16[768,128]{1,0:T(8,128)(2,1)S(1)}, u32[]{:S(2)}, u32[]{:S(2)}) collective-permute-start(bf16[768,128]{1,0:T(8,128)(2,1)} %get-tuple-element.41), channel_id=1, source_target_pairs={{0,1},{1,2},{2,3},{3,0},{4,5},{5,6},{6,7},{7,4},{8,9},{9,10},{10,1... | collective-permute-start | bytes 589832 | tf_op jit(solution)/shard_map/ppermute | solution.py:104
  89.5 18.7 %copy-start.4 = (s32[480]{0:T(512)S(1)}, s32[480]{0:T(512)}, u32[]{:S(2)}) copy-start(s32[480]{0:T(512)} %reshape_squeeze.3.pos_ref) | copy-start | bytes 5764
  96.9 11.4 %collective-permute-start.6 = (bf16[128,768]{1,0:T(8,128)(2,1)S(1)}, bf16[128,768]{1,0:T(8,128)(2,1)S(1)}, u32[]{:S(2)}, u32[]{:S(2)}) collective-permute-start(bf16[128,768]{1,0:T(8,128)(2,1)S(1)} %get-tuple-element.49), channel_id=1, source_target_pairs={{0,1},{1,2},{2,3},{3,0},{4,5},{5,6},{6,7},{7,4},{8,9},{9,10},{10,1... | collective-permute-start | bytes 589832 | tf_op jit(solution)/shard_map/ppermute | solution.py:104
  96.9 11.3 %collective-permute-start.7 = (bf16[128,768]{1,0:T(8,128)(2,1)S(1)}, bf16[128,768]{1,0:T(8,128)(2,1)S(1)}, u32[]{:S(2)}, u32[]{:S(2)}) collective-permute-start(bf16[128,768]{1,0:T(8,128)(2,1)S(1)} %get-tuple-element.50), channel_id=1, source_target_pairs={{0,2},{1,3},{2,0},{3,1},{4,6},{5,7},{6,4},{7,5},{8,10},{9,11},{10,... | collective-permute-start | bytes 589832 | tf_op jit(solution)/shard_map/ppermute | solution.py:104
  97.0 11.2 %collective-permute-start.8 = (bf16[128,768]{1,0:T(8,128)(2,1)S(1)}, bf16[128,768]{1,0:T(8,128)(2,1)S(1)}, u32[]{:S(2)}, u32[]{:S(2)}) collective-permute-start(bf16[128,768]{1,0:T(8,128)(2,1)S(1)} %get-tuple-element.51), channel_id=1, source_target_pairs={{0,3},{1,0},{2,1},{3,2},{4,7},{5,4},{6,5},{7,6},{8,11},{9,8},{10,9... | collective-permute-start | bytes 589832 | tf_op jit(solution)/shard_map/ppermute | solution.py:104
  99.6 24.8 %all-to-all-start.2 = ((bf16[32,4,32,128]{3,2,1,0:T(8,128)(2,1)}), bf16[32,4,32,128]{3,2,1,0:T(8,128)(2,1)S(1)}, u32[]{:S(2)}, u32[]{:S(2)}) async-start(bf16[32,4,32,128]{3,2,1,0:T(8,128)(2,1)} %get-tuple-element.62), calls=%async_computation.2 | async-start | bytes 2097152 | tf_op jit(solution)/shard_map/all_to_all | solution.py:640
  125.4 43.4 %all-to-all-start.1 = ((bf16[96,128,128]{2,1,0:T(8,128)(2,1)}), bf16[96,128,128]{2,1,0:T(8,128)(2,1)S(1)}, u32[]{:S(2)}, u32[]{:S(2)}) async-start(bf16[96,128,128]{2,1,0:T(8,128)(2,1)} %get-tuple-element.55.after_ref), calls=%async_computation.1 | async-start | bytes 6291456 | tf_op jit(solution)/shard_map/all_to_all | solution.py:643
  135.9 20.6 %copy-start.3 = (f32[24,128,128]{2,1,0:T(8,128)S(1)}, f32[24,128,128]{2,1,0:T(8,128)}, u32[]{:S(2)}) copy-start(f32[24,128,128]{2,1,0:T(8,128)} %get-tuple-element.52.ext_ref) | copy-start | bytes 4718596
  135.9 11.8 %collective-permute-start.9 = (bf16[2,768,128]{2,1,0:T(8,128)(2,1)S(1)}, bf16[2,768,128]{2,1,0:T(8,128)(2,1)S(1)}, u32[]{:S(2)}, u32[]{:S(2)}) collective-permute-start(bf16[2,768,128]{2,1,0:T(8,128)(2,1)S(1)} %get-tuple-element.57), channel_id=1, source_target_pairs={{0,1},{1,2},{2,3},{3,0},{4,5},{5,6},{6,7},{7,4},{8,9},{9,10},{10,1... | collective-permute-start | bytes 1179656 | tf_op jit(solution)/shard_map/ppermute | solution.py:104
  136.7 19.7 %collective-permute-start.10 = (bf16[2,768,128]{2,1,0:T(8,128)(2,1)S(1)}, bf16[2,768,128]{2,1,0:T(8,128)(2,1)S(1)}, u32[]{:S(2)}, u32[]{:S(2)}) collective-permute-start(bf16[2,768,128]{2,1,0:T(8,128)(2,1)S(1)} %get-tuple-element.58), channel_id=1, source_target_pairs={{0,2},{1,3},{2,0},{3,1},{4,6},{5,7},{6,4},{7,5},{8,10},{9,11},{10,... | collective-permute-start | bytes 1179656 | tf_op jit(solution)/shard_map/ppermute | solution.py:104
  138.9 17.6 %collective-permute-start.11 = (bf16[2,768,128]{2,1,0:T(8,128)(2,1)S(1)}, bf16[2,768,128]{2,1,0:T(8,128)(2,1)S(1)}, u32[]{:S(2)}, u32[]{:S(2)}) collective-permute-start(bf16[2,768,128]{2,1,0:T(8,128)(2,1)S(1)} %get-tuple-element.59), channel_id=1, source_target_pairs={{0,3},{1,0},{2,1},{3,2},{4,7},{5,4},{6,5},{7,6},{8,11},{9,8},{10,9... | collective-permute-start | bytes 1179656 | tf_op jit(solution)/shard_map/ppermute | solution.py:104
  141.0 17.6 %collective-permute-start.12 = (bf16[32,128]{1,0:T(8,128)(2,1)S(1)}, bf16[32,128]{1,0:T(8,128)(2,1)S(1)}, u32[]{:S(2)}, u32[]{:S(2)}) collective-permute-start(bf16[32,128]{1,0:T(8,128)(2,1)S(1)} %get-tuple-element.64), channel_id=1, source_target_pairs={{0,1},{1,2},{2,3},{3,0},{4,5},{5,6},{6,7},{7,4},{8,9},{9,10},{10,1... | collective-permute-start | bytes 24584 | tf_op jit(solution)/shard_map/ppermute | solution.py:104
  141.1 17.5 %collective-permute-start.13 = (bf16[32,128]{1,0:T(8,128)(2,1)S(1)}, bf16[32,128]{1,0:T(8,128)(2,1)S(1)}, u32[]{:S(2)}, u32[]{:S(2)}) collective-permute-start(bf16[32,128]{1,0:T(8,128)(2,1)S(1)} %get-tuple-element.65), channel_id=1, source_target_pairs={{0,2},{1,3},{2,0},{3,1},{4,6},{5,7},{6,4},{7,5},{8,10},{9,11},{10,... | collective-permute-start | bytes 24584 | tf_op jit(solution)/shard_map/ppermute | solution.py:104
  147.8 10.9 %collective-permute-start.14 = (bf16[32,128]{1,0:T(8,128)(2,1)S(1)}, bf16[32,128]{1,0:T(8,128)(2,1)S(1)}, u32[]{:S(2)}, u32[]{:S(2)}) collective-permute-start(bf16[32,128]{1,0:T(8,128)(2,1)S(1)} %get-tuple-element.66), channel_id=1, source_target_pairs={{0,3},{1,0},{2,1},{3,2},{4,7},{5,4},{6,5},{7,6},{8,11},{9,8},{10,9... | collective-permute-start | bytes 24584 | tf_op jit(solution)/shard_map/ppermute | solution.py:104
  156.5 18.7 %copy-start.5 = (s32[1,32,384]{2,1,0:T(8,128)S(1)}, s32[1,32,384]{2,1,0:T(8,128)}, u32[]{:S(2)}) copy-start(s32[1,32,384]{2,1,0:T(8,128)} %param.16) | copy-start | bytes 147460
  156.5 18.7 %copy-start.6 = (s32[1,32]{1,0:T(1,128)S(1)}, s32[1,32]{1,0:T(1,128)}, u32[]{:S(2)}) copy-start(s32[1,32]{1,0:T(1,128)} %counts_ref.3) | copy-start | bytes 388
  168.8 18.9 %all-to-all-start.3 = ((bf16[32,32,128]{2,1,0:T(8,128)(2,1)}), bf16[32,32,128]{2,1,0:T(8,128)(2,1)S(1)}, u32[]{:S(2)}, u32[]{:S(2)}) async-start(bf16[32,32,128]{2,1,0:T(8,128)(2,1)} %tie.1), calls=%async_computation.3 | async-start | bytes 524288 | tf_op jit(solution)/shard_map/all_to_all | solution.py:648
  (9 other events, 23.6 us)
